TPU v7x, 32 devices: a whole 2x2x4 slice. The times are simulated.
32 devices in a mesh: dp: 8 (over z, y), head: 4 (over x, core).
Axes of the slice: x: 2, y: 2, z: 4, core: 2. Of those that a mesh axis runs over, the one named last changes fastest.
Arguments:
- tokens: bfloat16 [192, 136, 768], P(('dp', 'head')), may hold values from -6 to 6
- cotangent: bfloat16 [192, 136, 768], P(('dp', 'head')), may hold values from -6 to 6
- ratios: int32 [192], P('dp'), may hold values from 40 to 90, as said below
- patch_index: int32 [192, 136], P('dp'), may hold values from 0 to 224, as said below
- encoder_gains: float32 [2, 2, 768], replicated, may hold values from 0.25 to 1.75
- encoder_attend_in: bfloat16 [2, 768, 3, 768], P(None, None, None, 'head'), may hold values from -0.21875 to 0.21875
- encoder_attend_out: bfloat16 [2, 768, 768], P(None, 'head'), may hold values from -0.625 to 0.625
- encoder_expand: bfloat16 [2, 768, 3072], P(None, None, 'head'), may hold values from -0.21875 to 0.21875
- encoder_reduce: bfloat16 [2, 3072, 768], P(None, 'head'), may hold values from -0.109375 to 0.109375
- uniting_gains: float32 [3, 768], replicated, may hold values from 0.25 to 1.75
- uniting_query: bfloat16 [768, 768], P(None, 'head'), may hold values from -0.21875 to 0.21875
- uniting_pair: bfloat16 [768, 2, 768], P(None, None, 'head'), may hold values from -0.21875 to 0.21875
- uniting_attend_out: bfloat16 [768, 768], P('head'), may hold values from -0.625 to 0.625
- uniting_expand: bfloat16 [768, 3072], P(None, 'head'), may hold values from -0.21875 to 0.21875
- uniting_reduce: bfloat16 [3072, 768], P('head'), may hold values from -0.109375 to 0.109375
Outputs:
- layer_output: bfloat16 [192, 136, 768], P(('dp', 'head'))
- tokens_delta: float32 [192, 136, 768], P(('dp', 'head'))
- encoder_gains_delta: float32 [2, 2, 768], replicated
- encoder_attend_in_delta: float32 [2, 768, 3, 768], P(None, None, None, 'head')
- encoder_attend_out_delta: float32 [2, 768, 768], P(None, 'head')
- encoder_expand_delta: float32 [2, 768, 3072], P(None, None, 'head')
- encoder_reduce_delta: float32 [2, 3072, 768], P(None, 'head')
- uniting_gains_delta: float32 [3, 768], replicated
- uniting_query_delta: float32 [768, 768], P(None, 'head')
- uniting_pair_delta: float32 [768, 2, 768], P(None, None, 'head')
- uniting_attend_out_delta: float32 [768, 768], P('head')
- uniting_expand_delta: float32 [768, 3072], P(None, 'head')
- uniting_reduce_delta: float32 [3072, 768], P('head')
Inputs may be any that keep to these rules, and one draw needn't show every extreme that they name: `ratios`: image i and image i + 96 (its radar partner) have the same ratio; some image has 40 and some 90 in every draw. `patch_index`: patch numbers are distinct within an image and equal for an image and its partner 96 later; only the first 225 * (100 - ratio) // 100 slots of an image are visible, the others are ignored.
All inputs are finite; a program needn't handle non-finite values.
Results may differ from a plain program's by a relative error of at most 0.035.
Values may be sent and summed in bfloat16 or wider, within the bound.
No kernel may reach another device: no remote copies, remote signals or barrier semaphores. Data moves between devices by JAX's collectives and lax.ppermute only.
A program may use at most 320 MiB of HBM per device.

v0:
```python
import jax
import jax.numpy as jnp
from jax import lax
from jax.sharding import PartitionSpec as P

HEADS = 12
HEAD_DIM = 64
GRID = 15
PATCHES = 225
SLOTS = 136


EPSILON = 1e-06
NEGATIVE = -1e30


def from_behind(array, axis, by):
    size = lax.axis_size(axis)
    pairs = [(i, i + by) for i in range(size) if 0 <= i + by < size]
    return lax.ppermute(array, axis, pairs)


def layer_norm(values, gain_vector):
    centered = values - jnp.mean(values, -1, keepdims=True)
    spread = jnp.mean(centered * centered, -1, keepdims=True)
    return centered * lax.rsqrt(spread + EPSILON) * gain_vector


def norm_back(values, gain_vector, incoming):
    unused, pullback = jax.vjp(layer_norm, values, gain_vector)
    delta_values, delta_gain = pullback(incoming)
    return (delta_values, delta_gain)


def gelu_exact(values):
    return jax.nn.gelu(values, approximate=False)


def split_heads(tensor):
    return tensor.reshape(tensor.shape[:-1] + (-1, HEAD_DIM))


def merge_heads(tensor):
    return tensor.reshape(tensor.shape[:-2] + (-1,))


def row_product(operand, weight):
    flattened = operand.reshape(-1, operand.shape[-1])
    result = jnp.dot(flattened, weight, preferred_element_type=jnp.float32)
    return result.reshape(operand.shape[:-1] + (weight.shape[1],))


def back_product(operand, weight):
    flattened = operand.reshape(-1, operand.shape[-1])
    result = lax.dot_general(
        flattened, weight, (((1,), (1,)), ((), ())), preferred_element_type=jnp.float32
    )
    return result.reshape(operand.shape[:-1] + (weight.shape[0],))


def weight_delta(left_side, right_side):
    return lax.dot_general(
        left_side.reshape(-1, left_side.shape[-1]),
        right_side.reshape(-1, right_side.shape[-1]),
        (((0,), (0,)), ((), ())),
        preferred_element_type=jnp.float32,
    )


def spread_rows(values):
    return lax.all_gather(values, "head", axis=0, tiled=True)


def gather_deltas(values):
    return lax.all_gather(values, "head", axis=0, tiled=True)


def branch_sum(gathered, weight):
    return lax.psum_scatter(
        row_product(gathered, weight).astype(jnp.bfloat16), "head", scatter_dimension=0, tiled=True
    ).astype(jnp.float32)


def delta_sum(gathered, weight):
    return lax.psum_scatter(
        back_product(gathered, weight).astype(jnp.bfloat16), "head", scatter_dimension=0, tiled=True
    ).astype(jnp.float32)


def score_block(queries, key_rows, alibi_bias, visible):
    raw_scores = jnp.einsum(
        "bqhd,bkhd->bhqk", queries, key_rows, preferred_element_type=jnp.float32
    )
    raw_scores = raw_scores * HEAD_DIM ** (-0.5) + alibi_bias
    return jnp.where(visible[:, None, None, :], raw_scores, NEGATIVE)


def attend(queries, key_rows, value_rows, alibi_bias, visible):
    scores = score_block(queries, key_rows, alibi_bias, visible)
    row_max = jnp.max(scores, -1, keepdims=True)
    exponent = jnp.exp(scores - row_max)
    row_total = jnp.sum(exponent, -1, keepdims=True)
    weights = (exponent / row_total).astype(jnp.bfloat16)
    mixed_rows = jnp.einsum(
        "bhqk,bkhd->bqhd", weights, value_rows, preferred_element_type=jnp.float32
    )
    return (mixed_rows.astype(jnp.bfloat16), row_max + jnp.log(row_total))


def attend_back(queries, key_rows, value_rows, alibi_bias, visible, log_total, delta_mixed):
    probabilities = jnp.exp(score_block(queries, key_rows, alibi_bias, visible) - log_total)
    weights = probabilities.astype(jnp.bfloat16)
    delta_values = jnp.einsum(
        "bhqk,bqhd->bkhd", weights, delta_mixed, preferred_element_type=jnp.float32
    )
    delta_weights = jnp.einsum(
        "bqhd,bkhd->bhqk", delta_mixed, value_rows, preferred_element_type=jnp.float32
    )
    delta_scores = probabilities * (
        delta_weights - jnp.sum(delta_weights * probabilities, -1, keepdims=True)
    )
    delta_scores = delta_scores.astype(jnp.bfloat16)
    scale_factor = HEAD_DIM ** (-0.5)
    delta_queries = (
        jnp.einsum("bhqk,bkhd->bqhd", delta_scores, key_rows, preferred_element_type=jnp.float32)
        * scale_factor
    )
    delta_keys = (
        jnp.einsum("bhqk,bqhd->bkhd", delta_scores, queries, preferred_element_type=jnp.float32)
        * scale_factor
    )
    return (
        delta_queries.astype(jnp.bfloat16),
        delta_keys.astype(jnp.bfloat16),
        delta_values.astype(jnp.bfloat16),
    )


def attention_forward(inputs, query_rows, pair_rows, output_weight, alibi_bias, visible):
    queries = split_heads(query_rows)
    key_rows = split_heads(pair_rows[:, :, 0])
    value_rows = split_heads(pair_rows[:, :, 1])
    mixed_rows, log_total = attend(queries, key_rows, value_rows, alibi_bias, visible)
    mixed_rows = merge_heads(mixed_rows)
    middle = inputs + branch_sum(mixed_rows, output_weight)
    return (middle, (queries, key_rows, value_rows, mixed_rows, log_total))


def attention_back(delta_middle, output_weight, alibi_bias, visible, stored):
    queries, key_rows, value_rows, mixed_rows, log_total = stored
    delta_branch = gather_deltas(delta_middle.astype(jnp.bfloat16))
    delta_output = weight_delta(mixed_rows, delta_branch)
    delta_mixed = split_heads(back_product(delta_branch, output_weight).astype(jnp.bfloat16))
    delta_queries, delta_keys, delta_values = attend_back(
        queries, key_rows, value_rows, alibi_bias, visible, log_total, delta_mixed
    )
    delta_pair = jnp.stack([merge_heads(delta_keys), merge_heads(delta_values)], 2)
    return (merge_heads(delta_queries), delta_pair, delta_output)


def feed_forward(inputs, gain_vector, expand_weight, reduce_weight):
    normed_rows = spread_rows(layer_norm(inputs, gain_vector).astype(jnp.bfloat16))
    hidden_pre = row_product(normed_rows, expand_weight)
    hidden = gelu_exact(hidden_pre).astype(jnp.bfloat16)
    output = inputs + branch_sum(hidden, reduce_weight)
    return (output, (normed_rows, hidden_pre, hidden))


def feed_back(delta_out, inputs, gain_vector, expand_weight, reduce_weight, stored):
    normed_rows, hidden_pre, hidden = stored
    delta_branch = gather_deltas(delta_out.astype(jnp.bfloat16))
    delta_reduce = weight_delta(hidden, delta_branch)
    delta_hidden = back_product(delta_branch, reduce_weight)
    unused, pullback = jax.vjp(gelu_exact, hidden_pre)
    delta_pre = pullback(delta_hidden)[0].astype(jnp.bfloat16)
    delta_expand = weight_delta(normed_rows, delta_pre)
    delta_normed = delta_sum(delta_pre, expand_weight)
    delta_inputs, delta_gain = norm_back(inputs, gain_vector, delta_normed)
    return (delta_out + delta_inputs, delta_gain, delta_expand, delta_reduce)


def encoder_forward(
    inputs, gains, qkv_weight, output_weight, expand_weight, reduce_weight, alibi_bias, visible
):
    normed_rows = spread_rows(layer_norm(inputs, gains[0]).astype(jnp.bfloat16))
    qkv_rows = row_product(normed_rows, qkv_weight.reshape(qkv_weight.shape[0], -1)).astype(
        jnp.bfloat16
    )
    qkv_rows = qkv_rows.reshape(qkv_rows.shape[:-1] + (3, -1))
    middle, mixing_stored = attention_forward(
        inputs, qkv_rows[:, :, 0], qkv_rows[:, :, 1:], output_weight, alibi_bias, visible
    )
    output, feed_stored = feed_forward(middle, gains[1], expand_weight, reduce_weight)
    return (output, (normed_rows, middle, mixing_stored, feed_stored))


def encoder_back(
    delta_out,
    inputs,
    gains,
    qkv_weight,
    output_weight,
    expand_weight,
    reduce_weight,
    alibi_bias,
    visible,
    stored,
):
    normed_rows, middle, mixing_stored, feed_stored = stored
    delta_middle, delta_gain_two, delta_expand, delta_reduce = feed_back(
        delta_out, middle, gains[1], expand_weight, reduce_weight, feed_stored
    )
    delta_queries, delta_pair, delta_output = attention_back(
        delta_middle, output_weight, alibi_bias, visible, mixing_stored
    )
    delta_rows = jnp.concatenate([delta_queries[:, :, None], delta_pair], 2)
    delta_rows = delta_rows.reshape(delta_rows.shape[:2] + (-1,))
    flat_weight = qkv_weight.reshape(qkv_weight.shape[0], -1)
    delta_qkv = weight_delta(normed_rows, delta_rows).reshape(qkv_weight.shape)
    delta_normed = delta_sum(delta_rows, flat_weight)
    delta_inputs, delta_gain_one = norm_back(inputs, gains[0], delta_normed)
    return (
        delta_middle + delta_inputs,
        jnp.stack([delta_gain_one, delta_gain_two]),
        delta_qkv,
        delta_output,
        delta_expand,
        delta_reduce,
    )


def on_device(
    tokens,
    cotangent,
    ratios,
    patch_index,
    encoder_gains,
    encoder_attend_in,
    encoder_attend_out,
    encoder_expand,
    encoder_reduce,
    uniting_gains,
    uniting_query,
    uniting_pair,
    uniting_attend_out,
    uniting_expand,
    uniting_reduce,
):
    half_axis = lax.axis_size("dp") // 2
    modality = (lax.axis_index("dp") >= half_axis).astype(jnp.int32)
    radar_flag = modality.astype(jnp.float32)
    local_rows = tokens.shape[0]
    row_first = lax.axis_index("head") * local_rows
    counts = PATCHES * (100 - ratios) // 100
    visible = jnp.arange(SLOTS)[None, :] < counts[:, None]
    grid_row = (patch_index // GRID).astype(jnp.float32)
    grid_col = (patch_index % GRID).astype(jnp.float32)
    row_gap = grid_row[:, :, None] - grid_row[:, None, :]
    col_gap = grid_col[:, :, None] - grid_col[:, None, :]
    distance = jnp.sqrt(row_gap * row_gap + col_gap * col_gap)
    own_visible = lax.dynamic_slice_in_dim(visible, row_first, local_rows, 0)
    slopes = 2.0 ** (-8.0 * (jnp.arange(HEADS).astype(jnp.float32) + 1.0) / HEADS)

    def select_slot(stacked):
        return lax.dynamic_index_in_dim(stacked, modality, 0, keepdims=False)

    enc_gains = select_slot(encoder_gains)
    local_heads = HEADS // lax.axis_size("head")
    head_slopes = lax.dynamic_slice_in_dim(
        slopes, lax.axis_index("head") * local_heads, local_heads, 0
    )
    matrices = (
        select_slot(encoder_attend_in),
        select_slot(encoder_attend_out),
        select_slot(encoder_expand),
        select_slot(encoder_reduce),
        uniting_query,
        uniting_pair,
        uniting_attend_out,
        uniting_expand,
        uniting_reduce,
    )
    (
        matrix_attend_in,
        matrix_attend_out,
        matrix_expand,
        matrix_reduce,
        matrix_query,
        matrix_pair,
        matrix_unite_out,
        matrix_unite_expand,
        matrix_unite_reduce,
    ) = matrices
    alibi_bias = -head_slopes[None, :, None, None] * distance[:, None]
    inputs = tokens.astype(jnp.float32)
    encoded, unused_stored = encoder_forward(
        inputs,
        enc_gains,
        matrix_attend_in,
        matrix_attend_out,
        matrix_expand,
        matrix_reduce,
        alibi_bias,
        visible,
    )
    context = layer_norm(encoded, uniting_gains[0]).astype(jnp.bfloat16)
    pair_flat = matrix_pair.reshape(matrix_pair.shape[0], -1)
    arrived = from_behind(context, "dp", half_axis)
    context_rows = spread_rows(arrived)
    pair_rows = row_product(context_rows, pair_flat).astype(jnp.bfloat16)
    pair_rows = pair_rows.reshape(pair_rows.shape[:-1] + (2, -1))
    normed_rows = spread_rows(layer_norm(encoded, uniting_gains[1]).astype(jnp.bfloat16))
    query_rows = row_product(normed_rows, matrix_query).astype(jnp.bfloat16)
    middle, mixing_stored = attention_forward(
        encoded, query_rows, pair_rows, matrix_unite_out, alibi_bias, visible
    )
    combined, feed_stored = feed_forward(
        middle, uniting_gains[2], matrix_unite_expand, matrix_unite_reduce
    )
    row_mask = own_visible.astype(jnp.float32)[:, :, None]
    layer_output = (row_mask * jnp.where(radar_flag > 0.5, combined, encoded)).astype(jnp.bfloat16)
    delta_rows = row_mask * cotangent.astype(jnp.float32)
    delta_combined = radar_flag * delta_rows
    delta_middle, delta_gain_three, delta_fexpand, delta_freduce = feed_back(
        delta_combined,
        middle,
        uniting_gains[2],
        matrix_unite_expand,
        matrix_unite_reduce,
        feed_stored,
    )
    delta_queries, delta_pair, delta_fout = attention_back(
        delta_middle, matrix_unite_out, alibi_bias, visible, mixing_stored
    )
    delta_fquery = weight_delta(normed_rows, delta_queries)
    delta_normed = delta_sum(delta_queries, matrix_query)
    delta_radar, delta_gain_two = norm_back(encoded, uniting_gains[1], delta_normed)
    delta_pair = delta_pair.reshape(delta_pair.shape[:2] + (-1,))
    delta_fpair = weight_delta(context_rows, delta_pair)
    delta_context = delta_sum(delta_pair, pair_flat).astype(jnp.bfloat16)
    returned = from_behind(delta_context, "dp", -half_axis).astype(jnp.float32)
    delta_optical, delta_gain_one = norm_back(encoded, uniting_gains[0], returned)
    delta_encoded = (1.0 - radar_flag) * delta_rows + delta_middle + delta_radar + delta_optical
    again = lax.optimization_barrier((inputs, delta_encoded))[0]
    unused_output, encoder_stored = encoder_forward(
        again,
        enc_gains,
        matrix_attend_in,
        matrix_attend_out,
        matrix_expand,
        matrix_reduce,
        alibi_bias,
        visible,
    )
    delta_inputs, delta_enc_gains, delta_qkv, delta_out, delta_expand, delta_reduce = encoder_back(
        delta_encoded,
        again,
        enc_gains,
        matrix_attend_in,
        matrix_attend_out,
        matrix_expand,
        matrix_reduce,
        alibi_bias,
        visible,
        encoder_stored,
    )
    delta_fpair = delta_fpair.reshape(matrix_pair.shape)
    slot_mask = (jnp.arange(2) == modality).astype(jnp.float32)

    def into_slot(gradient_part):
        return slot_mask.reshape((2,) + (1,) * gradient_part.ndim) * gradient_part[None]

    summed = (
        lax.psum(into_slot(delta_qkv).astype(jnp.bfloat16), "dp").astype(jnp.float32),
        lax.psum(into_slot(delta_out).astype(jnp.bfloat16), "dp").astype(jnp.float32),
        lax.psum(into_slot(delta_expand).astype(jnp.bfloat16), "dp").astype(jnp.float32),
        lax.psum(into_slot(delta_reduce).astype(jnp.bfloat16), "dp").astype(jnp.float32),
        lax.psum(delta_fquery.astype(jnp.bfloat16), "dp").astype(jnp.float32),
        lax.psum(delta_fpair.astype(jnp.bfloat16), "dp").astype(jnp.float32),
        lax.psum(delta_fout.astype(jnp.bfloat16), "dp").astype(jnp.float32),
        lax.psum(delta_fexpand.astype(jnp.bfloat16), "dp").astype(jnp.float32),
        lax.psum(delta_freduce.astype(jnp.bfloat16), "dp").astype(jnp.float32),
    )
    gain_totals = lax.psum(
        (into_slot(delta_enc_gains), jnp.stack([delta_gain_one, delta_gain_two, delta_gain_three])),
        ("dp", "head"),
    )
    return (
        layer_output,
        delta_inputs,
        gain_totals[0],
        summed[0],
        summed[1],
        summed[2],
        summed[3],
        gain_totals[1],
        summed[4],
        summed[5],
        summed[6],
        summed[7],
        summed[8],
    )


def solution(mesh):
    return jax.shard_map(
        on_device,
        mesh=mesh,
        in_specs=(
            P(("dp", "head"), None, None),
            P(("dp", "head"), None, None),
            P("dp"),
            P("dp", None),
            P(),
            P(None, None, None, "head"),
            P(None, "head", None),
            P(None, None, "head"),
            P(None, "head", None),
            P(),
            P(None, "head"),
            P(None, None, "head"),
            P("head", None),
            P(None, "head"),
            P("head", None),
        ),
        out_specs=(
            P(("dp", "head"), None, None),
            P(("dp", "head"), None, None),
            P(),
            P(None, None, None, "head"),
            P(None, "head", None),
            P(None, None, "head"),
            P(None, "head", None),
            P(),
            P(None, "head"),
            P(None, None, "head"),
            P("head", None),
            P(None, "head"),
            P("head", None),
        ),
        check_vma=False,
    )
```

profile of v0, /device:TPU:0, one launch (start us, length us, event | category | flops | bytes accessed | tf_op | source)
XLA Modules:
  0.0 1872.0 jit_solution(18237053665268813379)
XLA Ops:
  19.3 37.7 %all-gather.12.cloned.1.call-done = bf16[24,136,768]{2,1,0:T(8,128)(2,1)} async-done(((bf16[6,136,768]{2,1,0:T(8,128)(2,1)}), bf16[24,136,768]{2,1,0:T(8,128)(2,1)}) %all-gather.12.cloned.1.call-update) | async-done | bytes 5013520 | tf_op jit(solution)/shard_map/all_gather | solution.py:71
  57.0 8.6 convolution_convert_fusion.8
  65.6 14.2 reshape.392
  79.8 16.4 fusion.186
  96.2 8.5 copy.97
  104.7 8.5 copy.96
  121.6 9.5 fusion.188
  141.0 50.0 %reduce-scatter.11.cloned.1.call-done = bf16[6,136,768]{2,1,0:T(8,128)(2,1)} async-done(((bf16[24,136,768]{2,1,0:T(8,128)(2,1)}), bf16[6,136,768]{2,1,0:T(8,128)(2,1)}) %reduce-scatter.11.cloned.1.call-update) | async-done | bytes 1253392 | tf_op jit(solution)/shard_map/reduce_scatter | solution.py:79
  197.2 39.2 %all-gather.14.cloned.1.call-done = bf16[24,136,768]{2,1,0:T(8,128)(2,1)} async-done(((bf16[6,136,768]{2,1,0:T(8,128)(2,1)}), bf16[24,136,768]{2,1,0:T(8,128)(2,1)}) %all-gather.14.cloned.1.call-update) | async-done | bytes 5013520 | tf_op jit(solution)/shard_map/all_gather | solution.py:71
  236.5 9.2 convert_reduce_fusion.5
  245.6 26.9 %fusion.53 = bf16[24,136,768]{2,1,0:T(8,128)(2,1)} fusion(f32[24,136,768]{2,1,0:T(8,128)S(1)} %get-tuple-element.80, u32[136,768]{1,0:T(8,128)S(1)} %get-tuple-element.20, u32[136,768]{1,0:T(8,128)S(1)} %get-tuple-element.19, bf16[2,768,768]{2,1,0:T(8,128)(2,1)S(1)} %copy-done.77, s32[]{:T(128)S(6)} %select_n.57), kind=kOutput, calls=%fused_computation.128 | convolution fusion | flops 4023336960 | bytes 17055748 | tf_op jit(solution)/shard_map/dot_general | solution.py:49
  273.3 49.3 %reduce-scatter.13.cloned.1.call-done = bf16[6,136,768]{2,1,0:T(8,128)(2,1)} async-done(((bf16[24,136,768]{2,1,0:T(8,128)(2,1)}), bf16[6,136,768]{2,1,0:T(8,128)(2,1)}) %reduce-scatter.13.cloned.1.call-update) | async-done | bytes 1253392 | tf_op jit(solution)/shard_map/reduce_scatter | solution.py:79
  334.1 26.1 %collective-permute-done = bf16[6,136,768]{2,1,0:T(8,128)(2,1)} collective-permute-done((bf16[6,136,768]{2,1,0:T(8,128)(2,1)}, bf16[6,136,768]{2,1,0:T(8,128)(2,1)}, u32[]{:S(2)}, u32[]{:S(2)}) %collective-permute-start) | collective-permute-done | bytes 1253408 | tf_op jit(solution)/shard_map/ppermute | solution.py:20
  360.2 11.2 reduce-scatter.15.cloned.1.call-start
  380.6 46.7 %all-gather.16.cloned.1.call-done = bf16[24,136,768]{2,1,0:T(8,128)(2,1)} async-done(((bf16[6,136,768]{2,1,0:T(8,128)(2,1)}), bf16[24,136,768]{2,1,0:T(8,128)(2,1)}) %all-gather.16.cloned.1.call-update) | async-done | bytes 5013520 | tf_op jit(solution)/shard_map/all_gather | solution.py:71
  442.3 9.9 fusion.187
  460.6 8.5 copy.101
  487.0 50.0 %reduce-scatter.15.cloned.1.call-done = bf16[6,136,768]{2,1,0:T(8,128)(2,1)} async-done(((bf16[24,136,768]{2,1,0:T(8,128)(2,1)}), bf16[6,136,768]{2,1,0:T(8,128)(2,1)}) %reduce-scatter.15.cloned.1.call-update) | async-done | bytes 1253392 | tf_op jit(solution)/shard_map/reduce_scatter | solution.py:79
  547.4 36.4 %all-gather.20.cloned.1.call-done = bf16[24,136,768]{2,1,0:T(8,128)(2,1)} async-done(((bf16[6,136,768]{2,1,0:T(8,128)(2,1)}), bf16[24,136,768]{2,1,0:T(8,128)(2,1)}) %all-gather.20.cloned.1.call-update) | async-done | bytes 5013520 | tf_op jit(solution)/shard_map/all_gather | solution.py:71
  583.9 9.7 convert_reduce_fusion.3
  597.9 23.5 %multiply_convert_fusion.3 = (bf16[24,136,768]{2,1,0:T(8,128)(2,1)}, f32[24,136,768]{2,1,0:T(8,128)}) fusion(f32[24,136,768]{2,1,0:T(8,128)S(1)} %get-tuple-element.83, u32[136,768]{1,0:T(8,128)S(1)} %get-tuple-element.18, u32[136,768]{1,0:T(8,128)S(1)} %get-tuple-element.17), kind=kLoop, calls=%fused_computation.52 | loop fusion | flops 170459136 | bytes 25903104 | tf_op jit(solution)/shard_map/convert_element_type | solution.py:164
  625.3 13.6 add_convert_fusion.1
  647.1 50.0 %reduce-scatter.19.cloned.1.call-done = bf16[6,136,768]{2,1,0:T(8,128)(2,1)} async-done(((bf16[24,136,768]{2,1,0:T(8,128)(2,1)}), bf16[6,136,768]{2,1,0:T(8,128)(2,1)}) %reduce-scatter.19.cloned.1.call-update) | async-done | bytes 1253392 | tf_op jit(solution)/shard_map/reduce_scatter | solution.py:85
  705.4 39.0 %all-gather.24.cloned.1.call-done = bf16[24,136,768]{2,1,0:T(8,128)(2,1)} async-done(((bf16[6,136,768]{2,1,0:T(8,128)(2,1)}), bf16[24,136,768]{2,1,0:T(8,128)(2,1)}) %all-gather.24.cloned.1.call-update) | async-done | bytes 5013520 | tf_op jit(solution)/shard_map/all_gather | solution.py:75
  773.1 11.1 multiply_convert_fusion.2
  812.6 9.5 convolution_convert_fusion.6
  822.2 29.9 %reduce-scatter.23.cloned.1.call-done = bf16[6,136,768]{2,1,0:T(8,128)(2,1)} async-done(((bf16[24,136,768]{2,1,0:T(8,128)(2,1)}), bf16[6,136,768]{2,1,0:T(8,128)(2,1)}) %reduce-scatter.23.cloned.1.call-update) | async-done | bytes 1253392 | tf_op jit(solution)/shard_map/reduce_scatter | solution.py:85
  856.4 48.2 %reduce-scatter.21.cloned.1.call-done = bf16[6,136,768]{2,1,0:T(8,128)(2,1)} async-done(((bf16[24,136,768]{2,1,0:T(8,128)(2,1)}), bf16[6,136,768]{2,1,0:T(8,128)(2,1)}) %reduce-scatter.21.cloned.1.call-update) | async-done | bytes 1253392 | tf_op jit(solution)/shard_map/reduce_scatter | solution.py:85
  915.5 41.4 %reduce-scatter.17.cloned.1.call-done = bf16[6,136,768]{2,1,0:T(8,128)(2,1)} async-done(((bf16[24,136,768]{2,1,0:T(8,128)(2,1)}), bf16[6,136,768]{2,1,0:T(8,128)(2,1)}) %reduce-scatter.17.cloned.1.call-update) | async-done | bytes 1253392 | tf_op jit(solution)/shard_map/reduce_scatter | solution.py:79
  976.4 39.1 %all-gather.26.cloned.1.call-done = bf16[24,136,768]{2,1,0:T(8,128)(2,1)} async-done(((bf16[6,136,768]{2,1,0:T(8,128)(2,1)}), bf16[24,136,768]{2,1,0:T(8,128)(2,1)}) %all-gather.26.cloned.1.call-update) | async-done | bytes 5013520 | tf_op jit(solution)/shard_map/all_gather | solution.py:71
  1015.5 8.6 convolution_convert_fusion.7
  1024.1 14.2 reshape.397
  1038.3 16.5 fusion.185
  1063.3 8.5 copy.115
  1098.0 50.0 %reduce-scatter.25.cloned.1.call-done = bf16[6,136,768]{2,1,0:T(8,128)(2,1)} async-done(((bf16[24,136,768]{2,1,0:T(8,128)(2,1)}), bf16[6,136,768]{2,1,0:T(8,128)(2,1)}) %reduce-scatter.25.cloned.1.call-update) | async-done | bytes 1253392 | tf_op jit(solution)/shard_map/reduce_scatter | solution.py:79
  1153.9 38.7 %all-gather.28.cloned.1.call-done = bf16[24,136,768]{2,1,0:T(8,128)(2,1)} async-done(((bf16[6,136,768]{2,1,0:T(8,128)(2,1)}), bf16[24,136,768]{2,1,0:T(8,128)(2,1)}) %all-gather.28.cloned.1.call-update) | async-done | bytes 5013520 | tf_op jit(solution)/shard_map/all_gather | solution.py:71
  1192.5 9.4 convert_reduce_fusion.1
  1206.1 22.2 %fusion.5 = f32[24,136,768]{2,1,0:T(8,128)} fusion(f32[24,136,768]{2,1,0:T(8,128)S(1)} %get-tuple-element.88, u32[136,768]{1,0:T(8,128)S(1)} %get-tuple-element.16, u32[136,768]{1,0:T(8,128)S(1)} %get-tuple-element.15), kind=kLoop, calls=%fused_computation.11 | loop fusion | flops 162938880 | bytes 20889600 | tf_op jit(solution)/shard_map/jvp()/erfc | solution.py:36
  1233.1 13.5 add_convert_fusion
  1254.8 50.0 %reduce-scatter.27.cloned.1.call-done = bf16[6,136,768]{2,1,0:T(8,128)(2,1)} async-done(((bf16[24,136,768]{2,1,0:T(8,128)(2,1)}), bf16[6,136,768]{2,1,0:T(8,128)(2,1)}) %reduce-scatter.27.cloned.1.call-update) | async-done | bytes 1253392 | tf_op jit(solution)/shard_map/reduce_scatter | solution.py:85
  1322.6 9.3 bitcast_convert_fusion.1
  1331.9 20.2 %all-gather.32.cloned.1.call-done = bf16[24,136,768]{2,1,0:T(8,128)(2,1)} async-done(((bf16[6,136,768]{2,1,0:T(8,128)(2,1)}), bf16[24,136,768]{2,1,0:T(8,128)(2,1)}) %all-gather.32.cloned.1.call-update) | async-done | bytes 5013520 | tf_op jit(solution)/shard_map/all_gather | solution.py:75
  1377.0 11.1 multiply_convert_fusion.1
  1409.6 9.3 bitcast_convert_fusion.2
  1473.0 9.0 fusion.94
  1485.3 11.3 reshape_reshape.10
  1515.6 44.4 %all-reduce = (f32[2,2,768]{2,1,0:T(2,128)}, f32[3,768]{1,0:T(4,128)}) all-reduce(f32[2,2,768]{2,1,0:T(2,128)S(1)} %broadcast_multiply_fusion, f32[3,768]{1,0:T(4,128)S(1)} %pad_maximum_fusion.1), channel_id=1, replica_groups=mesh['dp'=8,'head'=4] {'dp','head'}, use_global_device_ids=true, to_apply=%region_42.43 | all-reduce | flops 5376 | bytes 43008 | tf_op jit(solution)/shard_map/psum | solution.py:384
  1565.9 280.3 %all-reduce.4.cloned.1.call-done = (bf16[2,768,3,192]{1,3,2,0:T(8,128)(2,1)}, bf16[2,192,768]{2,1,0:T(8,128)(2,1)}, bf16[2,768,768]{2,1,0:T(8,128)(2,1)}, bf16[2...) async-done(((bf16[2,768,3,192]{1,3,2,0:T(8,128)(2,1)}, ...) | async-done | bytes 10616848 | tf_op jit(solution)/shard_map/psum | solution.py:374
  (369 shorter events, 448.0 us)
Async XLA Ops:
  7.2 229.3 %copy-start = (bf16[2,768,768]{2,1,0:T(8,128)(2,1)S(1)}, bf16[2,768,768]{2,1,0:T(8,128)(2,1)}, u32[]{:S(2)}) copy-start(bf16[2,768,768]{2,1,0:T(8,128)(2,1)} %param.22) | copy-start | bytes 7077892
  7.2 9.2 copy-start.81
  7.2 9.3 copy-start.68
  7.2 49.8 %all-gather.12.cloned.1.call-start = ((), (), s32[]{:S(2)}) async-start(), calls=%async_computation.10 | async-start | bytes 6266880 | tf_op jit(solution)/shard_map/all_gather | solution.py:71
  11.7 183.9 %copy-start.54 = (f32[768]{0:T(1024)}, f32[768]{0:T(1024)S(1)}, u32[]{:S(2)}) copy-start(f32[768]{0:T(1024)S(1)} %get-tuple-element.38) | copy-start | bytes 9220
  15.0 176.0 %reduce-scatter.11.cloned.1.call-start = ((), (), s32[]{:S(2)}) async-start(), calls=%async_computation.11 | async-start | bytes 6266880 | tf_op jit(solution)/shard_map/reduce_scatter | solution.py:79
  15.2 453.9 %copy-start.75 = (f32[3]{0:T(128)}, f32[3]{0:T(128)S(1)}, u32[]{:S(2)}) copy-start(f32[3]{0:T(128)S(1)} %dynamic-slice_negate_fusion) | copy-start | bytes 40
  16.4 49.2 %copy-start.46 = (bf16[1,768,3,192]{1,3,2,0:T(8,128)(2,1)}, bf16[1,768,3,192]{1,3,2,0:T(8,128)(2,1)S(1)}, u32[]{:S(2)}) copy-start(bf16[1,768,3,192]{1,3,2,0:T(8,128)(2,1)S(1)} %constant_dynamic-slice_fusion) | copy-start | bytes 2654212
  141.0 95.5 %all-gather.14.cloned.1.call-start = ((), (), s32[]{:S(2)}) async-start(), calls=%async_computation.12 | async-start | bytes 6266880 | tf_op jit(solution)/shard_map/all_gather | solution.py:71
  197.2 125.4 %reduce-scatter.13.cloned.1.call-start = ((), (), s32[]{:S(2)}) async-start(), calls=%async_computation.13 | async-start | bytes 6266880 | tf_op jit(solution)/shard_map/reduce_scatter | solution.py:79
  236.5 9.2 copy-start.77
  272.6 98.9 %all-gather.18.cloned.1.call-start = ((), (), s32[]{:S(2)}) async-start(), calls=%async_computation.15 | async-start | bytes 6266880 | tf_op jit(solution)/shard_map/all_gather | solution.py:71
  325.3 46.2 %copy-start.51 = (bf16[768,192]{0,1:T(8,128)(2,1)S(1)}, bf16[768,192]{0,1:T(8,128)(2,1)}, u32[]{:S(2)}) copy-start(bf16[768,192]{0,1:T(8,128)(2,1)} %param.25) | copy-start | bytes 884740
  328.7 98.6 %all-gather.16.cloned.1.call-start = ((), (), s32[]{:S(2)}) async-start(), calls=%async_computation.14 | async-start | bytes 6266880 | tf_op jit(solution)/shard_map/all_gather | solution.py:71
  328.7 31.5 %collective-permute-start = (bf16[6,136,768]{2,1,0:T(8,128)(2,1)}, bf16[6,136,768]{2,1,0:T(8,128)(2,1)}, u32[]{:S(2)}, u32[]{:S(2)}) collective-permute-start(bf16[6,136,768]{2,1,0:T(8,128)(2,1)} %get-tuple-element.70), channel_id=1, source_target_pairs={{0,16},{4,20},{8,24},{12,28},{1,17},{5,21},{9,25},{13,29},{2,18},{... | collective-permute-start | bytes 3760136 | tf_op jit(solution)/shard_map/ppermute | solution.py:20
  360.2 67.1 %copy-start.79 = (bf16[768,2,192]{0,2,1:T(8,128)(2,1)S(1)}, bf16[768,2,192]{0,2,1:T(8,128)(2,1)}, u32[]{:S(2)}) copy-start(bf16[768,2,192]{0,2,1:T(8,128)(2,1)} %param.26) | copy-start | bytes 1769476
  360.2 176.8 %reduce-scatter.15.cloned.1.call-start = ((), (), s32[]{:S(2)}) async-start(), calls=%async_computation.16 | async-start | bytes 6266880 | tf_op jit(solution)/shard_map/reduce_scatter | solution.py:79
  487.0 96.9 %all-gather.20.cloned.1.call-start = ((), (), s32[]{:S(2)}) async-start(), calls=%async_computation.17 | async-start | bytes 6266880 | tf_op jit(solution)/shard_map/all_gather | solution.py:71
  544.6 80.7 %all-gather.22.cloned.1.call-start = ((), (), s32[]{:S(2)}) async-start(), calls=%async_computation.19 | async-start | bytes 6266880 | tf_op jit(solution)/shard_map/all_gather | solution.py:75
  547.4 149.7 %reduce-scatter.19.cloned.1.call-start = ((), (), s32[]{:S(2)}) async-start(), calls=%async_computation.20 | async-start | bytes 6266880 | tf_op jit(solution)/shard_map/reduce_scatter | solution.py:85
  625.3 15.9 copy-start.78
  647.1 97.4 %all-gather.24.cloned.1.call-start = ((), (), s32[]{:S(2)}) async-start(), calls=%async_computation.21 | async-start | bytes 6266880 | tf_op jit(solution)/shard_map/all_gather | solution.py:75
  705.2 146.9 %reduce-scatter.23.cloned.1.call-start = ((), (), s32[]{:S(2)}) async-start(), calls=%async_computation.23 | async-start | bytes 6266880 | tf_op jit(solution)/shard_map/reduce_scatter | solution.py:85
  784.2 10.6 copy-start.80
  802.0 102.6 %reduce-scatter.21.cloned.1.call-start = ((), (), s32[]{:S(2)}) async-start(), calls=%async_computation.22 | async-start | bytes 6266880 | tf_op jit(solution)/shard_map/reduce_scatter | solution.py:85
  812.5 144.4 %reduce-scatter.17.cloned.1.call-start = ((), (), s32[]{:S(2)}) async-start(), calls=%async_computation.18 | async-start | bytes 6266880 | tf_op jit(solution)/shard_map/reduce_scatter | solution.py:79
  822.1 193.4 %all-gather.26.cloned.1.call-start = ((), (), s32[]{:S(2)}) async-start(), calls=%async_computation.24 | async-start | bytes 6266880 | tf_op jit(solution)/shard_map/all_gather | solution.py:71
  852.0 59.2 %collective-permute-start.1 = (bf16[6,136,768]{2,1,0:T(8,128)(2,1)}, bf16[6,136,768]{2,1,0:T(8,128)(2,1)}, u32[]{:S(2)}, u32[]{:S(2)}) collective-permute-start(bf16[6,136,768]{2,1,0:T(8,128)(2,1)} %reduce-scatter.23.cloned.1.call-done), channel_id=1, source_target_pairs={{16,0},{20,4},{24,8},{28,12},{17,1},{21,5},{25,9},{29,13},{18,2},{... | collective-permute-start | bytes 3760136 | tf_op jit(solution)/shard_map/ppermute | solution.py:20
  968.7 46.8 %copy-start.47 = (bf16[1,768,3,192]{1,3,2,0:T(8,128)(2,1)S(1)}, bf16[1,768,3,192]{1,3,2,0:T(8,128)(2,1)}, u32[]{:S(2)}) copy-start(bf16[1,768,3,192]{1,3,2,0:T(8,128)(2,1)} %copy-done.46) | copy-start | bytes 2654212
  973.0 51.1 %copy-start.64 = (f32[6,136]{1,0:T(8,128)}, f32[6,136]{1,0:T(8,128)S(1)}, u32[]{:S(2)}) copy-start(f32[6,136]{1,0:T(8,128)S(1)} %multiply_reduce_fusion.3) | copy-start | bytes 9796
  973.1 51.0 %copy-start.62 = (f32[6,136]{1,0:T(8,128)}, f32[6,136]{1,0:T(8,128)S(1)}, u32[]{:S(2)}) copy-start(f32[6,136]{1,0:T(8,128)S(1)} %fusion.134) | copy-start | bytes 9796
  976.2 171.8 %reduce-scatter.25.cloned.1.call-start = ((), (), s32[]{:S(2)}) async-start(), calls=%async_computation.25 | async-start | bytes 6266880 | tf_op jit(solution)/shard_map/reduce_scatter | solution.py:79
  1063.3 16.9 copy-start.76
  1097.9 53.9 %copy-start.55 = (f32[768]{0:T(1024)S(1)}, f32[768]{0:T(1024)}, u32[]{:S(2)}) copy-start(f32[768]{0:T(1024)} %copy-done.54) | copy-start | bytes 9220
  1097.9 94.6 %all-gather.28.cloned.1.call-start = ((), (), s32[]{:S(2)}) async-start(), calls=%async_computation.26 | async-start | bytes 6266880 | tf_op jit(solution)/shard_map/all_gather | solution.py:71
  1153.2 79.9 %all-gather.30.cloned.1.call-start = ((), (), s32[]{:S(2)}) async-start(), calls=%async_computation.27 | async-start | bytes 6266880 | tf_op jit(solution)/shard_map/all_gather | solution.py:75
  1153.8 151.0 %reduce-scatter.27.cloned.1.call-start = ((), (), s32[]{:S(2)}) async-start(), calls=%async_computation.28 | async-start | bytes 6266880 | tf_op jit(solution)/shard_map/reduce_scatter | solution.py:85
  1254.7 97.4 %all-gather.32.cloned.1.call-start = ((), (), s32[]{:S(2)}) async-start(), calls=%async_computation.29 | async-start | bytes 6266880 | tf_op jit(solution)/shard_map/all_gather | solution.py:75
  1312.9 196.9 %reduce-scatter.29.cloned.1.call-start = ((), (), s32[]{:S(2)}) async-start(), calls=%async_computation.30 | async-start | bytes 6266880 | tf_op jit(solution)/shard_map/reduce_scatter | solution.py:85
  1409.4 436.8 %all-reduce.4.cloned.1.call-start = ((), (), s32[]{:S(2)}) async-start(), calls=%async_computation.31 | async-start | bytes 21233664 | tf_op jit(solution)/shard_map/psum | solution.py:374
  1409.6 9.3 copy-start.20
  1433.1 21.5 %slice-start.2 = ((s8[5013504]{0:T(1024)(128)(4,1)}), s8[819200]{0:T(1024)(128)(4,1)S(1)}, s32[]{:S(2)}) async-start(s8[5013504]{0:T(1024)(128)(4,1)} %bitcast.242), calls=%async_computation.34 | async-start | bytes 1638400
  1445.2 9.4 slice-start.3
  1457.6 15.3 slice-start
  1473.0 9.0 copy-start.73
  1509.0 51.0 %copy-start.56 = (f32[768]{0:T(1024)S(1)}, f32[768]{0:T(1024)}, u32[]{:S(2)}) copy-start(f32[768]{0:T(1024)} %copy-done.54) | copy-start | bytes 9220
  1509.0 51.0 %copy-start.61 = (f32[6,136]{1,0:T(8,128)S(1)}, f32[6,136]{1,0:T(8,128)}, u32[]{:S(2)}) copy-start(f32[6,136]{1,0:T(8,128)} %copy-done.60) | copy-start | bytes 9796
  1509.0 51.0 %copy-start.67 = (f32[6,136]{1,0:T(8,128)S(1)}, f32[6,136]{1,0:T(8,128)}, u32[]{:S(2)}) copy-start(f32[6,136]{1,0:T(8,128)} %copy-done.66) | copy-start | bytes 9796
  (64 other events, 261.3 us)
Sparse Core Ops, SparseCore 0:
  15.2 41.8 all-gather.11
  141.1 49.8 reduce-scatter.10
  197.3 39.1 all-gather.13
  272.7 49.8 reduce-scatter.12
  328.8 39.1 all-gather.17
  369.4 57.8 all-gather.15
  487.1 49.8 reduce-scatter.14
  544.7 39.1 all-gather.19
  586.1 39.1 all-gather.21
  647.2 49.8 reduce-scatter.18
  705.3 39.1 all-gather.23
  802.1 49.8 reduce-scatter.22
  854.7 49.8 reduce-scatter.20
  907.0 49.8 reduce-scatter.16
  976.3 39.1 all-gather.25
  1098.1 49.8 reduce-scatter.24
  1153.4 39.1 all-gather.27
  1193.9 39.1 all-gather.29
  1254.9 49.8 reduce-scatter.26
  1313.0 39.1 all-gather.31
  1409.5 49.8 reduce-scatter.28
  1509.1 336.9 all-reduce.3
where the time goes:
time: 1880 us; the launch traced here: 1870 us
  waiting for transfers between devices  1040 us (55%)
  matrix products  311 us (17%)
  local copies, waits for them, and re-layouts  255 us (14%)
  other arithmetic  187 us (10%)
  blocking collectives  44.4 us (2%)
  starting transfers between devices  19.6 us (1%)
    psum x1, waiting for transfers between devices, on_device(): lax.psum(into_slot(delta_qkv).astype(jnp.bfloat16), 'dp')  280 us
    reduce_scatter x5, waiting for transfers between devices, branch_sum(): lax.psum_scatter(row_product(gathered, weight).astype(jnp.bfloat16), 'hea...  241 us
    all_gather x7, waiting for transfers between devices, spread_rows(): return lax.all_gather(values, 'head', axis=0, tiled=True)  238 us
    reduce_scatter x5, waiting for transfers between devices, delta_sum(): lax.psum_scatter(back_product(gathered, weight).astype(jnp.bfloat16), 'he...  178 us
    dot_general x12, matrix products, row_product(): result = jnp.dot(flattened, weight, preferred_element_type=jnp.float32)  106 us
    dot_general x9, matrix products, back_product(): lax.dot_general(flattened, weight, (((1,), (1,)), ((), ())), preferred_el...  68.8 us
    all_gather x4, waiting for transfers between devices, gather_deltas(): return lax.all_gather(values, 'head', axis=0, tiled=True)  67.9 us
    dot_general x9, matrix products, weight_delta(): lax.dot_general(left_side.reshape(-1, left_side.shape[-1]), right_side.re...  57.5 us
  transfers between devices with their start and end apart: 24, of which 22 were waited for; matrix products, arithmetic and copies ran while one was open for 13% of the time, Pallas kernels for 0%

commit v1 on v0

v1 whole, which is shorter than its diff:
```python
import jax
import jax.numpy as jnp
from jax import lax
from jax.experimental import pallas as pl
from jax.experimental.pallas import tpu as pltpu
from jax.sharding import PartitionSpec as P

D = 768
HEADS = 12
HEAD_DIM = 64
GRID = 15
PATCHES = 225
SLOTS = 136
PARTS = 4
CORE, ACROSS = 1, 2

EPSILON = 1e-06
NEGATIVE = -1e30
F32, BF16 = jnp.float32, jnp.bfloat16


def swap(array, dp_mask=0, head_mask=0):
    groups, lanes = lax.axis_size("dp"), lax.axis_size("head")
    pairs = [
        (g * lanes + h, (g ^ dp_mask) * lanes + (h ^ head_mask))
        for g in range(groups)
        for h in range(lanes)
    ]
    return lax.ppermute(array, ("dp", "head"), pairs)


def rows_nt(left, right):
    return lax.dot_general(left, right, (((1,), (1,)), ((), ())), preferred_element_type=F32)


def rows_nn(left, right):
    return lax.dot_general(left, right, (((1,), (0,)), ((), ())), preferred_element_type=F32)


def rows_tn(left, right):
    return lax.dot_general(left, right, (((0,), (0,)), ((), ())), preferred_element_type=F32)


def normalize(values):
    centered = values - jnp.mean(values, -1, keepdims=True)
    spread = lax.rsqrt(jnp.mean(centered * centered, -1, keepdims=True) + EPSILON)
    return centered * spread, spread


def layer_norm(values, gain):
    return normalize(values)[0] * gain


def norm_back(values, gain, incoming):
    unit, spread = normalize(values)
    scaled = incoming * gain
    delta = spread * (
        scaled
        - jnp.mean(scaled, -1, keepdims=True)
        - unit * jnp.mean(scaled * unit, -1, keepdims=True)
    )
    return delta, jnp.sum(incoming * unit, 0)


def gelu_pair(values):
    bell = jnp.exp(-0.5 * values * values) * 0.3989422804014327
    share = 0.5 * (1.0 + lax.erf(values * 0.7071067811865476))
    return (values * share).astype(BF16), (share + values * bell).astype(BF16)


def head_masks(rows):
    lanes = lax.broadcasted_iota(jnp.int32, (rows, 2 * HEAD_DIM), 1)
    return lanes < HEAD_DIM


def two_heads(block, first):
    zero = jnp.zeros_like(block)
    return jnp.concatenate([jnp.where(first, block, zero), jnp.where(first, zero, block)], 0)


def pick_heads(stacked, first):
    rows = stacked.shape[0] // 2
    return jnp.where(first, stacked[:rows], stacked[rows:])


def score_setup(count, key_place, query_place):
    rows = key_place.shape[0]
    row_gap = key_place[:, 0:1] - query_place[0:1, :]
    col_gap = key_place[:, 1:2] - query_place[1:2, :]
    distance = jnp.sqrt(row_gap * row_gap + col_gap * col_gap)
    seen = lax.broadcasted_iota(jnp.int32, (rows, 1), 0) < count
    return distance, seen


def scores_of(queries_two, keys, distance, slope, seen):
    raw = rows_nt(keys, queries_two) - distance * slope
    return jnp.where(seen, raw, NEGATIVE)


def attend_kernel(count, q_ref, k_ref, v_ref, key_place, query_place, slopes, o_ref, lse_ref):
    distance, seen = score_setup(count[pl.program_id(0)], key_place[0], query_place[0])
    first = head_masks(SLOTS)
    for pair in range(q_ref.shape[2] // (2 * HEAD_DIM)):
        span = slice(pair * 2 * HEAD_DIM, (pair + 1) * 2 * HEAD_DIM)
        queries = two_heads(q_ref[0, :, span].astype(F32) * HEAD_DIM**-0.5, first).astype(BF16)
        scores = scores_of(queries, k_ref[0, :, span], distance, slopes[pair : pair + 1, :], seen)
        top = jnp.max(scores, 0, keepdims=True)
        exponent = jnp.exp(scores - top)
        total = jnp.sum(exponent, 0, keepdims=True)
        weights = (exponent * (1.0 / total)).astype(BF16)
        mixed = rows_tn(weights, v_ref[0, :, span])
        o_ref[0, :, span] = pick_heads(mixed, first).astype(BF16)
        lse_ref[0, pair : pair + 1, :] = top + jnp.log(total)


def attend_back_kernel(
    count, q_ref, k_ref, v_ref, e_ref, lse_ref, key_place, query_place, slopes, dq_ref, dkv_ref
):
    distance, seen = score_setup(count[pl.program_id(0)], key_place[0], query_place[0])
    first = head_masks(SLOTS)
    width = q_ref.shape[2]
    scale = HEAD_DIM**-0.5
    for pair in range(width // (2 * HEAD_DIM)):
        low, high = pair * 2 * HEAD_DIM, (pair + 1) * 2 * HEAD_DIM
        queries = two_heads(q_ref[0, :, low:high].astype(F32) * scale, first).astype(BF16)
        incoming = two_heads(e_ref[0, :, low:high].astype(F32), first).astype(BF16)
        keys, values = k_ref[0, :, low:high], v_ref[0, :, low:high]
        scores = scores_of(queries, keys, distance, slopes[pair : pair + 1, :], seen)
        probable = jnp.exp(scores - lse_ref[0, pair : pair + 1, :])
        delta_p = rows_nt(values, incoming)
        inner = jnp.sum(delta_p * probable, 0, keepdims=True)
        delta_s = (probable * (delta_p - inner)).astype(BF16)
        dkv_ref[0, :, low:high] = rows_nn(delta_s, queries).astype(BF16)
        dkv_ref[0, :, width + low : width + high] = rows_nn(
            probable.astype(BF16), incoming
        ).astype(BF16)
        dq_ref[0, :, low:high] = (pick_heads(rows_tn(delta_s, keys), first) * scale).astype(BF16)


def lane_block(width, index):
    return pl.BlockSpec((1, SLOTS, width), lambda i, c, index=index: (i, 0, index))


def place_blocks(pairs):
    return [
        pl.BlockSpec((1, SLOTS, 2), lambda i, c: (i, 0, 0)),
        pl.BlockSpec((1, 2, 2 * SLOTS), lambda i, c: (i, 0, 0)),
        pl.BlockSpec((pairs, 2 * SLOTS), lambda i, c: (0, 0)),
    ]


def attend(q_from, k_from, v_from, width, geometry, slopes):
    counts, key_place, query_place = geometry
    images, pairs = counts.shape[0], width // (2 * HEAD_DIM)
    return pl.pallas_call(
        attend_kernel,
        grid_spec=pltpu.PrefetchScalarGridSpec(
            num_scalar_prefetch=1,
            grid=(images,),
            in_specs=[lane_block(width, part[1]) for part in (q_from, k_from, v_from)]
            + place_blocks(pairs),
            out_specs=[
                pl.BlockSpec((1, SLOTS, width), lambda i, c: (i, 0, 0)),
                pl.BlockSpec((1, pairs, 2 * SLOTS), lambda i, c: (i, 0, 0)),
            ],
        ),
        out_shape=[
            jax.ShapeDtypeStruct((images, SLOTS, width), BF16),
            jax.ShapeDtypeStruct((images, pairs, 2 * SLOTS), F32),
        ],
        cost_estimate=pl.CostEstimate(
            flops=images * pairs * 4 * 2 * SLOTS * SLOTS * 256 * 2,
            bytes_accessed=images * SLOTS * width * 8,
            transcendentals=images * pairs * 2 * SLOTS * SLOTS,
        ),
        name="attend",
    )(counts, q_from[0], k_from[0], v_from[0], key_place, query_place, slopes)


def attend_back(q_from, k_from, v_from, e_from, lse, width, geometry, slopes):
    counts, key_place, query_place = geometry
    images, pairs = counts.shape[0], width // (2 * HEAD_DIM)
    return pl.pallas_call(
        attend_back_kernel,
        grid_spec=pltpu.PrefetchScalarGridSpec(
            num_scalar_prefetch=1,
            grid=(images,),
            in_specs=[lane_block(width, part[1]) for part in (q_from, k_from, v_from, e_from)]
            + [pl.BlockSpec((1, pairs, 2 * SLOTS), lambda i, c: (i, 0, 0))]
            + place_blocks(pairs),
            out_specs=[
                pl.BlockSpec((1, SLOTS, width), lambda i, c: (i, 0, 0)),
                pl.BlockSpec((1, SLOTS, 2 * width), lambda i, c: (i, 0, 0)),
            ],
        ),
        out_shape=[
            jax.ShapeDtypeStruct((images, SLOTS, width), BF16),
            jax.ShapeDtypeStruct((images, SLOTS, 2 * width), BF16),
        ],
        cost_estimate=pl.CostEstimate(
            flops=images * pairs * 10 * 2 * SLOTS * SLOTS * 256 * 2,
            bytes_accessed=images * SLOTS * width * 16,
            transcendentals=images * pairs * 2 * SLOTS * SLOTS,
        ),
        name="attend_back",
    )(
        counts, q_from[0], k_from[0], v_from[0], e_from[0], lse, key_place, query_place, slopes
    )


def relative_parts(parts, own):
    return jnp.stack(
        [lax.dynamic_index_in_dim(parts, r ^ own, 0, keepdims=False) for r in range(PARTS)]
    )


def pack_attend(triple, out_weight, own):
    rows = jnp.concatenate([triple.transpose(1, 2, 0), out_weight[None]], 0)
    kinds = rows.shape[0]
    rows = rows.reshape(kinds, -1, PARTS, HEAD_DIM // PARTS, rows.shape[2])
    return relative_parts(rows.transpose(2, 0, 1, 3, 4), own)


def unpack_attend(parts, own):
    rows = relative_parts(parts, own).transpose(1, 2, 0, 3, 4)
    rows = rows.reshape(rows.shape[0], -1, rows.shape[4])
    return rows[:-1].transpose(2, 0, 1).astype(F32), rows[-1].astype(F32)


def pack_feed(expand, reduce, own):
    rows = jnp.stack([expand.T, reduce])
    rows = rows.reshape(2, PARTS, -1, rows.shape[2])
    return relative_parts(rows.transpose(1, 0, 2, 3), own)


def unpack_feed(parts, own):
    rows = relative_parts(parts, own).transpose(1, 0, 2, 3)
    rows = rows.reshape(2, -1, rows.shape[3])
    return rows[0].T.astype(F32), rows[1].astype(F32)


def fetch(quarter):
    beside = swap(quarter, head_mask=CORE)
    direct = swap(jnp.stack([quarter[0], quarter[3]]), head_mask=ACROSS)
    second = swap(direct[0], dp_mask=1)
    third = swap(direct[0], dp_mask=2)
    across = jnp.stack([direct[0], second, third, direct[1]])
    return (quarter, beside), (across, swap(across, head_mask=CORE))


def attend_rows(half):
    rows = jnp.stack(half).transpose(2, 0, 3, 1, 4, 5)
    return rows.reshape(rows.shape[0], -1, rows.shape[5])


def attend_parts(rows):
    split = rows.reshape(rows.shape[0], 2, -1, PARTS, HEAD_DIM // PARTS, rows.shape[2])
    return split.transpose(1, 3, 0, 2, 4, 5)


def feed_rows(half):
    rows = jnp.stack(half).transpose(2, 0, 1, 3, 4)
    return rows.reshape(2, -1, rows.shape[4])


def feed_parts(rows):
    split = rows.reshape(2, 2, PARTS, -1, rows.shape[2])
    return split.transpose(1, 2, 0, 3, 4)


def reduce_parts(near, far, order):
    received = swap(jnp.stack([near[1], far[1]]), head_mask=CORE)
    kept = jnp.stack([near[0], far[0]]) + received
    for step in order:
        if step == "x":
            kept = kept[:1] + swap(kept[1:], head_mask=ACROSS)
        elif step == "y":
            take = kept.reshape((kept.shape[0], -1, 2) + kept.shape[2:])
            kept = take[:, :, 0] + swap(take[:, :, 1], dp_mask=1)
        else:
            take = kept.reshape((kept.shape[0], 2, -1) + kept.shape[2:])
            kept = take[:, 0] + swap(take[:, 1], dp_mask=2)
    return kept[0, 0]


def gather_parts(part, order):
    if order == "yz":
        pair = jnp.stack([part, swap(part, dp_mask=1)])
        return jnp.concatenate([pair, swap(pair, dp_mask=2)], 0)
    pair = jnp.stack([part, swap(part, dp_mask=2)])
    other = swap(pair, dp_mask=1)
    return jnp.stack([pair[0], other[0], pair[1], other[1]])


def as_images(rows):
    return rows.reshape(-1, SLOTS, rows.shape[-1])


def as_rows(images):
    return images.reshape(-1, images.shape[-1])


def mix_forward(own_rows, side_rows, halves, geometry, slopes):
    total, stored = 0.0, []
    for weights, slope in zip(halves, slopes, strict=True):
        width = weights.shape[1]
        if side_rows is None:
            qkv = rows_nt(own_rows, weights[:3].reshape(-1, D)).astype(BF16)
            qkv = as_images(qkv)
            places = ((qkv, 0), (qkv, 1), (qkv, 2))
        else:
            q = as_images(rows_nt(own_rows, weights[0]).astype(BF16))
            kv = as_images(rows_nt(side_rows, weights[1:3].reshape(-1, D)).astype(BF16))
            places = ((q, 0), (kv, 0), (kv, 1))
        mixed, lse = attend(*places, width, geometry, slope)
        total = total + rows_nn(as_rows(mixed), weights[3])
        stored.append((places, mixed, lse))
    return total, stored


def mix_back(delta, own_rows, side_rows, halves, geometry, slopes, stored):
    delta = delta.astype(BF16)
    delta_own, delta_side, grads = 0.0, 0.0, []
    for weights, slope, (places, mixed, lse) in zip(halves, slopes, stored, strict=True):
        width = weights.shape[1]
        delta_out = rows_tn(as_rows(mixed), delta).astype(BF16)
        delta_mixed = as_images(rows_nt(delta, weights[3]).astype(BF16))
        dq, dkv = attend_back(*places, (delta_mixed, 0), lse, width, geometry, slope)
        dq, dkv = as_rows(dq), as_rows(dkv)
        source = own_rows if side_rows is None else side_rows
        grad_q = rows_tn(dq, own_rows).astype(BF16)
        grad_kv = rows_tn(dkv, source).astype(BF16)
        grads.append(
            attend_parts(
                jnp.concatenate([grad_q[None], grad_kv.reshape(2, width, D), delta_out[None]], 0)
            )
        )
        delta_own = delta_own + rows_nn(dq, weights[0])
        delta_side = delta_side + rows_nn(dkv, weights[1:3].reshape(-1, D))
    return delta_own, delta_side, grads


def feed_forward(normed, halves):
    total, stored = 0.0, []
    for weights in halves:
        hidden, slope = gelu_pair(rows_nt(normed, weights[0]))
        total = total + rows_nn(hidden, weights[1])
        stored.append((hidden, slope))
    return total, stored


def feed_back(delta, normed, halves, stored):
    delta = delta.astype(BF16)
    total, grads = 0.0, []
    for weights, (hidden, slope) in zip(halves, stored, strict=True):
        delta_pre = (rows_nt(delta, weights[1]) * slope.astype(F32)).astype(BF16)
        delta_reduce = rows_tn(hidden, delta).astype(BF16)
        delta_expand = rows_tn(delta_pre, normed).astype(BF16)
        grads.append(feed_parts(jnp.stack([delta_expand, delta_reduce])))
        total = total + rows_nn(delta_pre, weights[0])
    return total, grads


def on_device(
    tokens,
    cotangent,
    ratios,
    patch_index,
    encoder_gains,
    encoder_attend_in,
    encoder_attend_out,
    encoder_expand,
    encoder_reduce,
    uniting_gains,
    uniting_query,
    uniting_pair,
    uniting_attend_out,
    uniting_expand,
    uniting_reduce,
):
    groups = lax.axis_size("dp")
    side = groups // 2
    group, lane = lax.axis_index("dp"), lax.axis_index("head")
    radar = group >= side
    modality = radar.astype(jnp.int32)
    own = group % PARTS
    images = tokens.shape[0]
    some = images // 2

    def select_slot(stacked):
        return lax.dynamic_index_in_dim(stacked, modality, 0, keepdims=False)

    gains = select_slot(encoder_gains)

    enc_attend = fetch(
        pack_attend(select_slot(encoder_attend_in), select_slot(encoder_attend_out), own)
    )
    enc_feed = fetch(pack_feed(select_slot(encoder_expand), select_slot(encoder_reduce), own))
    uni_attend = fetch(
        pack_attend(
            jnp.concatenate([uniting_query[:, None], uniting_pair], 1), uniting_attend_out, own
        )
    )
    uni_feed = fetch(pack_feed(uniting_expand, uniting_reduce, own))
    enc_attend = [attend_rows(half) for half in enc_attend]
    enc_feed = [feed_rows(half) for half in enc_feed]
    uni_attend = [attend_rows(half) for half in uni_attend]
    uni_feed = [feed_rows(half) for half in uni_feed]

    own_ratios = lax.dynamic_slice_in_dim(ratios, lane * images, images, 0)
    own_patches = lax.dynamic_slice_in_dim(patch_index, lane * images, images, 0)
    counts = PATCHES * (100 - own_ratios) // 100
    place = jnp.stack([own_patches // GRID, own_patches % GRID], 1).astype(F32)
    geometry = (counts, place.transpose(0, 2, 1), jnp.concatenate([place, place], 2))

    def own_pairs(array):
        return lax.dynamic_slice_in_dim(array, modality * some, some, 0)

    pair_geometry = tuple(own_pairs(part) for part in geometry)
    visible = (jnp.arange(SLOTS)[None, :] < counts[:, None]).astype(F32)[:, :, None]

    table = 2.0 ** (-8.0 * (jnp.arange(HEADS).astype(F32) + 1.0) / HEADS)
    table = table.reshape(lax.axis_size("head"), -1)

    def slopes_of(*masks):
        heads = jnp.concatenate(
            [lax.dynamic_index_in_dim(table, lane ^ mask, 0, keepdims=False) for mask in masks]
        )
        return jnp.repeat(heads.reshape(-1, 2), SLOTS, 1)

    slopes = (slopes_of(0, CORE), slopes_of(ACROSS, ACROSS | CORE))

    inputs = as_rows(tokens).astype(F32)
    normed_one = layer_norm(inputs, gains[0]).astype(BF16)
    mixed, mix_stored = mix_forward(normed_one, None, enc_attend, geometry, slopes)
    middle = inputs + mixed
    normed_two = layer_norm(middle, gains[1]).astype(BF16)
    fed, feed_stored = feed_forward(normed_two, enc_feed)
    encoded = middle + fed

    context = layer_norm(encoded, uniting_gains[0]).astype(BF16)
    cut = some * SLOTS
    received = swap(
        jnp.where(radar, encoded[:cut].astype(BF16), context[cut:]), dp_mask=side
    )
    radar_rows = jnp.where(radar, encoded[cut:], received.astype(F32))
    context_rows = jnp.where(radar, received, context[:cut])
    sent_cotangent = swap(cotangent[:some], dp_mask=side)
    pair_cotangent = jnp.where(radar, cotangent[some:], sent_cotangent)

    normed_query = layer_norm(radar_rows, uniting_gains[1]).astype(BF16)
    mixed, unite_stored = mix_forward(
        normed_query, context_rows, uni_attend, pair_geometry, slopes
    )
    unite_middle = radar_rows + mixed
    normed_three = layer_norm(unite_middle, uniting_gains[2]).astype(BF16)
    fed, unite_feed_stored = feed_forward(normed_three, uni_feed)
    joined = unite_middle + fed

    joined_half = as_images(joined).astype(BF16)
    other_half = swap(joined_half, dp_mask=side)
    encoded_images = as_images(encoded).astype(BF16)
    layer_output = visible.astype(BF16) * jnp.where(
        radar, jnp.concatenate([other_half, joined_half], 0), encoded_images
    )

    delta_joined = as_rows(own_pairs(visible) * pair_cotangent.astype(F32))
    delta_normed, uni_feed_grads = feed_back(
        delta_joined, normed_three, uni_feed, unite_feed_stored
    )
    delta_part, gain_three = norm_back(unite_middle, uniting_gains[2], delta_normed)
    delta_middle = delta_joined + delta_part
    delta_query, delta_context, uni_attend_grads = mix_back(
        delta_middle,
        normed_query,
        context_rows,
        uni_attend,
        pair_geometry,
        slopes,
        unite_stored,
    )
    delta_part, gain_two = norm_back(radar_rows, uniting_gains[1], delta_query)
    delta_radar = delta_middle + delta_part
    delta_context = delta_context.astype(BF16)
    returned = swap(
        jnp.where(radar, delta_context, delta_radar.astype(BF16)), dp_mask=side
    )
    nothing = jnp.zeros_like(returned)
    into_context = jnp.where(
        radar, 0, jnp.concatenate([delta_context, returned], 0)
    ).astype(F32)
    delta_part, gain_one = norm_back(encoded, uniting_gains[0], into_context)
    direct = jnp.where(
        radar,
        jnp.concatenate([returned.astype(F32), delta_radar], 0),
        as_rows(visible * cotangent.astype(F32)),
    )
    delta_encoded = direct + delta_part

    delta_normed, enc_feed_grads = feed_back(delta_encoded, normed_two, enc_feed, feed_stored)
    delta_part, gain_b = norm_back(middle, gains[1], delta_normed)
    delta_middle = delta_encoded + delta_part
    delta_own, delta_side, enc_attend_grads = mix_back(
        delta_middle, normed_one, None, enc_attend, geometry, slopes, mix_stored
    )
    delta_part, gain_a = norm_back(inputs, gains[0], delta_own + delta_side)
    tokens_delta = as_images(delta_middle + delta_part)

    def over_rest(array, stop):
        mask = PARTS
        while mask < stop:
            array = array + swap(array, dp_mask=mask)
            mask *= 2
        return array

    def united(grads, order, spread):
        return gather_parts(over_rest(reduce_parts(*grads, order), groups), spread)

    def of_encoders(grads, order, spread):
        part = over_rest(reduce_parts(*grads, order), side)
        other = swap(part, dp_mask=side)
        both = jnp.stack([jnp.where(radar, other, part), jnp.where(radar, part, other)])
        gathered = gather_parts(both, spread)
        return gathered[:, 0], gathered[:, 1]

    fexpand, freduce = unpack_feed(united(uni_feed_grads, "xyz", "yz"), own)
    ftriple, fout = unpack_attend(united(uni_attend_grads, "yzx", "zy"), own)
    feeds = [unpack_feed(g, own) for g in of_encoders(enc_feed_grads, "zyx", "yz")]
    attends = [unpack_attend(g, own) for g in of_encoders(enc_attend_grads, "xzy", "zy")]

    slot_mask = (jnp.arange(2) == modality).astype(F32)[:, None, None]
    gain_totals = lax.psum(
        (
            slot_mask * jnp.stack([gain_a, gain_b])[None],
            jnp.stack([gain_one, gain_two, gain_three]),
        ),
        ("dp", "head"),
    )
    return (
        layer_output,
        tokens_delta,
        gain_totals[0],
        jnp.stack([attends[0][0], attends[1][0]]),
        jnp.stack([attends[0][1], attends[1][1]]),
        jnp.stack([feeds[0][0], feeds[1][0]]),
        jnp.stack([feeds[0][1], feeds[1][1]]),
        gain_totals[1],
        ftriple[:, 0],
        ftriple[:, 1:],
        fout,
        fexpand,
        freduce,
    )


def solution(mesh):
    return jax.shard_map(
        on_device,
        mesh=mesh,
        in_specs=(
            P(("dp", "head"), None, None),
            P(("dp", "head"), None, None),
            P("dp"),
            P("dp", None),
            P(),
            P(None, None, None, "head"),
            P(None, "head", None),
            P(None, None, "head"),
            P(None, "head", None),
            P(),
            P(None, "head"),
            P(None, None, "head"),
            P("head", None),
            P(None, "head"),
            P("head", None),
        ),
        out_specs=(
            P(("dp", "head"), None, None),
            P(("dp", "head"), None, None),
            P(),
            P(None, None, None, "head"),
            P(None, "head", None),
            P(None, None, "head"),
            P(None, "head", None),
            P(),
            P(None, "head"),
            P(None, None, "head"),
            P("head", None),
            P(None, "head"),
            P("head", None),
        ),
        check_vma=False,
    )
```

time: 1880 us -> 798 us (0.42)
  waiting for transfers between devices: 1040 us -> 261 us
  matrix products: 311 us -> 126 us
  local copies, waits for them, and re-layouts: 255 us -> 92.6 us
  other arithmetic: 187 us -> 119 us
  Pallas kernels: 0 us -> 56.4 us
  blocking collectives: 44.4 us -> 77.2 us
  starting transfers between devices: 19.6 us -> 51.5 us
    reduce_scatter x10 -> x0, waiting for transfers between devices: 419 us -> none  [the longest x5 241 us: branch_sum(): lax.psum_scatter(row_product(gathered, weight).astype(jnp.bfloat16), 'hea...]
    all_gather x11 -> x0, waiting for transfers between devices: 306 us -> none  [the longest x7 238 us: spread_rows(): return lax.all_gather(values, 'head', axis=0, tiled=True)]
    psum x1 -> x0, waiting for transfers between devices: 280 us -> none  [on_device(): lax.psum(into_slot(delta_qkv).astype(jnp.bfloat16), 'dp')]
    ppermute x2 -> x52, waiting for transfers between devices: 32.7 us -> 261 us  [swap(): return lax.ppermute(array, ('dp', 'head'), pairs)]
    dot_general x43 -> x58, matrix products: 302 us -> 126 us  [the longest x20 46.9 us: rows_tn(): lax.dot_general(left, right, (((0,), (0,)), ((), ())), preferred_element_...]
    convert_element_type x29 -> x18, other arithmetic: 97.5 us -> 15.8 us  [the longest x3 4.94 us: feed_back(): delta = delta.astype(BF16)]
    slice x13 -> x59, local copies, waits for them, and re-layouts: 111 us -> 38.2 us  [the longest x8 8.36 us: reduce_parts(): kept = jnp.stack([near[0], far[0]]) + received]
    pallas_call x0 -> x8, Pallas kernels: none -> 56.4 us  [the longest x4 32.4 us: attend_back(): pl.pallas_call(attend_back_kernel, grid_spec=pltpu.PrefetchScalarGridSpec...]
  transfers between devices with their start and end apart: 24 -> 52, of which waited for: 22 -> 18; matrix products, arithmetic and copies ran while one was open for 13% -> 29% of each run, Pallas kernels for 0% -> 5%
where the time goes in v1:
time: 798 us; the launch traced here: 786 us
  waiting for transfers between devices  261 us (33%)
  matrix products  126 us (16%)
  other arithmetic  119 us (15%)
  local copies, waits for them, and re-layouts  92.6 us (12%)
  blocking collectives  77.2 us (10%)
  Pallas kernels  56.4 us (7%)
  starting transfers between devices  51.5 us (6%)
    ppermute x52, waiting for transfers between devices, swap(): return lax.ppermute(array, ('dp', 'head'), pairs)  261 us
    psum x1, blocking collectives, on_device(): lax.psum((slot_mask * jnp.stack([gain_a, gain_b])[None], jnp.stack([gain_...  77.2 us
    ppermute x52, starting transfers between devices, swap(): return lax.ppermute(array, ('dp', 'head'), pairs)  51.5 us
    dot_general x20, matrix products, rows_tn(): lax.dot_general(left, right, (((0,), (0,)), ((), ())), preferred_element_...  46.9 us
    dot_general x18, matrix products, rows_nt(): lax.dot_general(left, right, (((1,), (1,)), ((), ())), preferred_element_...  44.2 us
    unnamed x337, local copies, waits for them, and re-layouts  42.2 us
    dot_general x20, matrix products, rows_nn(): lax.dot_general(left, right, (((1,), (0,)), ((), ())), preferred_element_...  34.5 us
    pallas_call x4, Pallas kernels, attend_back(): pl.pallas_call(attend_back_kernel, grid_spec=pltpu.PrefetchScalarGridSpec...  32.4 us
  transfers between devices with their start and end apart: 52, of which 18 were waited for; matrix products, arithmetic and copies ran while one was open for 29% of the time, Pallas kernels for 5%

profile of v1, /device:TPU:0, one launch (start us, length us, event | category | flops | bytes accessed | tf_op | source)
XLA Modules:
  0.0 786.4 jit_solution(3766783593431335301)
XLA Ops:
  6.4 2.9 collective-permute-start.1
  26.8 3.1 convert_multiply_fusion.2
  45.5 3.6 fusion.100
  54.5 7.2 collective-permute-done.12
  76.1 3.1 collective-permute-done.13
  91.1 3.1 convolution_convert_fusion.1
  98.8 7.2 attend.4
  109.1 3.5 fusion.99
  113.1 3.6 fusion.97
  120.5 3.1 convolution_convert_fusion
  128.9 7.2 attend.5
  152.4 4.4 multiply_convert_fusion.3
  156.8 3.0 maximum_bitcast_fusion.1
  160.3 5.2 multiply_convert_fusion.2
  178.4 23.5 %collective-permute-done.10 = bf16[408,768]{1,0:T(8,128)(2,1)S(1)} collective-permute-done((bf16[408,768]{1,0:T(8,128)(2,1)S(1)}, bf16[408,768]{1,0:T(8,128)(2,1)S(1)}, u32[]{:S(2)}, u32[]{:S(2)}) %collective-permute-start.10) | collective-permute-done | bytes 626720 | tf_op jit(solution)/shard_map/ppermute | solution.py:29
  209.2 4.7 attend.7
  216.6 4.7 attend.6
  243.9 6.1 attend_back.5
  250.0 3.3 fusion.144
  274.0 6.6 attend_back.4
  286.6 3.0 collective-permute-start.23
  304.2 27.0 %collective-permute-done.23 = bf16[408,768]{1,0:T(8,128)(2,1)S(1)} collective-permute-done((bf16[408,768]{1,0:T(8,128)(2,1)S(1)}, bf16[408,768]{1,0:T(8,128)(2,1)S(1)}, u32[]{:S(2)}, u32[]{:S(2)}) %collective-permute-start.23) | collective-permute-done | bytes 626720 | tf_op jit(solution)/shard_map/ppermute | solution.py:29
  335.3 4.2 multiply_convert_fusion
  341.8 4.4 multiply_convert_fusion.1
  356.7 3.9 convolution_convert_fusion.6
  360.6 3.9 convolution_convert_fusion.7
  364.6 3.9 convolution_convert_fusion.8
  368.5 4.0 convolution_convert_fusion.9
  372.5 9.7 %attend_back.7 = (bf16[6,136,384]{2,1,0:T(8,128)(2,1)}, bf16[6,136,768]{2,1,0:T(8,128)(2,1)}) custom-call(s32[6]{0:T(128)} %copy-done.145, bf16[6,136,1152]{2,1,0:T(8,128)(2,1)} %bitcast.598, bf16[6,136,1152]{2,1,0:T(8,128)(2,1)} %bitcast.599, bf16[6,136,1152]{2,1,0:T(8,128)(2,1)} %bitcast.600, bf16[6,136,384]{2,1,0:T(8,128)(2,1)} %bitcast.732, ...), custom_call_target="tpu_custom_call" | custom-call | flops 3409182720 | bytes 5013504 | tf_op jit(solution)/shard_map/attend_back/pallas_call | solution.py:183
  382.1 3.2 bitcast_convert_fusion
  388.3 10.1 %attend_back.6 = (bf16[6,136,384]{2,1,0:T(8,128)(2,1)}, bf16[6,136,768]{2,1,0:T(8,128)(2,1)}) custom-call(s32[6]{0:T(128)} %copy-done.145, bf16[6,136,1152]{2,1,0:T(8,128)(2,1)} %bitcast.592, bf16[6,136,1152]{2,1,0:T(8,128)(2,1)} %bitcast.593, bf16[6,136,1152]{2,1,0:T(8,128)(2,1)} %bitcast.594, bf16[6,136,384]{2,1,0:T(8,128)(2,1)} %bitcast.731, ...), custom_call_target="tpu_custom_call" | custom-call | flops 3409182720 | bytes 5013504 | tf_op jit(solution)/shard_map/attend_back/pallas_call | solution.py:183
  398.5 3.2 bitcast_convert_fusion.1
  428.0 20.8 %collective-permute-done.39 = bf16[2,2,4,3,16,768]{5,4,3,2,0,1:T(8,128)(2,1)S(1)} collective-permute-done((bf16[2,2,4,3,16,768]{5,4,3,2,0,1:T(8,128)(2,1)S(1)}, bf16[2,2,4,3,16,768]{5,4,3,2,0,1:T(8,128)(2,1)S(1)}, u32[]{:S(2)}, u32[]{:S(2)}) %collective-permute-start.39) | collective-permute-done | bytes 1179680 | tf_op jit(solution)/shard_map/ppermute | solution.py:29
  451.2 12.7 %collective-permute-done.40 = bf16[2,1,4,3,16,768]{5,4,3,2,1,0:T(8,128)(2,1)S(1)} collective-permute-done((bf16[2,1,4,3,16,768]{5,4,3,2,1,0:T(8,128)(2,1)S(1)}, bf16[2,1,4,3,16,768]{5,4,3,2,1,0:T(8,128)(2,1)S(1)}, u32[]{:S(2)}, u32[]{:S(2)}) %collective-permute-start.40) | collective-permute-done | bytes 589856 | tf_op jit(solution)/shard_map/ppermute | solution.py:29
  467.0 3.0 maximum_add_fusion.1
  473.2 3.0 maximum_add_fusion
  480.8 77.2 %all-reduce = (f32[2,2,768]{2,1,0:T(2,128)}, f32[3,768]{1,0:T(4,128)}) all-reduce(f32[2,2,768]{2,1,0:T(2,128)S(1)} %broadcast_multiply_fusion, f32[3,768]{1,0:T(4,128)S(1)} %pad_maximum_fusion.29), channel_id=1, replica_groups=mesh['dp'=8,'head'=4] {'dp','head'}, use_global_device_ids=true, to_apply=%region_22.23 | all-reduce | flops 5376 | bytes 43008 | tf_op jit(solution)/shard_map/psum | solution.py:532
  579.4 4.7 collective-permute-done.28
  584.3 25.0 %collective-permute-done.47 = bf16[1,2,2,192,768]{4,3,2,1,0:T(8,128)(2,1)S(1)} collective-permute-done((bf16[1,2,2,192,768]{4,3,2,1,0:T(8,128)(2,1)S(1)}, bf16[1,2,2,192,768]{4,3,2,1,0:T(8,128)(2,1)S(1)}, u32[]{:S(2)}, u32[]{:S(2)}) %collective-permute-start.47) | collective-permute-done | bytes 1179680 | tf_op jit(solution)/shard_map/ppermute | solution.py:29
  610.2 22.9 %collective-permute-done.33 = bf16[2,1,2,192,768]{4,3,2,1,0:T(8,128)(2,1)S(1)} collective-permute-done((bf16[2,1,2,192,768]{4,3,2,1,0:T(8,128)(2,1)S(1)}, bf16[2,1,2,192,768]{4,3,2,1,0:T(8,128)(2,1)S(1)}, u32[]{:S(2)}, u32[]{:S(2)}) %collective-permute-start.33) | collective-permute-done | bytes 1179680 | tf_op jit(solution)/shard_map/ppermute | solution.py:29
  637.1 10.3 %collective-permute-done.34 = bf16[1,1,2,192,768]{4,3,2,1,0:T(8,128)(2,1)S(1)} collective-permute-done((bf16[1,1,2,192,768]{4,3,2,1,0:T(8,128)(2,1)S(1)}, bf16[1,1,2,192,768]{4,3,2,1,0:T(8,128)(2,1)S(1)}, u32[]{:S(2)}, u32[]{:S(2)}) %collective-permute-start.34) | collective-permute-done | bytes 589856 | tf_op jit(solution)/shard_map/ppermute | solution.py:29
  651.3 24.4 %collective-permute-done.49 = bf16[2,192,768]{2,1,0:T(8,128)(2,1)S(1)} collective-permute-done((bf16[2,192,768]{2,1,0:T(8,128)(2,1)S(1)}, bf16[2,192,768]{2,1,0:T(8,128)(2,1)S(1)}, u32[]{:S(2)}, u32[]{:S(2)}) %collective-permute-start.49) | collective-permute-done | bytes 589856 | tf_op jit(solution)/shard_map/ppermute | solution.py:29
  677.0 10.7 %collective-permute-done.35 = bf16[2,192,768]{2,1,0:T(8,128)(2,1)S(1)} collective-permute-done((bf16[2,192,768]{2,1,0:T(8,128)(2,1)S(1)}, bf16[2,192,768]{2,1,0:T(8,128)(2,1)S(1)}, u32[]{:S(2)}, u32[]{:S(2)}) %collective-permute-start.35) | collective-permute-done | bytes 589856 | tf_op jit(solution)/shard_map/ppermute | solution.py:29
  691.4 23.8 %collective-permute-done.36 = bf16[2,2,192,768]{3,2,1,0:T(8,128)(2,1)S(1)} collective-permute-done((bf16[2,2,192,768]{3,2,1,0:T(8,128)(2,1)S(1)}, bf16[2,2,192,768]{3,2,1,0:T(8,128)(2,1)S(1)}, u32[]{:S(2)}, u32[]{:S(2)}) %collective-permute-start.36) | collective-permute-done | bytes 1179680 | tf_op jit(solution)/shard_map/ppermute | solution.py:29
  726.5 2.9 bitcast_convert_fusion.3
  729.4 39.7 %collective-permute-done.37 = bf16[2,2,2,192,768]{4,3,2,1,0:T(8,128)(2,1)} collective-permute-done((bf16[2,2,2,192,768]{4,3,2,1,0:T(8,128)(2,1)}, bf16[2,2,2,192,768]{4,3,2,1,0:T(8,128)(2,1)}, u32[]{:S(2)}, u32[]{:S(2)}) %collective-permute-start.37) | collective-permute-done | bytes 2359328 | tf_op jit(solution)/shard_map/ppermute | solution.py:29
  776.3 6.0 copy.133
  782.3 3.9 maximum_convert_fusion.1
  (698 shorter events, 302.3 us)
Async XLA Ops:
  6.4 45.4 %collective-permute-start.1 = (bf16[2,4,3,16,768]{4,3,0,2,1:T(8,128)(2,1)}, bf16[2,4,3,16,768]{4,3,0,2,1:T(8,128)(2,1)}, u32[]{:S(2)}, u32[]{:S(2)}) collective-permute-start(bf16[2,4,3,16,768]{4,3,0,2,1:T(8,128)(2,1)} %pad_maximum_fusion.24), channel_id=1, source_target_pairs={{0,2},{1,3},{2,0},{3,1},{4,6},{5,7},{6,4},{7,5},{8,10},{9,11},{10,... | collective-permute-start | bytes 1769480 | tf_op jit(solution)/shard_map/ppermute | solution.py:29
  10.9 72.5 %collective-permute-start = (bf16[4,4,3,16,768]{4,3,0,2,1:T(8,128)(2,1)}, bf16[4,4,3,16,768]{4,3,0,2,1:T(8,128)(2,1)}, u32[]{:S(2)}, u32[]{:S(2)}) collective-permute-start(bf16[4,4,3,16,768]{4,3,0,2,1:T(8,128)(2,1)} %get-tuple-element.216), channel_id=1, source_target_pairs={{0,1},{1,0},{2,3},{3,2},{4,5},{5,4},{6,7},{7,6},{8,9},{9,8},{10,11... | collective-permute-start | bytes 3538952 | tf_op jit(solution)/shard_map/ppermute | solution.py:29
  17.4 63.3 %collective-permute-start.6 = (bf16[2,2,192,768]{3,2,1,0:T(8,128)(2,1)}, bf16[2,2,192,768]{3,2,1,0:T(8,128)(2,1)}, u32[]{:S(2)}, u32[]{:S(2)}) collective-permute-start(bf16[2,2,192,768]{3,2,1,0:T(8,128)(2,1)} %pad_maximum_fusion.15), channel_id=1, source_target_pairs={{0,2},{1,3},{2,0},{3,1},{4,6},{5,7},{6,4},{7,5},{8,10},{9,11},{10,... | collective-permute-start | bytes 3538952 | tf_op jit(solution)/shard_map/ppermute | solution.py:29
  19.4 42.3 %collective-permute-start.12 = (bf16[2,4,3,16,768]{4,3,0,2,1:T(8,128)(2,1)}, bf16[2,4,3,16,768]{4,3,0,2,1:T(8,128)(2,1)}, u32[]{:S(2)}, u32[]{:S(2)}) collective-permute-start(bf16[2,4,3,16,768]{4,3,0,2,1:T(8,128)(2,1)} %pad_maximum_fusion.25), channel_id=1, source_target_pairs={{0,2},{1,3},{2,0},{3,1},{4,6},{5,7},{6,4},{7,5},{8,10},{9,11},{10,... | collective-permute-start | bytes 1769480 | tf_op jit(solution)/shard_map/ppermute | solution.py:29
  21.3 43.7 %collective-permute-start.22 = (bf16[3,136,768]{2,1,0:T(8,128)(2,1)}, bf16[3,136,768]{2,1,0:T(8,128)(2,1)}, u32[]{:S(2)}, u32[]{:S(2)}) collective-permute-start(bf16[3,136,768]{2,1,0:T(8,128)(2,1)} %slice.411), channel_id=1, source_target_pairs={{0,16},{1,17},{2,18},{3,19},{4,20},{5,21},{6,22},{7,23},{8,24},{9,... | collective-permute-start | bytes 1880072 | tf_op jit(solution)/shard_map/ppermute | solution.py:29
  52.8 35.4 %collective-permute-start.17 = (bf16[2,2,192,768]{3,2,1,0:T(8,128)(2,1)S(1)}, bf16[2,2,192,768]{3,2,1,0:T(8,128)(2,1)S(1)}, u32[]{:S(2)}, u32[]{:S(2)}) collective-permute-start(bf16[2,2,192,768]{3,2,1,0:T(8,128)(2,1)S(1)} %copy-done.100), channel_id=1, source_target_pairs={{0,2},{1,3},{2,0},{3,1},{4,6},{5,7},{6,4},{7,5},{8,10},{9,11},{10,... | collective-permute-start | bytes 3538952 | tf_op jit(solution)/shard_map/ppermute | solution.py:29
  76.1 18.2 %collective-permute-start.11 = (bf16[4,4,3,16,768]{4,3,0,2,1:T(8,128)(2,1)S(1)}, bf16[4,4,3,16,768]{4,3,0,2,1:T(8,128)(2,1)S(1)}, u32[]{:S(2)}, u32[]{:S(2)}) collective-permute-start(bf16[4,4,3,16,768]{4,3,0,2,1:T(8,128)(2,1)S(1)} %get-tuple-element.205), channel_id=1, source_target_pairs={{0,1},{1,0},{2,3},{3,2},{4,5},{5,4},{6,7},{7,6},{8,9},{9,8},{10,11... | collective-permute-start | bytes 3538952 | tf_op jit(solution)/shard_map/ppermute | solution.py:29
  79.2 37.5 %collective-permute-start.4 = (bf16[4,4,3,16,768]{4,3,0,2,1:T(8,128)(2,1)}, bf16[4,4,3,16,768]{4,3,0,2,1:T(8,128)(2,1)}, u32[]{:S(2)}, u32[]{:S(2)}) collective-permute-start(bf16[4,4,3,16,768]{4,3,0,2,1:T(8,128)(2,1)} %get-tuple-element.222), channel_id=1, source_target_pairs={{0,1},{1,0},{2,3},{3,2},{4,5},{5,4},{6,7},{7,6},{8,9},{9,8},{10,11... | collective-permute-start | bytes 3538952 | tf_op jit(solution)/shard_map/ppermute | solution.py:29
  83.4 25.2 %collective-permute-start.8 = (bf16[2,192,768]{2,1,0:T(8,128)(2,1)}, bf16[2,192,768]{2,1,0:T(8,128)(2,1)}, u32[]{:S(2)}, u32[]{:S(2)}) collective-permute-start(bf16[2,192,768]{2,1,0:T(8,128)(2,1)} %get-tuple-element.213), channel_id=1, source_target_pairs={{0,8},{1,9},{2,10},{3,11},{4,12},{5,13},{6,14},{7,15},{8,0},{9,1},... | collective-permute-start | bytes 1769480 | tf_op jit(solution)/shard_map/ppermute | solution.py:29
  83.4 25.2 %collective-permute-start.7 = (bf16[2,192,768]{2,1,0:T(8,128)(2,1)}, bf16[2,192,768]{2,1,0:T(8,128)(2,1)}, u32[]{:S(2)}, u32[]{:S(2)}) collective-permute-start(bf16[2,192,768]{2,1,0:T(8,128)(2,1)} %get-tuple-element.213), channel_id=1, source_target_pairs={{0,4},{1,5},{2,6},{3,7},{4,0},{5,1},{6,2},{7,3},{8,12},{9,13},{10,... | collective-permute-start | bytes 1769480 | tf_op jit(solution)/shard_map/ppermute | solution.py:29
  89.6 23.1 %collective-permute-start.19 = (bf16[2,192,768]{2,1,0:T(8,128)(2,1)}, bf16[2,192,768]{2,1,0:T(8,128)(2,1)}, u32[]{:S(2)}, u32[]{:S(2)}) collective-permute-start(bf16[2,192,768]{2,1,0:T(8,128)(2,1)} %get-tuple-element.202), channel_id=1, source_target_pairs={{0,8},{1,9},{2,10},{3,11},{4,12},{5,13},{6,14},{7,15},{8,0},{9,1},... | collective-permute-start | bytes 1769480 | tf_op jit(solution)/shard_map/ppermute | solution.py:29
  94.2 18.5 %collective-permute-start.18 = (bf16[2,192,768]{2,1,0:T(8,128)(2,1)}, bf16[2,192,768]{2,1,0:T(8,128)(2,1)}, u32[]{:S(2)}, u32[]{:S(2)}) collective-permute-start(bf16[2,192,768]{2,1,0:T(8,128)(2,1)} %get-tuple-element.202), channel_id=1, source_target_pairs={{0,4},{1,5},{2,6},{3,7},{4,0},{5,1},{6,2},{7,3},{8,12},{9,13},{10,... | collective-permute-start | bytes 1769480 | tf_op jit(solution)/shard_map/ppermute | solution.py:29
  108.6 34.5 %collective-permute-start.5 = (bf16[4,2,192,768]{3,2,1,0:T(8,128)(2,1)}, bf16[4,2,192,768]{3,2,1,0:T(8,128)(2,1)}, u32[]{:S(2)}, u32[]{:S(2)}) collective-permute-start(bf16[4,2,192,768]{3,2,1,0:T(8,128)(2,1)} %get-tuple-element.176), channel_id=1, source_target_pairs={{0,1},{1,0},{2,3},{3,2},{4,5},{5,4},{6,7},{7,6},{8,9},{9,8},{10,11... | collective-permute-start | bytes 7077896 | tf_op jit(solution)/shard_map/ppermute | solution.py:29
  108.6 15.9 %collective-permute-start.15 = (bf16[4,4,3,16,768]{4,3,0,2,1:T(8,128)(2,1)S(1)}, bf16[4,4,3,16,768]{4,3,0,2,1:T(8,128)(2,1)S(1)}, u32[]{:S(2)}, u32[]{:S(2)}) collective-permute-start(bf16[4,4,3,16,768]{4,3,0,2,1:T(8,128)(2,1)S(1)} %copy-done.98), channel_id=1, source_target_pairs={{0,1},{1,0},{2,3},{3,2},{4,5},{5,4},{6,7},{7,6},{8,9},{9,8},{10,11... | collective-permute-start | bytes 3538952 | tf_op jit(solution)/shard_map/ppermute | solution.py:29
  112.6 34.4 %collective-permute-start.16 = (bf16[4,2,192,768]{3,2,1,0:T(8,128)(2,1)}, bf16[4,2,192,768]{3,2,1,0:T(8,128)(2,1)}, u32[]{:S(2)}, u32[]{:S(2)}) collective-permute-start(bf16[4,2,192,768]{3,2,1,0:T(8,128)(2,1)} %get-tuple-element.164), channel_id=1, source_target_pairs={{0,1},{1,0},{2,3},{3,2},{4,5},{5,4},{6,7},{7,6},{8,9},{9,8},{10,11... | collective-permute-start | bytes 7077896 | tf_op jit(solution)/shard_map/ppermute | solution.py:29
  112.7 44.1 %collective-permute-start.9 = (bf16[4,2,192,768]{3,2,1,0:T(8,128)(2,1)}, bf16[4,2,192,768]{3,2,1,0:T(8,128)(2,1)}, u32[]{:S(2)}, u32[]{:S(2)}) collective-permute-start(bf16[4,2,192,768]{3,2,1,0:T(8,128)(2,1)} %get-tuple-element.182), channel_id=1, source_target_pairs={{0,1},{1,0},{2,3},{3,2},{4,5},{5,4},{6,7},{7,6},{8,9},{9,8},{10,11... | collective-permute-start | bytes 7077896 | tf_op jit(solution)/shard_map/ppermute | solution.py:29
  116.7 57.0 %collective-permute-start.20 = (bf16[4,2,192,768]{3,2,1,0:T(8,128)(2,1)}, bf16[4,2,192,768]{3,2,1,0:T(8,128)(2,1)}, u32[]{:S(2)}, u32[]{:S(2)}) collective-permute-start(bf16[4,2,192,768]{3,2,1,0:T(8,128)(2,1)} %get-tuple-element.170), channel_id=1, source_target_pairs={{0,1},{1,0},{2,3},{3,2},{4,5},{5,4},{6,7},{7,6},{8,9},{9,8},{10,11... | collective-permute-start | bytes 7077896 | tf_op jit(solution)/shard_map/ppermute | solution.py:29
  171.0 30.9 %collective-permute-start.10 = (bf16[408,768]{1,0:T(8,128)(2,1)S(1)}, bf16[408,768]{1,0:T(8,128)(2,1)S(1)}, u32[]{:S(2)}, u32[]{:S(2)}) collective-permute-start(bf16[408,768]{1,0:T(8,128)(2,1)S(1)} %slice_select_fusion.2), channel_id=1, source_target_pairs={{0,16},{1,17},{2,18},{3,19},{4,20},{5,21},{6,22},{7,23},{8,24},{9,... | collective-permute-start | bytes 1880072 | tf_op jit(solution)/shard_map/ppermute | solution.py:29
  274.0 289.9 %collective-permute-start.21 = (bf16[3,136,768]{2,1,0:T(8,128)(2,1)}, bf16[3,136,768]{2,1,0:T(8,128)(2,1)}, u32[]{:S(2)}, u32[]{:S(2)}) collective-permute-start(bf16[3,136,768]{2,1,0:T(8,128)(2,1)} %bitcast.110), channel_id=1, source_target_pairs={{0,16},{1,17},{2,18},{3,19},{4,20},{5,21},{6,22},{7,23},{8,24},{9,... | collective-permute-start | bytes 1880072 | tf_op jit(solution)/shard_map/ppermute | solution.py:29
  286.6 44.6 %collective-permute-start.23 = (bf16[408,768]{1,0:T(8,128)(2,1)S(1)}, bf16[408,768]{1,0:T(8,128)(2,1)S(1)}, u32[]{:S(2)}, u32[]{:S(2)}) collective-permute-start(bf16[408,768]{1,0:T(8,128)(2,1)S(1)} %get-tuple-element.97), channel_id=1, source_target_pairs={{0,16},{1,17},{2,18},{3,19},{4,20},{5,21},{6,22},{7,23},{8,24},{9,... | collective-permute-start | bytes 1880072 | tf_op jit(solution)/shard_map/ppermute | solution.py:29
  294.2 123.3 %collective-permute-start.38 = (bf16[2,4,4,3,16,768]{5,4,1,3,0,2:T(8,128)(2,1)}, bf16[2,4,4,3,16,768]{5,4,1,3,0,2:T(8,128)(2,1)}, u32[]{:S(2)}, u32[]{:S(2)}) collective-permute-start(bf16[2,4,4,3,16,768]{5,4,1,3,0,2:T(8,128)(2,1)} %pad_maximum_fusion.10), channel_id=1, source_target_pairs={{0,1},{1,0},{2,3},{3,2},{4,5},{5,4},{6,7},{7,6},{8,9},{9,8},{10,11... | collective-permute-start | bytes 7077896 | tf_op jit(solution)/shard_map/ppermute | solution.py:29
  304.2 162.7 %collective-permute-start.45 = (bf16[2,4,2,192,768]{4,3,2,1,0:T(8,128)(2,1)}, bf16[2,4,2,192,768]{4,3,2,1,0:T(8,128)(2,1)}, u32[]{:S(2)}, u32[]{:S(2)}) collective-permute-start(bf16[2,4,2,192,768]{4,3,2,1,0:T(8,128)(2,1)} %pad_maximum_fusion.2), channel_id=1, source_target_pairs={{0,1},{1,0},{2,3},{3,2},{4,5},{5,4},{6,7},{7,6},{8,9},{9,8},{10,11... | collective-permute-start | bytes 14155784 | tf_op jit(solution)/shard_map/ppermute | solution.py:29
  406.0 18.4 %collective-permute-start.24 = (bf16[2,4,4,3,16,768]{5,4,1,3,0,2:T(8,128)(2,1)}, bf16[2,4,4,3,16,768]{5,4,1,3,0,2:T(8,128)(2,1)}, u32[]{:S(2)}, u32[]{:S(2)}) collective-permute-start(bf16[2,4,4,3,16,768]{5,4,1,3,0,2:T(8,128)(2,1)} %pad_maximum_fusion.7), channel_id=1, source_target_pairs={{0,1},{1,0},{2,3},{3,2},{4,5},{5,4},{6,7},{7,6},{8,9},{9,8},{10,11... | collective-permute-start | bytes 7077896 | tf_op jit(solution)/shard_map/ppermute | solution.py:29
  413.8 59.4 %collective-permute-start.31 = (bf16[2,4,2,192,768]{4,3,1,0,2:T(8,128)(2,1)}, bf16[2,4,2,192,768]{4,3,1,0,2:T(8,128)(2,1)}, u32[]{:S(2)}, u32[]{:S(2)}) collective-permute-start(bf16[2,4,2,192,768]{4,3,1,0,2:T(8,128)(2,1)} %pad_maximum_fusion), channel_id=1, source_target_pairs={{0,1},{1,0},{2,3},{3,2},{4,5},{5,4},{6,7},{7,6},{8,9},{9,8},{10,11... | collective-permute-start | bytes 14155784 | tf_op jit(solution)/shard_map/ppermute | solution.py:29
  420.3 28.4 %collective-permute-start.39 = (bf16[2,2,4,3,16,768]{5,4,3,2,0,1:T(8,128)(2,1)S(1)}, bf16[2,2,4,3,16,768]{5,4,3,2,0,1:T(8,128)(2,1)S(1)}, u32[]{:S(2)}, u32[]{:S(2)}) collective-permute-start(bf16[2,2,4,3,16,768]{5,4,3,2,0,1:T(8,128)(2,1)S(1)} %bitcast.680), channel_id=1, source_target_pairs={{0,4},{1,5},{2,6},{3,7},{4,0},{5,1},{6,2},{7,3},{8,12},{9,13},{10,... | collective-permute-start | bytes 3538952 | tf_op jit(solution)/shard_map/ppermute | solution.py:29
  426.4 39.2 %collective-permute-start.25 = (bf16[1,4,4,3,16,768]{5,4,1,3,0,2:T(8,128)(2,1)S(1)}, bf16[1,4,4,3,16,768]{5,4,1,3,0,2:T(8,128)(2,1)S(1)}, u32[]{:S(2)}, u32[]{:S(2)}) collective-permute-start(bf16[1,4,4,3,16,768]{5,4,1,3,0,2:T(8,128)(2,1)S(1)} %slice.517), channel_id=1, source_target_pairs={{0,2},{1,3},{2,0},{3,1},{4,6},{5,7},{6,4},{7,5},{8,10},{9,11},{10,... | collective-permute-start | bytes 3538952 | tf_op jit(solution)/shard_map/ppermute | solution.py:29
  449.0 15.0 %collective-permute-start.40 = (bf16[2,1,4,3,16,768]{5,4,3,2,1,0:T(8,128)(2,1)S(1)}, bf16[2,1,4,3,16,768]{5,4,3,2,1,0:T(8,128)(2,1)S(1)}, u32[]{:S(2)}, u32[]{:S(2)}) collective-permute-start(bf16[2,1,4,3,16,768]{5,4,3,2,1,0:T(8,128)(2,1)S(1)} %slice_bitcast_fusion.7), channel_id=1, source_target_pairs={{0,8},{1,9},{2,10},{3,11},{4,12},{5,13},{6,14},{7,15},{8,0},{9,1},... | collective-permute-start | bytes 1769480 | tf_op jit(solution)/shard_map/ppermute | solution.py:29
  464.0 15.5 %collective-permute-start.41 = (bf16[1,1,4,3,16,768]{5,4,3,2,1,0:T(8,128)(2,1)S(1)}, bf16[1,1,4,3,16,768]{5,4,3,2,1,0:T(8,128)(2,1)S(1)}, u32[]{:S(2)}, u32[]{:S(2)}) collective-permute-start(bf16[1,1,4,3,16,768]{5,4,3,2,1,0:T(8,128)(2,1)S(1)} %slice.555), channel_id=1, source_target_pairs={{0,2},{1,3},{2,0},{3,1},{4,6},{5,7},{6,4},{7,5},{8,10},{9,11},{10,... | collective-permute-start | bytes 884744 | tf_op jit(solution)/shard_map/ppermute | solution.py:29
  466.7 93.0 %collective-permute-start.26 = (bf16[1,2,4,3,16,768]{5,4,1,3,2,0:T(8,128)(2,1)}, bf16[1,2,4,3,16,768]{5,4,1,3,2,0:T(8,128)(2,1)}, u32[]{:S(2)}, u32[]{:S(2)}) collective-permute-start(bf16[1,2,4,3,16,768]{5,4,1,3,2,0:T(8,128)(2,1)} %slice_bitcast_fusion.9), channel_id=1, source_target_pairs={{0,8},{1,9},{2,10},{3,11},{4,12},{5,13},{6,14},{7,15},{8,0},{9,1},... | collective-permute-start | bytes 1769480 | tf_op jit(solution)/shard_map/ppermute | solution.py:29
  471.7 101.5 %collective-permute-start.46 = (bf16[1,4,2,192,768]{4,3,2,1,0:T(8,128)(2,1)}, bf16[1,4,2,192,768]{4,3,2,1,0:T(8,128)(2,1)}, u32[]{:S(2)}, u32[]{:S(2)}) collective-permute-start(bf16[1,4,2,192,768]{4,3,2,1,0:T(8,128)(2,1)} %slice.567), channel_id=1, source_target_pairs={{0,2},{1,3},{2,0},{3,1},{4,6},{5,7},{6,4},{7,5},{8,10},{9,11},{10,... | collective-permute-start | bytes 7077896 | tf_op jit(solution)/shard_map/ppermute | solution.py:29
  478.2 99.0 %collective-permute-start.32 = (bf16[2,2,2,192,768]{4,3,2,0,1:T(8,128)(2,1)}, bf16[2,2,2,192,768]{4,3,2,0,1:T(8,128)(2,1)}, u32[]{:S(2)}, u32[]{:S(2)}) collective-permute-start(bf16[2,2,2,192,768]{4,3,2,0,1:T(8,128)(2,1)} %bitcast.580), channel_id=1, source_target_pairs={{0,8},{1,9},{2,10},{3,11},{4,12},{5,13},{6,14},{7,15},{8,0},{9,1},... | collective-permute-start | bytes 7077896 | tf_op jit(solution)/shard_map/ppermute | solution.py:29
  480.3 77.7 %collective-permute-start.42 = (bf16[4,3,16,768]{3,2,1,0:T(8,128)(2,1)}, bf16[4,3,16,768]{3,2,1,0:T(8,128)(2,1)S(1)}, u32[]{:S(2)}, u32[]{:S(2)}) collective-permute-start(bf16[4,3,16,768]{3,2,1,0:T(8,128)(2,1)} %fusion.75), channel_id=1, source_target_pairs={{0,16},{1,17},{2,18},{3,19},{4,20},{5,21},{6,22},{7,23},{8,24},{9,... | collective-permute-start | bytes 884744 | tf_op jit(solution)/shard_map/ppermute | solution.py:29
  559.1 8.3 %collective-permute-start.43 = (bf16[4,3,16,768]{3,2,1,0:T(8,128)(2,1)S(1)}, bf16[4,3,16,768]{3,2,1,0:T(8,128)(2,1)S(1)}, u32[]{:S(2)}, u32[]{:S(2)}) collective-permute-start(bf16[4,3,16,768]{3,2,1,0:T(8,128)(2,1)S(1)} %add.352), channel_id=1, source_target_pairs={{0,8},{1,9},{2,10},{3,11},{4,12},{5,13},{6,14},{7,15},{8,0},{9,1},... | collective-permute-start | bytes 884744 | tf_op jit(solution)/shard_map/ppermute | solution.py:29
  561.2 10.1 %collective-permute-start.27 = (bf16[1,1,4,3,16,768]{5,4,3,2,1,0:T(8,128)(2,1)S(1)}, bf16[1,1,4,3,16,768]{5,4,3,2,1,0:T(8,128)(2,1)S(1)}, u32[]{:S(2)}, u32[]{:S(2)}) collective-permute-start(bf16[1,1,4,3,16,768]{5,4,3,2,1,0:T(8,128)(2,1)S(1)} %slice_bitcast_fusion.11), channel_id=1, source_target_pairs={{0,4},{1,5},{2,6},{3,7},{4,0},{5,1},{6,2},{7,3},{8,12},{9,13},{10,... | collective-permute-start | bytes 884744 | tf_op jit(solution)/shard_map/ppermute | solution.py:29
  567.5 16.7 %collective-permute-start.44 = (bf16[2,4,3,16,768]{4,3,0,2,1:T(8,128)(2,1)S(1)}, bf16[2,4,3,16,768]{4,3,0,2,1:T(8,128)(2,1)S(1)}, u32[]{:S(2)}, u32[]{:S(2)}) collective-permute-start(bf16[2,4,3,16,768]{4,3,0,2,1:T(8,128)(2,1)S(1)} %pad_maximum_fusion.27), channel_id=1, source_target_pairs={{0,4},{1,5},{2,6},{3,7},{4,0},{5,1},{6,2},{7,3},{8,12},{9,13},{10,... | collective-permute-start | bytes 1769480 | tf_op jit(solution)/shard_map/ppermute | solution.py:29
  571.4 12.7 %collective-permute-start.28 = (bf16[4,3,16,768]{3,2,1,0:T(8,128)(2,1)S(1)}, bf16[4,3,16,768]{3,2,1,0:T(8,128)(2,1)S(1)}, u32[]{:S(2)}, u32[]{:S(2)}) collective-permute-start(bf16[4,3,16,768]{3,2,1,0:T(8,128)(2,1)S(1)} %fusion.77), channel_id=1, source_target_pairs={{0,16},{1,17},{2,18},{3,19},{4,20},{5,21},{6,22},{7,23},{8,24},{9,... | collective-permute-start | bytes 884744 | tf_op jit(solution)/shard_map/ppermute | solution.py:29
  575.2 34.1 %collective-permute-start.47 = (bf16[1,2,2,192,768]{4,3,2,1,0:T(8,128)(2,1)S(1)}, bf16[1,2,2,192,768]{4,3,2,1,0:T(8,128)(2,1)S(1)}, u32[]{:S(2)}, u32[]{:S(2)}) collective-permute-start(bf16[1,2,2,192,768]{4,3,2,1,0:T(8,128)(2,1)S(1)} %slice_bitcast_fusion), channel_id=1, source_target_pairs={{0,4},{1,5},{2,6},{3,7},{4,0},{5,1},{6,2},{7,3},{8,12},{9,13},{10,... | collective-permute-start | bytes 3538952 | tf_op jit(solution)/shard_map/ppermute | solution.py:29
  579.1 53.9 %collective-permute-start.33 = (bf16[2,1,2,192,768]{4,3,2,1,0:T(8,128)(2,1)S(1)}, bf16[2,1,2,192,768]{4,3,2,1,0:T(8,128)(2,1)S(1)}, u32[]{:S(2)}, u32[]{:S(2)}) collective-permute-start(bf16[2,1,2,192,768]{4,3,2,1,0:T(8,128)(2,1)S(1)} %slice_bitcast_fusion.2), channel_id=1, source_target_pairs={{0,4},{1,5},{2,6},{3,7},{4,0},{5,1},{6,2},{7,3},{8,12},{9,13},{10,... | collective-permute-start | bytes 3538952 | tf_op jit(solution)/shard_map/ppermute | solution.py:29
  584.2 64.5 %collective-permute-start.29 = (bf16[2,4,3,16,768]{4,3,2,1,0:T(8,128)(2,1)S(1)}, bf16[2,4,3,16,768]{4,3,2,1,0:T(8,128)(2,1)S(1)}, u32[]{:S(2)}, u32[]{:S(2)}) collective-permute-start(bf16[2,4,3,16,768]{4,3,2,1,0:T(8,128)(2,1)S(1)} %get-tuple-element.226), channel_id=1, source_target_pairs={{0,8},{1,9},{2,10},{3,11},{4,12},{5,13},{6,14},{7,15},{8,0},{9,1},... | collective-permute-start | bytes 1769480 | tf_op jit(solution)/shard_map/ppermute | solution.py:29
  609.5 26.0 %collective-permute-start.48 = (bf16[1,1,2,192,768]{4,3,2,1,0:T(8,128)(2,1)S(1)}, bf16[1,1,2,192,768]{4,3,2,1,0:T(8,128)(2,1)S(1)}, u32[]{:S(2)}, u32[]{:S(2)}) collective-permute-start(bf16[1,1,2,192,768]{4,3,2,1,0:T(8,128)(2,1)S(1)} %slice_bitcast_fusion.4), channel_id=1, source_target_pairs={{0,8},{1,9},{2,10},{3,11},{4,12},{5,13},{6,14},{7,15},{8,0},{9,1},... | collective-permute-start | bytes 1769480 | tf_op jit(solution)/shard_map/ppermute | solution.py:29
  633.3 14.1 %collective-permute-start.34 = (bf16[1,1,2,192,768]{4,3,2,1,0:T(8,128)(2,1)S(1)}, bf16[1,1,2,192,768]{4,3,2,1,0:T(8,128)(2,1)S(1)}, u32[]{:S(2)}, u32[]{:S(2)}) collective-permute-start(bf16[1,1,2,192,768]{4,3,2,1,0:T(8,128)(2,1)S(1)} %slice.539), channel_id=1, source_target_pairs={{0,2},{1,3},{2,0},{3,1},{4,6},{5,7},{6,4},{7,5},{8,10},{9,11},{10,... | collective-permute-start | bytes 1769480 | tf_op jit(solution)/shard_map/ppermute | solution.py:29
  635.6 40.2 %collective-permute-start.49 = (bf16[2,192,768]{2,1,0:T(8,128)(2,1)S(1)}, bf16[2,192,768]{2,1,0:T(8,128)(2,1)S(1)}, u32[]{:S(2)}, u32[]{:S(2)}) collective-permute-start(bf16[2,192,768]{2,1,0:T(8,128)(2,1)S(1)} %fusion.60), channel_id=1, source_target_pairs={{0,16},{1,17},{2,18},{3,19},{4,20},{5,21},{6,22},{7,23},{8,24},{9,... | collective-permute-start | bytes 1769480 | tf_op jit(solution)/shard_map/ppermute | solution.py:29
  647.4 40.2 %collective-permute-start.35 = (bf16[2,192,768]{2,1,0:T(8,128)(2,1)S(1)}, bf16[2,192,768]{2,1,0:T(8,128)(2,1)S(1)}, u32[]{:S(2)}, u32[]{:S(2)}) collective-permute-start(bf16[2,192,768]{2,1,0:T(8,128)(2,1)S(1)} %fusion.62), channel_id=1, source_target_pairs={{0,16},{1,17},{2,18},{3,19},{4,20},{5,21},{6,22},{7,23},{8,24},{9,... | collective-permute-start | bytes 1769480 | tf_op jit(solution)/shard_map/ppermute | solution.py:29
  648.8 41.9 %collective-permute-start.30 = (bf16[2,2,4,3,16,768]{5,4,3,2,1,0:T(8,128)(2,1)S(1)}, bf16[2,2,4,3,16,768]{5,4,3,2,1,0:T(8,128)(2,1)S(1)}, u32[]{:S(2)}, u32[]{:S(2)}) collective-permute-start(bf16[2,2,4,3,16,768]{5,4,3,2,1,0:T(8,128)(2,1)S(1)} %pad_maximum_fusion.19), channel_id=1, source_target_pairs={{0,4},{1,5},{2,6},{3,7},{4,0},{5,1},{6,2},{7,3},{8,12},{9,13},{10,... | collective-permute-start | bytes 3538952 | tf_op jit(solution)/shard_map/ppermute | solution.py:29
  675.9 15.2 %collective-permute-start.50 = (bf16[2,192,768]{2,1,0:T(8,128)(2,1)S(1)}, bf16[2,192,768]{2,1,0:T(8,128)(2,1)S(1)}, u32[]{:S(2)}, u32[]{:S(2)}) collective-permute-start(bf16[2,192,768]{2,1,0:T(8,128)(2,1)S(1)} %add.357), channel_id=1, source_target_pairs={{0,4},{1,5},{2,6},{3,7},{4,0},{5,1},{6,2},{7,3},{8,12},{9,13},{10,... | collective-permute-start | bytes 1769480 | tf_op jit(solution)/shard_map/ppermute | solution.py:29
  687.9 27.3 %collective-permute-start.36 = (bf16[2,2,192,768]{3,2,1,0:T(8,128)(2,1)S(1)}, bf16[2,2,192,768]{3,2,1,0:T(8,128)(2,1)S(1)}, u32[]{:S(2)}, u32[]{:S(2)}) collective-permute-start(bf16[2,2,192,768]{3,2,1,0:T(8,128)(2,1)S(1)} %get-tuple-element.188), channel_id=1, source_target_pairs={{0,4},{1,5},{2,6},{3,7},{4,0},{5,1},{6,2},{7,3},{8,12},{9,13},{10,... | collective-permute-start | bytes 3538952 | tf_op jit(solution)/shard_map/ppermute | solution.py:29
  691.2 31.2 %collective-permute-start.51 = (bf16[2,2,192,768]{3,2,1,0:T(8,128)(2,1)S(1)}, bf16[2,2,192,768]{3,2,1,0:T(8,128)(2,1)S(1)}, u32[]{:S(2)}, u32[]{:S(2)}) collective-permute-start(bf16[2,2,192,768]{3,2,1,0:T(8,128)(2,1)S(1)} %pad_maximum_fusion.22), channel_id=1, source_target_pairs={{0,8},{1,9},{2,10},{3,11},{4,12},{5,13},{6,14},{7,15},{8,0},{9,1},... | collective-permute-start | bytes 3538952 | tf_op jit(solution)/shard_map/ppermute | solution.py:29
  717.0 52.2 %collective-permute-start.37 = (bf16[2,2,2,192,768]{4,3,2,1,0:T(8,128)(2,1)}, bf16[2,2,2,192,768]{4,3,2,1,0:T(8,128)(2,1)}, u32[]{:S(2)}, u32[]{:S(2)}) collective-permute-start(bf16[2,2,2,192,768]{4,3,2,1,0:T(8,128)(2,1)} %pad_maximum_fusion.9), channel_id=1, source_target_pairs={{0,8},{1,9},{2,10},{3,11},{4,12},{5,13},{6,14},{7,15},{8,0},{9,1},... | collective-permute-start | bytes 7077896 | tf_op jit(solution)/shard_map/ppermute | solution.py:29
  (177 other events, 1086.7 us)

commit v2 on v1

v2 whole, which is shorter than its diff:
```python
import functools

import jax
import jax.numpy as jnp
from jax import lax
from jax.experimental import pallas as pl
from jax.experimental.pallas import tpu as pltpu
from jax.sharding import PartitionSpec as P

D = 768
HEADS = 12
HEAD_DIM = 64
GRID = 15
PATCHES = 225
SLOTS = 136
PARTS = 4
PIECE = D // PARTS
CORE, ACROSS = 1, 2
SCALE = HEAD_DIM**-0.5

EPSILON = 1e-06
NEGATIVE = -1e30
F32, BF16 = jnp.float32, jnp.bfloat16
WHOLE = pl.BlockSpec(memory_space=pltpu.VMEM)
ANYWHERE = pl.BlockSpec(memory_space=pl.ANY)
SCALARS = pl.BlockSpec(memory_space=pltpu.SMEM)
ROOM = 56 << 20


def cost(rows, fixed, each):
    return pl.CostEstimate(
        flops=int((fixed + each * rows / 816) * 1e7), bytes_accessed=1, transcendentals=0
    )


def swap(array, dp_mask=0, head_mask=0, senders=None):
    groups, lanes = lax.axis_size("dp"), lax.axis_size("head")
    pairs = [
        (g * lanes + h, (g ^ dp_mask) * lanes + (h ^ head_mask))
        for g in (range(groups) if senders is None else senders)
        for h in range(lanes)
    ]
    return lax.ppermute(array, ("dp", "head"), pairs)


def tie(*arrays):
    return lax.optimization_barrier(arrays)


def rows_nt(left, right):
    return lax.dot_general(left, right, (((1,), (1,)), ((), ())), preferred_element_type=F32)


def rows_nn(left, right):
    return lax.dot_general(left, right, (((1,), (0,)), ((), ())), preferred_element_type=F32)


def rows_tn(left, right):
    return lax.dot_general(left, right, (((0,), (0,)), ((), ())), preferred_element_type=F32)


def normalize(values):
    centered = values - jnp.mean(values, -1, keepdims=True)
    spread = lax.rsqrt(jnp.mean(centered * centered, -1, keepdims=True) + EPSILON)
    return centered * spread, spread


def layer_norm(values, gain):
    return normalize(values)[0] * gain


def norm_back(values, gain, incoming):
    unit, spread = normalize(values)
    scaled = incoming * gain
    delta = spread * (
        scaled
        - jnp.mean(scaled, -1, keepdims=True)
        - unit * jnp.mean(scaled * unit, -1, keepdims=True)
    )
    return delta, jnp.sum(incoming * unit, 0, keepdims=True)


def glue(function, *arrays):
    leaves, tree = jax.tree.flatten(arrays)
    results, result_tree = jax.tree.flatten(jax.eval_shape(function, *arrays))

    def kernel(*refs):
        values = tree.unflatten([ref[...] for ref in refs[: len(leaves)]])
        for ref, value in zip(refs[len(leaves) :], jax.tree.leaves(function(*values))):
            ref[...] = value

    out = pl.pallas_call(
        kernel,
        in_specs=[WHOLE] * len(leaves),
        out_specs=[WHOLE] * len(results),
        out_shape=results,
        compiler_params=pltpu.CompilerParams(vmem_limit_bytes=ROOM),
        cost_estimate=cost(816, 1, 0),
        name="glue",
    )(*leaves)
    return result_tree.unflatten(out)


def chunks_of(rows):
    step = 2 * SLOTS if rows % (2 * SLOTS) == 0 else rows
    return [slice(start, start + step) for start in range(0, rows, step)]


QUARTERS_IN = {1: 4, 2: 2, 8: 2, 10: 4}


def feed_copies(pieces, meta, room, sems):
    if len(pieces) == 1:
        return [
            [pltpu.make_async_copy(pieces[0].at[meta[1] ^ q], room.at[q], sems.at[q])]
            for q in range(4)
        ]
    near = len(pieces) % 8
    copies = [
        [pltpu.make_async_copy(pieces[q], room.at[q], sems.at[q])] for q in range(near)
    ]
    for q in range(near, near + (len(pieces) - near) // PARTS):
        group = []
        for r in range(PARTS):
            at = near + (q - near) * PARTS + r
            rows = pl.ds(pl.multiple_of((meta[0] ^ r) * PIECE, PIECE), PIECE)
            group.append(
                pltpu.make_async_copy(pieces[at], room.at[q, :, rows, :], sems.at[at])
            )
        copies.append(group)
    return copies


def mix_copies(pieces, meta, room, sems):
    near = len(pieces) % 8
    copies = [
        pltpu.make_async_copy(
            pieces[q], room.at[:, pl.ds(q * PIECE, PIECE), :], sems.at[q]
        )
        for q in range(near)
    ]
    for at in range(near, len(pieces)):
        q, r = divmod(at - near, PARTS)
        rows = pl.ds((near + q) * PIECE, PIECE)
        copies.append(
            pltpu.make_async_copy(pieces[at], room.at[meta[0] ^ r, rows, :], sems.at[at])
        )
    return copies


SIZES = (64, 96, 128, SLOTS)


def by_size(count, branch):
    which = sum((count > size).astype(jnp.int32) for size in SIZES[:-1])
    lax.switch(which, [functools.partial(branch, size) for size in SIZES])


def two_heads(block, first):
    zero = jnp.zeros_like(block)
    return jnp.concatenate(
        [jnp.where(first, block, zero), jnp.where(first, zero, block)], 0
    ).astype(BF16)


def pick_heads(stacked, first):
    size = stacked.shape[0] // 2
    return jnp.where(first, stacked[:size], stacked[size:])


def image_setup(size, distance_ref, image, count):
    first = lax.broadcasted_iota(jnp.int32, (size, 2 * HEAD_DIM), 1) < HEAD_DIM
    distance = distance_ref[image, :size, :size]
    distance = jnp.concatenate([distance, distance], 1)
    seen = lax.broadcasted_iota(jnp.int32, (size, 1), 0) < count
    lanes = lax.broadcasted_iota(jnp.int32, (1, 2 * size), 1) < size

    def scores_of(keys, queries, slopes, head):
        slope = jnp.where(lanes, slopes[head], slopes[head + 1])
        return jnp.where(seen, rows_nt(keys, queries) - distance * slope, NEGATIVE)

    return first, scores_of


def mix_forward_kernel(local, cross, images, head, n_pieces, *refs):
    meta, slopes, x_ref = refs[:3]
    refs = refs[3:]
    if cross:
        c_ref, refs = refs[0], refs[1:]
    if local:
        gain_ref, refs = refs[0], refs[1:]
    else:
        a_ref, refs = refs[0], refs[1:]
    pieces, refs = refs[:n_pieces], refs[n_pieces:]
    distance_ref, refs = refs[0], refs[1:]
    if local:
        a_ref, refs = refs[0], refs[1:]
    out_ref, qkv_ref, o_ref, lse_ref, room, wide, sems = refs
    copies = mix_copies(pieces, meta, room, sems)
    for copy in copies:
        copy.start()
    chunks = chunks_of(images * SLOTS)
    if local:
        for rows in chunks:
            a_ref[rows, :] = layer_norm(x_ref[rows, :].astype(F32), gain_ref[...]).astype(BF16)
    for copy in copies:
        copy.wait()
    width = o_ref.shape[1]
    if cross:
        wide[:, :width] = rows_nt(a_ref[...], room[0])
        wide[:, width:] = rows_nt(c_ref[...], room[1:3].reshape(2 * width, D))
    else:
        wide[...] = rows_nt(a_ref[...], room[:3].reshape(3 * width, D))

    def one_image(i, carry):
        image = meta[2] + i
        start = pl.multiple_of(i * SLOTS, 8)
        qkv_ref[i] = wide[pl.ds(start, SLOTS), :].astype(BF16)

        def work(size):
            first, scores_of = image_setup(size, distance_ref, image, meta[3 + image])
            rows = pl.ds(start, size)
            for pair in range(width // (2 * HEAD_DIM)):
                low, high = pair * 2 * HEAD_DIM, (pair + 1) * 2 * HEAD_DIM
                k = wide[rows, width + low : width + high].astype(BF16)
                v = wide[rows, 2 * width + low : 2 * width + high].astype(BF16)
                queries = two_heads(
                    wide[rows, low:high].astype(BF16).astype(F32) * SCALE, first
                )
                scores = scores_of(k, queries, slopes, head + 2 * pair)
                top = jnp.max(scores, 0, keepdims=True)
                exponent = jnp.exp(scores - top)
                total = jnp.sum(exponent, 0, keepdims=True)
                weights = (exponent * (1.0 / total)).astype(BF16)
                wide[rows, low:high] = pick_heads(rows_tn(weights, v), first)
                lse_ref[i, pair : pair + 1, : 2 * size] = top + jnp.log(total)
            if size < SLOTS:
                rest = pl.ds(pl.multiple_of(start + size, 8), SLOTS - size)
                wide[rest, :width] = jnp.zeros((SLOTS - size, width), F32)

        by_size(meta[3 + image], work)
        return carry

    lax.fori_loop(0, images, one_image, 0)
    for rows in chunks:
        o_ref[rows, :] = wide[rows, :width].astype(BF16)
    out_ref[...] = x_ref[...].astype(F32) + rows_nn(o_ref[...], room[3])


def mix_forward(meta, slopes, x, context, gain, normed, pieces, distance, head=0):
    images = x.shape[0] // SLOTS
    rows = images * SLOTS
    cross, local = context is not None, normed is None
    width = PIECE * QUARTERS_IN[len(pieces)]
    operands = [meta, slopes, x] + ([context] if cross else [])
    operands += [gain if local else normed, *pieces, distance]
    specs = [SCALARS] * 2 + [WHOLE] * (3 if cross else 2) + [ANYWHERE] * len(pieces) + [WHOLE]
    narrow = jax.ShapeDtypeStruct((rows, D), BF16)
    return pl.pallas_call(
        functools.partial(mix_forward_kernel, local, cross, images, head, len(pieces)),
        in_specs=specs,
        out_specs=[WHOLE] * (5 if local else 4),
        out_shape=([narrow] if local else [])
        + [
            jax.ShapeDtypeStruct((rows, D), F32),
            jax.ShapeDtypeStruct((images, SLOTS, 3 * width), BF16),
            jax.ShapeDtypeStruct((rows, width), BF16),
            jax.ShapeDtypeStruct((images, width // (2 * HEAD_DIM), 2 * SLOTS), F32),
        ],
        scratch_shapes=[
            pltpu.VMEM((4, width, D), BF16),
            pltpu.VMEM((rows, 3 * width), F32),
            pltpu.SemaphoreType.DMA((16,)),
        ],
        compiler_params=pltpu.CompilerParams(vmem_limit_bytes=ROOM),
        cost_estimate=cost(rows, 4, 8 * width / 384),
        name="mix_forward",
    )(*operands)


def mix_back_kernel(cross, images, spans, *refs):
    meta, slopes, e_ref, x_ref, gain_ref = refs[:5]
    refs = refs[5:]
    qkv_refs, lse_refs, refs = refs[:spans], refs[spans : 2 * spans], refs[2 * spans :]
    pieces, refs = refs[:10], refs[10:]
    distance_ref, dx_ref, dgain_ref, dqkv_ref, eb_ref = refs[:5]
    refs = refs[5:]
    if cross:
        dc_ref, refs = refs[0], refs[1:]
    room, inner_ref, wide, sems = refs
    copies = mix_copies(pieces, meta, room, sems)
    for copy in copies:
        copy.start()
    chunks = chunks_of(images * SLOTS)
    for rows in chunks:
        eb_ref[rows, :] = e_ref[rows, :].astype(BF16)
    for copy in copies:
        copy.wait()
    inner_ref[...] = rows_nt(eb_ref[...], room[3])

    width = D // spans

    def one_image(i, carry):
        image = meta[2] + i
        start = pl.multiple_of(i * SLOTS, 8)

        def work(size):
            first, scores_of = image_setup(size, distance_ref, image, meta[3 + image])
            rows = pl.ds(start, size)
            for pair in range(HEADS // 2):
                low, high = pair * 2 * HEAD_DIM, (pair + 1) * 2 * HEAD_DIM
                half, inside = divmod(pair, HEADS // 2 // spans)
                qkv_ref, lse_ref = qkv_refs[half], lse_refs[half]
                at, to = inside * 2 * HEAD_DIM, (inside + 1) * 2 * HEAD_DIM
                queries = two_heads(qkv_ref[i, :size, at:to].astype(F32) * SCALE, first)
                incoming = two_heads(inner_ref[rows, low:high], first)
                k = qkv_ref[i, :size, width + at : width + to]
                v = qkv_ref[i, :size, 2 * width + at : 2 * width + to]
                scores = scores_of(k, queries, slopes, 2 * pair)
                probable = jnp.exp(scores - lse_ref[i, inside : inside + 1, : 2 * size])
                delta_p = rows_nt(v, incoming)
                shared = jnp.sum(delta_p * probable, 0, keepdims=True)
                delta_s = (probable * (delta_p - shared)).astype(BF16)
                wide[rows, low:high] = pick_heads(rows_tn(delta_s, k), first) * SCALE
                wide[rows, D + low : D + high] = rows_nn(delta_s, queries)
                wide[rows, 2 * D + low : 2 * D + high] = rows_nn(
                    probable.astype(BF16), incoming
                )
            if size < SLOTS:
                rest = pl.ds(pl.multiple_of(start + size, 8), SLOTS - size)
                wide[rest, :] = jnp.zeros((SLOTS - size, 3 * D), F32)

        by_size(meta[3 + image], work)
        return carry

    lax.fori_loop(0, images, one_image, 0)
    for rows in chunks:
        dqkv_ref[rows, :] = wide[rows, :].astype(BF16)
    delta = rows_nn(dqkv_ref[:, :D], room[0])
    side = rows_nn(dqkv_ref[:, D : 2 * D], room[1]) + rows_nn(dqkv_ref[:, 2 * D :], room[2])
    if cross:
        dc_ref[...] = side.astype(BF16)
        inner_ref[...] = delta
    else:
        inner_ref[...] = delta + side
    gain_total = jnp.zeros((1, D), F32)
    for rows in chunks:
        part, gain_part = norm_back(x_ref[rows, :].astype(F32), gain_ref[...], inner_ref[rows, :])
        dx_ref[rows, :] = e_ref[rows, :] + part
        gain_total = gain_total + gain_part
    dgain_ref[...] = gain_total


def mix_back(meta, slopes, delta, x, gain, qkv, lse, pieces, distance, cross):
    images = qkv[0].shape[0]
    rows = images * SLOTS
    wide_rows = jax.ShapeDtypeStruct((rows, D), BF16)
    return pl.pallas_call(
        functools.partial(mix_back_kernel, cross, images, len(qkv)),
        in_specs=[SCALARS] * 2
        + [WHOLE] * (3 + 2 * len(qkv))
        + [ANYWHERE] * len(pieces)
        + [WHOLE],
        out_specs=[WHOLE] * (5 if cross else 4),
        out_shape=[
            jax.ShapeDtypeStruct((rows, D), F32),
            jax.ShapeDtypeStruct((1, D), F32),
            jax.ShapeDtypeStruct((rows, 3 * D), BF16),
            wide_rows,
        ]
        + ([wide_rows] if cross else []),
        scratch_shapes=[
            pltpu.VMEM((4, D, D), BF16),
            pltpu.VMEM((rows, D), F32),
            pltpu.VMEM((rows, 3 * D), F32),
            pltpu.SemaphoreType.DMA((16,)),
        ],
        compiler_params=pltpu.CompilerParams(vmem_limit_bytes=ROOM),
        cost_estimate=cost(rows, 5, 23),
        name="mix_back",
    )(meta, slopes, delta, x, gain, *qkv, *lse, *pieces, distance)


def mix_weights_kernel(more, place, dqkv_ref, *refs):
    if more:
        *refs, scratch = refs
        refs, outs = refs[:-2], refs[-2:]
        refs = (*refs, scratch)
    else:
        refs, outs = refs[:-2], refs[-2:]
    if more:
        gain_refs, refs, gains_ref = refs[:5], refs[5:-1], refs[-1]
    o_refs, (a_ref, c_ref, eb_ref) = refs[:-3], refs[-3:]
    kind = pl.program_id(0)

    def put(first, delta):
        for q in range(delta.shape[0] // PIECE):
            part = delta[q * PIECE : (q + 1) * PIECE].astype(BF16)
            outs[(first + q) % 2][(first + q) // 2, 0, :PIECE] = part

    @pl.when(kind == 0)
    def _():
        put(0, rows_tn(dqkv_ref[...], a_ref[...]))

    @pl.when(jnp.logical_or(kind == 1, kind == 2))
    def _():
        put(0, rows_tn(dqkv_ref[...], c_ref[...]))

    @pl.when(kind == 3)
    def _():
        for span, o_ref in enumerate(o_refs):
            put(span * 4 // len(o_refs), rows_tn(o_ref[...], eb_ref[...]))

    if more:
        gains_ref[...] = jnp.zeros_like(gains_ref)
        for i in range(2):
            gains_ref[pl.ds(2 * place[2] + i, 1), :] = gain_refs[i][...]
        for i in range(2, 5):
            gains_ref[2 + i : 3 + i, :] = gain_refs[i][...]
        for out in outs:
            for half in range(2):
                out[half, 0, PIECE:] = gains_ref[...].astype(BF16)


def mix_weights(place, dqkv, o, a, c, eb, gains=None):
    rows = a.shape[0]
    more = gains is not None
    fixed = pl.BlockSpec((rows, D), lambda kind, place: (0, 0))
    narrow = pl.BlockSpec((rows, D // len(o)), lambda kind, place: (0, 0))
    tall = PIECE + (16 if more else 0)
    out = pl.BlockSpec((2, 1, tall, D), lambda kind, place: (0, kind ^ place[0], 0, 0))
    shape = jax.ShapeDtypeStruct((2, PARTS, tall, D), BF16)
    return pl.pallas_call(
        functools.partial(mix_weights_kernel, more),
        grid_spec=pltpu.PrefetchScalarGridSpec(
            num_scalar_prefetch=1,
            grid=(4,),
            in_specs=[pl.BlockSpec((rows, D), lambda kind, place: (0, jnp.minimum(kind, 2)))]
            + [pl.BlockSpec((1, D), lambda kind, place: (0, 0))] * (5 if more else 0)
            + [narrow] * len(o)
            + [fixed] * 3,
            out_specs=[out, out],
            scratch_shapes=[pltpu.VMEM((16, D), F32)] if more else [],
        ),
        out_shape=[shape, shape],
        compiler_params=pltpu.CompilerParams(vmem_limit_bytes=ROOM),
        cost_estimate=cost(rows, 3.5, 7),
        name="mix_weights",
    )(place, dqkv, *(gains if more else []), *o, a, c, eb)


def fetch_quarter(step, copies):
    @pl.when(step == 0)
    def _():
        for group in copies:
            for copy in group:
                copy.start()

    for q, group in enumerate(copies):

        @pl.when(step == q)
        def _(group=group):
            for copy in group:
                copy.wait()


def feed_forward_kernel(local, n_pieces, meta, x_ref, norm_ref, *refs):
    pieces, refs = refs[:n_pieces], refs[n_pieces:]
    if local:
        b_ref, refs = refs[0], refs[1:]
    else:
        b_ref = norm_ref
    y_ref, h_ref, g_ref, room, sems = refs
    step = pl.program_id(0)
    fetch_quarter(step, feed_copies(pieces, meta, room, sems))

    @pl.when(step == 0)
    def _():
        for rows in chunks_of(x_ref.shape[0]):
            values = x_ref[rows, :]
            y_ref[rows, :] = values
            if local:
                b_ref[rows, :] = layer_norm(values, norm_ref[...]).astype(BF16)

    before = rows_nn(b_ref[...], room[step, 0])
    bell = jnp.exp(-0.5 * before * before) * 0.3989422804014327
    share = 0.5 * (1.0 + lax.erf(before * 0.7071067811865476))
    h_ref[...] = (before * share).astype(BF16)
    g_ref[...] = (share + before * bell).astype(BF16)
    y_ref[...] += rows_nn(h_ref[...], room[step, 1])


def feed_forward(meta, x, gain, normed, pieces):
    rows = x.shape[0]
    local = normed is None
    quarters = QUARTERS_IN[len(pieces)]
    fixed = pl.BlockSpec((rows, D), lambda q: (0, 0))
    moving = pl.BlockSpec((rows, D), lambda q: (0, q))
    hidden = jax.ShapeDtypeStruct((rows, quarters * D), BF16)
    return pl.pallas_call(
        functools.partial(feed_forward_kernel, local, len(pieces)),
        grid=(quarters,),
        in_specs=[SCALARS, fixed, pl.BlockSpec((1, D), lambda q: (0, 0)) if local else fixed]
        + [ANYWHERE] * len(pieces),
        out_specs=([fixed] if local else []) + [fixed, moving, moving],
        out_shape=([jax.ShapeDtypeStruct((rows, D), BF16)] if local else [])
        + [jax.ShapeDtypeStruct((rows, D), F32), hidden, hidden],
        scratch_shapes=[pltpu.VMEM((quarters, 2, D, D), BF16), pltpu.SemaphoreType.DMA((16,))],
        compiler_params=pltpu.CompilerParams(vmem_limit_bytes=ROOM),
        cost_estimate=cost(rows, 3.6, 4 * quarters),
        name="feed_forward",
    )(meta, x, gain if local else normed, *pieces)


def feed_rows_kernel(leaving, meta, x_ref, gain_ref, next_gain_ref, *refs):
    pieces, refs = refs[:10], refs[10:]
    if not leaving:
        refs = refs[4:]
    y_ref, b_ref, h_ref, g_ref, out_ref, room, sems = refs
    step = pl.program_id(0)
    fetch_quarter(step, feed_copies(pieces, meta, room, sems))

    @pl.when(step == 0)
    def _():
        values = x_ref[...]
        y_ref[...] = values
        b_ref[...] = layer_norm(values, gain_ref[...]).astype(BF16)

    before = rows_nn(b_ref[...], room[step, 0])
    bell = jnp.exp(-0.5 * before * before) * 0.3989422804014327
    share = 0.5 * (1.0 + lax.erf(before * 0.7071067811865476))
    h_ref[...] = (before * share).astype(BF16)
    g_ref[...] = (share + before * bell).astype(BF16)
    y_ref[...] += rows_nn(h_ref[...], room[step, 1])

    @pl.when(jnp.logical_and(step == 3, jnp.logical_or(not leaving, meta[2] == 0)))
    def _():
        out_ref[...] = layer_norm(y_ref[...], next_gain_ref[...]).astype(BF16)

    if leaving:

        @pl.when(jnp.logical_and(step == 3, meta[2] == 1))
        def _():
            out_ref[...] = y_ref[...].astype(BF16)


def feed_rows(place, x, gain, next_gain, pieces, first=None):
    rows = x.shape[0] // 2
    leaving = first is None

    def block(place):
        return 1 - place[2] if leaving else place[2]

    fixed = pl.BlockSpec((rows, D), lambda q, place: (block(place), 0))
    moving = pl.BlockSpec((rows, D), lambda q, place: (block(place), q))
    narrow = pl.BlockSpec((1, D), lambda q, place: (0, 0))
    hidden = jax.ShapeDtypeStruct((2 * rows, 4 * D), BF16)
    return pl.pallas_call(
        functools.partial(feed_rows_kernel, leaving),
        grid_spec=pltpu.PrefetchScalarGridSpec(
            num_scalar_prefetch=1,
            grid=(4,),
            in_specs=[fixed, narrow, narrow] + [ANYWHERE] * (10 if leaving else 14),
            out_specs=[fixed, fixed, moving, moving]
            + [pl.BlockSpec((rows, D), lambda q, place: (0, 0))],
            scratch_shapes=[pltpu.VMEM((4, 2, D, D), BF16), pltpu.SemaphoreType.DMA((16,))],
        ),
        out_shape=[
            jax.ShapeDtypeStruct((2 * rows, D), F32),
            jax.ShapeDtypeStruct((2 * rows, D), BF16),
            hidden,
            hidden,
            jax.ShapeDtypeStruct((rows, D), BF16),
        ],
        input_output_aliases={} if leaving else {14 + i: i for i in range(4)},
        compiler_params=pltpu.CompilerParams(vmem_limit_bytes=ROOM),
        cost_estimate=cost(rows, 3.6, 16),
        name="feed_rows",
    )(place, x, gain, next_gain, *pieces, *([] if leaving else first))


def feed_back_kernel(spans, n_pieces, meta, e_ref, x_ref, gain_ref, *refs):
    slopes, refs = refs[:spans], refs[spans:]
    pieces, refs = refs[:n_pieces], refs[n_pieces:]
    dx_ref, dgain_ref, eb_ref, eu_ref, room, sems = refs
    step = pl.program_id(0)
    fetch_quarter(step, feed_copies(pieces, meta, room, sems))
    chunks = chunks_of(x_ref.shape[0])

    @pl.when(step == 0)
    def _():
        for rows in chunks:
            eb_ref[rows, :] = e_ref[rows, :].astype(BF16)
            dx_ref[rows, :] = jnp.zeros_like(dx_ref[rows, :])

    slope = slopes[0][...]
    if spans == 2:
        slope = jnp.where(step < 2, slope, slopes[1][...])
    slope = slope.astype(F32)
    eu_ref[...] = (rows_nt(eb_ref[...], room[step, 1]) * slope).astype(BF16)
    dx_ref[...] += rows_nt(eu_ref[...], room[step, 0])

    @pl.when(step == 3)
    def _():
        gain_total = jnp.zeros((1, D), F32)
        for rows in chunks:
            part, gain_part = norm_back(x_ref[rows, :], gain_ref[...], dx_ref[rows, :])
            dx_ref[rows, :] = e_ref[rows, :] + part
            gain_total = gain_total + gain_part
        dgain_ref[...] = gain_total


def feed_back(meta, delta, x, gain, slope, pieces):
    rows = x.shape[0]
    fixed = pl.BlockSpec((rows, D), lambda q: (0, 0))
    moving = pl.BlockSpec((rows, D), lambda q: (0, q))
    narrow = pl.BlockSpec((1, D), lambda q: (0, 0))
    slopes = [moving]
    if len(slope) == 2:
        slopes = [
            pl.BlockSpec((rows, D), lambda q: (0, jnp.minimum(q, 1))),
            pl.BlockSpec((rows, D), lambda q: (0, jnp.maximum(q - 2, 0))),
        ]
    return pl.pallas_call(
        functools.partial(feed_back_kernel, len(slope), len(pieces)),
        grid=(4,),
        in_specs=[SCALARS, fixed, fixed, narrow] + slopes + [ANYWHERE] * len(pieces),
        out_specs=[fixed, narrow, fixed, moving],
        out_shape=[
            jax.ShapeDtypeStruct((rows, D), F32),
            jax.ShapeDtypeStruct((1, D), F32),
            jax.ShapeDtypeStruct((rows, D), BF16),
            jax.ShapeDtypeStruct((rows, 4 * D), BF16),
        ],
        scratch_shapes=[pltpu.VMEM((4, 2, D, D), BF16), pltpu.SemaphoreType.DMA((16,))],
        compiler_params=pltpu.CompilerParams(vmem_limit_bytes=ROOM),
        cost_estimate=cost(rows, 5, 13.5),
        name="feed_back",
    )(meta, delta, x, gain, *slope, *pieces)


def feed_weights_kernel(place, eu_ref, *refs):
    h_refs, (b_ref, eb_ref, out_ref) = refs[:-3], refs[-3:]
    j, kind = pl.program_id(0), pl.program_id(1)

    def put(delta):
        for p in range(PARTS):
            rows = pl.ds(pl.multiple_of((place[0] ^ p) * PIECE, PIECE), PIECE)
            out_ref[0, 0, rows, :] = delta[p * PIECE : (p + 1) * PIECE].astype(BF16)

    @pl.when(kind == 0)
    def _():
        put(rows_tn(b_ref[...], eu_ref[...]))

    for span, h_ref in enumerate(h_refs):

        @pl.when(jnp.logical_and(kind == 1, jnp.logical_or(len(h_refs) == 1, j == span)))
        def _(h_ref=h_ref):
            put(rows_tn(h_ref[...], eb_ref[...]))


def feed_weights(place, eu, h, b, eb, first):
    rows = b.shape[0]
    fixed = pl.BlockSpec((rows, D), lambda j, kind, place: (0, 0))
    moving = pl.BlockSpec((rows, D), lambda j, kind, place: (0, 2 * j + first))
    hidden = [moving]
    if len(h) == 2:
        hidden = [pl.BlockSpec((rows, D), lambda j, kind, place: (0, first))] * 2
    return pl.pallas_call(
        feed_weights_kernel,
        grid_spec=pltpu.PrefetchScalarGridSpec(
            num_scalar_prefetch=1,
            grid=(2, 2),
            in_specs=[moving] + hidden + [fixed, fixed],
            out_specs=pl.BlockSpec((1, 1, D, D), lambda j, kind, place: (j, kind, 0, 0)),
        ),
        out_shape=jax.ShapeDtypeStruct((2, 2, D, D), BF16),
        compiler_params=pltpu.CompilerParams(vmem_limit_bytes=ROOM),
        cost_estimate=cost(rows, 4, 6),
        name="feed_weights",
    )(place, eu, *h, b, eb)


def turn_back_kernel(
    meta, side, encoded, gain, context, returned, radar_part, cotangent, out, gain_out
):
    cut = context.shape[0]

    @pl.when(side[0] == 1)
    def _():
        out[:cut] = returned[...].astype(F32)
        out[cut:] = radar_part[...]
        gain_out[...] = jnp.zeros_like(gain_out)

    @pl.when(side[0] == 0)
    def _():
        total = jnp.zeros_like(gain_out)
        for part, incoming in enumerate((context, returned)):
            rows = slice(part * cut, (part + 1) * cut)
            delta, gain_part = norm_back(encoded[rows], gain[...], incoming[...].astype(F32))
            total = total + gain_part
            out[rows] = delta
        gain_out[...] = total

        def one_image(i, carry):
            rows = pl.ds(pl.multiple_of(i * SLOTS, 8), SLOTS)
            seen = lax.broadcasted_iota(jnp.int32, (SLOTS, 1), 0) < meta[3 + i]
            out[rows] += jnp.where(seen, cotangent[i].astype(F32), 0.0)
            return carry

        lax.fori_loop(0, cotangent.shape[0], one_image, 0)


def turn_back(meta, modality, encoded, gain, context, returned, radar_part, cotangent):
    return pl.pallas_call(
        turn_back_kernel,
        in_specs=[SCALARS] * 2 + [WHOLE] * 6,
        out_specs=[WHOLE] * 2,
        out_shape=[
            jax.ShapeDtypeStruct(encoded.shape, F32),
            jax.ShapeDtypeStruct((1, D), F32),
        ],
        compiler_params=pltpu.CompilerParams(vmem_limit_bytes=ROOM),
        cost_estimate=cost(816, 5, 0),
        name="turn_back",
    )(meta, modality[None], encoded, gain, context, returned, radar_part, cotangent)


def relative_parts(parts, own):
    return jnp.stack(
        [lax.dynamic_index_in_dim(parts, r ^ own, 0, keepdims=False) for r in range(PARTS)]
    )


def pack_mix(triple, out_weight):
    return jnp.concatenate([triple.transpose(1, 2, 0), out_weight[None]], 0)


def piece_of(quarter, part):
    if quarter.shape[1] == PIECE:
        return lax.dynamic_index_in_dim(quarter, part, 0, keepdims=False)
    return lax.dynamic_slice_in_dim(quarter, part * PIECE, PIECE, 1)


def unpack_mix(parts):
    return parts[:3].transpose(2, 0, 1).astype(F32), parts[3].astype(F32)


def unpack_feed_kernel(place, *refs):
    refs, (expand_ref, reduce_ref) = refs[:-2], refs[-2:]
    step = PIECE // 2
    for n in range(len(refs) // 5):

        @pl.when(pl.program_id(0) == n)
        def _(n=n):
            part, low, high, low_far, high_far = refs[5 * n : 5 * n + 5]
            for kind, out in enumerate((expand_ref, reduce_ref)):
                lows = [part[kind, :step], low[kind], low_far[0, kind], low_far[1, kind]]
                highs = [part[kind, step:], high_far[0, kind], high[kind], high_far[1, kind]]
                for p in range(PARTS):
                    start = pl.multiple_of((place[0] ^ p) * PIECE, PIECE)
                    out[0, pl.ds(start, step), :] = lows[p].astype(F32)
                    out[0, pl.ds(start + step, step), :] = highs[p].astype(F32)


def unpack_feed(place, *gathered):
    count = len(gathered)
    operands = [piece for pieces in gathered for piece in pieces]
    if count == 1:
        out = pl.BlockSpec((1, D, D), lambda n, place: (n, 0, 0))
    else:
        out = pl.BlockSpec((1, D, D), lambda n, place: (n ^ place[2], 0, 0))
    shape = jax.ShapeDtypeStruct((count, D, D), F32)
    return pl.pallas_call(
        unpack_feed_kernel,
        grid_spec=pltpu.PrefetchScalarGridSpec(
            num_scalar_prefetch=1,
            grid=(count,),
            in_specs=[WHOLE] * len(operands),
            out_specs=[out, out],
        ),
        out_shape=[shape, shape],
        compiler_params=pltpu.CompilerParams(vmem_limit_bytes=ROOM),
        cost_estimate=cost(816, 1, 2 * count),
        name="unpack_feed",
    )(place, *operands)


def fetch_relayed(zero, three):
    return (zero, swap(zero, dp_mask=1), swap(zero, dp_mask=2), three)


def fetch_beside(pieces):
    return pieces + tuple(swap(piece, head_mask=CORE) for piece in pieces)


AXES = {"x": (0, 0, ACROSS), "y": (3, 1, 0), "z": (2, 2, 0)}
THIRDS = ("xyz", "yxz", "zxy")
HALVES = ("xyz", "yzx")
LAST = ("xyz", "yxz")


def halves(array, axis):
    return lax.slice_in_dim(array, 0, 1, axis=axis), lax.slice_in_dim(array, 1, 2, axis=axis)


def add_split(keep, beside, orders=THIRDS):
    kinds, rows = keep.shape[1:3]
    kinds, rows = (1, rows) if kinds == PARTS else (kinds, rows // PARTS)
    total = (keep + beside).reshape(2, kinds, 2, 2, rows, D)
    step = PIECE // len(orders)
    cuts = [i * step for i in range(len(orders))] + [rows]
    return [total[:, :, :, :, low:high] for low, high in zip(cuts[:-1], cuts[1:])]


def link_send(shares, stage, orders=THIRDS):
    out = []
    for array, order in zip(shares, orders, strict=True):
        axis, dp_mask, head_mask = AXES[order[stage]]
        keep, sent = halves(array, axis)
        out.append((keep, swap(sent, dp_mask, head_mask)))
    return out


def link_next(pairs, stage, orders=THIRDS):
    def split(pairs):
        return [
            halves(keep + received, AXES[order[stage]][0])
            for (keep, received), order in zip(pairs, orders, strict=True)
        ]

    return [
        (keep, swap(sent, *AXES[order[stage]][1:]))
        for (keep, sent), order in zip(glue(split, pairs), orders, strict=True)
    ]


def link_add(pairs):
    return [keep + received for keep, received in pairs]


def join(shares):
    return jnp.concatenate([share[0, :, 0, 0] for share in shares], 1)


def rest_send(array, stop):
    mask = PARTS
    while 2 * mask < stop:
        array = array + swap(array, dp_mask=mask)
        mask *= 2
    return array, swap(array, dp_mask=mask)


def rest_add(pair):
    return pair[0] + pair[1]


def over_rest(array, stop):
    mask = PARTS
    while mask < stop:
        array = array + swap(array, dp_mask=mask)
        mask *= 2
    return array


def gather_first(part):
    step = PIECE // 2
    return part, swap(part[:, :step], dp_mask=1), swap(part[:, step:PIECE], dp_mask=2)


def gather_second(first):
    part, low, high = first
    step = PIECE // 2
    return (
        part,
        low,
        high,
        swap(jnp.stack([part[:, :step], low]), dp_mask=2),
        swap(jnp.stack([part[:, step:PIECE], high]), dp_mask=1),
    )


def gather_join(pieces):
    part, low, high, low_far, high_far = pieces
    step = PIECE // 2
    lows = [part[:, :step], low, low_far[0], low_far[1]]
    highs = [part[:, step:PIECE], high_far[0], high, high_far[1]]
    return jnp.stack([jnp.concatenate(pair, 1) for pair in zip(lows, highs, strict=True)])


def on_device(
    tokens,
    cotangent,
    ratios,
    patch_index,
    encoder_gains,
    encoder_attend_in,
    encoder_attend_out,
    encoder_expand,
    encoder_reduce,
    uniting_gains,
    uniting_query,
    uniting_pair,
    uniting_attend_out,
    uniting_expand,
    uniting_reduce,
):
    groups = lax.axis_size("dp")
    side = groups // 2
    group, lane = lax.axis_index("dp"), lax.axis_index("head")
    radar = group >= side
    modality = radar.astype(jnp.int32)
    own = group % PARTS
    images = tokens.shape[0]
    some = images // 2
    cut = some * SLOTS

    def select_slot(stacked):
        return lax.dynamic_index_in_dim(stacked, modality, 0, keepdims=False)

    gains = select_slot(encoder_gains)[:, None]
    uni_gains = uniting_gains[:, None]

    own_ratios = lax.dynamic_slice_in_dim(ratios, lane * images, images, 0)
    patches = lax.dynamic_slice_in_dim(patch_index, lane * images, images, 0)
    counts = PATCHES * (100 - own_ratios) // 100
    first = modality * some
    meta = jnp.concatenate([jnp.stack([own, lane, 0 * first]), counts])
    pair_meta = jnp.concatenate([jnp.stack([own, lane, first]), counts])
    place = jnp.stack([own, lane, modality])
    visible = (jnp.arange(SLOTS)[None, :] < counts[:, None])[:, :, None]
    queries = patches[:, None, :]
    row_gap = (patches // GRID)[:, :, None] - queries // GRID
    col_gap = (patches % GRID)[:, :, None] - queries % GRID
    distance = jnp.sqrt((row_gap * row_gap + col_gap * col_gap).astype(F32))
    per_lane = HEADS // lax.axis_size("head")
    heads = jnp.concatenate(
        [(lane ^ mask) * per_lane + jnp.arange(per_lane) for mask in range(4)]
    )
    slopes = 2.0 ** (-8.0 * (heads.astype(F32) + 1.0) / HEADS)

    mix_quarter = pack_mix(select_slot(encoder_attend_in), select_slot(encoder_attend_out))
    mix_zero = swap(piece_of(mix_quarter, own), head_mask=ACROSS)
    mix_near = (mix_quarter, swap(mix_quarter, head_mask=CORE))
    mix_quarter, encoder_expand, encoder_reduce = tie(
        mix_quarter, encoder_expand, encoder_reduce
    )
    feed_quarter = jnp.stack([select_slot(encoder_expand), select_slot(encoder_reduce)])
    feed_quarter, mix_quarter, mix_zero, flat, uni_feed_quarter = tie(
        feed_quarter,
        mix_quarter,
        mix_zero,
        tokens.reshape(-1, D),
        jnp.stack([uniting_expand, uniting_reduce]),
    )
    mix_pieces = fetch_relayed(
        mix_zero, swap(piece_of(mix_quarter, own ^ 3), head_mask=ACROSS)
    )
    feed_zero = swap(piece_of(feed_quarter, own), head_mask=ACROSS)
    feed_near = (feed_quarter, swap(feed_quarter, head_mask=CORE))

    normed_one, middle, *near = mix_forward(
        meta, slopes, flat, None, gains[0], None, mix_near, distance
    )
    middle, mix_pieces, feed_zero, feed_near = tie(middle, mix_pieces, feed_zero, feed_near)
    feed_quarter = feed_near[0]
    mix_far = fetch_beside(mix_pieces)
    feed_pieces = fetch_relayed(
        feed_zero, swap(piece_of(feed_quarter, own ^ 3), head_mask=ACROSS)
    )
    feed_zero, uniting_query, uniting_pair, uniting_attend_out = tie(
        feed_zero, uniting_query, uniting_pair, uniting_attend_out
    )
    uni_quarter = pack_mix(
        jnp.concatenate([uniting_query[:, None], uniting_pair], 1), uniting_attend_out
    )
    middle, mix_far, uni_feed_quarter = tie(middle, mix_far, uni_feed_quarter)
    uni_feed = (lax.all_gather(uni_feed_quarter, "head"),)
    middle, *far = mix_forward(
        meta, slopes, middle, None, None, normed_one, mix_far, distance, HEADS // 2
    )
    qkv, mixed, lse = zip(near, far)
    middle, feed_pieces, uni_quarter = tie(middle, feed_pieces, uni_quarter)
    feed_far = fetch_beside(feed_pieces)
    uni_zero = swap(piece_of(uni_quarter, own), head_mask=ACROSS)
    uni_three = swap(piece_of(uni_quarter, own ^ 3), head_mask=ACROSS)
    enc_mix, enc_feed = mix_near + mix_far, feed_near + feed_far

    *half_fed, leaving = feed_rows(place, middle, gains[1], uni_gains[0], enc_feed)
    leaving, half_fed, uni_zero = tie(leaving, half_fed, uni_zero)
    received = swap(leaving, dp_mask=side)
    uni_mix_pieces = fetch_relayed(uni_zero, uni_three)
    uni_mix_near = (uni_quarter, swap(uni_quarter, head_mask=CORE))
    encoded, normed_two, *stored, context = feed_rows(
        place, middle, gains[1], uni_gains[0], enc_feed, half_fed
    )
    hidden, bend = ([part] for part in stored)
    encoded, received, uni_mix_pieces = tie(encoded, received, uni_mix_pieces)
    uni_mix = uni_mix_near + fetch_beside(uni_mix_pieces)
    received, cotangent = tie(received, cotangent)
    sent_cotangent = swap(cotangent[:some], dp_mask=side)
    radar_rows = jnp.where(radar, encoded[cut:], received.astype(F32))
    context_rows = jnp.where(radar, received, context)

    uni_normed, uni_middle, *stored = mix_forward(
        pair_meta, slopes, radar_rows, context_rows, uni_gains[1], None, uni_mix, distance
    )
    uni_qkv, uni_mixed, uni_lse = ([part] for part in stored)
    uni_normed_two, joined, *stored = feed_forward(
        meta, uni_middle, uni_gains[2], None, uni_feed
    )
    uni_hidden, uni_bend = ([part] for part in stored)

    joined, sent_cotangent = tie(joined, sent_cotangent)
    joined_half = joined.astype(BF16).reshape(some, SLOTS, D)
    other_half = [swap(joined_half[i : i + 1], dp_mask=side) for i in range(some)]
    pair_cotangent = jnp.where(radar, cotangent[some:], sent_cotangent)
    pair_visible = lax.dynamic_slice_in_dim(visible, first, some, 0)
    delta_joined = jnp.where(pair_visible, pair_cotangent, 0).astype(F32).reshape(-1, D)
    delta_middle, gain_three, eb, eu = feed_back(
        meta, delta_joined, uni_middle, uni_gains[2], uni_bend, uni_feed
    )
    eu, other_half[0] = tie(eu, other_half[0])
    sent = feed_weights(place, eu, uni_hidden, uni_normed_two, eb, 1)
    sent, eu, other_half[1] = tie(sent, eu, other_half[1])
    beside = swap(sent, head_mask=CORE)
    keep = feed_weights(place, eu, uni_hidden, uni_normed_two, eb, 0)
    keep, beside = tie(keep, beside)
    uni_feed_sum, delta_middle = tie(add_split(keep, beside), delta_middle)
    uni_feed_pairs = link_send(uni_feed_sum, 0)
    delta_radar, gain_two, dqkv, mix_eb, delta_context = mix_back(
        pair_meta,
        slopes,
        delta_middle,
        radar_rows,
        uni_gains[1],
        uni_qkv,
        uni_lse,
        uni_mix,
        distance,
        True,
    )
    leaving = jnp.where(radar, delta_context, delta_radar.astype(BF16))
    leaving, dqkv, uni_feed_pairs, other_half = tie(leaving, dqkv, uni_feed_pairs, other_half)
    other_half = jnp.concatenate(other_half, 0)
    returned = swap(leaving, dp_mask=side)
    uni_feed_pairs = link_next(uni_feed_pairs, 1)
    keep, sent = mix_weights(place, dqkv, uni_mixed, uni_normed, context_rows, mix_eb)
    layer_output = jnp.where(
        visible,
        jnp.where(
            radar,
            jnp.concatenate([other_half, joined_half], 0),
            encoded.astype(BF16).reshape(images, SLOTS, D),
        ),
        0,
    )
    sent, returned, uni_feed_pairs, layer_output = tie(
        sent, returned, uni_feed_pairs, layer_output
    )
    beside = swap(sent, head_mask=CORE)
    uni_feed_pairs = link_send(link_add(uni_feed_pairs), 2)
    delta_encoded, gain_one = turn_back(
        meta, modality, encoded, uni_gains[0], delta_context, returned, delta_radar, cotangent
    )
    delta_encoded, beside, uni_feed_pairs = tie(delta_encoded, beside, uni_feed_pairs)
    uni_mix_sum, uni_feed_part = add_split(keep, beside, HALVES), join(link_add(uni_feed_pairs))
    delta_encoded, uni_mix_sum, uni_feed_part = tie(delta_encoded, uni_mix_sum, uni_feed_part)
    uni_feed_rest = rest_send(uni_feed_part, groups)
    uni_mix_pairs = link_send(uni_mix_sum, 0, HALVES)

    delta_middle, gain_b, eb, eu = feed_back(
        meta, delta_encoded, middle, gains[1], bend, enc_feed
    )
    eu, uni_mix_pairs = tie(eu, uni_mix_pairs)
    uni_mix_sum, eu = tie(link_add(uni_mix_pairs), eu)
    uni_mix_pairs = link_send(uni_mix_sum, 1, HALVES)
    sent = feed_weights(place, eu, hidden, normed_two, eb, 1)
    sent, eu, uni_feed_rest, uni_mix_pairs = tie(sent, eu, uni_feed_rest, uni_mix_pairs)
    uni_feed_part, uni_mix_sum = rest_add(uni_feed_rest), link_add(uni_mix_pairs)
    eu, uni_feed_part, uni_mix_sum = tie(eu, uni_feed_part, uni_mix_sum)
    beside = swap(sent, head_mask=CORE)
    uni_feed_near = swap(uni_feed_part, dp_mask=1)
    uni_mix_pairs = link_send(uni_mix_sum, 2, HALVES)
    keep = feed_weights(place, eu, hidden, normed_two, eb, 0)
    keep, beside, uni_feed_near, uni_mix_pairs = tie(keep, beside, uni_feed_near, uni_mix_pairs)
    uni_feed_near = jnp.stack([uni_feed_part, uni_feed_near])
    enc_feed_sum, uni_mix_part = add_split(keep, beside, HALVES), join(link_add(uni_mix_pairs))
    delta_middle, enc_feed_sum, uni_mix_part, uni_feed_near = tie(
        delta_middle, enc_feed_sum, uni_mix_part, uni_feed_near
    )
    enc_feed_pairs = link_send(enc_feed_sum, 0, HALVES)
    uni_mix_rest = rest_send(uni_mix_part, groups)
    uni_feed_far = swap(uni_feed_near, dp_mask=2)
    delta_inputs, gain_a, dqkv, eb = mix_back(
        meta, slopes, delta_middle, flat, gains[0], qkv, lse, enc_mix, distance, False
    )
    dqkv, enc_feed_pairs, uni_mix_rest, uni_feed_far = tie(
        dqkv, enc_feed_pairs, uni_mix_rest, uni_feed_far
    )
    enc_feed_sum, uni_mix_part = link_add(enc_feed_pairs), rest_add(uni_mix_rest)
    dqkv, enc_feed_sum, uni_mix_part = tie(dqkv, enc_feed_sum, uni_mix_part)
    enc_feed_pairs = link_send(enc_feed_sum, 1, HALVES)
    uni_mix_gather = gather_first(uni_mix_part)

    totals = (gain_a, gain_b, gain_one, gain_two, gain_three)
    keep, sent = mix_weights(place, dqkv, mixed, normed_one, normed_one, eb, totals)
    sent, enc_feed_pairs, uni_mix_gather = tie(sent, enc_feed_pairs, uni_mix_gather)
    beside = swap(sent, head_mask=CORE)
    enc_feed_pairs = link_send(link_add(enc_feed_pairs), 2, HALVES)
    enc_mix_pairs = link_send(add_split(keep, beside, LAST), 0, LAST)
    feed_part = over_rest(join(link_add(enc_feed_pairs)), side)
    feed_other = swap(feed_part, dp_mask=side)
    enc_mix_pairs, feed_part = tie(enc_mix_pairs, feed_part)
    enc_mix_pairs = link_send(link_add(enc_mix_pairs), 1, LAST)
    feed_gather = gather_first(feed_part)
    enc_mix_pairs = link_send(link_add(enc_mix_pairs), 2, LAST)
    enc_mix_pairs, feed_gather = tie(enc_mix_pairs, feed_gather)
    feed_gather = gather_second(feed_gather)
    enc_mix_pairs, feed_other = tie(enc_mix_pairs, feed_other)
    mix_part = over_rest(join(link_add(enc_mix_pairs)), side)
    mix_part, feed_other = tie(mix_part, feed_other)
    mix_other = swap(mix_part, dp_mask=side)
    feed_other_gather = gather_first(feed_other)
    feed_gather, uni_feed_near = tie(feed_gather, uni_feed_near)
    uni_feed_all = relative_parts(jnp.concatenate([uni_feed_near, uni_feed_far], 0), own)
    fexpand, freduce = (uni_feed_all[:, i].reshape(D, D).astype(F32) for i in range(2))
    mix_other, feed_other_gather, feed_gather, uni_mix_gather, fexpand, freduce = tie(
        mix_other, feed_other_gather, feed_gather, uni_mix_gather, fexpand, freduce
    )
    mix_gather = gather_first(jnp.concatenate([mix_part, mix_other], 0))
    feed_other_gather = gather_second(feed_other_gather)
    mix_gather, uni_mix_gather = tie(mix_gather, uni_mix_gather)
    mix_gather, uni_mix_gather = gather_second(mix_gather), gather_second(uni_mix_gather)
    totals = (mix_part + mix_other)[0, PIECE:].astype(F32)

    ftriple, fout = unpack_mix(relative_parts(gather_join(uni_mix_gather)[:, 0], own))
    expands, reduces = unpack_feed(place, feed_gather, feed_other_gather)
    mix_all = gather_join(mix_gather)
    mine, theirs = mix_all[:, 0], mix_all[:, 1]
    mixes = [
        unpack_mix(relative_parts(part, own))
        for part in (jnp.where(radar, theirs, mine), jnp.where(radar, mine, theirs))
    ]

    return (
        layer_output,
        delta_inputs.reshape(images, SLOTS, D),
        totals[:4].reshape(2, 2, D),
        jnp.stack([mixes[0][0], mixes[1][0]]),
        jnp.stack([mixes[0][1], mixes[1][1]]),
        expands,
        reduces,
        totals[4:7],
        ftriple[:, 0],
        ftriple[:, 1:],
        fout,
        fexpand,
        freduce,
    )


def solution(mesh):
    return jax.shard_map(
        on_device,
        mesh=mesh,
        in_specs=(
            P(("dp", "head"), None, None),
            P(("dp", "head"), None, None),
            P("dp"),
            P("dp", None),
            P(),
            P(None, None, None, "head"),
            P(None, "head", None),
            P(None, None, "head"),
            P(None, "head", None),
            P(),
            P(None, "head"),
            P(None, None, "head"),
            P("head", None),
            P(None, "head"),
            P("head", None),
        ),
        out_specs=(
            P(("dp", "head"), None, None),
            P(("dp", "head"), None, None),
            P(),
            P(None, None, None, "head"),
            P(None, "head", None),
            P(None, None, "head"),
            P(None, "head", None),
            P(),
            P(None, "head"),
            P(None, None, "head"),
            P("head", None),
            P(None, "head"),
            P("head", None),
        ),
        check_vma=False,
    )
```

time: 798 us -> 520 us (0.65)
  Pallas kernels: 56.4 us -> 222 us
  waiting for transfers between devices: 261 us -> 118 us
  matrix products: 126 us -> 0 us
  blocking collectives: 77.2 us -> 0 us
  other arithmetic: 119 us -> 45.7 us
  local copies, waits for them, and re-layouts: 92.6 us -> 32.4 us
  starting transfers between devices: 51.5 us -> 81.2 us
  between operations: 3.34 us -> 16 us
    pallas_call x8 -> x19, Pallas kernels: 56.4 us -> 222 us  [the longest x3 42.5 us: mix_forward(): pl.pallas_call(functools.partial(mix_forward_kernel, local, cross, images...]
    ppermute x52 -> x86, waiting for transfers between devices: 261 us -> 118 us  [swap(): return lax.ppermute(array, ('dp', 'head'), pairs)]
    dot_general x58 -> x0, matrix products: 126 us -> none  [the longest x20 46.9 us: rows_tn(): lax.dot_general(left, right, (((0,), (0,)), ((), ())), preferred_element_...]
    psum x1 -> x0, blocking collectives: 77.2 us -> none  [on_device(): lax.psum((slot_mask * jnp.stack([gain_a, gain_b])[None], jnp.stack([gain_...]
    another operation x33 -> x25, other arithmetic: 43.1 us -> 8.86 us  [the longest x3 2.22 us: on_device(): jnp.stack([mixes[0][0], mixes[1][0]])]
    unnamed x337 -> x152, local copies, waits for them, and re-layouts: 42.2 us -> 10.3 us
    ppermute x52 -> x86, starting transfers between devices: 51.5 us -> 81.1 us  [swap(): return lax.ppermute(array, ('dp', 'head'), pairs)]
    slice x57 -> x36, local copies, waits for them, and re-layouts: 36.3 us -> 11.8 us  [the longest x24 7.6 us: halves(): lax.slice_in_dim(array, 1, 2, axis=axis)]
  transfers between devices with their start and end apart: 52 -> 87, of which waited for: 18 -> 40; matrix products, arithmetic and copies ran while one was open for 29% -> 9% of each run, Pallas kernels for 5% -> 43%
where the time goes in v2:
time: 520 us; the launch traced here: 515 us
  Pallas kernels  222 us (43%)
  waiting for transfers between devices  118 us (23%)
  starting transfers between devices  81.2 us (16%)
  other arithmetic  45.7 us (9%)
  local copies, waits for them, and re-layouts  32.4 us (6%)
  between operations  16 us (3%)
    ppermute x86, waiting for transfers between devices, swap(): return lax.ppermute(array, ('dp', 'head'), pairs)  118 us
    ppermute x86, starting transfers between devices, swap(): return lax.ppermute(array, ('dp', 'head'), pairs)  81.1 us
    pallas_call x3, Pallas kernels, mix_forward(): pl.pallas_call(functools.partial(mix_forward_kernel, local, cross, images...  42.5 us
    pallas_call x2, Pallas kernels, mix_back(): pl.pallas_call(functools.partial(mix_back_kernel, cross, images, len(qkv)...  38.2 us
    pallas_call x4, Pallas kernels, feed_weights(): pl.pallas_call(feed_weights_kernel, grid_spec=pltpu.PrefetchScalarGridSpe...  36.7 us
    pallas_call x2, Pallas kernels, feed_back(): pl.pallas_call(functools.partial(feed_back_kernel, len(slope), len(pieces...  30.2 us
    pallas_call x2, Pallas kernels, feed_rows(): pl.pallas_call(functools.partial(feed_rows_kernel, leaving), grid_spec=pl...  26.7 us
    pallas_call x2, Pallas kernels, mix_weights(): pl.pallas_call(functools.partial(mix_weights_kernel, more), grid_spec=plt...  19.1 us
  transfers between devices with their start and end apart: 87, of which 40 were waited for; matrix products, arithmetic and copies ran while one was open for 9% of the time, Pallas kernels for 43%

profile of v2, /device:TPU:0, one launch (start us, length us, event | category | flops | bytes accessed | tf_op | source)
XLA Modules:
  0.0 515.0 jit_solution(8139641665647526819)
XLA Ops:
  9.8 2.9 collective-permute-start
  14.0 2.0 constant_dynamic-slice_fusion.9
  30.9 13.9 %mix_forward.3 = (bf16[816,768]{1,0:T(8,128)(2,1)}, f32[816,768]{1,0:T(8,128)}, bf16[6,136,1152]{2,1,0:T(8,128)(2,1)}, bf16[816,384]{1,0:T(8,128)(2,1)}, f32[6,3,272]{2,1,0:T(4,128)}) custom-call(s32[9]{0:T(128)} %get-tuple-element.616.refs_0_.meta, f32[12]{0:T(128)} %fusion.11.refs_1_, bf16[816,768]{1,0:T(8,128)(2,1)} %bitcast.176, ...), custom_call_target="tpu_custom_call" | custom-call | flops 120000000 | bytes 1 | tf_op jit(solution)/shard_map/mix_forward/pallas_call | solution.py:259
  55.9 15.2 %mix_forward.4 = (f32[816,768]{1,0:T(8,128)}, bf16[6,136,1152]{2,1,0:T(8,128)(2,1)}, bf16[816,384]{1,0:T(8,128)(2,1)}, f32[6,3,272]{2,1,0:T(4,128)}) custom-call(s32[9]{0:T(128)} %get-tuple-element.616.refs_0_.meta, f32[12]{0:T(128)} %fusion.11.refs_1_, f32[816,768]{1,0:T(8,128)} %get-tuple-element.277.refs_2_, ...), custom_call_target="tpu_custom_call" | custom-call | flops 120000000 | bytes 1 | tf_op jit(solution)/shard_map/mix_forward/pallas_call | solution.py:259
  78.7 13.1 %feed_rows.2 = (f32[816,768]{1,0:T(8,128)}, bf16[816,768]{1,0:T(8,128)(2,1)}, bf16[816,3072]{1,0:T(8,128)(2,1)}, bf16[816,3072]{1,0:T(8,128)(2,1)}, bf16[408,768]{1,0:T(8,128)(2,1)}) custom-call(s32[3]{0:T(128)} %pad_add_fusion.meta.place, f32[816,768]{1,0:T(8,128)} %get-tuple-element.293.x_ref, f32[1,768]{1,0:T(1,128)} %get-tuple-element.614.gain_ref, ...), custom_call_target="tpu_custom_call" | custom-call | flops 116000000 | bytes 1 | tf_op jit(solution)/shard_map/feed_rows/pallas_call | solution.py:558
  91.8 2.3 collective-permute-start.19
  98.7 13.7 %feed_rows.3 = (f32[816,768]{1,0:T(8,128)}, bf16[816,768]{1,0:T(8,128)(2,1)}, bf16[816,3072]{1,0:T(8,128)(2,1)}, bf16[816,3072]{1,0:T(8,128)(2,1)}, bf16[408,768]{1,0:T(8,128)(2,1)}) custom-call(s32[3]{0:T(128)} %pad_add_fusion.meta.place, ...), custom_call_target="tpu_custom_call", output_to_operand_aliasing={{0}: (14, {}), {1}: (15, {}), {2}: (16, {}), {3}: (17, {})} | custom-call | flops 116000000 | bytes 1 | tf_op jit(solution)/shard_map/feed_rows/pallas_call | solution.py:558
  112.4 2.0 collective-permute-done.21.refs_9_.refs_11_
  114.4 8.0 %collective-permute-done.19 = bf16[408,768]{1,0:T(8,128)(2,1)S(1)} collective-permute-done((bf16[408,768]{1,0:T(8,128)(2,1)}, bf16[408,768]{1,0:T(8,128)(2,1)S(1)}, u32[]{:S(2)}, u32[]{:S(2)}) %collective-permute-start.19) | collective-permute-done | bytes 626720 | tf_op jit(solution)/shard_map/ppermute | solution.py:43
  127.6 13.5 %mix_forward.5 = (bf16[408,768]{1,0:T(8,128)(2,1)}, f32[408,768]{1,0:T(8,128)}, bf16[3,136,2304]{2,1,0:T(8,128)(2,1)}, bf16[408,768]{1,0:T(8,128)(2,1)}, f32[3,6,272]{2,1,0:T(8,128)}) custom-call(s32[9]{0:T(128)} %get-tuple-element.617.refs_0_, f32[12]{0:T(128)} %fusion.11.refs_1_, f32[408,768]{1,0:T(8,128)} %convert_select_fusion.refs_2_.refs_3_, ...), custom_call_target="tpu_custom_call" | custom-call | flops 120000000 | bytes 1 | tf_op jit(solution)/shard_map/mix_forward/pallas_call | solution.py:259
  141.1 11.0 %feed_forward.1 = (bf16[408,768]{1,0:T(8,128)(2,1)}, f32[408,768]{1,0:T(8,128)}, bf16[408,3072]{1,0:T(8,128)(2,1)}, bf16[408,3072]{1,0:T(8,128)(2,1)}) custom-call(s32[9]{0:T(128)} %get-tuple-element.616.refs_0_.meta, f32[408,768]{1,0:T(8,128)} %get-tuple-element.321.x_ref, f32[1,768]{1,0:T(1,128)} %get-tuple-element.611.norm_ref.gain_ref, ...), custom_call_target="tpu_custom_call" | custom-call | flops 116000000 | bytes 1 | tf_op jit(solution)/shard_map/feed_forward/pallas_call | solution.py:500
  154.5 2.1 collective-permute-start.29
  159.9 11.9 %feed_back.2 = (f32[408,768]{1,0:T(8,128)}, f32[1,768]{1,0:T(1,128)}, bf16[408,768]{1,0:T(8,128)(2,1)}, bf16[408,3072]{1,0:T(8,128)(2,1)}) custom-call(s32[9]{0:T(128)} %get-tuple-element.616.refs_0_.meta, f32[408,768]{1,0:T(8,128)} %bitcast_convert_fusion.2.e_ref, f32[408,768]{1,0:T(8,128)} %get-tuple-element.321.x_ref, ...), custom_call_target="tpu_custom_call" | custom-call | flops 117500000 | bytes 1 | tf_op jit(solution)/shard_map/feed_back/pallas_call | solution.py:624
  172.5 7.6 %feed_weights.4 = bf16[2,2,768,768]{3,2,1,0:T(8,128)(2,1)} custom-call(s32[3]{0:T(128)} %pad_add_fusion.meta.place, bf16[408,3072]{1,0:T(8,128)(2,1)} %get-tuple-element.332.eu_ref, bf16[408,3072]{1,0:T(8,128)(2,1)} %get-tuple-element.329.refs_0_, bf16[408,768]{1,0:T(8,128)(2,1)} %get-tuple-element.330.refs_1_, bf16[408,768]{1,0:T(8,128)(2,1)} %get-tuple-element.331.refs_2_), custom_call_target="tpu_custom_call" | custom-call | flops 70000000 | bytes 1 | tf_op jit(solution)/shard_map/feed_weights/pallas_call | solution.py:669
  180.2 7.6 %feed_weights.5 = bf16[2,2,768,768]{3,2,1,0:T(8,128)(2,1)} custom-call(s32[3]{0:T(128)} %pad_add_fusion.meta.place, bf16[408,3072]{1,0:T(8,128)(2,1)} %get-tuple-element.332.eu_ref, bf16[408,3072]{1,0:T(8,128)(2,1)} %get-tuple-element.329.refs_0_, bf16[408,768]{1,0:T(8,128)(2,1)} %get-tuple-element.330.refs_1_, bf16[408,768]{1,0:T(8,128)(2,1)} %get-tuple-element.331.refs_2_), custom_call_target="tpu_custom_call" | custom-call | flops 70000000 | bytes 1 | tf_op jit(solution)/shard_map/feed_weights/pallas_call | solution.py:669
  188.5 4.9 add.212
  201.5 14.1 %mix_back.2 = (f32[408,768]{1,0:T(8,128)}, f32[1,768]{1,0:T(1,128)}, bf16[408,2304]{1,0:T(8,128)(2,1)}, bf16[408,768]{1,0:T(8,128)(2,1)}, bf16[408,768]{1,0:T(8,128)(2,1)}) custom-call(s32[9]{0:T(128)} %get-tuple-element.617.refs_0_, f32[12]{0:T(128)} %fusion.11.refs_1_, f32[408,768]{1,0:T(8,128)} %get-tuple-element.337.refs_2_, ...), custom_call_target="tpu_custom_call" | custom-call | flops 165000000 | bytes 1 | tf_op jit(solution)/shard_map/mix_back/pallas_call | solution.py:358
  215.7 2.2 convert_select_fusion.1
  217.9 4.5 collective-permute-done.35
  223.3 2.6 collective-permute-start.36
  225.9 3.8 glue.1
  235.3 7.8 %mix_weights.2 = (bf16[2,4,192,768]{3,2,1,0:T(8,128)(2,1)}, bf16[2,4,192,768]{3,2,1,0:T(8,128)(2,1)}) custom-call(s32[3]{0:T(128)} %pad_add_fusion.meta.place, bf16[408,2304]{1,0:T(8,128)(2,1)} %get-tuple-element.348.dqkv_ref, bf16[408,768]{1,0:T(8,128)(2,1)} %get-tuple-element.349.refs_0_, bf16[408,768]{1,0:T(8,128)(2,1)} %get-tuple-element.350.refs_1_, ...), custom_call_target="tpu_custom_call" | custom-call | flops 70000000 | bytes 1 | tf_op jit(solution)/shard_map/mix_weights/pallas_call | solution.py:433
  245.2 5.5 %collective-permute-done.39 = bf16[1,2,1,2,64,768]{5,4,3,2,1,0:T(8,128)(2,1)S(1)} collective-permute-done((bf16[1,2,1,2,64,768]{5,4,3,2,1,0:T(8,128)(2,1)S(1)}, bf16[1,2,1,2,64,768]{5,4,3,2,1,0:T(8,128)(2,1)S(1)}, u32[]{:S(2)}, u32[]{:S(2)}) %collective-permute-start.39) | collective-permute-done | bytes 393248 | tf_op jit(solution)/shard_map/ppermute | solution.py:43
  255.7 2.1 collective-permute-start.41
  257.8 6.8 %turn_back.1 = (f32[816,768]{1,0:T(8,128)}, f32[1,768]{1,0:T(1,128)}) custom-call(s32[9]{0:T(128)} %get-tuple-element.616.refs_0_.meta, s32[1]{0:T(128)} %bitcast.2.side, f32[816,768]{1,0:T(8,128)} %get-tuple-element.314.encoded, f32[1,768]{1,0:T(1,128)} %get-tuple-element.612.next_gain_ref.gain, bf16[408,768]{1,0:T(8,128)(2,1)} %get-tuple-element.340.context, ...), custom_call_target="tpu_custom_call" | custom-call | flops 50000000 | bytes 1 | tf_op jit(solution)/shard_map/turn_back/pallas_call | solution.py:715
  264.6 2.0 collective-permute-done.41
  269.5 18.3 %feed_back.3 = (f32[816,768]{1,0:T(8,128)}, f32[1,768]{1,0:T(1,128)}, bf16[816,768]{1,0:T(8,128)(2,1)}, bf16[816,3072]{1,0:T(8,128)(2,1)}) custom-call(s32[9]{0:T(128)} %get-tuple-element.616.refs_0_.meta, f32[816,768]{1,0:T(8,128)} %get-tuple-element.388.e_ref, f32[816,768]{1,0:T(8,128)} %get-tuple-element.293.x_ref, f32[1,768]{1,0:T(1,128)} %get-tuple-element.614.gain_ref, ...), custom_call_target="tpu_custom_call" | custom-call | flops 185000000 | bytes 1 | tf_op jit(solution)/shard_map/feed_back/pallas_call | solution.py:624
  291.4 10.6 %feed_weights.6 = bf16[2,2,768,768]{3,2,1,0:T(8,128)(2,1)} custom-call(s32[3]{0:T(128)} %pad_add_fusion.meta.place, bf16[816,3072]{1,0:T(8,128)(2,1)} %get-tuple-element.413.eu_ref, bf16[816,3072]{1,0:T(8,128)(2,1)} %get-tuple-element.400.refs_0_, bf16[816,768]{1,0:T(8,128)(2,1)} %get-tuple-element.401.refs_1_, bf16[816,768]{1,0:T(8,128)(2,1)} %get-tuple-element.402.refs_2_), custom_call_target="tpu_custom_call" | custom-call | flops 100000000 | bytes 1 | tf_op jit(solution)/shard_map/feed_weights/pallas_call | solution.py:669
  306.0 10.8 %feed_weights.7 = bf16[2,2,768,768]{3,2,1,0:T(8,128)(2,1)} custom-call(s32[3]{0:T(128)} %pad_add_fusion.meta.place, bf16[816,3072]{1,0:T(8,128)(2,1)} %get-tuple-element.413.eu_ref, bf16[816,3072]{1,0:T(8,128)(2,1)} %get-tuple-element.400.refs_0_, bf16[816,768]{1,0:T(8,128)(2,1)} %get-tuple-element.401.refs_1_, bf16[816,768]{1,0:T(8,128)(2,1)} %get-tuple-element.402.refs_2_), custom_call_target="tpu_custom_call" | custom-call | flops 100000000 | bytes 1 | tf_op jit(solution)/shard_map/feed_weights/pallas_call | solution.py:669
  318.6 3.4 add.225
  328.3 2.4 collective-permute-start.55
  330.7 24.0 %mix_back.3 = (f32[816,768]{1,0:T(8,128)}, f32[1,768]{1,0:T(1,128)}, bf16[816,2304]{1,0:T(8,128)(2,1)}, bf16[816,768]{1,0:T(8,128)(2,1)}) custom-call(s32[9]{0:T(128)} %get-tuple-element.616.refs_0_.meta, f32[12]{0:T(128)} %fusion.11.refs_1_, f32[816,768]{1,0:T(8,128)} %get-tuple-element.425.refs_2_, bf16[816,768]{1,0:T(8,128)(2,1)} %bitcast.177, ...), custom_call_target="tpu_custom_call" | custom-call | flops 280000000 | bytes 1 | tf_op jit(solution)/shard_map/mix_back/pallas_call | solution.py:358
  354.8 4.7 collective-permute-done.55
  359.5 2.2 collective-permute-done.56
  367.8 11.3 %mix_weights.3 = (bf16[2,4,208,768]{3,2,1,0:T(8,128)(2,1)}, bf16[2,4,208,768]{3,2,1,0:T(8,128)(2,1)}) custom-call(s32[3]{0:T(128)} %pad_add_fusion.meta.place, bf16[816,2304]{1,0:T(8,128)(2,1)} %get-tuple-element.443.dqkv_ref, f32[1,768]{1,0:T(1,128)} %get-tuple-element.444.refs_0_, f32[1,768]{1,0:T(1,128)} %get-tuple-element.445.refs_1_, ...), custom_call_target="tpu_custom_call" | custom-call | flops 105000000 | bytes 1 | tf_op jit(solution)/shard_map/mix_weights/pallas_call | solution.py:433
  382.8 3.6 collective-permute-done.61
  391.4 12.7 %collective-permute-done.62 = bf16[1,1,2,2,96,768]{5,4,3,2,1,0:T(8,128)(2,1)S(1)} collective-permute-done((bf16[1,1,2,2,96,768]{5,4,3,2,1,0:T(8,128)(2,1)S(1)}, bf16[1,1,2,2,96,768]{5,4,3,2,1,0:T(8,128)(2,1)S(1)}, u32[]{:S(2)}, u32[]{:S(2)}) %collective-permute-start.62) | collective-permute-done | bytes 589856 | tf_op jit(solution)/shard_map/ppermute | solution.py:43
  409.7 5.3 %collective-permute-done.66 = bf16[1,1,2,1,96,768]{5,4,3,2,1,0:T(8,128)(2,1)S(1)} collective-permute-done((bf16[1,1,2,1,96,768]{5,4,3,2,1,0:T(8,128)(2,1)S(1)}, bf16[1,1,2,1,96,768]{5,4,3,2,1,0:T(8,128)(2,1)S(1)}, u32[]{:S(2)}, u32[]{:S(2)}) %collective-permute-start.66) | collective-permute-done | bytes 294944 | tf_op jit(solution)/shard_map/ppermute | solution.py:43
  420.7 9.9 %collective-permute-done.67 = bf16[1,1,1,1,96,768]{5,4,3,2,1,0:T(8,128)(2,1)} collective-permute-done((bf16[1,1,1,1,96,768]{5,4,3,2,1,0:T(8,128)(2,1)}, bf16[1,1,1,1,96,768]{5,4,3,2,1,0:T(8,128)(2,1)}, u32[]{:S(2)}, u32[]{:S(2)}) %collective-permute-start.67) | collective-permute-done | bytes 147488 | tf_op jit(solution)/shard_map/ppermute | solution.py:43
  431.0 14.8 %collective-permute-done.72.refs_5_ = bf16[2,192,768]{2,1,0:T(8,128)(2,1)S(1)} collective-permute-done((bf16[2,192,768]{2,1,0:T(8,128)(2,1)S(1)}, bf16[2,192,768]{2,1,0:T(8,128)(2,1)S(1)}, u32[]{:S(2)}, u32[]{:S(2)}) %collective-permute-start.72) | collective-permute-done | bytes 589856 | tf_op jit(solution)/shard_map/ppermute | solution.py:43
  448.4 2.4 collective-permute-start.73
  451.7 5.9 %collective-permute-done.76.refs_3_ = bf16[2,2,96,768]{3,2,1,0:T(8,128)(2,1)} collective-permute-done((bf16[2,2,96,768]{3,2,1,0:T(8,128)(2,1)S(1)}, bf16[2,2,96,768]{3,2,1,0:T(8,128)(2,1)}, u32[]{:S(2)}, u32[]{:S(2)}) %collective-permute-start.76) | collective-permute-done | bytes 589856 | tf_op jit(solution)/shard_map/ppermute | solution.py:43
  463.6 2.0 collective-permute-start.78
  470.7 3.1 collective-permute-done.78
  478.3 8.2 %collective-permute-done.83.refs_9_ = bf16[2,2,96,768]{3,2,1,0:T(8,128)(2,1)} collective-permute-done((bf16[2,2,96,768]{3,2,1,0:T(8,128)(2,1)}, bf16[2,2,96,768]{3,2,1,0:T(8,128)(2,1)}, u32[]{:S(2)}, u32[]{:S(2)}) %collective-permute-start.83) | collective-permute-done | bytes 589856 | tf_op jit(solution)/shard_map/ppermute | solution.py:43
  489.2 7.0 %unpack_feed.1 = (f32[2,768,768]{2,1,0:T(8,128)}, f32[2,768,768]{2,1,0:T(8,128)}) custom-call(s32[3]{0:T(128)} %pad_add_fusion.meta.place, bf16[2,192,768]{2,1,0:T(8,128)(2,1)} %copy-done.6, bf16[2,96,768]{2,1,0:T(8,128)(2,1)} %copy-done.30, bf16[2,96,768]{2,1,0:T(8,128)(2,1)} %copy-done.31, bf16[2,2,96,768]{3,2,1,0:T(8,128)(2,1)} %collective-permute-done.76.refs_3_, ...), custom_call_target="tpu_custom_call" | custom-call | flops 50000000 | bytes 1 | tf_op jit(solution)/shard_map/unpack_feed/pallas_call | solution.py:774
  499.5 3.4 collective-permute-done.80
  505.8 2.0 maximum_convert_fusion
  (450 shorter events, 147.9 us)
Async XLA Ops:
  7.2 133.9 %all-gather.3.cloned.1.call-start = ((), (), s32[]{:S(2)}) async-start(), calls=%async_computation | async-start | bytes 11796480 | tf_op jit(solution)/shard_map/all_gather | solution.py:978
  20.1 24.7 %collective-permute-start.6 = (bf16[2,768,768]{2,1,0:T(8,128)(2,1)S(1)}, bf16[2,768,768]{2,1,0:T(8,128)(2,1)}, u32[]{:S(2)}, u32[]{:S(2)}) collective-permute-start(bf16[2,768,768]{2,1,0:T(8,128)(2,1)S(1)} %pad_maximum_fusion.refs_0_.refs_1_), channel_id=1, source_target_pairs={{0,1},{1,0},{2,3},{3,2},{4,5},{5,4},{6,7},{7,6},{8,9},{9,8},{10,11... | collective-permute-start | bytes 7077896 | tf_op jit(solution)/shard_map/ppermute | solution.py:43
  22.8 22.0 %collective-permute-start.5 = (bf16[2,192,768]{2,1,0:T(8,128)(2,1)S(1)}, bf16[2,192,768]{2,1,0:T(8,128)(2,1)S(1)}, u32[]{:S(2)}, u32[]{:S(2)}) collective-permute-start(bf16[2,192,768]{2,1,0:T(8,128)(2,1)S(1)} %constant_dynamic-slice_fusion.6), channel_id=1, source_target_pairs={{0,2},{1,3},{2,0},{3,1},{4,6},{5,7},{6,4},{7,5},{8,10},{9,11},{10,... | collective-permute-start | bytes 1769480 | tf_op jit(solution)/shard_map/ppermute | solution.py:43
  25.2 19.6 %collective-permute-start.2 = (bf16[192,768]{1,0:T(8,128)(2,1)}, bf16[192,768]{1,0:T(8,128)(2,1)S(1)}, u32[]{:S(2)}, u32[]{:S(2)}) collective-permute-start(bf16[192,768]{1,0:T(8,128)(2,1)} %collective-permute-done.refs_4_.refs_11_), channel_id=1, source_target_pairs={{0,4},{1,5},{2,6},{3,7},{4,0},{5,1},{6,2},{7,3},{8,12},{9,13},{10,... | collective-permute-start | bytes 884744 | tf_op jit(solution)/shard_map/ppermute | solution.py:43
  26.7 18.1 %collective-permute-start.3 = (bf16[192,768]{1,0:T(8,128)(2,1)}, bf16[192,768]{1,0:T(8,128)(2,1)S(1)}, u32[]{:S(2)}, u32[]{:S(2)}) collective-permute-start(bf16[192,768]{1,0:T(8,128)(2,1)} %collective-permute-done.refs_4_.refs_11_), channel_id=1, source_target_pairs={{0,8},{1,9},{2,10},{3,11},{4,12},{5,13},{6,14},{7,15},{8,0},{9,1},... | collective-permute-start | bytes 884744 | tf_op jit(solution)/shard_map/ppermute | solution.py:43
  28.3 16.5 %collective-permute-start.4 = (bf16[192,768]{1,0:T(8,128)(2,1)S(1)}, bf16[192,768]{1,0:T(8,128)(2,1)S(1)}, u32[]{:S(2)}, u32[]{:S(2)}) collective-permute-start(bf16[192,768]{1,0:T(8,128)(2,1)S(1)} %dynamic-slice_bitcast_fusion.14), channel_id=1, source_target_pairs={{0,2},{1,3},{2,0},{3,1},{4,6},{5,7},{6,4},{7,5},{8,10},{9,11},{10,... | collective-permute-start | bytes 884744 | tf_op jit(solution)/shard_map/ppermute | solution.py:43
  50.4 20.8 %collective-permute-start.13 = (bf16[2,192,768]{2,1,0:T(8,128)(2,1)}, bf16[2,192,768]{2,1,0:T(8,128)(2,1)S(1)}, u32[]{:S(2)}, u32[]{:S(2)}) collective-permute-start(bf16[2,192,768]{2,1,0:T(8,128)(2,1)} %constant_dynamic-slice_fusion.5), channel_id=1, source_target_pairs={{0,2},{1,3},{2,0},{3,1},{4,6},{5,7},{6,4},{7,5},{8,10},{9,11},{10,... | collective-permute-start | bytes 1769480 | tf_op jit(solution)/shard_map/ppermute | solution.py:43
  51.6 19.5 %collective-permute-start.11 = (bf16[2,192,768]{2,1,0:T(8,128)(2,1)S(1)}, bf16[2,192,768]{2,1,0:T(8,128)(2,1)S(1)}, u32[]{:S(2)}, u32[]{:S(2)}) collective-permute-start(bf16[2,192,768]{2,1,0:T(8,128)(2,1)S(1)} %copy-done.9), channel_id=1, source_target_pairs={{0,4},{1,5},{2,6},{3,7},{4,0},{5,1},{6,2},{7,3},{8,12},{9,13},{10,... | collective-permute-start | bytes 1769480 | tf_op jit(solution)/shard_map/ppermute | solution.py:43
  53.2 18.0 %collective-permute-start.12 = (bf16[2,192,768]{2,1,0:T(8,128)(2,1)S(1)}, bf16[2,192,768]{2,1,0:T(8,128)(2,1)S(1)}, u32[]{:S(2)}, u32[]{:S(2)}) collective-permute-start(bf16[2,192,768]{2,1,0:T(8,128)(2,1)S(1)} %copy-done.9), channel_id=1, source_target_pairs={{0,8},{1,9},{2,10},{3,11},{4,12},{5,13},{6,14},{7,15},{8,0},{9,1},... | collective-permute-start | bytes 1769480 | tf_op jit(solution)/shard_map/ppermute | solution.py:43
  72.3 52.6 %collective-permute-start.23 = (bf16[4,192,768]{2,1,0:T(8,128)(2,1)S(1)}, bf16[4,192,768]{2,1,0:T(8,128)(2,1)}, u32[]{:S(2)}, u32[]{:S(2)}) collective-permute-start(bf16[4,192,768]{2,1,0:T(8,128)(2,1)S(1)} %pad_maximum_fusion.5.refs_5_.refs_7_), channel_id=1, source_target_pairs={{0,1},{1,0},{2,3},{3,2},{4,5},{5,4},{6,7},{7,6},{8,9},{9,8},{10,11... | collective-permute-start | bytes 3538952 | tf_op jit(solution)/shard_map/ppermute | solution.py:43
  73.3 18.5 %collective-permute-start.18 = (bf16[192,768]{1,0:T(8,128)(2,1)S(1)}, bf16[192,768]{1,0:T(8,128)(2,1)S(1)}, u32[]{:S(2)}, u32[]{:S(2)}) collective-permute-start(bf16[192,768]{1,0:T(8,128)(2,1)S(1)} %get-tuple-element.563), channel_id=1, source_target_pairs={{0,2},{1,3},{2,0},{3,1},{4,6},{5,7},{6,4},{7,5},{8,10},{9,11},{10,... | collective-permute-start | bytes 884744 | tf_op jit(solution)/shard_map/ppermute | solution.py:43
  91.8 30.6 %collective-permute-start.19 = (bf16[408,768]{1,0:T(8,128)(2,1)}, bf16[408,768]{1,0:T(8,128)(2,1)S(1)}, u32[]{:S(2)}, u32[]{:S(2)}) collective-permute-start(bf16[408,768]{1,0:T(8,128)(2,1)} %get-tuple-element.310), channel_id=1, source_target_pairs={{0,16},{1,17},{2,18},{3,19},{4,20},{5,21},{6,22},{7,23},{8,24},{9,... | collective-permute-start | bytes 1880072 | tf_op jit(solution)/shard_map/ppermute | solution.py:43
  94.1 18.2 %collective-permute-start.22 = (bf16[192,768]{1,0:T(8,128)(2,1)S(1)}, bf16[192,768]{1,0:T(8,128)(2,1)S(1)}, u32[]{:S(2)}, u32[]{:S(2)}) collective-permute-start(bf16[192,768]{1,0:T(8,128)(2,1)S(1)} %get-tuple-element.562), channel_id=1, source_target_pairs={{0,2},{1,3},{2,0},{3,1},{4,6},{5,7},{6,4},{7,5},{8,10},{9,11},{10,... | collective-permute-start | bytes 884744 | tf_op jit(solution)/shard_map/ppermute | solution.py:43
  95.4 17.0 %collective-permute-start.20 = (bf16[192,768]{1,0:T(8,128)(2,1)S(1)}, bf16[192,768]{1,0:T(8,128)(2,1)S(1)}, u32[]{:S(2)}, u32[]{:S(2)}) collective-permute-start(bf16[192,768]{1,0:T(8,128)(2,1)S(1)} %collective-permute-done.18.refs_7_.refs_9_), channel_id=1, source_target_pairs={{0,4},{1,5},{2,6},{3,7},{4,0},{5,1},{6,2},{7,3},{8,12},{9,13},{10,... | collective-permute-start | bytes 884744 | tf_op jit(solution)/shard_map/ppermute | solution.py:43
  97.0 17.4 %collective-permute-start.21 = (bf16[192,768]{1,0:T(8,128)(2,1)S(1)}, bf16[192,768]{1,0:T(8,128)(2,1)S(1)}, u32[]{:S(2)}, u32[]{:S(2)}) collective-permute-start(bf16[192,768]{1,0:T(8,128)(2,1)S(1)} %collective-permute-done.18.refs_7_.refs_9_), channel_id=1, source_target_pairs={{0,8},{1,9},{2,10},{3,11},{4,12},{5,13},{6,14},{7,15},{8,0},{9,1},... | collective-permute-start | bytes 884744 | tf_op jit(solution)/shard_map/ppermute | solution.py:43
  123.2 29.8 %collective-permute-start.28 = (bf16[3,136,768]{2,1,0:T(8,128)(2,1)}, bf16[3,136,768]{2,1,0:T(8,128)(2,1)}, u32[]{:S(2)}, u32[]{:S(2)}) collective-permute-start(bf16[3,136,768]{2,1,0:T(8,128)(2,1)} %slice.341), channel_id=1, source_target_pairs={{0,16},{1,17},{2,18},{3,19},{4,20},{5,21},{6,22},{7,23},{8,24},{9,... | collective-permute-start | bytes 1880072 | tf_op jit(solution)/shard_map/ppermute | solution.py:43
  154.5 17.9 %collective-permute-start.29 = (bf16[1,136,768]{2,1,0:T(8,128)(2,1)S(1)}, bf16[1,136,768]{2,1,0:T(8,128)(2,1)S(1)}, u32[]{:S(2)}, u32[]{:S(2)}) collective-permute-start(bf16[1,136,768]{2,1,0:T(8,128)(2,1)S(1)} %get-tuple-element.570), channel_id=1, source_target_pairs={{0,16},{1,17},{2,18},{3,19},{4,20},{5,21},{6,22},{7,23},{8,24},{9,... | collective-permute-start | bytes 626696 | tf_op jit(solution)/shard_map/ppermute | solution.py:43
  156.6 23.5 %collective-permute-start.30 = (bf16[1,136,768]{2,1,0:T(8,128)(2,1)S(1)}, bf16[1,136,768]{2,1,0:T(8,128)(2,1)S(1)}, u32[]{:S(2)}, u32[]{:S(2)}) collective-permute-start(bf16[1,136,768]{2,1,0:T(8,128)(2,1)S(1)} %get-tuple-element.569), channel_id=1, source_target_pairs={{0,16},{1,17},{2,18},{3,19},{4,20},{5,21},{6,22},{7,23},{8,24},{9,... | collective-permute-start | bytes 626696 | tf_op jit(solution)/shard_map/ppermute | solution.py:43
  194.9 27.5 %collective-permute-start.32 = (bf16[1,2,2,2,64,768]{5,4,3,2,1,0:T(8,128)(2,1)S(1)}, bf16[1,2,2,2,64,768]{5,4,3,2,1,0:T(8,128)(2,1)S(1)}, u32[]{:S(2)}, u32[]{:S(2)}) collective-permute-start(bf16[1,2,2,2,64,768]{5,4,3,2,1,0:T(8,128)(2,1)S(1)} %get-tuple-element.540), channel_id=1, source_target_pairs={{0,2},{1,3},{2,0},{3,1},{4,6},{5,7},{6,4},{7,5},{8,10},{9,11},{10,... | collective-permute-start | bytes 2359304 | tf_op jit(solution)/shard_map/ppermute | solution.py:43
  197.0 25.4 %collective-permute-start.33 = (bf16[2,2,2,1,64,768]{5,4,3,2,1,0:T(8,128)(2,1)S(1)}, bf16[2,2,2,1,64,768]{5,4,3,2,1,0:T(8,128)(2,1)S(1)}, u32[]{:S(2)}, u32[]{:S(2)}) collective-permute-start(bf16[2,2,2,1,64,768]{5,4,3,2,1,0:T(8,128)(2,1)S(1)} %get-tuple-element.538), channel_id=1, source_target_pairs={{0,4},{1,5},{2,6},{3,7},{4,0},{5,1},{6,2},{7,3},{8,12},{9,13},{10,... | collective-permute-start | bytes 2359304 | tf_op jit(solution)/shard_map/ppermute | solution.py:43
  199.8 23.5 %collective-permute-start.34 = (bf16[2,2,1,2,64,768]{5,4,3,2,1,0:T(8,128)(2,1)S(1)}, bf16[2,2,1,2,64,768]{5,4,3,2,1,0:T(8,128)(2,1)S(1)}, u32[]{:S(2)}, u32[]{:S(2)}) collective-permute-start(bf16[2,2,1,2,64,768]{5,4,3,2,1,0:T(8,128)(2,1)S(1)} %get-tuple-element.536), channel_id=1, source_target_pairs={{0,8},{1,9},{2,10},{3,11},{4,12},{5,13},{6,14},{7,15},{8,0},{9,1},... | collective-permute-start | bytes 2359304 | tf_op jit(solution)/shard_map/ppermute | solution.py:43
  201.4 21.0 %collective-permute-start.35 = (bf16[1,136,768]{2,1,0:T(8,128)(2,1)S(1)}, bf16[1,136,768]{2,1,0:T(8,128)(2,1)S(1)}, u32[]{:S(2)}, u32[]{:S(2)}) collective-permute-start(bf16[1,136,768]{2,1,0:T(8,128)(2,1)S(1)} %get-tuple-element.568), channel_id=1, source_target_pairs={{0,16},{1,17},{2,18},{3,19},{4,20},{5,21},{6,22},{7,23},{8,24},{9,... | collective-permute-start | bytes 626696 | tf_op jit(solution)/shard_map/ppermute | solution.py:43
  223.3 29.1 %collective-permute-start.36 = (bf16[408,768]{1,0:T(8,128)(2,1)}, bf16[408,768]{1,0:T(8,128)(2,1)S(1)}, u32[]{:S(2)}, u32[]{:S(2)}) collective-permute-start(bf16[408,768]{1,0:T(8,128)(2,1)} %convert_select_fusion.1), channel_id=1, source_target_pairs={{0,16},{1,17},{2,18},{3,19},{4,20},{5,21},{6,22},{7,23},{8,24},{9,... | collective-permute-start | bytes 1880072 | tf_op jit(solution)/shard_map/ppermute | solution.py:43
  233.4 17.3 %collective-permute-start.39 = (bf16[1,2,1,2,64,768]{5,4,3,2,1,0:T(8,128)(2,1)S(1)}, bf16[1,2,1,2,64,768]{5,4,3,2,1,0:T(8,128)(2,1)S(1)}, u32[]{:S(2)}, u32[]{:S(2)}) collective-permute-start(bf16[1,2,1,2,64,768]{5,4,3,2,1,0:T(8,128)(2,1)S(1)} %copy-done.74), channel_id=1, source_target_pairs={{0,2},{1,3},{2,0},{3,1},{4,6},{5,7},{6,4},{7,5},{8,10},{9,11},{10,... | collective-permute-start | bytes 1179656 | tf_op jit(solution)/shard_map/ppermute | solution.py:43
  267.6 20.3 %collective-permute-start.44 = (bf16[1,1,2,2,96,768]{5,4,3,2,1,0:T(8,128)(2,1)S(1)}, bf16[1,1,2,2,96,768]{5,4,3,2,1,0:T(8,128)(2,1)S(1)}, u32[]{:S(2)}, u32[]{:S(2)}) collective-permute-start(bf16[1,1,2,2,96,768]{5,4,3,2,1,0:T(8,128)(2,1)S(1)} %get-tuple-element.560), channel_id=1, source_target_pairs={{0,2},{1,3},{2,0},{3,1},{4,6},{5,7},{6,4},{7,5},{8,10},{9,11},{10,... | collective-permute-start | bytes 1769480 | tf_op jit(solution)/shard_map/ppermute | solution.py:43
  268.1 19.7 %collective-permute-start.45 = (bf16[2,1,2,1,96,768]{5,4,3,2,1,0:T(8,128)(2,1)S(1)}, bf16[2,1,2,1,96,768]{5,4,3,2,1,0:T(8,128)(2,1)S(1)}, u32[]{:S(2)}, u32[]{:S(2)}) collective-permute-start(bf16[2,1,2,1,96,768]{5,4,3,2,1,0:T(8,128)(2,1)S(1)} %get-tuple-element.558), channel_id=1, source_target_pairs={{0,4},{1,5},{2,6},{3,7},{4,0},{5,1},{6,2},{7,3},{8,12},{9,13},{10,... | collective-permute-start | bytes 1769480 | tf_op jit(solution)/shard_map/ppermute | solution.py:43
  268.9 33.2 %collective-permute-start.46 = (bf16[2,192,768]{2,1,0:T(8,128)(2,1)S(1)}, bf16[2,192,768]{2,1,0:T(8,128)(2,1)S(1)}, u32[]{:S(2)}, u32[]{:S(2)}) collective-permute-start(bf16[2,192,768]{2,1,0:T(8,128)(2,1)S(1)} %pad_maximum_fusion.8), channel_id=1, source_target_pairs={{0,16},{1,17},{2,18},{3,19},{4,20},{5,21},{6,22},{7,23},{8,24},{9,... | collective-permute-start | bytes 1769480 | tf_op jit(solution)/shard_map/ppermute | solution.py:43
  302.5 16.1 %collective-permute-start.49 = (bf16[2,2,768,768]{3,2,1,0:T(8,128)(2,1)}, bf16[2,2,768,768]{3,2,1,0:T(8,128)(2,1)S(1)}, u32[]{:S(2)}, u32[]{:S(2)}) collective-permute-start(bf16[2,2,768,768]{3,2,1,0:T(8,128)(2,1)} %feed_weights.6), channel_id=1, source_target_pairs={{0,1},{1,0},{2,3},{3,2},{4,5},{5,4},{6,7},{7,6},{8,9},{9,8},{10,11... | collective-permute-start | bytes 14155784 | tf_op jit(solution)/shard_map/ppermute | solution.py:43
  302.8 15.8 %collective-permute-start.50 = (bf16[2,192,768]{2,1,0:T(8,128)(2,1)S(1)}, bf16[2,192,768]{2,1,0:T(8,128)(2,1)S(1)}, u32[]{:S(2)}, u32[]{:S(2)}) collective-permute-start(bf16[2,192,768]{2,1,0:T(8,128)(2,1)S(1)} %add.222), channel_id=1, source_target_pairs={{0,4},{1,5},{2,6},{3,7},{4,0},{5,1},{6,2},{7,3},{8,12},{9,13},{10,... | collective-permute-start | bytes 1769480 | tf_op jit(solution)/shard_map/ppermute | solution.py:43
  324.2 35.3 %collective-permute-start.53 = (bf16[1,2,2,2,96,768]{5,4,1,3,2,0:T(8,128)(2,1)}, bf16[1,2,2,2,96,768]{5,4,1,3,2,0:T(8,128)(2,1)S(1)}, u32[]{:S(2)}, u32[]{:S(2)}) collective-permute-start(bf16[1,2,2,2,96,768]{5,4,1,3,2,0:T(8,128)(2,1)} %get-tuple-element.532), channel_id=1, source_target_pairs={{0,2},{1,3},{2,0},{3,1},{4,6},{5,7},{6,4},{7,5},{8,10},{9,11},{10,... | collective-permute-start | bytes 3538952 | tf_op jit(solution)/shard_map/ppermute | solution.py:43
  326.8 32.7 %collective-permute-start.54 = (bf16[2,2,2,1,96,768]{5,4,1,3,2,0:T(8,128)(2,1)}, bf16[2,2,2,1,96,768]{5,4,1,3,2,0:T(8,128)(2,1)S(1)}, u32[]{:S(2)}, u32[]{:S(2)}) collective-permute-start(bf16[2,2,2,1,96,768]{5,4,1,3,2,0:T(8,128)(2,1)} %get-tuple-element.530), channel_id=1, source_target_pairs={{0,4},{1,5},{2,6},{3,7},{4,0},{5,1},{6,2},{7,3},{8,12},{9,13},{10,... | collective-permute-start | bytes 3538952 | tf_op jit(solution)/shard_map/ppermute | solution.py:43
  328.3 33.3 %collective-permute-start.56 = (bf16[2,2,192,768]{3,2,1,0:T(8,128)(2,1)S(1)}, bf16[2,2,192,768]{3,2,1,0:T(8,128)(2,1)S(1)}, u32[]{:S(2)}, u32[]{:S(2)}) collective-permute-start(bf16[2,2,192,768]{3,2,1,0:T(8,128)(2,1)S(1)} %pad_maximum_fusion.6), channel_id=1, source_target_pairs={{0,8},{1,9},{2,10},{3,11},{4,12},{5,13},{6,14},{7,15},{8,0},{9,1},... | collective-permute-start | bytes 3538952 | tf_op jit(solution)/shard_map/ppermute | solution.py:43
  328.3 31.1 %collective-permute-start.55 = (bf16[1,192,768]{2,1,0:T(8,128)(2,1)S(1)}, bf16[1,192,768]{2,1,0:T(8,128)(2,1)S(1)}, u32[]{:S(2)}, u32[]{:S(2)}) collective-permute-start(bf16[1,192,768]{2,1,0:T(8,128)(2,1)S(1)} %pad_maximum_fusion.17), channel_id=1, source_target_pairs={{0,16},{1,17},{2,18},{3,19},{4,20},{5,21},{6,22},{7,23},{8,24},{9,... | collective-permute-start | bytes 884744 | tf_op jit(solution)/shard_map/ppermute | solution.py:43
  363.4 17.9 %collective-permute-start.57 = (bf16[1,2,2,1,96,768]{5,4,1,3,2,0:T(8,128)(2,1)S(1)}, bf16[1,2,2,1,96,768]{5,4,1,3,2,0:T(8,128)(2,1)S(1)}, u32[]{:S(2)}, u32[]{:S(2)}) collective-permute-start(bf16[1,2,2,1,96,768]{5,4,1,3,2,0:T(8,128)(2,1)S(1)} %get-tuple-element.556), channel_id=1, source_target_pairs={{0,4},{1,5},{2,6},{3,7},{4,0},{5,1},{6,2},{7,3},{8,12},{9,13},{10,... | collective-permute-start | bytes 1769480 | tf_op jit(solution)/shard_map/ppermute | solution.py:43
  364.0 17.2 %collective-permute-start.58 = (bf16[2,2,1,1,96,768]{5,4,1,3,2,0:T(8,128)(2,1)S(1)}, bf16[2,2,1,1,96,768]{5,4,1,3,2,0:T(8,128)(2,1)S(1)}, u32[]{:S(2)}, u32[]{:S(2)}) collective-permute-start(bf16[2,2,1,1,96,768]{5,4,1,3,2,0:T(8,128)(2,1)S(1)} %get-tuple-element.554), channel_id=1, source_target_pairs={{0,8},{1,9},{2,10},{3,11},{4,12},{5,13},{6,14},{7,15},{8,0},{9,1},... | collective-permute-start | bytes 1769480 | tf_op jit(solution)/shard_map/ppermute | solution.py:43
  364.9 16.1 %collective-permute-start.59 = (bf16[1,96,768]{2,1,0:T(8,128)(2,1)S(1)}, bf16[1,96,768]{2,1,0:T(8,128)(2,1)S(1)}, u32[]{:S(2)}, u32[]{:S(2)}) collective-permute-start(bf16[1,96,768]{2,1,0:T(8,128)(2,1)S(1)} %get-tuple-element.604), channel_id=1, source_target_pairs={{0,4},{1,5},{2,6},{3,7},{4,0},{5,1},{6,2},{7,3},{8,12},{9,13},{10,... | collective-permute-start | bytes 442376 | tf_op jit(solution)/shard_map/ppermute | solution.py:43
  366.4 14.8 %collective-permute-start.60 = (bf16[1,96,768]{2,1,0:T(8,128)(2,1)S(1)}, bf16[1,96,768]{2,1,0:T(8,128)(2,1)S(1)}, u32[]{:S(2)}, u32[]{:S(2)}) collective-permute-start(bf16[1,96,768]{2,1,0:T(8,128)(2,1)S(1)} %get-tuple-element.603), channel_id=1, source_target_pairs={{0,8},{1,9},{2,10},{3,11},{4,12},{5,13},{6,14},{7,15},{8,0},{9,1},... | collective-permute-start | bytes 442376 | tf_op jit(solution)/shard_map/ppermute | solution.py:43
  387.2 17.5 %collective-permute-start.63 = (bf16[2,1,2,1,112,768]{5,4,3,2,1,0:T(8,128)(2,1)S(1)}, bf16[2,1,2,1,112,768]{5,4,3,2,1,0:T(8,128)(2,1)S(1)}, u32[]{:S(2)}, u32[]{:S(2)}) collective-permute-start(bf16[2,1,2,1,112,768]{5,4,3,2,1,0:T(8,128)(2,1)S(1)} %get-tuple-element.518), channel_id=1, source_target_pairs={{0,4},{1,5},{2,6},{3,7},{4,0},{5,1},{6,2},{7,3},{8,12},{9,13},{10,... | collective-permute-start | bytes 2064392 | tf_op jit(solution)/shard_map/ppermute | solution.py:43
  388.9 15.2 %collective-permute-start.62 = (bf16[1,1,2,2,96,768]{5,4,3,2,1,0:T(8,128)(2,1)S(1)}, bf16[1,1,2,2,96,768]{5,4,3,2,1,0:T(8,128)(2,1)S(1)}, u32[]{:S(2)}, u32[]{:S(2)}) collective-permute-start(bf16[1,1,2,2,96,768]{5,4,3,2,1,0:T(8,128)(2,1)S(1)} %get-tuple-element.520), channel_id=1, source_target_pairs={{0,2},{1,3},{2,0},{3,1},{4,6},{5,7},{6,4},{7,5},{8,10},{9,11},{10,... | collective-permute-start | bytes 1769480 | tf_op jit(solution)/shard_map/ppermute | solution.py:43
  419.3 26.5 %collective-permute-start.72 = (bf16[2,192,768]{2,1,0:T(8,128)(2,1)S(1)}, bf16[2,192,768]{2,1,0:T(8,128)(2,1)S(1)}, u32[]{:S(2)}, u32[]{:S(2)}) collective-permute-start(bf16[2,192,768]{2,1,0:T(8,128)(2,1)S(1)} %pad_maximum_fusion.9.refs_0_), channel_id=1, source_target_pairs={{0,16},{1,17},{2,18},{3,19},{4,20},{5,21},{6,22},{7,23},{8,24},{9,... | collective-permute-start | bytes 1769480 | tf_op jit(solution)/shard_map/ppermute | solution.py:43
  430.7 20.2 %collective-permute-start.77 = (bf16[2,2,96,768]{3,2,1,0:T(8,128)(2,1)S(1)}, bf16[2,2,96,768]{3,2,1,0:T(8,128)(2,1)S(1)}, u32[]{:S(2)}, u32[]{:S(2)}) collective-permute-start(bf16[2,2,96,768]{3,2,1,0:T(8,128)(2,1)S(1)} %pad_maximum_fusion.11), channel_id=1, source_target_pairs={{0,4},{1,5},{2,6},{3,7},{4,0},{5,1},{6,2},{7,3},{8,12},{9,13},{10,... | collective-permute-start | bytes 1769480 | tf_op jit(solution)/shard_map/ppermute | solution.py:43
  430.9 26.8 %collective-permute-start.76 = (bf16[2,2,96,768]{3,2,1,0:T(8,128)(2,1)S(1)}, bf16[2,2,96,768]{3,2,1,0:T(8,128)(2,1)}, u32[]{:S(2)}, u32[]{:S(2)}) collective-permute-start(bf16[2,2,96,768]{3,2,1,0:T(8,128)(2,1)S(1)} %pad_maximum_fusion.10), channel_id=1, source_target_pairs={{0,8},{1,9},{2,10},{3,11},{4,12},{5,13},{6,14},{7,15},{8,0},{9,1},... | collective-permute-start | bytes 1769480 | tf_op jit(solution)/shard_map/ppermute | solution.py:43
  466.7 19.9 %collective-permute-start.83 = (bf16[2,2,96,768]{3,2,1,0:T(8,128)(2,1)}, bf16[2,2,96,768]{3,2,1,0:T(8,128)(2,1)}, u32[]{:S(2)}, u32[]{:S(2)}) collective-permute-start(bf16[2,2,96,768]{3,2,1,0:T(8,128)(2,1)} %pad_maximum_fusion.15), channel_id=1, source_target_pairs={{0,4},{1,5},{2,6},{3,7},{4,0},{5,1},{6,2},{7,3},{8,12},{9,13},{10,... | collective-permute-start | bytes 1769480 | tf_op jit(solution)/shard_map/ppermute | solution.py:43
  469.0 19.4 %collective-permute-start.82 = (bf16[2,2,96,768]{3,2,1,0:T(8,128)(2,1)}, bf16[2,2,96,768]{3,2,1,0:T(8,128)(2,1)S(1)}, u32[]{:S(2)}, u32[]{:S(2)}) collective-permute-start(bf16[2,2,96,768]{3,2,1,0:T(8,128)(2,1)} %pad_maximum_fusion.14), channel_id=1, source_target_pairs={{0,8},{1,9},{2,10},{3,11},{4,12},{5,13},{6,14},{7,15},{8,0},{9,1},... | collective-permute-start | bytes 1769480 | tf_op jit(solution)/shard_map/ppermute | solution.py:43
  475.8 20.4 %collective-permute-start.84 = (bf16[2,1,96,768]{3,2,1,0:T(8,128)(2,1)S(1)}, bf16[2,1,96,768]{3,2,1,0:T(8,128)(2,1)S(1)}, u32[]{:S(2)}, u32[]{:S(2)}) collective-permute-start(bf16[2,1,96,768]{3,2,1,0:T(8,128)(2,1)S(1)} %pad_maximum_fusion.18), channel_id=1, source_target_pairs={{0,4},{1,5},{2,6},{3,7},{4,0},{5,1},{6,2},{7,3},{8,12},{9,13},{10,... | collective-permute-start | bytes 884744 | tf_op jit(solution)/shard_map/ppermute | solution.py:43
  476.0 20.3 %collective-permute-start.85 = (bf16[2,1,96,768]{3,2,1,0:T(8,128)(2,1)S(1)}, bf16[2,1,96,768]{3,2,1,0:T(8,128)(2,1)S(1)}, u32[]{:S(2)}, u32[]{:S(2)}) collective-permute-start(bf16[2,1,96,768]{3,2,1,0:T(8,128)(2,1)S(1)} %pad_maximum_fusion.19), channel_id=1, source_target_pairs={{0,8},{1,9},{2,10},{3,11},{4,12},{5,13},{6,14},{7,15},{8,0},{9,1},... | collective-permute-start | bytes 884744 | tf_op jit(solution)/shard_map/ppermute | solution.py:43
  477.5 25.5 %collective-permute-start.80 = (bf16[2,2,96,768]{3,2,1,0:T(8,128)(2,1)S(1)}, bf16[2,2,96,768]{3,2,1,0:T(8,128)(2,1)S(1)}, u32[]{:S(2)}, u32[]{:S(2)}) collective-permute-start(bf16[2,2,96,768]{3,2,1,0:T(8,128)(2,1)S(1)} %pad_maximum_fusion.12), channel_id=1, source_target_pairs={{0,4},{1,5},{2,6},{3,7},{4,0},{5,1},{6,2},{7,3},{8,12},{9,13},{10,... | collective-permute-start | bytes 1769480 | tf_op jit(solution)/shard_map/ppermute | solution.py:43
  486.5 17.1 %collective-permute-start.81 = (bf16[2,2,96,768]{3,2,1,0:T(8,128)(2,1)S(1)}, bf16[2,2,96,768]{3,2,1,0:T(8,128)(2,1)S(1)}, u32[]{:S(2)}, u32[]{:S(2)}) collective-permute-start(bf16[2,2,96,768]{3,2,1,0:T(8,128)(2,1)S(1)} %pad_maximum_fusion.13), channel_id=1, source_target_pairs={{0,8},{1,9},{2,10},{3,11},{4,12},{5,13},{6,14},{7,15},{8,0},{9,1},... | collective-permute-start | bytes 1769480 | tf_op jit(solution)/shard_map/ppermute | solution.py:43
  (114 other events, 875.3 us)
Sparse Core Ops, SparseCore 0:
  49.6 81.5 all-gather.2

commit v3 on v2

--- a/solution.py
+++ b/solution.py
@@ -286,7 +286,7 @@
     distance_ref, dx_ref, dgain_ref, dqkv_ref, eb_ref = refs[:5]
     refs = refs[5:]
     if cross:
-        dc_ref, refs = refs[0], refs[1:]
+        dc_ref, leaving_ref, refs = refs[0], refs[1], refs[2:]
     room, inner_ref, wide, sems = refs
     copies = mix_copies(pieces, meta, room, sems)
     for copy in copies:
@@ -349,6 +349,15 @@
         dx_ref[rows, :] = e_ref[rows, :] + part
         gain_total = gain_total + gain_part
     dgain_ref[...] = gain_total
+    if cross:
+
+        @pl.when(meta[2] > 0)
+        def _():
+            leaving_ref[...] = dc_ref[...]
+
+        @pl.when(meta[2] == 0)
+        def _():
+            leaving_ref[...] = dx_ref[...].astype(BF16)
 
 
 def mix_back(meta, slopes, delta, x, gain, qkv, lse, pieces, distance, cross):
@@ -361,14 +370,14 @@
         + [WHOLE] * (3 + 2 * len(qkv))
         + [ANYWHERE] * len(pieces)
         + [WHOLE],
-        out_specs=[WHOLE] * (5 if cross else 4),
+        out_specs=[WHOLE] * (6 if cross else 4),
         out_shape=[
             jax.ShapeDtypeStruct((rows, D), F32),
             jax.ShapeDtypeStruct((1, D), F32),
             jax.ShapeDtypeStruct((rows, 3 * D), BF16),
             wide_rows,
         ]
-        + ([wide_rows] if cross else []),
+        + ([wide_rows] * 2 if cross else []),
         scratch_shapes=[
             pltpu.VMEM((4, D, D), BF16),
             pltpu.VMEM((rows, D), F32),
@@ -452,16 +461,19 @@
 def fetch_quarter(step, copies):
     @pl.when(step == 0)
     def _():
-        for group in copies:
+        for group in copies[:2]:
             for copy in group:
                 copy.start()
 
     for q, group in enumerate(copies):
 
         @pl.when(step == q)
-        def _(group=group):
+        def _(q=q, group=group):
             for copy in group:
                 copy.wait()
+            for later in copies[q + 2 : q + 3]:
+                for copy in later:
+                    copy.start()
 
 
 def feed_forward_kernel(local, n_pieces, meta, x_ref, norm_ref, *refs):
@@ -470,7 +482,7 @@
         b_ref, refs = refs[0], refs[1:]
     else:
         b_ref = norm_ref
-    y_ref, h_ref, g_ref, room, sems = refs
+    out_ref, h_ref, g_ref, room, sems, y_ref = refs
     step = pl.program_id(0)
     fetch_quarter(step, feed_copies(pieces, meta, room, sems))
 
@@ -488,6 +500,10 @@
     h_ref[...] = (before * share).astype(BF16)
     g_ref[...] = (share + before * bell).astype(BF16)
     y_ref[...] += rows_nn(h_ref[...], room[step, 1])
+
+    @pl.when(step == pl.num_programs(0) - 1)
+    def _():
+        out_ref[...] = y_ref[...].astype(BF16)
 
 
 def feed_forward(meta, x, gain, normed, pieces):
@@ -504,8 +520,12 @@
         + [ANYWHERE] * len(pieces),
         out_specs=([fixed] if local else []) + [fixed, moving, moving],
         out_shape=([jax.ShapeDtypeStruct((rows, D), BF16)] if local else [])
-        + [jax.ShapeDtypeStruct((rows, D), F32), hidden, hidden],
-        scratch_shapes=[pltpu.VMEM((quarters, 2, D, D), BF16), pltpu.SemaphoreType.DMA((16,))],
+        + [jax.ShapeDtypeStruct((rows, D), BF16), hidden, hidden],
+        scratch_shapes=[
+            pltpu.VMEM((quarters, 2, D, D), BF16),
+            pltpu.SemaphoreType.DMA((16,)),
+            pltpu.VMEM((rows, D), F32),
+        ],
         compiler_params=pltpu.CompilerParams(vmem_limit_bytes=ROOM),
         cost_estimate=cost(rows, 3.6, 4 * quarters),
         name="feed_forward",
@@ -579,10 +599,9 @@
     )(place, x, gain, next_gain, *pieces, *([] if leaving else first))
 
 
-def feed_back_kernel(spans, n_pieces, meta, e_ref, x_ref, gain_ref, *refs):
-    slopes, refs = refs[:spans], refs[spans:]
+def feed_back_kernel(n_pieces, meta, e_ref, x_ref, gain_ref, slope_ref, b_ref, h_ref, *refs):
     pieces, refs = refs[:n_pieces], refs[n_pieces:]
-    dx_ref, dgain_ref, eb_ref, eu_ref, room, sems = refs
+    dx_ref, dgain_ref, eb_ref, eu_ref, sent_ref, room, sems = refs
     step = pl.program_id(0)
     fetch_quarter(step, feed_copies(pieces, meta, room, sems))
     chunks = chunks_of(x_ref.shape[0])
@@ -593,50 +612,53 @@
             eb_ref[rows, :] = e_ref[rows, :].astype(BF16)
             dx_ref[rows, :] = jnp.zeros_like(dx_ref[rows, :])
 
-    slope = slopes[0][...]
-    if spans == 2:
-        slope = jnp.where(step < 2, slope, slopes[1][...])
-    slope = slope.astype(F32)
+    slope = slope_ref[...].astype(F32)
     eu_ref[...] = (rows_nt(eb_ref[...], room[step, 1]) * slope).astype(BF16)
     dx_ref[...] += rows_nt(eu_ref[...], room[step, 0])
+
+    @pl.when(step % 2 == 1)
+    def _():
+        for kind, (left, right) in enumerate(((b_ref, eu_ref), (h_ref, eb_ref))):
+            delta = rows_tn(left[...], right[...])
+            for p in range(PARTS):
+                rows = pl.ds(pl.multiple_of((meta[0] ^ p) * PIECE, PIECE), PIECE)
+                sent_ref[0, kind, rows, :] = delta[p * PIECE : (p + 1) * PIECE].astype(BF16)
 
     @pl.when(step == 3)
     def _():
         gain_total = jnp.zeros((1, D), F32)
         for rows in chunks:
             part, gain_part = norm_back(x_ref[rows, :], gain_ref[...], dx_ref[rows, :])
-            dx_ref[rows, :] = e_ref[rows, :] + part
+            dx_ref[rows, :] = e_ref[rows, :].astype(F32) + part
             gain_total = gain_total + gain_part
         dgain_ref[...] = gain_total
 
 
-def feed_back(meta, delta, x, gain, slope, pieces):
+def feed_back(meta, delta, x, gain, slope, pieces, b, h):
     rows = x.shape[0]
     fixed = pl.BlockSpec((rows, D), lambda q: (0, 0))
     moving = pl.BlockSpec((rows, D), lambda q: (0, q))
     narrow = pl.BlockSpec((1, D), lambda q: (0, 0))
-    slopes = [moving]
-    if len(slope) == 2:
-        slopes = [
-            pl.BlockSpec((rows, D), lambda q: (0, jnp.minimum(q, 1))),
-            pl.BlockSpec((rows, D), lambda q: (0, jnp.maximum(q - 2, 0))),
-        ]
+    hidden = pl.BlockSpec((rows, D), lambda q: (0, 2 * (q // 2) + 1))
     return pl.pallas_call(
-        functools.partial(feed_back_kernel, len(slope), len(pieces)),
+        functools.partial(feed_back_kernel, len(pieces)),
         grid=(4,),
-        in_specs=[SCALARS, fixed, fixed, narrow] + slopes + [ANYWHERE] * len(pieces),
-        out_specs=[fixed, narrow, fixed, moving],
+        in_specs=[SCALARS, fixed, fixed, narrow, moving, fixed, hidden]
+        + [ANYWHERE] * len(pieces),
+        out_specs=[fixed, narrow, fixed, moving]
+        + [pl.BlockSpec((1, 2, D, D), lambda q: (q // 2, 0, 0, 0))],
         out_shape=[
             jax.ShapeDtypeStruct((rows, D), F32),
             jax.ShapeDtypeStruct((1, D), F32),
             jax.ShapeDtypeStruct((rows, D), BF16),
             jax.ShapeDtypeStruct((rows, 4 * D), BF16),
+            jax.ShapeDtypeStruct((2, 2, D, D), BF16),
         ],
         scratch_shapes=[pltpu.VMEM((4, 2, D, D), BF16), pltpu.SemaphoreType.DMA((16,))],
         compiler_params=pltpu.CompilerParams(vmem_limit_bytes=ROOM),
-        cost_estimate=cost(rows, 5, 13.5),
+        cost_estimate=cost(rows, 5, 19),
         name="feed_back",
-    )(meta, delta, x, gain, *slope, *pieces)
+    )(meta, delta, x, gain, slope, b, h, *pieces)
 
 
 def feed_weights_kernel(place, eu_ref, *refs):
@@ -798,6 +820,7 @@
 THIRDS = ("xyz", "yxz", "zxy")
 HALVES = ("xyz", "yzx")
 LAST = ("xyz", "yxz")
+CROSS = ("yxz", "zxy")
 
 
 def halves(array, axis):
@@ -822,6 +845,28 @@
     return out
 
 
+def link_first(keep, beside, orders=THIRDS):
+    shape = (2, -1, 2, 2, PIECE, D)
+    step = PIECE // len(orders)
+
+    def split(keep, beside):
+        out = []
+        for i, order in enumerate(orders):
+            rows = slice(i * step, (i + 1) * step)
+            share = keep[:, :, :, :, rows] + beside[:, :, :, :, rows]
+            out.append(halves(share, AXES[order[0]][0]))
+        return out
+
+    return glue(split, keep.reshape(shape), beside.reshape(shape))
+
+
+def link_swap(parts, stage, orders=THIRDS):
+    return [
+        (keep, swap(sent, *AXES[order[stage]][1:]))
+        for (keep, sent), order in zip(parts, orders, strict=True)
+    ]
+
+
 def link_next(pairs, stage, orders=THIRDS):
     def split(pairs):
         return [
@@ -829,10 +874,7 @@
             for (keep, received), order in zip(pairs, orders, strict=True)
         ]
 
-    return [
-        (keep, swap(sent, *AXES[order[stage]][1:]))
-        for (keep, sent), order in zip(glue(split, pairs), orders, strict=True)
-    ]
+    return link_swap(glue(split, pairs), stage, orders)
 
 
 def link_add(pairs):
@@ -946,12 +988,15 @@
         mix_quarter, encoder_expand, encoder_reduce
     )
     feed_quarter = jnp.stack([select_slot(encoder_expand), select_slot(encoder_reduce)])
-    feed_quarter, mix_quarter, mix_zero, flat, uni_feed_quarter = tie(
+    feed_quarter, mix_quarter, mix_zero, flat, uni_feed_quarter, meta, slopes, distance = tie(
         feed_quarter,
         mix_quarter,
         mix_zero,
         tokens.reshape(-1, D),
         jnp.stack([uniting_expand, uniting_reduce]),
+        meta,
+        slopes,
+        distance,
     )
     mix_pieces = fetch_relayed(
         mix_zero, swap(piece_of(mix_quarter, own ^ 3), head_mask=ACROSS)
@@ -1012,23 +1057,28 @@
     uni_hidden, uni_bend = ([part] for part in stored)
 
     joined, sent_cotangent = tie(joined, sent_cotangent)
-    joined_half = joined.astype(BF16).reshape(some, SLOTS, D)
+    joined_half = joined.reshape(some, SLOTS, D)
     other_half = [swap(joined_half[i : i + 1], dp_mask=side) for i in range(some)]
     pair_cotangent = jnp.where(radar, cotangent[some:], sent_cotangent)
     pair_visible = lax.dynamic_slice_in_dim(visible, first, some, 0)
-    delta_joined = jnp.where(pair_visible, pair_cotangent, 0).astype(F32).reshape(-1, D)
-    delta_middle, gain_three, eb, eu = feed_back(
-        meta, delta_joined, uni_middle, uni_gains[2], uni_bend, uni_feed
-    )
-    eu, other_half[0] = tie(eu, other_half[0])
-    sent = feed_weights(place, eu, uni_hidden, uni_normed_two, eb, 1)
-    sent, eu, other_half[1] = tie(sent, eu, other_half[1])
+    delta_joined = jnp.where(pair_visible, pair_cotangent, 0).reshape(-1, D)
+    delta_middle, gain_three, eb, eu, sent = feed_back(
+        meta,
+        delta_joined,
+        uni_middle,
+        uni_gains[2],
+        uni_bend[0],
+        uni_feed,
+        uni_normed_two,
+        uni_hidden[0],
+    )
+    sent, eu, other_half[:2] = tie(sent, eu, other_half[:2])
     beside = swap(sent, head_mask=CORE)
     keep = feed_weights(place, eu, uni_hidden, uni_normed_two, eb, 0)
-    keep, beside = tie(keep, beside)
-    uni_feed_sum, delta_middle = tie(add_split(keep, beside), delta_middle)
-    uni_feed_pairs = link_send(uni_feed_sum, 0)
-    delta_radar, gain_two, dqkv, mix_eb, delta_context = mix_back(
+    keep, beside, other_half[2:] = tie(keep, beside, other_half[2:])
+    uni_feed_parts, delta_middle = tie(link_first(keep, beside), delta_middle)
+    uni_feed_pairs = link_swap(uni_feed_parts, 0)
+    delta_radar, gain_two, dqkv, mix_eb, delta_context, leaving = mix_back(
         pair_meta,
         slopes,
         delta_middle,
@@ -1040,8 +1090,7 @@
         distance,
         True,
     )
-    leaving = jnp.where(radar, delta_context, delta_radar.astype(BF16))
-    leaving, dqkv, uni_feed_pairs, other_half = tie(leaving, dqkv, uni_feed_pairs, other_half)
+    leaving, dqkv, uni_feed_pairs = tie(leaving, dqkv, uni_feed_pairs)
     other_half = jnp.concatenate(other_half, 0)
     returned = swap(leaving, dp_mask=side)
     uni_feed_pairs = link_next(uni_feed_pairs, 1)
@@ -1064,54 +1113,51 @@
         meta, modality, encoded, uni_gains[0], delta_context, returned, delta_radar, cotangent
     )
     delta_encoded, beside, uni_feed_pairs = tie(delta_encoded, beside, uni_feed_pairs)
-    uni_mix_sum, uni_feed_part = add_split(keep, beside, HALVES), join(link_add(uni_feed_pairs))
+    uni_mix_sum, uni_feed_part = add_split(keep, beside, CROSS), join(link_add(uni_feed_pairs))
     delta_encoded, uni_mix_sum, uni_feed_part = tie(delta_encoded, uni_mix_sum, uni_feed_part)
     uni_feed_rest = rest_send(uni_feed_part, groups)
-    uni_mix_pairs = link_send(uni_mix_sum, 0, HALVES)
-
-    delta_middle, gain_b, eb, eu = feed_back(
-        meta, delta_encoded, middle, gains[1], bend, enc_feed
-    )
-    eu, uni_mix_pairs = tie(eu, uni_mix_pairs)
-    uni_mix_sum, eu = tie(link_add(uni_mix_pairs), eu)
-    uni_mix_pairs = link_send(uni_mix_sum, 1, HALVES)
-    sent = feed_weights(place, eu, hidden, normed_two, eb, 1)
+    uni_mix_pairs = link_send(uni_mix_sum, 0, CROSS)
+
+    delta_middle, gain_b, eb, eu, sent = feed_back(
+        meta, delta_encoded, middle, gains[1], bend[0], enc_feed, normed_two, hidden[0]
+    )
     sent, eu, uni_feed_rest, uni_mix_pairs = tie(sent, eu, uni_feed_rest, uni_mix_pairs)
     uni_feed_part, uni_mix_sum = rest_add(uni_feed_rest), link_add(uni_mix_pairs)
     eu, uni_feed_part, uni_mix_sum = tie(eu, uni_feed_part, uni_mix_sum)
     beside = swap(sent, head_mask=CORE)
     uni_feed_near = swap(uni_feed_part, dp_mask=1)
-    uni_mix_pairs = link_send(uni_mix_sum, 2, HALVES)
+    uni_mix_pairs = link_send(uni_mix_sum, 1, CROSS)
     keep = feed_weights(place, eu, hidden, normed_two, eb, 0)
     keep, beside, uni_feed_near, uni_mix_pairs = tie(keep, beside, uni_feed_near, uni_mix_pairs)
     uni_feed_near = jnp.stack([uni_feed_part, uni_feed_near])
-    enc_feed_sum, uni_mix_part = add_split(keep, beside, HALVES), join(link_add(uni_mix_pairs))
-    delta_middle, enc_feed_sum, uni_mix_part, uni_feed_near = tie(
-        delta_middle, enc_feed_sum, uni_mix_part, uni_feed_near
+    enc_feed_sum, uni_mix_sum = add_split(keep, beside, HALVES), link_add(uni_mix_pairs)
+    delta_middle, enc_feed_sum, uni_mix_sum, uni_feed_near = tie(
+        delta_middle, enc_feed_sum, uni_mix_sum, uni_feed_near
     )
     enc_feed_pairs = link_send(enc_feed_sum, 0, HALVES)
-    uni_mix_rest = rest_send(uni_mix_part, groups)
+    uni_mix_pairs = link_send(uni_mix_sum, 2, CROSS)
     uni_feed_far = swap(uni_feed_near, dp_mask=2)
     delta_inputs, gain_a, dqkv, eb = mix_back(
         meta, slopes, delta_middle, flat, gains[0], qkv, lse, enc_mix, distance, False
     )
-    dqkv, enc_feed_pairs, uni_mix_rest, uni_feed_far = tie(
-        dqkv, enc_feed_pairs, uni_mix_rest, uni_feed_far
-    )
-    enc_feed_sum, uni_mix_part = link_add(enc_feed_pairs), rest_add(uni_mix_rest)
+    dqkv, enc_feed_pairs, uni_mix_pairs, uni_feed_far = tie(
+        dqkv, enc_feed_pairs, uni_mix_pairs, uni_feed_far
+    )
+    enc_feed_sum, uni_mix_part = link_add(enc_feed_pairs), join(link_add(uni_mix_pairs))
     dqkv, enc_feed_sum, uni_mix_part = tie(dqkv, enc_feed_sum, uni_mix_part)
     enc_feed_pairs = link_send(enc_feed_sum, 1, HALVES)
-    uni_mix_gather = gather_first(uni_mix_part)
+    uni_mix_rest = rest_send(uni_mix_part, groups)
 
     totals = (gain_a, gain_b, gain_one, gain_two, gain_three)
     keep, sent = mix_weights(place, dqkv, mixed, normed_one, normed_one, eb, totals)
-    sent, enc_feed_pairs, uni_mix_gather = tie(sent, enc_feed_pairs, uni_mix_gather)
+    sent, enc_feed_pairs, uni_mix_rest = tie(sent, enc_feed_pairs, uni_mix_rest)
+    uni_mix_gather = gather_first(rest_add(uni_mix_rest))
     beside = swap(sent, head_mask=CORE)
     enc_feed_pairs = link_send(link_add(enc_feed_pairs), 2, HALVES)
     enc_mix_pairs = link_send(add_split(keep, beside, LAST), 0, LAST)
     feed_part = over_rest(join(link_add(enc_feed_pairs)), side)
     feed_other = swap(feed_part, dp_mask=side)
-    enc_mix_pairs, feed_part = tie(enc_mix_pairs, feed_part)
+    enc_mix_pairs, feed_part, uni_mix_gather = tie(enc_mix_pairs, feed_part, uni_mix_gather)
     enc_mix_pairs = link_send(link_add(enc_mix_pairs), 1, LAST)
     feed_gather = gather_first(feed_part)
     enc_mix_pairs = link_send(link_add(enc_mix_pairs), 2, LAST)

time: 520 us -> 513 us (0.987)
  other arithmetic: 45.7 us -> 38 us
    pallas_call x4 -> x2, Pallas kernels: 36.7 us -> 18.5 us  [feed_weights(): pl.pallas_call(feed_weights_kernel, grid_spec=pltpu.PrefetchScalarGridSpe...]
    pallas_call x2, Pallas kernels: 30.2 us -> 41.8 us  [feed_back(): pl.pallas_call(functools.partial(feed_back_kernel, len(pieces)), grid=(4,...]
    pallas_call x1 -> x2, Pallas kernels: 3.77 us -> 9.85 us  [glue(): pl.pallas_call(kernel, in_specs=[WHOLE] * len(leaves), out_specs=[WHOLE]...]
  transfers between devices with their start and end apart: 87 -> 87, of which waited for: 40 -> 35; matrix products, arithmetic and copies ran while one was open for 9% -> 9% of each run, Pallas kernels for 43% -> 43%
where the time goes in v3:
time: 513 us; the launch traced here: 509 us
  Pallas kernels  223 us (43%)
  waiting for transfers between devices  122 us (24%)
  starting transfers between devices  79.4 us (15%)
  other arithmetic  38 us (7%)
  local copies, waits for them, and re-layouts  31.7 us (6%)
  between operations  16 us (3%)
    ppermute x86, waiting for transfers between devices, swap(): return lax.ppermute(array, ('dp', 'head'), pairs)  121 us
    ppermute x86, starting transfers between devices, swap(): return lax.ppermute(array, ('dp', 'head'), pairs)  79.4 us
    pallas_call x3, Pallas kernels, mix_forward(): pl.pallas_call(functools.partial(mix_forward_kernel, local, cross, images...  42 us
    pallas_call x2, Pallas kernels, feed_back(): pl.pallas_call(functools.partial(feed_back_kernel, len(pieces)), grid=(4,...  41.8 us
    pallas_call x2, Pallas kernels, mix_back(): pl.pallas_call(functools.partial(mix_back_kernel, cross, images, len(qkv)...  39.8 us
    pallas_call x2, Pallas kernels, feed_rows(): pl.pallas_call(functools.partial(feed_rows_kernel, leaving), grid_spec=pl...  26.9 us
    pallas_call x2, Pallas kernels, mix_weights(): pl.pallas_call(functools.partial(mix_weights_kernel, more), grid_spec=plt...  19.1 us
    pallas_call x2, Pallas kernels, feed_weights(): pl.pallas_call(feed_weights_kernel, grid_spec=pltpu.PrefetchScalarGridSpe...  18.5 us
  transfers between devices with their start and end apart: 87, of which 35 were waited for; matrix products, arithmetic and copies ran while one was open for 9% of the time, Pallas kernels for 43%

profile of v3, /device:TPU:0, one launch (start us, length us, event | category | flops | bytes accessed | tf_op | source)
XLA Modules:
  0.0 509.4 jit_solution(2850569474560170707)
XLA Ops:
  9.8 2.9 collective-permute-start
  33.8 13.7 %mix_forward.3 = (bf16[816,768]{1,0:T(8,128)(2,1)}, f32[816,768]{1,0:T(8,128)}, bf16[6,136,1152]{2,1,0:T(8,128)(2,1)}, bf16[816,384]{1,0:T(8,128)(2,1)}, f32[6,3,272]{2,1,0:T(4,128)}) custom-call(s32[9]{0:T(128)} %get-tuple-element.276.refs_0_.meta, f32[12]{0:T(128)} %fusion.11.refs_1_, bf16[816,768]{1,0:T(8,128)(2,1)} %bitcast.174, ...), custom_call_target="tpu_custom_call" | custom-call | flops 120000000 | bytes 1 | tf_op jit(solution)/shard_map/mix_forward/pallas_call | solution.py:259
  57.0 14.9 %mix_forward.4 = (f32[816,768]{1,0:T(8,128)}, bf16[6,136,1152]{2,1,0:T(8,128)(2,1)}, bf16[816,384]{1,0:T(8,128)(2,1)}, f32[6,3,272]{2,1,0:T(4,128)}) custom-call(s32[9]{0:T(128)} %get-tuple-element.276.refs_0_.meta, f32[12]{0:T(128)} %fusion.11.refs_1_, f32[816,768]{1,0:T(8,128)} %get-tuple-element.289.refs_2_, ...), custom_call_target="tpu_custom_call" | custom-call | flops 120000000 | bytes 1 | tf_op jit(solution)/shard_map/mix_forward/pallas_call | solution.py:259
  76.6 2.0 collective-permute-done.17.refs_9_
  79.5 13.2 %feed_rows.2 = (f32[816,768]{1,0:T(8,128)}, bf16[816,768]{1,0:T(8,128)(2,1)}, bf16[816,3072]{1,0:T(8,128)(2,1)}, bf16[816,3072]{1,0:T(8,128)(2,1)}, bf16[408,768]{1,0:T(8,128)(2,1)}) custom-call(s32[3]{0:T(128)} %pad_add_fusion.meta.place, f32[816,768]{1,0:T(8,128)} %get-tuple-element.305.x_ref, f32[1,768]{1,0:T(1,128)} %get-tuple-element.623.gain_ref, ...), custom_call_target="tpu_custom_call" | custom-call | flops 116000000 | bytes 1 | tf_op jit(solution)/shard_map/feed_rows/pallas_call | solution.py:578
  92.7 2.4 collective-permute-start.19
  98.5 13.7 %feed_rows.3 = (f32[816,768]{1,0:T(8,128)}, bf16[816,768]{1,0:T(8,128)(2,1)}, bf16[816,3072]{1,0:T(8,128)(2,1)}, bf16[816,3072]{1,0:T(8,128)(2,1)}, bf16[408,768]{1,0:T(8,128)(2,1)}) custom-call(s32[3]{0:T(128)} %pad_add_fusion.meta.place, ...), custom_call_target="tpu_custom_call", output_to_operand_aliasing={{0}: (14, {}), {1}: (15, {}), {2}: (16, {}), {3}: (17, {})} | custom-call | flops 116000000 | bytes 1 | tf_op jit(solution)/shard_map/feed_rows/pallas_call | solution.py:578
  112.3 3.0 collective-permute-done.21.refs_9_.refs_11_
  115.3 8.2 %collective-permute-done.19 = bf16[408,768]{1,0:T(8,128)(2,1)S(1)} collective-permute-done((bf16[408,768]{1,0:T(8,128)(2,1)}, bf16[408,768]{1,0:T(8,128)(2,1)S(1)}, u32[]{:S(2)}, u32[]{:S(2)}) %collective-permute-start.19) | collective-permute-done | bytes 626720 | tf_op jit(solution)/shard_map/ppermute | solution.py:43
  128.6 13.4 %mix_forward.5 = (bf16[408,768]{1,0:T(8,128)(2,1)}, f32[408,768]{1,0:T(8,128)}, bf16[3,136,2304]{2,1,0:T(8,128)(2,1)}, bf16[408,768]{1,0:T(8,128)(2,1)}, f32[3,6,272]{2,1,0:T(8,128)}) custom-call(s32[9]{0:T(128)} %get-tuple-element.626.refs_0_, f32[12]{0:T(128)} %fusion.11.refs_1_, f32[408,768]{1,0:T(8,128)} %convert_select_fusion.refs_2_.refs_3_, ...), custom_call_target="tpu_custom_call" | custom-call | flops 120000000 | bytes 1 | tf_op jit(solution)/shard_map/mix_forward/pallas_call | solution.py:259
  142.1 11.5 %feed_forward.1 = (bf16[408,768]{1,0:T(8,128)(2,1)}, bf16[408,768]{1,0:T(8,128)(2,1)}, bf16[408,3072]{1,0:T(8,128)(2,1)}, bf16[408,3072]{1,0:T(8,128)(2,1)}) custom-call(s32[9]{0:T(128)} %get-tuple-element.276.refs_0_.meta, f32[408,768]{1,0:T(8,128)} %get-tuple-element.333.x_ref, f32[1,768]{1,0:T(1,128)} %get-tuple-element.620.norm_ref.gain_ref, ...), custom_call_target="tpu_custom_call" | custom-call | flops 116000000 | bytes 1 | tf_op jit(solution)/shard_map/feed_forward/pallas_call | solution.py:516
  158.6 2.0 select_select_fusion
  160.6 16.0 %feed_back.2 = (f32[408,768]{1,0:T(8,128)}, f32[1,768]{1,0:T(1,128)}, bf16[408,768]{1,0:T(8,128)(2,1)}, bf16[408,3072]{1,0:T(8,128)(2,1)}, bf16[2,2,768,768]{3,2,1,0:T(8,128)(2,1)}) custom-call(s32[9]{0:T(128)} %get-tuple-element.276.refs_0_.meta, bf16[408,768]{1,0:T(8,128)(2,1)} %bitcast.179, f32[408,768]{1,0:T(8,128)} %get-tuple-element.333.x_ref, ...), custom_call_target="tpu_custom_call" | custom-call | flops 145000000 | bytes 1 | tf_op jit(solution)/shard_map/feed_back/pallas_call | solution.py:643
  178.2 7.6 %feed_weights.2 = bf16[2,2,768,768]{3,2,1,0:T(8,128)(2,1)} custom-call(s32[3]{0:T(128)} %pad_add_fusion.meta.place, bf16[408,3072]{1,0:T(8,128)(2,1)} %get-tuple-element.343.eu_ref, bf16[408,3072]{1,0:T(8,128)(2,1)} %get-tuple-element.339.h_ref.refs_0_, bf16[408,768]{1,0:T(8,128)(2,1)} %get-tuple-element.338.b_ref.refs_1_, ...), custom_call_target="tpu_custom_call" | custom-call | flops 70000000 | bytes 1 | tf_op jit(solution)/shard_map/feed_weights/pallas_call | solution.py:691
  185.8 4.6 collective-permute-done.32
  190.4 2.2 copy-done.18
  192.6 6.1 %glue.2 = (bf16[1,2,2,2,64,768]{5,4,3,2,1,0:T(8,128)(2,1)}, bf16[1,2,2,2,64,768]{5,4,3,2,1,0:T(8,128)(2,1)}, bf16[2,2,2,1,64,768]{5,4,3,2,1,0:T(8,128)(2,1)}, bf...) custom-call(bf16[2,2,2,2,192,768]{5,4,3,2,1,0:T(8,128)(2,1)} %bitcas, ...), custom_call_target="tpu_custom_call" | custom-call | flops 10000000 | bytes 1 | tf_op jit(solution)/shard_map/glue/pallas_call | solution.py:92
  200.2 15.2 %mix_back.2 = (f32[408,768]{1,0:T(8,128)}, f32[1,768]{1,0:T(1,128)}, bf16[408,2304]{1,0:T(8,128)(2,1)}, bf16[408,768]{1,0:T(8,128)(2,1)}, bf16[408,768]{1,0:T(8,128)(2,1)}, /*index=5*/bf16[408,768]{1,0:T(8,128)(2,1)}) custom-call(s32[9]{0:T(128)} %get-tuple-element.626.refs_0_, f32[12]{0:T(128)} %fusion.11.refs_1_, f32[408,768]{1,0:T(8,128)} %get-tuple-element.355.refs_2_, ...), custom_call_target="tpu_custom_call" | custom-call | flops 165000000 | bytes 1 | tf_op jit(solution)/shard_map/mix_back/pallas_call | solution.py:367
  215.4 2.7 collective-permute-done.33.refs_1_
  220.4 3.8 glue.3
  231.5 7.8 %mix_weights.2 = (bf16[2,4,192,768]{3,2,1,0:T(8,128)(2,1)}, bf16[2,4,192,768]{3,2,1,0:T(8,128)(2,1)}) custom-call(s32[3]{0:T(128)} %pad_add_fusion.meta.place, bf16[408,2304]{1,0:T(8,128)(2,1)} %get-tuple-element.366.dqkv_ref, bf16[408,768]{1,0:T(8,128)(2,1)} %get-tuple-element.367.refs_0_, bf16[408,768]{1,0:T(8,128)(2,1)} %get-tuple-element.368.refs_1_, ...), custom_call_target="tpu_custom_call" | custom-call | flops 70000000 | bytes 1 | tf_op jit(solution)/shard_map/mix_weights/pallas_call | solution.py:442
  239.9 5.7 %collective-permute-done.39 = bf16[1,2,1,2,64,768]{5,4,3,2,1,0:T(8,128)(2,1)S(1)} collective-permute-done((bf16[1,2,1,2,64,768]{5,4,3,2,1,0:T(8,128)(2,1)S(1)}, bf16[1,2,1,2,64,768]{5,4,3,2,1,0:T(8,128)(2,1)S(1)}, u32[]{:S(2)}, u32[]{:S(2)}) %collective-permute-start.39) | collective-permute-done | bytes 393248 | tf_op jit(solution)/shard_map/ppermute | solution.py:43
  245.7 2.3 collective-permute-done.36.returned
  252.0 6.4 %turn_back.1 = (f32[816,768]{1,0:T(8,128)}, f32[1,768]{1,0:T(1,128)}) custom-call(s32[9]{0:T(128)} %get-tuple-element.276.refs_0_.meta, s32[1]{0:T(128)} %bitcast.2.side, f32[816,768]{1,0:T(8,128)} %get-tuple-element.326.encoded, f32[1,768]{1,0:T(1,128)} %get-tuple-element.621.next_gain_ref.gain, bf16[408,768]{1,0:T(8,128)(2,1)} %get-tuple-element.388.context, ...), custom_call_target="tpu_custom_call" | custom-call | flops 50000000 | bytes 1 | tf_op jit(solution)/shard_map/turn_back/pallas_call | solution.py:737
  258.4 2.7 collective-permute-done.41
  263.1 3.0 collective-permute-start.44
  266.1 25.7 %feed_back.3 = (f32[816,768]{1,0:T(8,128)}, f32[1,768]{1,0:T(1,128)}, bf16[816,768]{1,0:T(8,128)(2,1)}, bf16[816,3072]{1,0:T(8,128)(2,1)}, bf16[2,2,768,768]{3,2,1,0:T(8,128)(2,1)}) custom-call(s32[9]{0:T(128)} %get-tuple-element.276.refs_0_.meta, f32[816,768]{1,0:T(8,128)} %get-tuple-element.408.e_ref, f32[816,768]{1,0:T(8,128)} %get-tuple-element.305.x_ref, ...), custom_call_target="tpu_custom_call" | custom-call | flops 240000000 | bytes 1 | tf_op jit(solution)/shard_map/feed_back/pallas_call | solution.py:643
  296.2 10.8 %feed_weights.3 = bf16[2,2,768,768]{3,2,1,0:T(8,128)(2,1)} custom-call(s32[3]{0:T(128)} %pad_add_fusion.meta.place, bf16[816,3072]{1,0:T(8,128)(2,1)} %get-tuple-element.425.eu_ref, bf16[816,3072]{1,0:T(8,128)(2,1)} %get-tuple-element.411.h_ref.refs_0_, bf16[816,768]{1,0:T(8,128)(2,1)} %get-tuple-element.410.b_ref.refs_1_, ...), custom_call_target="tpu_custom_call" | custom-call | flops 100000000 | bytes 1 | tf_op jit(solution)/shard_map/feed_weights/pallas_call | solution.py:691
  307.1 2.4 collective-permute-done.50
  309.6 3.5 add.219
  322.2 24.7 %mix_back.3 = (f32[816,768]{1,0:T(8,128)}, f32[1,768]{1,0:T(1,128)}, bf16[816,2304]{1,0:T(8,128)(2,1)}, bf16[816,768]{1,0:T(8,128)(2,1)}) custom-call(s32[9]{0:T(128)} %get-tuple-element.276.refs_0_.meta, f32[12]{0:T(128)} %fusion.11.refs_1_, f32[816,768]{1,0:T(8,128)} %get-tuple-element.438.refs_2_, bf16[816,768]{1,0:T(8,128)(2,1)} %bitcast.175, ...), custom_call_target="tpu_custom_call" | custom-call | flops 280000000 | bytes 1 | tf_op jit(solution)/shard_map/mix_back/pallas_call | solution.py:367
  351.1 2.1 collective-permute-start.58
  353.2 11.3 %mix_weights.3 = (bf16[2,4,208,768]{3,2,1,0:T(8,128)(2,1)}, bf16[2,4,208,768]{3,2,1,0:T(8,128)(2,1)}) custom-call(s32[3]{0:T(128)} %pad_add_fusion.meta.place, bf16[816,2304]{1,0:T(8,128)(2,1)} %get-tuple-element.459.dqkv_ref, f32[1,768]{1,0:T(1,128)} %get-tuple-element.460.refs_0_, f32[1,768]{1,0:T(1,128)} %get-tuple-element.461.refs_1_, ...), custom_call_target="tpu_custom_call" | custom-call | flops 105000000 | bytes 1 | tf_op jit(solution)/shard_map/mix_weights/pallas_call | solution.py:442
  364.5 3.4 collective-permute-done.58
  367.9 2.2 collective-permute-done.57
  377.2 6.1 %collective-permute-done.62 = bf16[1,2,1,1,96,768]{5,4,1,3,2,0:T(8,128)(2,1)S(1)} collective-permute-done((bf16[1,2,1,1,96,768]{5,4,1,3,2,0:T(8,128)(2,1)S(1)}, bf16[1,2,1,1,96,768]{5,4,1,3,2,0:T(8,128)(2,1)S(1)}, u32[]{:S(2)}, u32[]{:S(2)}) %collective-permute-start.62) | collective-permute-done | bytes 294944 | tf_op jit(solution)/shard_map/ppermute | solution.py:43
  385.0 13.0 %collective-permute-done.60 = bf16[1,1,2,2,96,768]{5,4,3,2,1,0:T(8,128)(2,1)S(1)} collective-permute-done((bf16[1,1,2,2,96,768]{5,4,3,2,1,0:T(8,128)(2,1)S(1)}, bf16[1,1,2,2,96,768]{5,4,3,2,1,0:T(8,128)(2,1)S(1)}, u32[]{:S(2)}, u32[]{:S(2)}) %collective-permute-start.60) | collective-permute-done | bytes 589856 | tf_op jit(solution)/shard_map/ppermute | solution.py:43
  403.6 4.5 collective-permute-done.66
  412.9 9.5 %collective-permute-done.67 = bf16[1,1,1,1,96,768]{5,4,3,2,1,0:T(8,128)(2,1)} collective-permute-done((bf16[1,1,1,1,96,768]{5,4,3,2,1,0:T(8,128)(2,1)}, bf16[1,1,1,1,96,768]{5,4,3,2,1,0:T(8,128)(2,1)}, u32[]{:S(2)}, u32[]{:S(2)}) %collective-permute-start.67) | collective-permute-done | bytes 147488 | tf_op jit(solution)/shard_map/ppermute | solution.py:43
  424.5 12.5 %collective-permute-done.72.refs_5_ = bf16[2,192,768]{2,1,0:T(8,128)(2,1)S(1)} collective-permute-done((bf16[2,192,768]{2,1,0:T(8,128)(2,1)S(1)}, bf16[2,192,768]{2,1,0:T(8,128)(2,1)S(1)}, u32[]{:S(2)}, u32[]{:S(2)}) %collective-permute-start.72) | collective-permute-done | bytes 589856 | tf_op jit(solution)/shard_map/ppermute | solution.py:43
  440.0 2.4 collective-permute-start.73
  443.3 10.9 %collective-permute-done.76.refs_3_ = bf16[2,2,96,768]{3,2,1,0:T(8,128)(2,1)} collective-permute-done((bf16[2,2,96,768]{3,2,1,0:T(8,128)(2,1)S(1)}, bf16[2,2,96,768]{3,2,1,0:T(8,128)(2,1)}, u32[]{:S(2)}, u32[]{:S(2)}) %collective-permute-start.76) | collective-permute-done | bytes 589856 | tf_op jit(solution)/shard_map/ppermute | solution.py:43
  464.4 2.0 collective-permute-start.82
  467.7 3.1 collective-permute-done.78
  473.5 10.0 %collective-permute-done.83.refs_9_ = bf16[2,2,96,768]{3,2,1,0:T(8,128)(2,1)} collective-permute-done((bf16[2,2,96,768]{3,2,1,0:T(8,128)(2,1)}, bf16[2,2,96,768]{3,2,1,0:T(8,128)(2,1)}, u32[]{:S(2)}, u32[]{:S(2)}) %collective-permute-start.83) | collective-permute-done | bytes 589856 | tf_op jit(solution)/shard_map/ppermute | solution.py:43
  484.4 7.0 %unpack_feed.1 = (f32[2,768,768]{2,1,0:T(8,128)}, f32[2,768,768]{2,1,0:T(8,128)}) custom-call(s32[3]{0:T(128)} %pad_add_fusion.meta.place, bf16[2,192,768]{2,1,0:T(8,128)(2,1)} %copy-done.6, bf16[2,96,768]{2,1,0:T(8,128)(2,1)} %copy-done.30, bf16[2,96,768]{2,1,0:T(8,128)(2,1)} %copy-done.31, bf16[2,2,96,768]{3,2,1,0:T(8,128)(2,1)} %collective-permute-done.76.refs_3_, ...), custom_call_target="tpu_custom_call" | custom-call | flops 50000000 | bytes 1 | tf_op jit(solution)/shard_map/unpack_feed/pallas_call | solution.py:796
  494.7 3.1 collective-permute-done.80
  500.1 2.0 maximum_convert_fusion
  (435 shorter events, 134.0 us)
Async XLA Ops:
  7.2 134.9 %all-gather.3.cloned.1.call-start = ((), (), s32[]{:S(2)}) async-start(), calls=%async_computation | async-start | bytes 11796480 | tf_op jit(solution)/shard_map/all_gather | solution.py:1023
  25.3 23.3 %collective-permute-start.6 = (bf16[2,768,768]{2,1,0:T(8,128)(2,1)S(1)}, bf16[2,768,768]{2,1,0:T(8,128)(2,1)}, u32[]{:S(2)}, u32[]{:S(2)}) collective-permute-start(bf16[2,768,768]{2,1,0:T(8,128)(2,1)S(1)} %pad_maximum_fusion.refs_0_), channel_id=1, source_target_pairs={{0,1},{1,0},{2,3},{3,2},{4,5},{5,4},{6,7},{7,6},{8,9},{9,8},{10,11... | collective-permute-start | bytes 7077896 | tf_op jit(solution)/shard_map/ppermute | solution.py:43
  26.7 22.0 %collective-permute-start.5 = (bf16[2,192,768]{2,1,0:T(8,128)(2,1)}, bf16[2,192,768]{2,1,0:T(8,128)(2,1)}, u32[]{:S(2)}, u32[]{:S(2)}) collective-permute-start(bf16[2,192,768]{2,1,0:T(8,128)(2,1)} %constant_dynamic-slice_fusion.6), channel_id=1, source_target_pairs={{0,2},{1,3},{2,0},{3,1},{4,6},{5,7},{6,4},{7,5},{8,10},{9,11},{10,... | collective-permute-start | bytes 1769480 | tf_op jit(solution)/shard_map/ppermute | solution.py:43
  27.4 21.2 %collective-permute-start.4 = (bf16[192,768]{1,0:T(8,128)(2,1)}, bf16[192,768]{1,0:T(8,128)(2,1)}, u32[]{:S(2)}, u32[]{:S(2)}) collective-permute-start(bf16[192,768]{1,0:T(8,128)(2,1)} %dynamic-slice_bitcast_fusion.14), channel_id=1, source_target_pairs={{0,2},{1,3},{2,0},{3,1},{4,6},{5,7},{6,4},{7,5},{8,10},{9,11},{10,... | collective-permute-start | bytes 884744 | tf_op jit(solution)/shard_map/ppermute | solution.py:43
  29.4 19.2 %collective-permute-start.2 = (bf16[192,768]{1,0:T(8,128)(2,1)}, bf16[192,768]{1,0:T(8,128)(2,1)}, u32[]{:S(2)}, u32[]{:S(2)}) collective-permute-start(bf16[192,768]{1,0:T(8,128)(2,1)} %collective-permute-done.refs_4_.refs_11_), channel_id=1, source_target_pairs={{0,4},{1,5},{2,6},{3,7},{4,0},{5,1},{6,2},{7,3},{8,12},{9,13},{10,... | collective-permute-start | bytes 884744 | tf_op jit(solution)/shard_map/ppermute | solution.py:43
  31.7 17.0 %collective-permute-start.3 = (bf16[192,768]{1,0:T(8,128)(2,1)}, bf16[192,768]{1,0:T(8,128)(2,1)S(1)}, u32[]{:S(2)}, u32[]{:S(2)}) collective-permute-start(bf16[192,768]{1,0:T(8,128)(2,1)} %collective-permute-done.refs_4_.refs_11_), channel_id=1, source_target_pairs={{0,8},{1,9},{2,10},{3,11},{4,12},{5,13},{6,14},{7,15},{8,0},{9,1},... | collective-permute-start | bytes 884744 | tf_op jit(solution)/shard_map/ppermute | solution.py:43
  52.1 19.8 %collective-permute-start.13 = (bf16[2,192,768]{2,1,0:T(8,128)(2,1)S(1)}, bf16[2,192,768]{2,1,0:T(8,128)(2,1)S(1)}, u32[]{:S(2)}, u32[]{:S(2)}) collective-permute-start(bf16[2,192,768]{2,1,0:T(8,128)(2,1)S(1)} %constant_dynamic-slice_fusion.5), channel_id=1, source_target_pairs={{0,2},{1,3},{2,0},{3,1},{4,6},{5,7},{6,4},{7,5},{8,10},{9,11},{10,... | collective-permute-start | bytes 1769480 | tf_op jit(solution)/shard_map/ppermute | solution.py:43
  52.4 19.5 %collective-permute-start.11 = (bf16[2,192,768]{2,1,0:T(8,128)(2,1)}, bf16[2,192,768]{2,1,0:T(8,128)(2,1)S(1)}, u32[]{:S(2)}, u32[]{:S(2)}) collective-permute-start(bf16[2,192,768]{2,1,0:T(8,128)(2,1)} %collective-permute-done.5.refs_2_), channel_id=1, source_target_pairs={{0,4},{1,5},{2,6},{3,7},{4,0},{5,1},{6,2},{7,3},{8,12},{9,13},{10,... | collective-permute-start | bytes 1769480 | tf_op jit(solution)/shard_map/ppermute | solution.py:43
  54.2 17.7 %collective-permute-start.12 = (bf16[2,192,768]{2,1,0:T(8,128)(2,1)}, bf16[2,192,768]{2,1,0:T(8,128)(2,1)S(1)}, u32[]{:S(2)}, u32[]{:S(2)}) collective-permute-start(bf16[2,192,768]{2,1,0:T(8,128)(2,1)} %collective-permute-done.5.refs_2_), channel_id=1, source_target_pairs={{0,8},{1,9},{2,10},{3,11},{4,12},{5,13},{6,14},{7,15},{8,0},{9,1},... | collective-permute-start | bytes 1769480 | tf_op jit(solution)/shard_map/ppermute | solution.py:43
  73.0 52.9 %collective-permute-start.23 = (bf16[4,192,768]{2,1,0:T(8,128)(2,1)S(1)}, bf16[4,192,768]{2,1,0:T(8,128)(2,1)}, u32[]{:S(2)}, u32[]{:S(2)}) collective-permute-start(bf16[4,192,768]{2,1,0:T(8,128)(2,1)S(1)} %pad_maximum_fusion.5.refs_5_.refs_7_), channel_id=1, source_target_pairs={{0,1},{1,0},{2,3},{3,2},{4,5},{5,4},{6,7},{7,6},{8,9},{9,8},{10,11... | collective-permute-start | bytes 3538952 | tf_op jit(solution)/shard_map/ppermute | solution.py:43
  74.3 18.4 %collective-permute-start.18 = (bf16[192,768]{1,0:T(8,128)(2,1)S(1)}, bf16[192,768]{1,0:T(8,128)(2,1)S(1)}, u32[]{:S(2)}, u32[]{:S(2)}) collective-permute-start(bf16[192,768]{1,0:T(8,128)(2,1)S(1)} %get-tuple-element.572), channel_id=1, source_target_pairs={{0,2},{1,3},{2,0},{3,1},{4,6},{5,7},{6,4},{7,5},{8,10},{9,11},{10,... | collective-permute-start | bytes 884744 | tf_op jit(solution)/shard_map/ppermute | solution.py:43
  92.7 30.8 %collective-permute-start.19 = (bf16[408,768]{1,0:T(8,128)(2,1)}, bf16[408,768]{1,0:T(8,128)(2,1)S(1)}, u32[]{:S(2)}, u32[]{:S(2)}) collective-permute-start(bf16[408,768]{1,0:T(8,128)(2,1)} %get-tuple-element.322), channel_id=1, source_target_pairs={{0,16},{1,17},{2,18},{3,19},{4,20},{5,21},{6,22},{7,23},{8,24},{9,... | collective-permute-start | bytes 1880072 | tf_op jit(solution)/shard_map/ppermute | solution.py:43
  95.0 17.2 %collective-permute-start.22 = (bf16[192,768]{1,0:T(8,128)(2,1)S(1)}, bf16[192,768]{1,0:T(8,128)(2,1)S(1)}, u32[]{:S(2)}, u32[]{:S(2)}) collective-permute-start(bf16[192,768]{1,0:T(8,128)(2,1)S(1)} %get-tuple-element.571), channel_id=1, source_target_pairs={{0,2},{1,3},{2,0},{3,1},{4,6},{5,7},{6,4},{7,5},{8,10},{9,11},{10,... | collective-permute-start | bytes 884744 | tf_op jit(solution)/shard_map/ppermute | solution.py:43
  96.2 16.0 %collective-permute-start.20 = (bf16[192,768]{1,0:T(8,128)(2,1)S(1)}, bf16[192,768]{1,0:T(8,128)(2,1)S(1)}, u32[]{:S(2)}, u32[]{:S(2)}) collective-permute-start(bf16[192,768]{1,0:T(8,128)(2,1)S(1)} %collective-permute-done.18.refs_7_.refs_9_), channel_id=1, source_target_pairs={{0,4},{1,5},{2,6},{3,7},{4,0},{5,1},{6,2},{7,3},{8,12},{9,13},{10,... | collective-permute-start | bytes 884744 | tf_op jit(solution)/shard_map/ppermute | solution.py:43
  96.8 18.5 %collective-permute-start.21 = (bf16[192,768]{1,0:T(8,128)(2,1)S(1)}, bf16[192,768]{1,0:T(8,128)(2,1)S(1)}, u32[]{:S(2)}, u32[]{:S(2)}) collective-permute-start(bf16[192,768]{1,0:T(8,128)(2,1)S(1)} %collective-permute-done.18.refs_7_.refs_9_), channel_id=1, source_target_pairs={{0,8},{1,9},{2,10},{3,11},{4,12},{5,13},{6,14},{7,15},{8,0},{9,1},... | collective-permute-start | bytes 884744 | tf_op jit(solution)/shard_map/ppermute | solution.py:43
  124.3 30.1 %collective-permute-start.28 = (bf16[3,136,768]{2,1,0:T(8,128)(2,1)}, bf16[3,136,768]{2,1,0:T(8,128)(2,1)}, u32[]{:S(2)}, u32[]{:S(2)}) collective-permute-start(bf16[3,136,768]{2,1,0:T(8,128)(2,1)} %slice.314), channel_id=1, source_target_pairs={{0,16},{1,17},{2,18},{3,19},{4,20},{5,21},{6,22},{7,23},{8,24},{9,... | collective-permute-start | bytes 1880072 | tf_op jit(solution)/shard_map/ppermute | solution.py:43
  155.6 21.1 %collective-permute-start.29 = (bf16[1,136,768]{2,1,0:T(8,128)(2,1)S(1)}, bf16[1,136,768]{2,1,0:T(8,128)(2,1)S(1)}, u32[]{:S(2)}, u32[]{:S(2)}) collective-permute-start(bf16[1,136,768]{2,1,0:T(8,128)(2,1)S(1)} %get-tuple-element.579), channel_id=1, source_target_pairs={{0,16},{1,17},{2,18},{3,19},{4,20},{5,21},{6,22},{7,23},{8,24},{9,... | collective-permute-start | bytes 626696 | tf_op jit(solution)/shard_map/ppermute | solution.py:43
  157.1 19.6 %collective-permute-start.30 = (bf16[1,136,768]{2,1,0:T(8,128)(2,1)S(1)}, bf16[1,136,768]{2,1,0:T(8,128)(2,1)S(1)}, u32[]{:S(2)}, u32[]{:S(2)}) collective-permute-start(bf16[1,136,768]{2,1,0:T(8,128)(2,1)S(1)} %get-tuple-element.578), channel_id=1, source_target_pairs={{0,16},{1,17},{2,18},{3,19},{4,20},{5,21},{6,22},{7,23},{8,24},{9,... | collective-permute-start | bytes 626696 | tf_op jit(solution)/shard_map/ppermute | solution.py:43
  198.7 19.4 %collective-permute-start.33 = (bf16[1,2,2,2,64,768]{5,4,3,2,1,0:T(8,128)(2,1)}, bf16[1,2,2,2,64,768]{5,4,3,2,1,0:T(8,128)(2,1)S(1)}, u32[]{:S(2)}, u32[]{:S(2)}) collective-permute-start(bf16[1,2,2,2,64,768]{5,4,3,2,1,0:T(8,128)(2,1)} %get-tuple-element.361), channel_id=1, source_target_pairs={{0,2},{1,3},{2,0},{3,1},{4,6},{5,7},{6,4},{7,5},{8,10},{9,11},{10,... | collective-permute-start | bytes 2359304 | tf_op jit(solution)/shard_map/ppermute | solution.py:43
  199.8 19.1 %collective-permute-start.34 = (bf16[2,2,2,1,64,768]{5,4,3,2,1,0:T(8,128)(2,1)}, bf16[2,2,2,1,64,768]{5,4,3,2,1,0:T(8,128)(2,1)S(1)}, u32[]{:S(2)}, u32[]{:S(2)}) collective-permute-start(bf16[2,2,2,1,64,768]{5,4,3,2,1,0:T(8,128)(2,1)} %get-tuple-element.363), channel_id=1, source_target_pairs={{0,4},{1,5},{2,6},{3,7},{4,0},{5,1},{6,2},{7,3},{8,12},{9,13},{10,... | collective-permute-start | bytes 2359304 | tf_op jit(solution)/shard_map/ppermute | solution.py:43
  200.2 18.8 %collective-permute-start.35 = (bf16[2,2,1,2,64,768]{5,4,3,2,1,0:T(8,128)(2,1)}, bf16[2,2,1,2,64,768]{5,4,3,2,1,0:T(8,128)(2,1)S(1)}, u32[]{:S(2)}, u32[]{:S(2)}) collective-permute-start(bf16[2,2,1,2,64,768]{5,4,3,2,1,0:T(8,128)(2,1)} %get-tuple-element.365), channel_id=1, source_target_pairs={{0,8},{1,9},{2,10},{3,11},{4,12},{5,13},{6,14},{7,15},{8,0},{9,1},... | collective-permute-start | bytes 2359304 | tf_op jit(solution)/shard_map/ppermute | solution.py:43
  219.0 29.0 %collective-permute-start.36 = (bf16[408,768]{1,0:T(8,128)(2,1)}, bf16[408,768]{1,0:T(8,128)(2,1)S(1)}, u32[]{:S(2)}, u32[]{:S(2)}) collective-permute-start(bf16[408,768]{1,0:T(8,128)(2,1)} %get-tuple-element.371), channel_id=1, source_target_pairs={{0,16},{1,17},{2,18},{3,19},{4,20},{5,21},{6,22},{7,23},{8,24},{9,... | collective-permute-start | bytes 1880072 | tf_op jit(solution)/shard_map/ppermute | solution.py:43
  228.5 17.2 %collective-permute-start.39 = (bf16[1,2,1,2,64,768]{5,4,3,2,1,0:T(8,128)(2,1)S(1)}, bf16[1,2,1,2,64,768]{5,4,3,2,1,0:T(8,128)(2,1)S(1)}, u32[]{:S(2)}, u32[]{:S(2)}) collective-permute-start(bf16[1,2,1,2,64,768]{5,4,3,2,1,0:T(8,128)(2,1)S(1)} %copy-done.70), channel_id=1, source_target_pairs={{0,2},{1,3},{2,0},{3,1},{4,6},{5,7},{6,4},{7,5},{8,10},{9,11},{10,... | collective-permute-start | bytes 1179656 | tf_op jit(solution)/shard_map/ppermute | solution.py:43
  262.0 29.9 %collective-permute-start.45 = (bf16[2,1,2,1,96,768]{5,4,3,2,1,0:T(8,128)(2,1)S(1)}, bf16[2,1,2,1,96,768]{5,4,3,2,1,0:T(8,128)(2,1)S(1)}, u32[]{:S(2)}, u32[]{:S(2)}) collective-permute-start(bf16[2,1,2,1,96,768]{5,4,3,2,1,0:T(8,128)(2,1)S(1)} %get-tuple-element.569), channel_id=1, source_target_pairs={{0,4},{1,5},{2,6},{3,7},{4,0},{5,1},{6,2},{7,3},{8,12},{9,13},{10,... | collective-permute-start | bytes 1769480 | tf_op jit(solution)/shard_map/ppermute | solution.py:43
  262.8 29.1 %collective-permute-start.46 = (bf16[2,1,1,2,96,768]{5,4,3,2,1,0:T(8,128)(2,1)S(1)}, bf16[2,1,1,2,96,768]{5,4,3,2,1,0:T(8,128)(2,1)S(1)}, u32[]{:S(2)}, u32[]{:S(2)}) collective-permute-start(bf16[2,1,1,2,96,768]{5,4,3,2,1,0:T(8,128)(2,1)S(1)} %get-tuple-element.567), channel_id=1, source_target_pairs={{0,8},{1,9},{2,10},{3,11},{4,12},{5,13},{6,14},{7,15},{8,0},{9,1},... | collective-permute-start | bytes 1769480 | tf_op jit(solution)/shard_map/ppermute | solution.py:43
  263.1 28.8 %collective-permute-start.44 = (bf16[2,192,768]{2,1,0:T(8,128)(2,1)S(1)}, bf16[2,192,768]{2,1,0:T(8,128)(2,1)S(1)}, u32[]{:S(2)}, u32[]{:S(2)}) collective-permute-start(bf16[2,192,768]{2,1,0:T(8,128)(2,1)S(1)} %pad_maximum_fusion.8), channel_id=1, source_target_pairs={{0,16},{1,17},{2,18},{3,19},{4,20},{5,21},{6,22},{7,23},{8,24},{9,... | collective-permute-start | bytes 1769480 | tf_op jit(solution)/shard_map/ppermute | solution.py:43
  291.9 17.6 %collective-permute-start.47 = (bf16[2,2,768,768]{3,2,1,0:T(8,128)(2,1)}, bf16[2,2,768,768]{3,2,1,0:T(8,128)(2,1)S(1)}, u32[]{:S(2)}, u32[]{:S(2)}) collective-permute-start(bf16[2,2,768,768]{3,2,1,0:T(8,128)(2,1)} %get-tuple-element.427), channel_id=1, source_target_pairs={{0,1},{1,0},{2,3},{3,2},{4,5},{5,4},{6,7},{7,6},{8,9},{9,8},{10,11... | collective-permute-start | bytes 14155784 | tf_op jit(solution)/shard_map/ppermute | solution.py:43
  292.4 17.1 %collective-permute-start.48 = (bf16[2,192,768]{2,1,0:T(8,128)(2,1)S(1)}, bf16[2,192,768]{2,1,0:T(8,128)(2,1)S(1)}, u32[]{:S(2)}, u32[]{:S(2)}) collective-permute-start(bf16[2,192,768]{2,1,0:T(8,128)(2,1)S(1)} %add.216), channel_id=1, source_target_pairs={{0,4},{1,5},{2,6},{3,7},{4,0},{5,1},{6,2},{7,3},{8,12},{9,13},{10,... | collective-permute-start | bytes 1769480 | tf_op jit(solution)/shard_map/ppermute | solution.py:43
  316.2 32.1 %collective-permute-start.51 = (bf16[1,2,2,2,96,768]{5,4,1,3,2,0:T(8,128)(2,1)}, bf16[1,2,2,2,96,768]{5,4,1,3,2,0:T(8,128)(2,1)S(1)}, u32[]{:S(2)}, u32[]{:S(2)}) collective-permute-start(bf16[1,2,2,2,96,768]{5,4,1,3,2,0:T(8,128)(2,1)} %get-tuple-element.547), channel_id=1, source_target_pairs={{0,2},{1,3},{2,0},{3,1},{4,6},{5,7},{6,4},{7,5},{8,10},{9,11},{10,... | collective-permute-start | bytes 3538952 | tf_op jit(solution)/shard_map/ppermute | solution.py:43
  317.9 30.4 %collective-permute-start.52 = (bf16[2,2,2,1,96,768]{5,4,1,3,2,0:T(8,128)(2,1)}, bf16[2,2,2,1,96,768]{5,4,1,3,2,0:T(8,128)(2,1)S(1)}, u32[]{:S(2)}, u32[]{:S(2)}) collective-permute-start(bf16[2,2,2,1,96,768]{5,4,1,3,2,0:T(8,128)(2,1)} %get-tuple-element.545), channel_id=1, source_target_pairs={{0,4},{1,5},{2,6},{3,7},{4,0},{5,1},{6,2},{7,3},{8,12},{9,13},{10,... | collective-permute-start | bytes 3538952 | tf_op jit(solution)/shard_map/ppermute | solution.py:43
  318.4 29.9 %collective-permute-start.55 = (bf16[2,2,192,768]{3,2,1,0:T(8,128)(2,1)S(1)}, bf16[2,2,192,768]{3,2,1,0:T(8,128)(2,1)}, u32[]{:S(2)}, u32[]{:S(2)}) collective-permute-start(bf16[2,2,192,768]{3,2,1,0:T(8,128)(2,1)S(1)} %pad_maximum_fusion.6), channel_id=1, source_target_pairs={{0,8},{1,9},{2,10},{3,11},{4,12},{5,13},{6,14},{7,15},{8,0},{9,1},... | collective-permute-start | bytes 3538952 | tf_op jit(solution)/shard_map/ppermute | solution.py:43
  318.7 29.5 %collective-permute-start.53 = (bf16[1,1,1,1,96,768]{5,4,3,2,1,0:T(8,128)(2,1)S(1)}, bf16[1,1,1,1,96,768]{5,4,3,2,1,0:T(8,128)(2,1)S(1)}, u32[]{:S(2)}, u32[]{:S(2)}) collective-permute-start(bf16[1,1,1,1,96,768]{5,4,3,2,1,0:T(8,128)(2,1)S(1)} %get-tuple-element.616), channel_id=1, source_target_pairs={{0,8},{1,9},{2,10},{3,11},{4,12},{5,13},{6,14},{7,15},{8,0},{9,1},... | collective-permute-start | bytes 442376 | tf_op jit(solution)/shard_map/ppermute | solution.py:43
  320.5 27.8 %collective-permute-start.54 = (bf16[1,1,1,1,96,768]{5,4,3,2,1,0:T(8,128)(2,1)S(1)}, bf16[1,1,1,1,96,768]{5,4,3,2,1,0:T(8,128)(2,1)S(1)}, u32[]{:S(2)}, u32[]{:S(2)}) collective-permute-start(bf16[1,1,1,1,96,768]{5,4,3,2,1,0:T(8,128)(2,1)S(1)} %get-tuple-element.614), channel_id=1, source_target_pairs={{0,4},{1,5},{2,6},{3,7},{4,0},{5,1},{6,2},{7,3},{8,12},{9,13},{10,... | collective-permute-start | bytes 442376 | tf_op jit(solution)/shard_map/ppermute | solution.py:43
  349.0 18.9 %collective-permute-start.56 = (bf16[1,2,2,1,96,768]{5,4,1,3,2,0:T(8,128)(2,1)S(1)}, bf16[1,2,2,1,96,768]{5,4,1,3,2,0:T(8,128)(2,1)S(1)}, u32[]{:S(2)}, u32[]{:S(2)}) collective-permute-start(bf16[1,2,2,1,96,768]{5,4,1,3,2,0:T(8,128)(2,1)S(1)} %get-tuple-element.565), channel_id=1, source_target_pairs={{0,4},{1,5},{2,6},{3,7},{4,0},{5,1},{6,2},{7,3},{8,12},{9,13},{10,... | collective-permute-start | bytes 1769480 | tf_op jit(solution)/shard_map/ppermute | solution.py:43
  350.7 19.4 %collective-permute-start.57 = (bf16[2,2,1,1,96,768]{5,4,1,3,2,0:T(8,128)(2,1)S(1)}, bf16[2,2,1,1,96,768]{5,4,1,3,2,0:T(8,128)(2,1)S(1)}, u32[]{:S(2)}, u32[]{:S(2)}) collective-permute-start(bf16[2,2,1,1,96,768]{5,4,1,3,2,0:T(8,128)(2,1)S(1)} %get-tuple-element.563), channel_id=1, source_target_pairs={{0,8},{1,9},{2,10},{3,11},{4,12},{5,13},{6,14},{7,15},{8,0},{9,1},... | collective-permute-start | bytes 1769480 | tf_op jit(solution)/shard_map/ppermute | solution.py:43
  351.1 16.8 %collective-permute-start.58 = (bf16[1,192,768]{2,1,0:T(8,128)(2,1)S(1)}, bf16[1,192,768]{2,1,0:T(8,128)(2,1)S(1)}, u32[]{:S(2)}, u32[]{:S(2)}) collective-permute-start(bf16[1,192,768]{2,1,0:T(8,128)(2,1)S(1)} %pad_maximum_fusion.17), channel_id=1, source_target_pairs={{0,16},{1,17},{2,18},{3,19},{4,20},{5,21},{6,22},{7,23},{8,24},{9,... | collective-permute-start | bytes 884744 | tf_op jit(solution)/shard_map/ppermute | solution.py:43
  375.9 22.0 %collective-permute-start.61 = (bf16[2,1,2,1,112,768]{5,4,3,2,1,0:T(8,128)(2,1)S(1)}, bf16[2,1,2,1,112,768]{5,4,3,2,1,0:T(8,128)(2,1)S(1)}, u32[]{:S(2)}, u32[]{:S(2)}) collective-permute-start(bf16[2,1,2,1,112,768]{5,4,3,2,1,0:T(8,128)(2,1)S(1)} %get-tuple-element.533), channel_id=1, source_target_pairs={{0,4},{1,5},{2,6},{3,7},{4,0},{5,1},{6,2},{7,3},{8,12},{9,13},{10,... | collective-permute-start | bytes 2064392 | tf_op jit(solution)/shard_map/ppermute | solution.py:43
  411.7 25.4 %collective-permute-start.72 = (bf16[2,192,768]{2,1,0:T(8,128)(2,1)S(1)}, bf16[2,192,768]{2,1,0:T(8,128)(2,1)S(1)}, u32[]{:S(2)}, u32[]{:S(2)}) collective-permute-start(bf16[2,192,768]{2,1,0:T(8,128)(2,1)S(1)} %pad_maximum_fusion.9.refs_0_), channel_id=1, source_target_pairs={{0,16},{1,17},{2,18},{3,19},{4,20},{5,21},{6,22},{7,23},{8,24},{9,... | collective-permute-start | bytes 1769480 | tf_op jit(solution)/shard_map/ppermute | solution.py:43
  422.5 20.0 %collective-permute-start.77 = (bf16[2,2,96,768]{3,2,1,0:T(8,128)(2,1)S(1)}, bf16[2,2,96,768]{3,2,1,0:T(8,128)(2,1)S(1)}, u32[]{:S(2)}, u32[]{:S(2)}) collective-permute-start(bf16[2,2,96,768]{3,2,1,0:T(8,128)(2,1)S(1)} %pad_maximum_fusion.11), channel_id=1, source_target_pairs={{0,4},{1,5},{2,6},{3,7},{4,0},{5,1},{6,2},{7,3},{8,12},{9,13},{10,... | collective-permute-start | bytes 1769480 | tf_op jit(solution)/shard_map/ppermute | solution.py:43
  424.5 29.8 %collective-permute-start.76 = (bf16[2,2,96,768]{3,2,1,0:T(8,128)(2,1)S(1)}, bf16[2,2,96,768]{3,2,1,0:T(8,128)(2,1)}, u32[]{:S(2)}, u32[]{:S(2)}) collective-permute-start(bf16[2,2,96,768]{3,2,1,0:T(8,128)(2,1)S(1)} %pad_maximum_fusion.10), channel_id=1, source_target_pairs={{0,8},{1,9},{2,10},{3,11},{4,12},{5,13},{6,14},{7,15},{8,0},{9,1},... | collective-permute-start | bytes 1769480 | tf_op jit(solution)/shard_map/ppermute | solution.py:43
  439.2 20.4 %collective-permute-start.74 = (bf16[2,96,768]{2,1,0:T(8,128)(2,1)S(1)}, bf16[2,96,768]{2,1,0:T(8,128)(2,1)S(1)}, u32[]{:S(2)}, u32[]{:S(2)}) collective-permute-start(bf16[2,96,768]{2,1,0:T(8,128)(2,1)S(1)} %get-tuple-element.589), channel_id=1, source_target_pairs={{0,4},{1,5},{2,6},{3,7},{4,0},{5,1},{6,2},{7,3},{8,12},{9,13},{10,... | collective-permute-start | bytes 884744 | tf_op jit(solution)/shard_map/ppermute | solution.py:43
  440.0 19.6 %collective-permute-start.75 = (bf16[2,96,768]{2,1,0:T(8,128)(2,1)S(1)}, bf16[2,96,768]{2,1,0:T(8,128)(2,1)S(1)}, u32[]{:S(2)}, u32[]{:S(2)}) collective-permute-start(bf16[2,96,768]{2,1,0:T(8,128)(2,1)S(1)} %get-tuple-element.588), channel_id=1, source_target_pairs={{0,8},{1,9},{2,10},{3,11},{4,12},{5,13},{6,14},{7,15},{8,0},{9,1},... | collective-permute-start | bytes 884744 | tf_op jit(solution)/shard_map/ppermute | solution.py:43
  440.0 19.6 %collective-permute-start.73 = (bf16[1,208,768]{2,1,0:T(8,128)(2,1)S(1)}, bf16[1,208,768]{2,1,0:T(8,128)(2,1)S(1)}, u32[]{:S(2)}, u32[]{:S(2)}) collective-permute-start(bf16[1,208,768]{2,1,0:T(8,128)(2,1)S(1)} %pad_maximum_fusion.16), channel_id=1, source_target_pairs={{0,16},{1,17},{2,18},{3,19},{4,20},{5,21},{6,22},{7,23},{8,24},{9,... | collective-permute-start | bytes 958472 | tf_op jit(solution)/shard_map/ppermute | solution.py:43
  461.8 21.8 %collective-permute-start.83 = (bf16[2,2,96,768]{3,2,1,0:T(8,128)(2,1)}, bf16[2,2,96,768]{3,2,1,0:T(8,128)(2,1)}, u32[]{:S(2)}, u32[]{:S(2)}) collective-permute-start(bf16[2,2,96,768]{3,2,1,0:T(8,128)(2,1)} %pad_maximum_fusion.15), channel_id=1, source_target_pairs={{0,4},{1,5},{2,6},{3,7},{4,0},{5,1},{6,2},{7,3},{8,12},{9,13},{10,... | collective-permute-start | bytes 1769480 | tf_op jit(solution)/shard_map/ppermute | solution.py:43
  464.4 19.2 %collective-permute-start.82 = (bf16[2,2,96,768]{3,2,1,0:T(8,128)(2,1)}, bf16[2,2,96,768]{3,2,1,0:T(8,128)(2,1)S(1)}, u32[]{:S(2)}, u32[]{:S(2)}) collective-permute-start(bf16[2,2,96,768]{3,2,1,0:T(8,128)(2,1)} %pad_maximum_fusion.14), channel_id=1, source_target_pairs={{0,8},{1,9},{2,10},{3,11},{4,12},{5,13},{6,14},{7,15},{8,0},{9,1},... | collective-permute-start | bytes 1769480 | tf_op jit(solution)/shard_map/ppermute | solution.py:43
  471.0 20.4 %collective-permute-start.84 = (bf16[2,1,96,768]{3,2,1,0:T(8,128)(2,1)S(1)}, bf16[2,1,96,768]{3,2,1,0:T(8,128)(2,1)S(1)}, u32[]{:S(2)}, u32[]{:S(2)}) collective-permute-start(bf16[2,1,96,768]{3,2,1,0:T(8,128)(2,1)S(1)} %pad_maximum_fusion.18), channel_id=1, source_target_pairs={{0,4},{1,5},{2,6},{3,7},{4,0},{5,1},{6,2},{7,3},{8,12},{9,13},{10,... | collective-permute-start | bytes 884744 | tf_op jit(solution)/shard_map/ppermute | solution.py:43
  473.0 18.5 %collective-permute-start.85 = (bf16[2,1,96,768]{3,2,1,0:T(8,128)(2,1)S(1)}, bf16[2,1,96,768]{3,2,1,0:T(8,128)(2,1)S(1)}, u32[]{:S(2)}, u32[]{:S(2)}) collective-permute-start(bf16[2,1,96,768]{3,2,1,0:T(8,128)(2,1)S(1)} %pad_maximum_fusion.19), channel_id=1, source_target_pairs={{0,8},{1,9},{2,10},{3,11},{4,12},{5,13},{6,14},{7,15},{8,0},{9,1},... | collective-permute-start | bytes 884744 | tf_op jit(solution)/shard_map/ppermute | solution.py:43
  473.1 24.7 %collective-permute-start.80 = (bf16[2,2,96,768]{3,2,1,0:T(8,128)(2,1)S(1)}, bf16[2,2,96,768]{3,2,1,0:T(8,128)(2,1)S(1)}, u32[]{:S(2)}, u32[]{:S(2)}) collective-permute-start(bf16[2,2,96,768]{3,2,1,0:T(8,128)(2,1)S(1)} %pad_maximum_fusion.12), channel_id=1, source_target_pairs={{0,4},{1,5},{2,6},{3,7},{4,0},{5,1},{6,2},{7,3},{8,12},{9,13},{10,... | collective-permute-start | bytes 1769480 | tf_op jit(solution)/shard_map/ppermute | solution.py:43
  (111 other events, 878.6 us)
Sparse Core Ops, SparseCore 0:
  52.1 80.4 all-gather.2

commit v4 on v3

--- a/solution.py
+++ b/solution.py
@@ -817,7 +817,7 @@
 
 
 AXES = {"x": (0, 0, ACROSS), "y": (3, 1, 0), "z": (2, 2, 0)}
-THIRDS = ("xyz", "yxz", "zxy")
+THIRDS = ("xyz", "yzx", "zxy")
 HALVES = ("xyz", "yzx")
 LAST = ("xyz", "yxz")
 CROSS = ("yxz", "zxy")

time: 513 us -> 512 us (level)
  transfers between devices with their start and end apart: 87 -> 87, of which waited for: 35 -> 32; matrix products, arithmetic and copies ran while one was open for 9% -> 9% of each run, Pallas kernels for 43% -> 43%
where the time goes in v4:
time: 512 us; the launch traced here: 508 us
  Pallas kernels  224 us (44%)
  waiting for transfers between devices  121 us (24%)
  starting transfers between devices  77.8 us (15%)
  other arithmetic  38 us (7%)
  local copies, waits for them, and re-layouts  30.6 us (6%)
  between operations  16 us (3%)
    ppermute x86, waiting for transfers between devices, swap(): return lax.ppermute(array, ('dp', 'head'), pairs)  121 us
    ppermute x86, starting transfers between devices, swap(): return lax.ppermute(array, ('dp', 'head'), pairs)  77.8 us
    pallas_call x2, Pallas kernels, feed_back(): pl.pallas_call(functools.partial(feed_back_kernel, len(pieces)), grid=(4,...  41.8 us
    pallas_call x3, Pallas kernels, mix_forward(): pl.pallas_call(functools.partial(mix_forward_kernel, local, cross, images...  41.8 us
    pallas_call x2, Pallas kernels, mix_back(): pl.pallas_call(functools.partial(mix_back_kernel, cross, images, len(qkv)...  41 us
    pallas_call x2, Pallas kernels, feed_rows(): pl.pallas_call(functools.partial(feed_rows_kernel, leaving), grid_spec=pl...  26.9 us
    pallas_call x2, Pallas kernels, mix_weights(): pl.pallas_call(functools.partial(mix_weights_kernel, more), grid_spec=plt...  19.1 us
    pallas_call x2, Pallas kernels, feed_weights(): pl.pallas_call(feed_weights_kernel, grid_spec=pltpu.PrefetchScalarGridSpe...  18.4 us
  transfers between devices with their start and end apart: 87, of which 32 were waited for; matrix products, arithmetic and copies ran while one was open for 9% of the time, Pallas kernels for 43%

profile of v4, /device:TPU:0, one launch (start us, length us, event | category | flops | bytes accessed | tf_op | source)
XLA Modules:
  0.0 507.6 jit_solution(16654288989412224101)
XLA Ops:
  9.8 2.9 collective-permute-start
  27.4 2.0 collective-permute-start.4
  33.8 13.5 %mix_forward.3 = (bf16[816,768]{1,0:T(8,128)(2,1)}, f32[816,768]{1,0:T(8,128)}, bf16[6,136,1152]{2,1,0:T(8,128)(2,1)}, bf16[816,384]{1,0:T(8,128)(2,1)}, f32[6,3,272]{2,1,0:T(4,128)}) custom-call(s32[9]{0:T(128)} %get-tuple-element.276.refs_0_.meta, f32[12]{0:T(128)} %fusion.11.refs_1_, bf16[816,768]{1,0:T(8,128)(2,1)} %bitcast.177, ...), custom_call_target="tpu_custom_call" | custom-call | flops 120000000 | bytes 1 | tf_op jit(solution)/shard_map/mix_forward/pallas_call | solution.py:259
  56.9 14.8 %mix_forward.4 = (f32[816,768]{1,0:T(8,128)}, bf16[6,136,1152]{2,1,0:T(8,128)(2,1)}, bf16[816,384]{1,0:T(8,128)(2,1)}, f32[6,3,272]{2,1,0:T(4,128)}) custom-call(s32[9]{0:T(128)} %get-tuple-element.276.refs_0_.meta, f32[12]{0:T(128)} %fusion.11.refs_1_, f32[816,768]{1,0:T(8,128)} %get-tuple-element.289.refs_2_, ...), custom_call_target="tpu_custom_call" | custom-call | flops 120000000 | bytes 1 | tf_op jit(solution)/shard_map/mix_forward/pallas_call | solution.py:259
  79.3 13.2 %feed_rows.2 = (f32[816,768]{1,0:T(8,128)}, bf16[816,768]{1,0:T(8,128)(2,1)}, bf16[816,3072]{1,0:T(8,128)(2,1)}, bf16[816,3072]{1,0:T(8,128)(2,1)}, bf16[408,768]{1,0:T(8,128)(2,1)}) custom-call(s32[3]{0:T(128)} %pad_add_fusion.meta.place, f32[816,768]{1,0:T(8,128)} %get-tuple-element.305.x_ref, f32[1,768]{1,0:T(1,128)} %get-tuple-element.623.gain_ref, ...), custom_call_target="tpu_custom_call" | custom-call | flops 116000000 | bytes 1 | tf_op jit(solution)/shard_map/feed_rows/pallas_call | solution.py:578
  92.5 2.4 collective-permute-start.19
  98.5 13.7 %feed_rows.3 = (f32[816,768]{1,0:T(8,128)}, bf16[816,768]{1,0:T(8,128)(2,1)}, bf16[816,3072]{1,0:T(8,128)(2,1)}, bf16[816,3072]{1,0:T(8,128)(2,1)}, bf16[408,768]{1,0:T(8,128)(2,1)}) custom-call(s32[3]{0:T(128)} %pad_add_fusion.meta.place, ...), custom_call_target="tpu_custom_call", output_to_operand_aliasing={{0}: (14, {}), {1}: (15, {}), {2}: (16, {}), {3}: (17, {})} | custom-call | flops 116000000 | bytes 1 | tf_op jit(solution)/shard_map/feed_rows/pallas_call | solution.py:578
  112.2 2.9 collective-permute-done.21.refs_9_.refs_11_
  115.1 8.1 %collective-permute-done.19 = bf16[408,768]{1,0:T(8,128)(2,1)S(1)} collective-permute-done((bf16[408,768]{1,0:T(8,128)(2,1)}, bf16[408,768]{1,0:T(8,128)(2,1)S(1)}, u32[]{:S(2)}, u32[]{:S(2)}) %collective-permute-start.19) | collective-permute-done | bytes 626720 | tf_op jit(solution)/shard_map/ppermute | solution.py:43
  129.0 13.5 %mix_forward.5 = (bf16[408,768]{1,0:T(8,128)(2,1)}, f32[408,768]{1,0:T(8,128)}, bf16[3,136,2304]{2,1,0:T(8,128)(2,1)}, bf16[408,768]{1,0:T(8,128)(2,1)}, f32[3,6,272]{2,1,0:T(8,128)}) custom-call(s32[9]{0:T(128)} %get-tuple-element.626.refs_0_, f32[12]{0:T(128)} %fusion.11.refs_1_, f32[408,768]{1,0:T(8,128)} %convert_select_fusion.refs_2_.refs_3_, ...), custom_call_target="tpu_custom_call" | custom-call | flops 120000000 | bytes 1 | tf_op jit(solution)/shard_map/mix_forward/pallas_call | solution.py:259
  142.5 11.5 %feed_forward.1 = (bf16[408,768]{1,0:T(8,128)(2,1)}, bf16[408,768]{1,0:T(8,128)(2,1)}, bf16[408,3072]{1,0:T(8,128)(2,1)}, bf16[408,3072]{1,0:T(8,128)(2,1)}) custom-call(s32[9]{0:T(128)} %get-tuple-element.276.refs_0_.meta, f32[408,768]{1,0:T(8,128)} %get-tuple-element.333.x_ref, f32[1,768]{1,0:T(1,128)} %get-tuple-element.620.norm_ref.gain_ref, ...), custom_call_target="tpu_custom_call" | custom-call | flops 116000000 | bytes 1 | tf_op jit(solution)/shard_map/feed_forward/pallas_call | solution.py:516
  155.4 2.1 collective-permute-start.29
  158.4 2.1 select_select_fusion
  160.4 16.0 %feed_back.2 = (f32[408,768]{1,0:T(8,128)}, f32[1,768]{1,0:T(1,128)}, bf16[408,768]{1,0:T(8,128)(2,1)}, bf16[408,3072]{1,0:T(8,128)(2,1)}, bf16[2,2,768,768]{3,2,1,0:T(8,128)(2,1)}) custom-call(s32[9]{0:T(128)} %get-tuple-element.276.refs_0_.meta, bf16[408,768]{1,0:T(8,128)(2,1)} %bitcast.182, f32[408,768]{1,0:T(8,128)} %get-tuple-element.333.x_ref, ...), custom_call_target="tpu_custom_call" | custom-call | flops 145000000 | bytes 1 | tf_op jit(solution)/shard_map/feed_back/pallas_call | solution.py:643
  177.8 7.6 %feed_weights.2 = bf16[2,2,768,768]{3,2,1,0:T(8,128)(2,1)} custom-call(s32[3]{0:T(128)} %pad_add_fusion.meta.place, bf16[408,3072]{1,0:T(8,128)(2,1)} %get-tuple-element.343.eu_ref, bf16[408,3072]{1,0:T(8,128)(2,1)} %get-tuple-element.339.h_ref.refs_0_, bf16[408,768]{1,0:T(8,128)(2,1)} %get-tuple-element.338.b_ref.refs_1_, ...), custom_call_target="tpu_custom_call" | custom-call | flops 70000000 | bytes 1 | tf_op jit(solution)/shard_map/feed_weights/pallas_call | solution.py:691
  185.5 4.6 collective-permute-done.32
  190.1 2.2 copy-done.18
  192.3 6.1 %glue.2 = (bf16[1,2,2,2,64,768]{5,4,3,2,1,0:T(8,128)(2,1)}, bf16[1,2,2,2,64,768]{5,4,3,2,1,0:T(8,128)(2,1)}, bf16[2,2,2,1,64,768]{5,4,3,2,1,0:T(8,128)(2,1)}, bf...) custom-call(bf16[2,2,2,2,192,768]{5,4,3,2,1,0:T(8,128)(2,1)} %bitcas, ...), custom_call_target="tpu_custom_call" | custom-call | flops 10000000 | bytes 1 | tf_op jit(solution)/shard_map/glue/pallas_call | solution.py:92
  200.1 15.9 %mix_back.2 = (f32[408,768]{1,0:T(8,128)}, f32[1,768]{1,0:T(1,128)}, bf16[408,2304]{1,0:T(8,128)(2,1)}, bf16[408,768]{1,0:T(8,128)(2,1)}, bf16[408,768]{1,0:T(8,128)(2,1)}, /*index=5*/bf16[408,768]{1,0:T(8,128)(2,1)}) custom-call(s32[9]{0:T(128)} %get-tuple-element.626.refs_0_, f32[12]{0:T(128)} %fusion.11.refs_1_, f32[408,768]{1,0:T(8,128)} %get-tuple-element.355.refs_2_, ...), custom_call_target="tpu_custom_call" | custom-call | flops 165000000 | bytes 1 | tf_op jit(solution)/shard_map/mix_back/pallas_call | solution.py:367
  220.0 3.8 glue.3
  230.1 7.8 %mix_weights.2 = (bf16[2,4,192,768]{3,2,1,0:T(8,128)(2,1)}, bf16[2,4,192,768]{3,2,1,0:T(8,128)(2,1)}) custom-call(s32[3]{0:T(128)} %pad_add_fusion.meta.place, bf16[408,2304]{1,0:T(8,128)(2,1)} %get-tuple-element.366.dqkv_ref, bf16[408,768]{1,0:T(8,128)(2,1)} %get-tuple-element.367.refs_0_, bf16[408,768]{1,0:T(8,128)(2,1)} %get-tuple-element.368.refs_1_, ...), custom_call_target="tpu_custom_call" | custom-call | flops 70000000 | bytes 1 | tf_op jit(solution)/shard_map/mix_weights/pallas_call | solution.py:442
  237.9 10.5 %collective-permute-done.38 = bf16[2,2,1,1,64,768]{5,4,1,3,2,0:T(8,128)(2,1)S(1)} collective-permute-done((bf16[2,2,1,1,64,768]{5,4,1,3,2,0:T(8,128)(2,1)}, bf16[2,2,1,1,64,768]{5,4,1,3,2,0:T(8,128)(2,1)S(1)}, u32[]{:S(2)}, u32[]{:S(2)}) %collective-permute-start.38) | collective-permute-done | bytes 393248 | tf_op jit(solution)/shard_map/ppermute | solution.py:43
  252.1 6.4 %turn_back.1 = (f32[816,768]{1,0:T(8,128)}, f32[1,768]{1,0:T(1,128)}) custom-call(s32[9]{0:T(128)} %get-tuple-element.276.refs_0_.meta, s32[1]{0:T(128)} %bitcast.2.side, f32[816,768]{1,0:T(8,128)} %get-tuple-element.326.encoded, f32[1,768]{1,0:T(1,128)} %get-tuple-element.621.next_gain_ref.gain, bf16[408,768]{1,0:T(8,128)(2,1)} %get-tuple-element.388.context, ...), custom_call_target="tpu_custom_call" | custom-call | flops 50000000 | bytes 1 | tf_op jit(solution)/shard_map/turn_back/pallas_call | solution.py:737
  263.4 25.8 %feed_back.3 = (f32[816,768]{1,0:T(8,128)}, f32[1,768]{1,0:T(1,128)}, bf16[816,768]{1,0:T(8,128)(2,1)}, bf16[816,3072]{1,0:T(8,128)(2,1)}, bf16[2,2,768,768]{3,2,1,0:T(8,128)(2,1)}) custom-call(s32[9]{0:T(128)} %get-tuple-element.276.refs_0_.meta, f32[816,768]{1,0:T(8,128)} %get-tuple-element.408.e_ref, f32[816,768]{1,0:T(8,128)} %get-tuple-element.305.x_ref, ...), custom_call_target="tpu_custom_call" | custom-call | flops 240000000 | bytes 1 | tf_op jit(solution)/shard_map/feed_back/pallas_call | solution.py:643
  294.4 10.8 %feed_weights.3 = bf16[2,2,768,768]{3,2,1,0:T(8,128)(2,1)} custom-call(s32[3]{0:T(128)} %pad_add_fusion.meta.place, bf16[816,3072]{1,0:T(8,128)(2,1)} %get-tuple-element.425.eu_ref, bf16[816,3072]{1,0:T(8,128)(2,1)} %get-tuple-element.411.h_ref.refs_0_, bf16[816,768]{1,0:T(8,128)(2,1)} %get-tuple-element.410.b_ref.refs_1_, ...), custom_call_target="tpu_custom_call" | custom-call | flops 100000000 | bytes 1 | tf_op jit(solution)/shard_map/feed_weights/pallas_call | solution.py:691
  305.2 2.5 collective-permute-done.50
  307.7 3.5 add.219
  316.8 2.1 collective-permute-start.53
  320.4 25.1 %mix_back.3 = (f32[816,768]{1,0:T(8,128)}, f32[1,768]{1,0:T(1,128)}, bf16[816,2304]{1,0:T(8,128)(2,1)}, bf16[816,768]{1,0:T(8,128)(2,1)}) custom-call(s32[9]{0:T(128)} %get-tuple-element.276.refs_0_.meta, f32[12]{0:T(128)} %fusion.11.refs_1_, f32[816,768]{1,0:T(8,128)} %get-tuple-element.438.refs_2_, bf16[816,768]{1,0:T(8,128)(2,1)} %bitcast.178, ...), custom_call_target="tpu_custom_call" | custom-call | flops 280000000 | bytes 1 | tf_op jit(solution)/shard_map/mix_back/pallas_call | solution.py:367
  350.2 11.3 %mix_weights.3 = (bf16[2,4,208,768]{3,2,1,0:T(8,128)(2,1)}, bf16[2,4,208,768]{3,2,1,0:T(8,128)(2,1)}) custom-call(s32[3]{0:T(128)} %pad_add_fusion.meta.place, bf16[816,2304]{1,0:T(8,128)(2,1)} %get-tuple-element.459.dqkv_ref, f32[1,768]{1,0:T(1,128)} %get-tuple-element.460.refs_0_, f32[1,768]{1,0:T(1,128)} %get-tuple-element.461.refs_1_, ...), custom_call_target="tpu_custom_call" | custom-call | flops 105000000 | bytes 1 | tf_op jit(solution)/shard_map/mix_weights/pallas_call | solution.py:442
  361.5 4.9 collective-permute-done.58
  366.5 1.9 collective-permute-done.57
  375.4 6.2 %collective-permute-done.62 = bf16[1,2,1,1,96,768]{5,4,1,3,2,0:T(8,128)(2,1)S(1)} collective-permute-done((bf16[1,2,1,1,96,768]{5,4,1,3,2,0:T(8,128)(2,1)S(1)}, bf16[1,2,1,1,96,768]{5,4,1,3,2,0:T(8,128)(2,1)S(1)}, u32[]{:S(2)}, u32[]{:S(2)}) %collective-permute-start.62) | collective-permute-done | bytes 294944 | tf_op jit(solution)/shard_map/ppermute | solution.py:43
  383.2 13.1 %collective-permute-done.60 = bf16[1,1,2,2,96,768]{5,4,3,2,1,0:T(8,128)(2,1)S(1)} collective-permute-done((bf16[1,1,2,2,96,768]{5,4,3,2,1,0:T(8,128)(2,1)S(1)}, bf16[1,1,2,2,96,768]{5,4,3,2,1,0:T(8,128)(2,1)S(1)}, u32[]{:S(2)}, u32[]{:S(2)}) %collective-permute-start.60) | collective-permute-done | bytes 589856 | tf_op jit(solution)/shard_map/ppermute | solution.py:43
  401.9 4.5 collective-permute-done.66
  411.3 9.1 %collective-permute-done.67 = bf16[1,1,1,1,96,768]{5,4,3,2,1,0:T(8,128)(2,1)} collective-permute-done((bf16[1,1,1,1,96,768]{5,4,3,2,1,0:T(8,128)(2,1)}, bf16[1,1,1,1,96,768]{5,4,3,2,1,0:T(8,128)(2,1)}, u32[]{:S(2)}, u32[]{:S(2)}) %collective-permute-start.67) | collective-permute-done | bytes 147488 | tf_op jit(solution)/shard_map/ppermute | solution.py:43
  420.6 2.1 collective-permute-start.77
  422.8 12.5 %collective-permute-done.72.refs_5_ = bf16[2,192,768]{2,1,0:T(8,128)(2,1)S(1)} collective-permute-done((bf16[2,192,768]{2,1,0:T(8,128)(2,1)S(1)}, bf16[2,192,768]{2,1,0:T(8,128)(2,1)S(1)}, u32[]{:S(2)}, u32[]{:S(2)}) %collective-permute-start.72) | collective-permute-done | bytes 589856 | tf_op jit(solution)/shard_map/ppermute | solution.py:43
  438.3 2.6 collective-permute-start.73
  441.8 10.7 %collective-permute-done.76.refs_3_ = bf16[2,2,96,768]{3,2,1,0:T(8,128)(2,1)} collective-permute-done((bf16[2,2,96,768]{3,2,1,0:T(8,128)(2,1)S(1)}, bf16[2,2,96,768]{3,2,1,0:T(8,128)(2,1)}, u32[]{:S(2)}, u32[]{:S(2)}) %collective-permute-start.76) | collective-permute-done | bytes 589856 | tf_op jit(solution)/shard_map/ppermute | solution.py:43
  459.8 2.0 collective-permute-start.83
  462.7 2.0 collective-permute-start.82
  465.9 3.1 collective-permute-done.78
  469.1 2.1 collective-permute-start.84
  471.6 10.2 %collective-permute-done.83.refs_9_ = bf16[2,2,96,768]{3,2,1,0:T(8,128)(2,1)} collective-permute-done((bf16[2,2,96,768]{3,2,1,0:T(8,128)(2,1)}, bf16[2,2,96,768]{3,2,1,0:T(8,128)(2,1)}, u32[]{:S(2)}, u32[]{:S(2)}) %collective-permute-start.83) | collective-permute-done | bytes 589856 | tf_op jit(solution)/shard_map/ppermute | solution.py:43
  482.6 7.0 %unpack_feed.1 = (f32[2,768,768]{2,1,0:T(8,128)}, f32[2,768,768]{2,1,0:T(8,128)}) custom-call(s32[3]{0:T(128)} %pad_add_fusion.meta.place, bf16[2,192,768]{2,1,0:T(8,128)(2,1)} %copy-done.6, bf16[2,96,768]{2,1,0:T(8,128)(2,1)} %copy-done.30, bf16[2,96,768]{2,1,0:T(8,128)(2,1)} %copy-done.31, bf16[2,2,96,768]{3,2,1,0:T(8,128)(2,1)} %collective-permute-done.76.refs_3_, ...), custom_call_target="tpu_custom_call" | custom-call | flops 50000000 | bytes 1 | tf_op jit(solution)/shard_map/unpack_feed/pallas_call | solution.py:796
  492.9 3.2 collective-permute-done.80
  498.4 2.0 maximum_convert_fusion
  (426 shorter events, 127.7 us)
Async XLA Ops:
  7.2 135.3 %all-gather.3.cloned.1.call-start = ((), (), s32[]{:S(2)}) async-start(), calls=%async_computation | async-start | bytes 11796480 | tf_op jit(solution)/shard_map/all_gather | solution.py:1023
  25.3 23.3 %collective-permute-start.6 = (bf16[2,768,768]{2,1,0:T(8,128)(2,1)S(1)}, bf16[2,768,768]{2,1,0:T(8,128)(2,1)}, u32[]{:S(2)}, u32[]{:S(2)}) collective-permute-start(bf16[2,768,768]{2,1,0:T(8,128)(2,1)S(1)} %pad_maximum_fusion.refs_0_), channel_id=1, source_target_pairs={{0,1},{1,0},{2,3},{3,2},{4,5},{5,4},{6,7},{7,6},{8,9},{9,8},{10,11... | collective-permute-start | bytes 7077896 | tf_op jit(solution)/shard_map/ppermute | solution.py:43
  26.6 22.0 %collective-permute-start.5 = (bf16[2,192,768]{2,1,0:T(8,128)(2,1)}, bf16[2,192,768]{2,1,0:T(8,128)(2,1)}, u32[]{:S(2)}, u32[]{:S(2)}) collective-permute-start(bf16[2,192,768]{2,1,0:T(8,128)(2,1)} %constant_dynamic-slice_fusion.6), channel_id=1, source_target_pairs={{0,2},{1,3},{2,0},{3,1},{4,6},{5,7},{6,4},{7,5},{8,10},{9,11},{10,... | collective-permute-start | bytes 1769480 | tf_op jit(solution)/shard_map/ppermute | solution.py:43
  27.4 21.2 %collective-permute-start.4 = (bf16[192,768]{1,0:T(8,128)(2,1)}, bf16[192,768]{1,0:T(8,128)(2,1)}, u32[]{:S(2)}, u32[]{:S(2)}) collective-permute-start(bf16[192,768]{1,0:T(8,128)(2,1)} %dynamic-slice_bitcast_fusion.14), channel_id=1, source_target_pairs={{0,2},{1,3},{2,0},{3,1},{4,6},{5,7},{6,4},{7,5},{8,10},{9,11},{10,... | collective-permute-start | bytes 884744 | tf_op jit(solution)/shard_map/ppermute | solution.py:43
  29.4 19.2 %collective-permute-start.2 = (bf16[192,768]{1,0:T(8,128)(2,1)}, bf16[192,768]{1,0:T(8,128)(2,1)}, u32[]{:S(2)}, u32[]{:S(2)}) collective-permute-start(bf16[192,768]{1,0:T(8,128)(2,1)} %collective-permute-done.refs_4_.refs_11_), channel_id=1, source_target_pairs={{0,4},{1,5},{2,6},{3,7},{4,0},{5,1},{6,2},{7,3},{8,12},{9,13},{10,... | collective-permute-start | bytes 884744 | tf_op jit(solution)/shard_map/ppermute | solution.py:43
  31.6 17.0 %collective-permute-start.3 = (bf16[192,768]{1,0:T(8,128)(2,1)}, bf16[192,768]{1,0:T(8,128)(2,1)S(1)}, u32[]{:S(2)}, u32[]{:S(2)}) collective-permute-start(bf16[192,768]{1,0:T(8,128)(2,1)} %collective-permute-done.refs_4_.refs_11_), channel_id=1, source_target_pairs={{0,8},{1,9},{2,10},{3,11},{4,12},{5,13},{6,14},{7,15},{8,0},{9,1},... | collective-permute-start | bytes 884744 | tf_op jit(solution)/shard_map/ppermute | solution.py:43
  52.0 19.7 %collective-permute-start.13 = (bf16[2,192,768]{2,1,0:T(8,128)(2,1)S(1)}, bf16[2,192,768]{2,1,0:T(8,128)(2,1)S(1)}, u32[]{:S(2)}, u32[]{:S(2)}) collective-permute-start(bf16[2,192,768]{2,1,0:T(8,128)(2,1)S(1)} %constant_dynamic-slice_fusion.5), channel_id=1, source_target_pairs={{0,2},{1,3},{2,0},{3,1},{4,6},{5,7},{6,4},{7,5},{8,10},{9,11},{10,... | collective-permute-start | bytes 1769480 | tf_op jit(solution)/shard_map/ppermute | solution.py:43
  52.4 19.3 %collective-permute-start.11 = (bf16[2,192,768]{2,1,0:T(8,128)(2,1)}, bf16[2,192,768]{2,1,0:T(8,128)(2,1)S(1)}, u32[]{:S(2)}, u32[]{:S(2)}) collective-permute-start(bf16[2,192,768]{2,1,0:T(8,128)(2,1)} %collective-permute-done.5.refs_2_), channel_id=1, source_target_pairs={{0,4},{1,5},{2,6},{3,7},{4,0},{5,1},{6,2},{7,3},{8,12},{9,13},{10,... | collective-permute-start | bytes 1769480 | tf_op jit(solution)/shard_map/ppermute | solution.py:43
  54.2 17.6 %collective-permute-start.12 = (bf16[2,192,768]{2,1,0:T(8,128)(2,1)}, bf16[2,192,768]{2,1,0:T(8,128)(2,1)S(1)}, u32[]{:S(2)}, u32[]{:S(2)}) collective-permute-start(bf16[2,192,768]{2,1,0:T(8,128)(2,1)} %collective-permute-done.5.refs_2_), channel_id=1, source_target_pairs={{0,8},{1,9},{2,10},{3,11},{4,12},{5,13},{6,14},{7,15},{8,0},{9,1},... | collective-permute-start | bytes 1769480 | tf_op jit(solution)/shard_map/ppermute | solution.py:43
  72.8 53.3 %collective-permute-start.23 = (bf16[4,192,768]{2,1,0:T(8,128)(2,1)S(1)}, bf16[4,192,768]{2,1,0:T(8,128)(2,1)}, u32[]{:S(2)}, u32[]{:S(2)}) collective-permute-start(bf16[4,192,768]{2,1,0:T(8,128)(2,1)S(1)} %pad_maximum_fusion.5.refs_5_.refs_7_), channel_id=1, source_target_pairs={{0,1},{1,0},{2,3},{3,2},{4,5},{5,4},{6,7},{7,6},{8,9},{9,8},{10,11... | collective-permute-start | bytes 3538952 | tf_op jit(solution)/shard_map/ppermute | solution.py:43
  74.1 18.4 %collective-permute-start.18 = (bf16[192,768]{1,0:T(8,128)(2,1)S(1)}, bf16[192,768]{1,0:T(8,128)(2,1)S(1)}, u32[]{:S(2)}, u32[]{:S(2)}) collective-permute-start(bf16[192,768]{1,0:T(8,128)(2,1)S(1)} %get-tuple-element.572), channel_id=1, source_target_pairs={{0,2},{1,3},{2,0},{3,1},{4,6},{5,7},{6,4},{7,5},{8,10},{9,11},{10,... | collective-permute-start | bytes 884744 | tf_op jit(solution)/shard_map/ppermute | solution.py:43
  92.5 30.8 %collective-permute-start.19 = (bf16[408,768]{1,0:T(8,128)(2,1)}, bf16[408,768]{1,0:T(8,128)(2,1)S(1)}, u32[]{:S(2)}, u32[]{:S(2)}) collective-permute-start(bf16[408,768]{1,0:T(8,128)(2,1)} %get-tuple-element.322), channel_id=1, source_target_pairs={{0,16},{1,17},{2,18},{3,19},{4,20},{5,21},{6,22},{7,23},{8,24},{9,... | collective-permute-start | bytes 1880072 | tf_op jit(solution)/shard_map/ppermute | solution.py:43
  94.9 17.3 %collective-permute-start.22 = (bf16[192,768]{1,0:T(8,128)(2,1)S(1)}, bf16[192,768]{1,0:T(8,128)(2,1)S(1)}, u32[]{:S(2)}, u32[]{:S(2)}) collective-permute-start(bf16[192,768]{1,0:T(8,128)(2,1)S(1)} %get-tuple-element.571), channel_id=1, source_target_pairs={{0,2},{1,3},{2,0},{3,1},{4,6},{5,7},{6,4},{7,5},{8,10},{9,11},{10,... | collective-permute-start | bytes 884744 | tf_op jit(solution)/shard_map/ppermute | solution.py:43
  96.8 18.4 %collective-permute-start.21 = (bf16[192,768]{1,0:T(8,128)(2,1)S(1)}, bf16[192,768]{1,0:T(8,128)(2,1)S(1)}, u32[]{:S(2)}, u32[]{:S(2)}) collective-permute-start(bf16[192,768]{1,0:T(8,128)(2,1)S(1)} %collective-permute-done.18.refs_7_.refs_9_), channel_id=1, source_target_pairs={{0,8},{1,9},{2,10},{3,11},{4,12},{5,13},{6,14},{7,15},{8,0},{9,1},... | collective-permute-start | bytes 884744 | tf_op jit(solution)/shard_map/ppermute | solution.py:43
  124.1 30.0 %collective-permute-start.28 = (bf16[3,136,768]{2,1,0:T(8,128)(2,1)}, bf16[3,136,768]{2,1,0:T(8,128)(2,1)}, u32[]{:S(2)}, u32[]{:S(2)}) collective-permute-start(bf16[3,136,768]{2,1,0:T(8,128)(2,1)} %slice.314), channel_id=1, source_target_pairs={{0,16},{1,17},{2,18},{3,19},{4,20},{5,21},{6,22},{7,23},{8,24},{9,... | collective-permute-start | bytes 1880072 | tf_op jit(solution)/shard_map/ppermute | solution.py:43
  155.4 21.1 %collective-permute-start.29 = (bf16[1,136,768]{2,1,0:T(8,128)(2,1)S(1)}, bf16[1,136,768]{2,1,0:T(8,128)(2,1)S(1)}, u32[]{:S(2)}, u32[]{:S(2)}) collective-permute-start(bf16[1,136,768]{2,1,0:T(8,128)(2,1)S(1)} %get-tuple-element.579), channel_id=1, source_target_pairs={{0,16},{1,17},{2,18},{3,19},{4,20},{5,21},{6,22},{7,23},{8,24},{9,... | collective-permute-start | bytes 626696 | tf_op jit(solution)/shard_map/ppermute | solution.py:43
  157.4 19.7 %collective-permute-start.30 = (bf16[1,136,768]{2,1,0:T(8,128)(2,1)S(1)}, bf16[1,136,768]{2,1,0:T(8,128)(2,1)S(1)}, u32[]{:S(2)}, u32[]{:S(2)}) collective-permute-start(bf16[1,136,768]{2,1,0:T(8,128)(2,1)S(1)} %get-tuple-element.578), channel_id=1, source_target_pairs={{0,16},{1,17},{2,18},{3,19},{4,20},{5,21},{6,22},{7,23},{8,24},{9,... | collective-permute-start | bytes 626696 | tf_op jit(solution)/shard_map/ppermute | solution.py:43
  198.4 19.4 %collective-permute-start.33 = (bf16[1,2,2,2,64,768]{5,4,3,2,1,0:T(8,128)(2,1)}, bf16[1,2,2,2,64,768]{5,4,3,2,1,0:T(8,128)(2,1)S(1)}, u32[]{:S(2)}, u32[]{:S(2)}) collective-permute-start(bf16[1,2,2,2,64,768]{5,4,3,2,1,0:T(8,128)(2,1)} %get-tuple-element.361), channel_id=1, source_target_pairs={{0,2},{1,3},{2,0},{3,1},{4,6},{5,7},{6,4},{7,5},{8,10},{9,11},{10,... | collective-permute-start | bytes 2359304 | tf_op jit(solution)/shard_map/ppermute | solution.py:43
  199.2 19.1 %collective-permute-start.34 = (bf16[2,2,2,1,64,768]{5,4,3,2,1,0:T(8,128)(2,1)}, bf16[2,2,2,1,64,768]{5,4,3,2,1,0:T(8,128)(2,1)S(1)}, u32[]{:S(2)}, u32[]{:S(2)}) collective-permute-start(bf16[2,2,2,1,64,768]{5,4,3,2,1,0:T(8,128)(2,1)} %get-tuple-element.363), channel_id=1, source_target_pairs={{0,4},{1,5},{2,6},{3,7},{4,0},{5,1},{6,2},{7,3},{8,12},{9,13},{10,... | collective-permute-start | bytes 2359304 | tf_op jit(solution)/shard_map/ppermute | solution.py:43
  200.1 18.8 %collective-permute-start.35 = (bf16[2,2,1,2,64,768]{5,4,3,2,1,0:T(8,128)(2,1)}, bf16[2,2,1,2,64,768]{5,4,3,2,1,0:T(8,128)(2,1)S(1)}, u32[]{:S(2)}, u32[]{:S(2)}) collective-permute-start(bf16[2,2,1,2,64,768]{5,4,3,2,1,0:T(8,128)(2,1)} %get-tuple-element.365), channel_id=1, source_target_pairs={{0,8},{1,9},{2,10},{3,11},{4,12},{5,13},{6,14},{7,15},{8,0},{9,1},... | collective-permute-start | bytes 2359304 | tf_op jit(solution)/shard_map/ppermute | solution.py:43
  219.0 29.4 %collective-permute-start.36 = (bf16[408,768]{1,0:T(8,128)(2,1)}, bf16[408,768]{1,0:T(8,128)(2,1)S(1)}, u32[]{:S(2)}, u32[]{:S(2)}) collective-permute-start(bf16[408,768]{1,0:T(8,128)(2,1)} %get-tuple-element.371), channel_id=1, source_target_pairs={{0,16},{1,17},{2,18},{3,19},{4,20},{5,21},{6,22},{7,23},{8,24},{9,... | collective-permute-start | bytes 1880072 | tf_op jit(solution)/shard_map/ppermute | solution.py:43
  225.8 22.6 %collective-permute-start.38 = (bf16[2,2,1,1,64,768]{5,4,1,3,2,0:T(8,128)(2,1)}, bf16[2,2,1,1,64,768]{5,4,1,3,2,0:T(8,128)(2,1)S(1)}, u32[]{:S(2)}, u32[]{:S(2)}) collective-permute-start(bf16[2,2,1,1,64,768]{5,4,1,3,2,0:T(8,128)(2,1)} %bitcast.199), channel_id=1, source_target_pairs={{0,8},{1,9},{2,10},{3,11},{4,12},{5,13},{6,14},{7,15},{8,0},{9,1},... | collective-permute-start | bytes 1179656 | tf_op jit(solution)/shard_map/ppermute | solution.py:43
  227.5 20.9 %collective-permute-start.39 = (bf16[1,2,1,2,64,768]{5,4,3,2,1,0:T(8,128)(2,1)}, bf16[1,2,1,2,64,768]{5,4,3,2,1,0:T(8,128)(2,1)S(1)}, u32[]{:S(2)}, u32[]{:S(2)}) collective-permute-start(bf16[1,2,1,2,64,768]{5,4,3,2,1,0:T(8,128)(2,1)} %get-tuple-element.383), channel_id=1, source_target_pairs={{0,2},{1,3},{2,0},{3,1},{4,6},{5,7},{6,4},{7,5},{8,10},{9,11},{10,... | collective-permute-start | bytes 1179656 | tf_op jit(solution)/shard_map/ppermute | solution.py:43
  259.8 29.4 %collective-permute-start.45 = (bf16[2,1,2,1,96,768]{5,4,3,2,1,0:T(8,128)(2,1)S(1)}, bf16[2,1,2,1,96,768]{5,4,3,2,1,0:T(8,128)(2,1)S(1)}, u32[]{:S(2)}, u32[]{:S(2)}) collective-permute-start(bf16[2,1,2,1,96,768]{5,4,3,2,1,0:T(8,128)(2,1)S(1)} %get-tuple-element.569), channel_id=1, source_target_pairs={{0,4},{1,5},{2,6},{3,7},{4,0},{5,1},{6,2},{7,3},{8,12},{9,13},{10,... | collective-permute-start | bytes 1769480 | tf_op jit(solution)/shard_map/ppermute | solution.py:43
  260.4 28.8 %collective-permute-start.46 = (bf16[2,1,1,2,96,768]{5,4,3,2,1,0:T(8,128)(2,1)S(1)}, bf16[2,1,1,2,96,768]{5,4,3,2,1,0:T(8,128)(2,1)S(1)}, u32[]{:S(2)}, u32[]{:S(2)}) collective-permute-start(bf16[2,1,1,2,96,768]{5,4,3,2,1,0:T(8,128)(2,1)S(1)} %get-tuple-element.567), channel_id=1, source_target_pairs={{0,8},{1,9},{2,10},{3,11},{4,12},{5,13},{6,14},{7,15},{8,0},{9,1},... | collective-permute-start | bytes 1769480 | tf_op jit(solution)/shard_map/ppermute | solution.py:43
  262.2 27.9 %collective-permute-start.44 = (bf16[2,192,768]{2,1,0:T(8,128)(2,1)S(1)}, bf16[2,192,768]{2,1,0:T(8,128)(2,1)S(1)}, u32[]{:S(2)}, u32[]{:S(2)}) collective-permute-start(bf16[2,192,768]{2,1,0:T(8,128)(2,1)S(1)} %pad_maximum_fusion.8), channel_id=1, source_target_pairs={{0,16},{1,17},{2,18},{3,19},{4,20},{5,21},{6,22},{7,23},{8,24},{9,... | collective-permute-start | bytes 1769480 | tf_op jit(solution)/shard_map/ppermute | solution.py:43
  290.1 17.6 %collective-permute-start.47 = (bf16[2,2,768,768]{3,2,1,0:T(8,128)(2,1)}, bf16[2,2,768,768]{3,2,1,0:T(8,128)(2,1)S(1)}, u32[]{:S(2)}, u32[]{:S(2)}) collective-permute-start(bf16[2,2,768,768]{3,2,1,0:T(8,128)(2,1)} %get-tuple-element.427), channel_id=1, source_target_pairs={{0,1},{1,0},{2,3},{3,2},{4,5},{5,4},{6,7},{7,6},{8,9},{9,8},{10,11... | collective-permute-start | bytes 14155784 | tf_op jit(solution)/shard_map/ppermute | solution.py:43
  290.5 17.2 %collective-permute-start.48 = (bf16[2,192,768]{2,1,0:T(8,128)(2,1)S(1)}, bf16[2,192,768]{2,1,0:T(8,128)(2,1)S(1)}, u32[]{:S(2)}, u32[]{:S(2)}) collective-permute-start(bf16[2,192,768]{2,1,0:T(8,128)(2,1)S(1)} %add.216), channel_id=1, source_target_pairs={{0,4},{1,5},{2,6},{3,7},{4,0},{5,1},{6,2},{7,3},{8,12},{9,13},{10,... | collective-permute-start | bytes 1769480 | tf_op jit(solution)/shard_map/ppermute | solution.py:43
  314.3 32.4 %collective-permute-start.51 = (bf16[1,2,2,2,96,768]{5,4,1,3,2,0:T(8,128)(2,1)}, bf16[1,2,2,2,96,768]{5,4,1,3,2,0:T(8,128)(2,1)S(1)}, u32[]{:S(2)}, u32[]{:S(2)}) collective-permute-start(bf16[1,2,2,2,96,768]{5,4,1,3,2,0:T(8,128)(2,1)} %get-tuple-element.547), channel_id=1, source_target_pairs={{0,2},{1,3},{2,0},{3,1},{4,6},{5,7},{6,4},{7,5},{8,10},{9,11},{10,... | collective-permute-start | bytes 3538952 | tf_op jit(solution)/shard_map/ppermute | solution.py:43
  316.2 30.5 %collective-permute-start.52 = (bf16[2,2,2,1,96,768]{5,4,1,3,2,0:T(8,128)(2,1)}, bf16[2,2,2,1,96,768]{5,4,1,3,2,0:T(8,128)(2,1)S(1)}, u32[]{:S(2)}, u32[]{:S(2)}) collective-permute-start(bf16[2,2,2,1,96,768]{5,4,1,3,2,0:T(8,128)(2,1)} %get-tuple-element.545), channel_id=1, source_target_pairs={{0,4},{1,5},{2,6},{3,7},{4,0},{5,1},{6,2},{7,3},{8,12},{9,13},{10,... | collective-permute-start | bytes 3538952 | tf_op jit(solution)/shard_map/ppermute | solution.py:43
  316.8 29.9 %collective-permute-start.55 = (bf16[2,2,192,768]{3,2,1,0:T(8,128)(2,1)S(1)}, bf16[2,2,192,768]{3,2,1,0:T(8,128)(2,1)}, u32[]{:S(2)}, u32[]{:S(2)}) collective-permute-start(bf16[2,2,192,768]{3,2,1,0:T(8,128)(2,1)S(1)} %pad_maximum_fusion.6), channel_id=1, source_target_pairs={{0,8},{1,9},{2,10},{3,11},{4,12},{5,13},{6,14},{7,15},{8,0},{9,1},... | collective-permute-start | bytes 3538952 | tf_op jit(solution)/shard_map/ppermute | solution.py:43
  316.8 29.9 %collective-permute-start.53 = (bf16[1,1,1,1,96,768]{5,4,3,2,1,0:T(8,128)(2,1)S(1)}, bf16[1,1,1,1,96,768]{5,4,3,2,1,0:T(8,128)(2,1)S(1)}, u32[]{:S(2)}, u32[]{:S(2)}) collective-permute-start(bf16[1,1,1,1,96,768]{5,4,3,2,1,0:T(8,128)(2,1)S(1)} %get-tuple-element.616), channel_id=1, source_target_pairs={{0,8},{1,9},{2,10},{3,11},{4,12},{5,13},{6,14},{7,15},{8,0},{9,1},... | collective-permute-start | bytes 442376 | tf_op jit(solution)/shard_map/ppermute | solution.py:43
  318.9 27.7 %collective-permute-start.54 = (bf16[1,1,1,1,96,768]{5,4,3,2,1,0:T(8,128)(2,1)S(1)}, bf16[1,1,1,1,96,768]{5,4,3,2,1,0:T(8,128)(2,1)S(1)}, u32[]{:S(2)}, u32[]{:S(2)}) collective-permute-start(bf16[1,1,1,1,96,768]{5,4,3,2,1,0:T(8,128)(2,1)S(1)} %get-tuple-element.614), channel_id=1, source_target_pairs={{0,4},{1,5},{2,6},{3,7},{4,0},{5,1},{6,2},{7,3},{8,12},{9,13},{10,... | collective-permute-start | bytes 442376 | tf_op jit(solution)/shard_map/ppermute | solution.py:43
  347.5 19.0 %collective-permute-start.56 = (bf16[1,2,2,1,96,768]{5,4,1,3,2,0:T(8,128)(2,1)S(1)}, bf16[1,2,2,1,96,768]{5,4,1,3,2,0:T(8,128)(2,1)S(1)}, u32[]{:S(2)}, u32[]{:S(2)}) collective-permute-start(bf16[1,2,2,1,96,768]{5,4,1,3,2,0:T(8,128)(2,1)S(1)} %get-tuple-element.565), channel_id=1, source_target_pairs={{0,4},{1,5},{2,6},{3,7},{4,0},{5,1},{6,2},{7,3},{8,12},{9,13},{10,... | collective-permute-start | bytes 1769480 | tf_op jit(solution)/shard_map/ppermute | solution.py:43
  349.0 19.4 %collective-permute-start.57 = (bf16[2,2,1,1,96,768]{5,4,1,3,2,0:T(8,128)(2,1)S(1)}, bf16[2,2,1,1,96,768]{5,4,1,3,2,0:T(8,128)(2,1)S(1)}, u32[]{:S(2)}, u32[]{:S(2)}) collective-permute-start(bf16[2,2,1,1,96,768]{5,4,1,3,2,0:T(8,128)(2,1)S(1)} %get-tuple-element.563), channel_id=1, source_target_pairs={{0,8},{1,9},{2,10},{3,11},{4,12},{5,13},{6,14},{7,15},{8,0},{9,1},... | collective-permute-start | bytes 1769480 | tf_op jit(solution)/shard_map/ppermute | solution.py:43
  349.4 17.1 %collective-permute-start.58 = (bf16[1,192,768]{2,1,0:T(8,128)(2,1)S(1)}, bf16[1,192,768]{2,1,0:T(8,128)(2,1)S(1)}, u32[]{:S(2)}, u32[]{:S(2)}) collective-permute-start(bf16[1,192,768]{2,1,0:T(8,128)(2,1)S(1)} %pad_maximum_fusion.17), channel_id=1, source_target_pairs={{0,16},{1,17},{2,18},{3,19},{4,20},{5,21},{6,22},{7,23},{8,24},{9,... | collective-permute-start | bytes 884744 | tf_op jit(solution)/shard_map/ppermute | solution.py:43
  374.2 22.0 %collective-permute-start.61 = (bf16[2,1,2,1,112,768]{5,4,3,2,1,0:T(8,128)(2,1)S(1)}, bf16[2,1,2,1,112,768]{5,4,3,2,1,0:T(8,128)(2,1)S(1)}, u32[]{:S(2)}, u32[]{:S(2)}) collective-permute-start(bf16[2,1,2,1,112,768]{5,4,3,2,1,0:T(8,128)(2,1)S(1)} %get-tuple-element.533), channel_id=1, source_target_pairs={{0,4},{1,5},{2,6},{3,7},{4,0},{5,1},{6,2},{7,3},{8,12},{9,13},{10,... | collective-permute-start | bytes 2064392 | tf_op jit(solution)/shard_map/ppermute | solution.py:43
  410.0 25.4 %collective-permute-start.72 = (bf16[2,192,768]{2,1,0:T(8,128)(2,1)S(1)}, bf16[2,192,768]{2,1,0:T(8,128)(2,1)S(1)}, u32[]{:S(2)}, u32[]{:S(2)}) collective-permute-start(bf16[2,192,768]{2,1,0:T(8,128)(2,1)S(1)} %pad_maximum_fusion.9.refs_0_), channel_id=1, source_target_pairs={{0,16},{1,17},{2,18},{3,19},{4,20},{5,21},{6,22},{7,23},{8,24},{9,... | collective-permute-start | bytes 1769480 | tf_op jit(solution)/shard_map/ppermute | solution.py:43
  420.6 20.4 %collective-permute-start.77 = (bf16[2,2,96,768]{3,2,1,0:T(8,128)(2,1)S(1)}, bf16[2,2,96,768]{3,2,1,0:T(8,128)(2,1)S(1)}, u32[]{:S(2)}, u32[]{:S(2)}) collective-permute-start(bf16[2,2,96,768]{3,2,1,0:T(8,128)(2,1)S(1)} %pad_maximum_fusion.11), channel_id=1, source_target_pairs={{0,4},{1,5},{2,6},{3,7},{4,0},{5,1},{6,2},{7,3},{8,12},{9,13},{10,... | collective-permute-start | bytes 1769480 | tf_op jit(solution)/shard_map/ppermute | solution.py:43
  422.8 29.7 %collective-permute-start.76 = (bf16[2,2,96,768]{3,2,1,0:T(8,128)(2,1)S(1)}, bf16[2,2,96,768]{3,2,1,0:T(8,128)(2,1)}, u32[]{:S(2)}, u32[]{:S(2)}) collective-permute-start(bf16[2,2,96,768]{3,2,1,0:T(8,128)(2,1)S(1)} %pad_maximum_fusion.10), channel_id=1, source_target_pairs={{0,8},{1,9},{2,10},{3,11},{4,12},{5,13},{6,14},{7,15},{8,0},{9,1},... | collective-permute-start | bytes 1769480 | tf_op jit(solution)/shard_map/ppermute | solution.py:43
  437.5 20.3 %collective-permute-start.74 = (bf16[2,96,768]{2,1,0:T(8,128)(2,1)S(1)}, bf16[2,96,768]{2,1,0:T(8,128)(2,1)S(1)}, u32[]{:S(2)}, u32[]{:S(2)}) collective-permute-start(bf16[2,96,768]{2,1,0:T(8,128)(2,1)S(1)} %get-tuple-element.589), channel_id=1, source_target_pairs={{0,4},{1,5},{2,6},{3,7},{4,0},{5,1},{6,2},{7,3},{8,12},{9,13},{10,... | collective-permute-start | bytes 884744 | tf_op jit(solution)/shard_map/ppermute | solution.py:43
  438.3 19.5 %collective-permute-start.75 = (bf16[2,96,768]{2,1,0:T(8,128)(2,1)S(1)}, bf16[2,96,768]{2,1,0:T(8,128)(2,1)S(1)}, u32[]{:S(2)}, u32[]{:S(2)}) collective-permute-start(bf16[2,96,768]{2,1,0:T(8,128)(2,1)S(1)} %get-tuple-element.588), channel_id=1, source_target_pairs={{0,8},{1,9},{2,10},{3,11},{4,12},{5,13},{6,14},{7,15},{8,0},{9,1},... | collective-permute-start | bytes 884744 | tf_op jit(solution)/shard_map/ppermute | solution.py:43
  438.3 19.5 %collective-permute-start.73 = (bf16[1,208,768]{2,1,0:T(8,128)(2,1)S(1)}, bf16[1,208,768]{2,1,0:T(8,128)(2,1)S(1)}, u32[]{:S(2)}, u32[]{:S(2)}) collective-permute-start(bf16[1,208,768]{2,1,0:T(8,128)(2,1)S(1)} %pad_maximum_fusion.16), channel_id=1, source_target_pairs={{0,16},{1,17},{2,18},{3,19},{4,20},{5,21},{6,22},{7,23},{8,24},{9,... | collective-permute-start | bytes 958472 | tf_op jit(solution)/shard_map/ppermute | solution.py:43
  459.8 22.0 %collective-permute-start.83 = (bf16[2,2,96,768]{3,2,1,0:T(8,128)(2,1)}, bf16[2,2,96,768]{3,2,1,0:T(8,128)(2,1)}, u32[]{:S(2)}, u32[]{:S(2)}) collective-permute-start(bf16[2,2,96,768]{3,2,1,0:T(8,128)(2,1)} %pad_maximum_fusion.15), channel_id=1, source_target_pairs={{0,4},{1,5},{2,6},{3,7},{4,0},{5,1},{6,2},{7,3},{8,12},{9,13},{10,... | collective-permute-start | bytes 1769480 | tf_op jit(solution)/shard_map/ppermute | solution.py:43
  462.7 19.1 %collective-permute-start.82 = (bf16[2,2,96,768]{3,2,1,0:T(8,128)(2,1)}, bf16[2,2,96,768]{3,2,1,0:T(8,128)(2,1)S(1)}, u32[]{:S(2)}, u32[]{:S(2)}) collective-permute-start(bf16[2,2,96,768]{3,2,1,0:T(8,128)(2,1)} %pad_maximum_fusion.14), channel_id=1, source_target_pairs={{0,8},{1,9},{2,10},{3,11},{4,12},{5,13},{6,14},{7,15},{8,0},{9,1},... | collective-permute-start | bytes 1769480 | tf_op jit(solution)/shard_map/ppermute | solution.py:43
  469.1 20.5 %collective-permute-start.84 = (bf16[2,1,96,768]{3,2,1,0:T(8,128)(2,1)S(1)}, bf16[2,1,96,768]{3,2,1,0:T(8,128)(2,1)S(1)}, u32[]{:S(2)}, u32[]{:S(2)}) collective-permute-start(bf16[2,1,96,768]{3,2,1,0:T(8,128)(2,1)S(1)} %pad_maximum_fusion.18), channel_id=1, source_target_pairs={{0,4},{1,5},{2,6},{3,7},{4,0},{5,1},{6,2},{7,3},{8,12},{9,13},{10,... | collective-permute-start | bytes 884744 | tf_op jit(solution)/shard_map/ppermute | solution.py:43
  471.2 18.4 %collective-permute-start.85 = (bf16[2,1,96,768]{3,2,1,0:T(8,128)(2,1)S(1)}, bf16[2,1,96,768]{3,2,1,0:T(8,128)(2,1)S(1)}, u32[]{:S(2)}, u32[]{:S(2)}) collective-permute-start(bf16[2,1,96,768]{3,2,1,0:T(8,128)(2,1)S(1)} %pad_maximum_fusion.19), channel_id=1, source_target_pairs={{0,8},{1,9},{2,10},{3,11},{4,12},{5,13},{6,14},{7,15},{8,0},{9,1},... | collective-permute-start | bytes 884744 | tf_op jit(solution)/shard_map/ppermute | solution.py:43
  471.4 24.7 %collective-permute-start.80 = (bf16[2,2,96,768]{3,2,1,0:T(8,128)(2,1)S(1)}, bf16[2,2,96,768]{3,2,1,0:T(8,128)(2,1)S(1)}, u32[]{:S(2)}, u32[]{:S(2)}) collective-permute-start(bf16[2,2,96,768]{3,2,1,0:T(8,128)(2,1)S(1)} %pad_maximum_fusion.12), channel_id=1, source_target_pairs={{0,4},{1,5},{2,6},{3,7},{4,0},{5,1},{6,2},{7,3},{8,12},{9,13},{10,... | collective-permute-start | bytes 1769480 | tf_op jit(solution)/shard_map/ppermute | solution.py:43
  (107 other events, 872.1 us)
Sparse Core Ops, SparseCore 0:
  52.0 80.4 all-gather.2

commit v5 on v4

--- a/solution.py
+++ b/solution.py
@@ -818,9 +818,9 @@
 
 AXES = {"x": (0, 0, ACROSS), "y": (3, 1, 0), "z": (2, 2, 0)}
 THIRDS = ("xyz", "yzx", "zxy")
-HALVES = ("xyz", "yzx")
+HALVES = ("xyz", "yxz")
 LAST = ("xyz", "yxz")
-CROSS = ("yxz", "zxy")
+CROSS = ("yxz", "xzy")
 
 
 def halves(array, axis):

time: 512 us -> 506 us (0.988)
  starting transfers between devices: 77.8 us -> 72.2 us
    ppermute x86, starting transfers between devices: 77.8 us -> 72.1 us  [swap(): return lax.ppermute(array, ('dp', 'head'), pairs)]
  transfers between devices with their start and end apart: 87 -> 87, of which waited for: 32 -> 35; matrix products, arithmetic and copies ran while one was open for 9% -> 9% of each run, Pallas kernels for 43% -> 43%
where the time goes in v5:
time: 506 us; the launch traced here: 501 us
  Pallas kernels  222 us (44%)
  waiting for transfers between devices  121 us (24%)
  starting transfers between devices  72.2 us (14%)
  other arithmetic  37.9 us (7%)
  local copies, waits for them, and re-layouts  31.1 us (6%)
  between operations  16 us (3%)
    ppermute x86, waiting for transfers between devices, swap(): return lax.ppermute(array, ('dp', 'head'), pairs)  121 us
    ppermute x86, starting transfers between devices, swap(): return lax.ppermute(array, ('dp', 'head'), pairs)  72.1 us
    pallas_call x2, Pallas kernels, feed_back(): pl.pallas_call(functools.partial(feed_back_kernel, len(pieces)), grid=(4,...  41.8 us
    pallas_call x3, Pallas kernels, mix_forward(): pl.pallas_call(functools.partial(mix_forward_kernel, local, cross, images...  40.8 us
    pallas_call x2, Pallas kernels, mix_back(): pl.pallas_call(functools.partial(mix_back_kernel, cross, images, len(qkv)...  40.7 us
    pallas_call x2, Pallas kernels, feed_rows(): pl.pallas_call(functools.partial(feed_rows_kernel, leaving), grid_spec=pl...  26.9 us
    pallas_call x2, Pallas kernels, mix_weights(): pl.pallas_call(functools.partial(mix_weights_kernel, more), grid_spec=plt...  19.1 us
    pallas_call x2, Pallas kernels, feed_weights(): pl.pallas_call(feed_weights_kernel, grid_spec=pltpu.PrefetchScalarGridSpe...  18.4 us
  transfers between devices with their start and end apart: 87, of which 35 were waited for; matrix products, arithmetic and copies ran while one was open for 9% of the time, Pallas kernels for 43%

profile of v5, /device:TPU:0, one launch (start us, length us, event | category | flops | bytes accessed | tf_op | source)
XLA Modules:
  0.0 500.6 jit_solution(6908527813589088628)
XLA Ops:
  9.8 2.9 collective-permute-start
  15.5 1.8 constant_dynamic-slice_fusion.10
  27.4 2.0 collective-permute-start.4
  33.8 13.4 %mix_forward.3 = (bf16[816,768]{1,0:T(8,128)(2,1)}, f32[816,768]{1,0:T(8,128)}, bf16[6,136,1152]{2,1,0:T(8,128)(2,1)}, bf16[816,384]{1,0:T(8,128)(2,1)}, f32[6,3,272]{2,1,0:T(4,128)}) custom-call(s32[9]{0:T(128)} %get-tuple-element.276.refs_0_.meta, f32[12]{0:T(128)} %fusion.11.refs_1_, bf16[816,768]{1,0:T(8,128)(2,1)} %bitcast.177, ...), custom_call_target="tpu_custom_call" | custom-call | flops 120000000 | bytes 1 | tf_op jit(solution)/shard_map/mix_forward/pallas_call | solution.py:259
  52.4 1.8 collective-permute-start.11
  56.9 14.6 %mix_forward.4 = (f32[816,768]{1,0:T(8,128)}, bf16[6,136,1152]{2,1,0:T(8,128)(2,1)}, bf16[816,384]{1,0:T(8,128)(2,1)}, f32[6,3,272]{2,1,0:T(4,128)}) custom-call(s32[9]{0:T(128)} %get-tuple-element.276.refs_0_.meta, f32[12]{0:T(128)} %fusion.11.refs_1_, f32[816,768]{1,0:T(8,128)} %get-tuple-element.289.refs_2_, ...), custom_call_target="tpu_custom_call" | custom-call | flops 120000000 | bytes 1 | tf_op jit(solution)/shard_map/mix_forward/pallas_call | solution.py:259
  79.2 13.2 %feed_rows.2 = (f32[816,768]{1,0:T(8,128)}, bf16[816,768]{1,0:T(8,128)(2,1)}, bf16[816,3072]{1,0:T(8,128)(2,1)}, bf16[816,3072]{1,0:T(8,128)(2,1)}, bf16[408,768]{1,0:T(8,128)(2,1)}) custom-call(s32[3]{0:T(128)} %pad_add_fusion.meta.place, f32[816,768]{1,0:T(8,128)} %get-tuple-element.305.x_ref, f32[1,768]{1,0:T(1,128)} %get-tuple-element.623.gain_ref, ...), custom_call_target="tpu_custom_call" | custom-call | flops 116000000 | bytes 1 | tf_op jit(solution)/shard_map/feed_rows/pallas_call | solution.py:578
  92.4 2.4 collective-permute-start.19
  98.5 13.7 %feed_rows.3 = (f32[816,768]{1,0:T(8,128)}, bf16[816,768]{1,0:T(8,128)(2,1)}, bf16[816,3072]{1,0:T(8,128)(2,1)}, bf16[816,3072]{1,0:T(8,128)(2,1)}, bf16[408,768]{1,0:T(8,128)(2,1)}) custom-call(s32[3]{0:T(128)} %pad_add_fusion.meta.place, ...), custom_call_target="tpu_custom_call", output_to_operand_aliasing={{0}: (14, {}), {1}: (15, {}), {2}: (16, {}), {3}: (17, {})} | custom-call | flops 116000000 | bytes 1 | tf_op jit(solution)/shard_map/feed_rows/pallas_call | solution.py:578
  112.3 2.7 collective-permute-done.21.refs_9_.refs_11_
  115.0 8.1 %collective-permute-done.19 = bf16[408,768]{1,0:T(8,128)(2,1)S(1)} collective-permute-done((bf16[408,768]{1,0:T(8,128)(2,1)}, bf16[408,768]{1,0:T(8,128)(2,1)S(1)}, u32[]{:S(2)}, u32[]{:S(2)}) %collective-permute-start.19) | collective-permute-done | bytes 626720 | tf_op jit(solution)/shard_map/ppermute | solution.py:43
  128.8 12.7 %mix_forward.5 = (bf16[408,768]{1,0:T(8,128)(2,1)}, f32[408,768]{1,0:T(8,128)}, bf16[3,136,2304]{2,1,0:T(8,128)(2,1)}, bf16[408,768]{1,0:T(8,128)(2,1)}, f32[3,6,272]{2,1,0:T(8,128)}) custom-call(s32[9]{0:T(128)} %get-tuple-element.626.refs_0_, f32[12]{0:T(128)} %fusion.11.refs_1_, f32[408,768]{1,0:T(8,128)} %convert_select_fusion.refs_2_.refs_3_, ...), custom_call_target="tpu_custom_call" | custom-call | flops 120000000 | bytes 1 | tf_op jit(solution)/shard_map/mix_forward/pallas_call | solution.py:259
  141.6 11.5 %feed_forward.1 = (bf16[408,768]{1,0:T(8,128)(2,1)}, bf16[408,768]{1,0:T(8,128)(2,1)}, bf16[408,3072]{1,0:T(8,128)(2,1)}, bf16[408,3072]{1,0:T(8,128)(2,1)}) custom-call(s32[9]{0:T(128)} %get-tuple-element.276.refs_0_.meta, f32[408,768]{1,0:T(8,128)} %get-tuple-element.333.x_ref, f32[1,768]{1,0:T(1,128)} %get-tuple-element.620.norm_ref.gain_ref, ...), custom_call_target="tpu_custom_call" | custom-call | flops 116000000 | bytes 1 | tf_op jit(solution)/shard_map/feed_forward/pallas_call | solution.py:516
  158.2 2.1 select_select_fusion
  160.2 16.0 %feed_back.2 = (f32[408,768]{1,0:T(8,128)}, f32[1,768]{1,0:T(1,128)}, bf16[408,768]{1,0:T(8,128)(2,1)}, bf16[408,3072]{1,0:T(8,128)(2,1)}, bf16[2,2,768,768]{3,2,1,0:T(8,128)(2,1)}) custom-call(s32[9]{0:T(128)} %get-tuple-element.276.refs_0_.meta, bf16[408,768]{1,0:T(8,128)(2,1)} %bitcast.182, f32[408,768]{1,0:T(8,128)} %get-tuple-element.333.x_ref, ...), custom_call_target="tpu_custom_call" | custom-call | flops 145000000 | bytes 1 | tf_op jit(solution)/shard_map/feed_back/pallas_call | solution.py:643
  177.7 7.6 %feed_weights.2 = bf16[2,2,768,768]{3,2,1,0:T(8,128)(2,1)} custom-call(s32[3]{0:T(128)} %pad_add_fusion.meta.place, bf16[408,3072]{1,0:T(8,128)(2,1)} %get-tuple-element.343.eu_ref, bf16[408,3072]{1,0:T(8,128)(2,1)} %get-tuple-element.339.h_ref.refs_0_, bf16[408,768]{1,0:T(8,128)(2,1)} %get-tuple-element.338.b_ref.refs_1_, ...), custom_call_target="tpu_custom_call" | custom-call | flops 70000000 | bytes 1 | tf_op jit(solution)/shard_map/feed_weights/pallas_call | solution.py:691
  185.3 4.6 collective-permute-done.32
  189.9 2.2 copy-done.18
  192.1 6.1 %glue.2 = (bf16[1,2,2,2,64,768]{5,4,3,2,1,0:T(8,128)(2,1)}, bf16[1,2,2,2,64,768]{5,4,3,2,1,0:T(8,128)(2,1)}, bf16[2,2,2,1,64,768]{5,4,3,2,1,0:T(8,128)(2,1)}, bf...) custom-call(bf16[2,2,2,2,192,768]{5,4,3,2,1,0:T(8,128)(2,1)} %bitcas, ...), custom_call_target="tpu_custom_call" | custom-call | flops 10000000 | bytes 1 | tf_op jit(solution)/shard_map/glue/pallas_call | solution.py:92
  199.8 15.5 %mix_back.2 = (f32[408,768]{1,0:T(8,128)}, f32[1,768]{1,0:T(1,128)}, bf16[408,2304]{1,0:T(8,128)(2,1)}, bf16[408,768]{1,0:T(8,128)(2,1)}, bf16[408,768]{1,0:T(8,128)(2,1)}, /*index=5*/bf16[408,768]{1,0:T(8,128)(2,1)}) custom-call(s32[9]{0:T(128)} %get-tuple-element.626.refs_0_, f32[12]{0:T(128)} %fusion.11.refs_1_, f32[408,768]{1,0:T(8,128)} %get-tuple-element.355.refs_2_, ...), custom_call_target="tpu_custom_call" | custom-call | flops 165000000 | bytes 1 | tf_op jit(solution)/shard_map/mix_back/pallas_call | solution.py:367
  215.3 2.3 collective-permute-done.33.refs_1_
  220.0 3.8 glue.3
  226.5 1.7 collective-permute-start.38
  230.7 7.8 %mix_weights.2 = (bf16[2,4,192,768]{3,2,1,0:T(8,128)(2,1)}, bf16[2,4,192,768]{3,2,1,0:T(8,128)(2,1)}) custom-call(s32[3]{0:T(128)} %pad_add_fusion.meta.place, bf16[408,2304]{1,0:T(8,128)(2,1)} %get-tuple-element.366.dqkv_ref, bf16[408,768]{1,0:T(8,128)(2,1)} %get-tuple-element.367.refs_0_, bf16[408,768]{1,0:T(8,128)(2,1)} %get-tuple-element.368.refs_1_, ...), custom_call_target="tpu_custom_call" | custom-call | flops 70000000 | bytes 1 | tf_op jit(solution)/shard_map/mix_weights/pallas_call | solution.py:442
  238.5 10.7 %collective-permute-done.38 = bf16[2,2,1,1,64,768]{5,4,1,3,2,0:T(8,128)(2,1)S(1)} collective-permute-done((bf16[2,2,1,1,64,768]{5,4,1,3,2,0:T(8,128)(2,1)}, bf16[2,2,1,1,64,768]{5,4,1,3,2,0:T(8,128)(2,1)S(1)}, u32[]{:S(2)}, u32[]{:S(2)}) %collective-permute-start.38) | collective-permute-done | bytes 393248 | tf_op jit(solution)/shard_map/ppermute | solution.py:43
  252.0 6.4 %turn_back.1 = (f32[816,768]{1,0:T(8,128)}, f32[1,768]{1,0:T(1,128)}) custom-call(s32[9]{0:T(128)} %get-tuple-element.276.refs_0_.meta, s32[1]{0:T(128)} %bitcast.2.side, f32[816,768]{1,0:T(8,128)} %get-tuple-element.326.encoded, f32[1,768]{1,0:T(1,128)} %get-tuple-element.621.next_gain_ref.gain, bf16[408,768]{1,0:T(8,128)(2,1)} %get-tuple-element.388.context, ...), custom_call_target="tpu_custom_call" | custom-call | flops 50000000 | bytes 1 | tf_op jit(solution)/shard_map/turn_back/pallas_call | solution.py:737
  262.8 25.8 %feed_back.3 = (f32[816,768]{1,0:T(8,128)}, f32[1,768]{1,0:T(1,128)}, bf16[816,768]{1,0:T(8,128)(2,1)}, bf16[816,3072]{1,0:T(8,128)(2,1)}, bf16[2,2,768,768]{3,2,1,0:T(8,128)(2,1)}) custom-call(s32[9]{0:T(128)} %get-tuple-element.276.refs_0_.meta, f32[816,768]{1,0:T(8,128)} %get-tuple-element.408.e_ref, f32[816,768]{1,0:T(8,128)} %get-tuple-element.305.x_ref, ...), custom_call_target="tpu_custom_call" | custom-call | flops 240000000 | bytes 1 | tf_op jit(solution)/shard_map/feed_back/pallas_call | solution.py:643
  293.3 10.8 %feed_weights.3 = bf16[2,2,768,768]{3,2,1,0:T(8,128)(2,1)} custom-call(s32[3]{0:T(128)} %pad_add_fusion.meta.place, bf16[816,3072]{1,0:T(8,128)(2,1)} %get-tuple-element.425.eu_ref, bf16[816,3072]{1,0:T(8,128)(2,1)} %get-tuple-element.411.h_ref.refs_0_, bf16[816,768]{1,0:T(8,128)(2,1)} %get-tuple-element.410.b_ref.refs_1_, ...), custom_call_target="tpu_custom_call" | custom-call | flops 100000000 | bytes 1 | tf_op jit(solution)/shard_map/feed_weights/pallas_call | solution.py:691
  304.1 1.7 collective-permute-done.48
  305.8 3.4 add.219
  318.2 25.2 %mix_back.3 = (f32[816,768]{1,0:T(8,128)}, f32[1,768]{1,0:T(1,128)}, bf16[816,2304]{1,0:T(8,128)(2,1)}, bf16[816,768]{1,0:T(8,128)(2,1)}) custom-call(s32[9]{0:T(128)} %get-tuple-element.276.refs_0_.meta, f32[12]{0:T(128)} %fusion.11.refs_1_, f32[816,768]{1,0:T(8,128)} %get-tuple-element.438.refs_2_, bf16[816,768]{1,0:T(8,128)(2,1)} %bitcast.178, ...), custom_call_target="tpu_custom_call" | custom-call | flops 280000000 | bytes 1 | tf_op jit(solution)/shard_map/mix_back/pallas_call | solution.py:367
  343.5 2.5 collective-permute-done.53
  349.7 11.3 %mix_weights.3 = (bf16[2,4,208,768]{3,2,1,0:T(8,128)(2,1)}, bf16[2,4,208,768]{3,2,1,0:T(8,128)(2,1)}) custom-call(s32[3]{0:T(128)} %pad_add_fusion.meta.place, bf16[816,2304]{1,0:T(8,128)(2,1)} %get-tuple-element.459.dqkv_ref, f32[1,768]{1,0:T(1,128)} %get-tuple-element.460.refs_0_, f32[1,768]{1,0:T(1,128)} %get-tuple-element.461.refs_1_, ...), custom_call_target="tpu_custom_call" | custom-call | flops 105000000 | bytes 1 | tf_op jit(solution)/shard_map/mix_weights/pallas_call | solution.py:442
  364.0 2.0 collective-permute-start.62
  369.5 7.2 %collective-permute-done.62 = bf16[1,2,1,1,96,768]{5,4,1,3,2,0:T(8,128)(2,1)S(1)} collective-permute-done((bf16[1,2,1,1,96,768]{5,4,1,3,2,0:T(8,128)(2,1)S(1)}, bf16[1,2,1,1,96,768]{5,4,1,3,2,0:T(8,128)(2,1)S(1)}, u32[]{:S(2)}, u32[]{:S(2)}) %collective-permute-start.62) | collective-permute-done | bytes 294944 | tf_op jit(solution)/shard_map/ppermute | solution.py:43
  378.1 4.2 collective-permute-done.63
  382.4 8.2 %collective-permute-done.60 = bf16[1,1,2,2,96,768]{5,4,3,2,1,0:T(8,128)(2,1)S(1)} collective-permute-done((bf16[1,1,2,2,96,768]{5,4,3,2,1,0:T(8,128)(2,1)S(1)}, bf16[1,1,2,2,96,768]{5,4,3,2,1,0:T(8,128)(2,1)S(1)}, u32[]{:S(2)}, u32[]{:S(2)}) %collective-permute-start.60) | collective-permute-done | bytes 589856 | tf_op jit(solution)/shard_map/ppermute | solution.py:43
  395.9 4.8 collective-permute-done.66
  405.2 5.0 collective-permute-done.71.refs_2_
  410.2 5.8 %collective-permute-done.67 = bf16[1,1,1,1,96,768]{5,4,3,2,1,0:T(8,128)(2,1)} collective-permute-done((bf16[1,1,1,1,96,768]{5,4,3,2,1,0:T(8,128)(2,1)}, bf16[1,1,1,1,96,768]{5,4,3,2,1,0:T(8,128)(2,1)}, u32[]{:S(2)}, u32[]{:S(2)}) %collective-permute-start.67) | collective-permute-done | bytes 147488 | tf_op jit(solution)/shard_map/ppermute | solution.py:43
  416.9 11.9 %collective-permute-done.72.refs_5_ = bf16[2,192,768]{2,1,0:T(8,128)(2,1)S(1)} collective-permute-done((bf16[2,192,768]{2,1,0:T(8,128)(2,1)S(1)}, bf16[2,192,768]{2,1,0:T(8,128)(2,1)S(1)}, u32[]{:S(2)}, u32[]{:S(2)}) %collective-permute-start.72) | collective-permute-done | bytes 589856 | tf_op jit(solution)/shard_map/ppermute | solution.py:43
  431.2 2.6 collective-permute-start.73
  434.6 10.8 %collective-permute-done.76.refs_3_ = bf16[2,2,96,768]{3,2,1,0:T(8,128)(2,1)} collective-permute-done((bf16[2,2,96,768]{3,2,1,0:T(8,128)(2,1)S(1)}, bf16[2,2,96,768]{3,2,1,0:T(8,128)(2,1)}, u32[]{:S(2)}, u32[]{:S(2)}) %collective-permute-start.76) | collective-permute-done | bytes 589856 | tf_op jit(solution)/shard_map/ppermute | solution.py:43
  455.6 2.0 collective-permute-start.82
  458.9 3.1 collective-permute-done.78
  465.4 9.3 %collective-permute-done.83.refs_9_ = bf16[2,2,96,768]{3,2,1,0:T(8,128)(2,1)} collective-permute-done((bf16[2,2,96,768]{3,2,1,0:T(8,128)(2,1)}, bf16[2,2,96,768]{3,2,1,0:T(8,128)(2,1)}, u32[]{:S(2)}, u32[]{:S(2)}) %collective-permute-start.83) | collective-permute-done | bytes 589856 | tf_op jit(solution)/shard_map/ppermute | solution.py:43
  476.3 7.0 %unpack_feed.1 = (f32[2,768,768]{2,1,0:T(8,128)}, f32[2,768,768]{2,1,0:T(8,128)}) custom-call(s32[3]{0:T(128)} %pad_add_fusion.meta.place, bf16[2,192,768]{2,1,0:T(8,128)(2,1)} %copy-done.6, bf16[2,96,768]{2,1,0:T(8,128)(2,1)} %copy-done.30, bf16[2,96,768]{2,1,0:T(8,128)(2,1)} %copy-done.31, bf16[2,2,96,768]{3,2,1,0:T(8,128)(2,1)} %collective-permute-done.76.refs_3_, ...), custom_call_target="tpu_custom_call" | custom-call | flops 50000000 | bytes 1 | tf_op jit(solution)/shard_map/unpack_feed/pallas_call | solution.py:796
  491.3 2.0 maximum_convert_fusion
  (426 shorter events, 130.5 us)
Async XLA Ops:
  7.2 134.3 %all-gather.3.cloned.1.call-start = ((), (), s32[]{:S(2)}) async-start(), calls=%async_computation | async-start | bytes 11796480 | tf_op jit(solution)/shard_map/all_gather | solution.py:1023
  25.3 23.3 %collective-permute-start.6 = (bf16[2,768,768]{2,1,0:T(8,128)(2,1)S(1)}, bf16[2,768,768]{2,1,0:T(8,128)(2,1)}, u32[]{:S(2)}, u32[]{:S(2)}) collective-permute-start(bf16[2,768,768]{2,1,0:T(8,128)(2,1)S(1)} %pad_maximum_fusion.refs_0_), channel_id=1, source_target_pairs={{0,1},{1,0},{2,3},{3,2},{4,5},{5,4},{6,7},{7,6},{8,9},{9,8},{10,11... | collective-permute-start | bytes 7077896 | tf_op jit(solution)/shard_map/ppermute | solution.py:43
  26.6 22.0 %collective-permute-start.5 = (bf16[2,192,768]{2,1,0:T(8,128)(2,1)}, bf16[2,192,768]{2,1,0:T(8,128)(2,1)}, u32[]{:S(2)}, u32[]{:S(2)}) collective-permute-start(bf16[2,192,768]{2,1,0:T(8,128)(2,1)} %constant_dynamic-slice_fusion.6), channel_id=1, source_target_pairs={{0,2},{1,3},{2,0},{3,1},{4,6},{5,7},{6,4},{7,5},{8,10},{9,11},{10,... | collective-permute-start | bytes 1769480 | tf_op jit(solution)/shard_map/ppermute | solution.py:43
  27.4 21.2 %collective-permute-start.4 = (bf16[192,768]{1,0:T(8,128)(2,1)}, bf16[192,768]{1,0:T(8,128)(2,1)}, u32[]{:S(2)}, u32[]{:S(2)}) collective-permute-start(bf16[192,768]{1,0:T(8,128)(2,1)} %dynamic-slice_bitcast_fusion.14), channel_id=1, source_target_pairs={{0,2},{1,3},{2,0},{3,1},{4,6},{5,7},{6,4},{7,5},{8,10},{9,11},{10,... | collective-permute-start | bytes 884744 | tf_op jit(solution)/shard_map/ppermute | solution.py:43
  29.4 19.2 %collective-permute-start.2 = (bf16[192,768]{1,0:T(8,128)(2,1)}, bf16[192,768]{1,0:T(8,128)(2,1)}, u32[]{:S(2)}, u32[]{:S(2)}) collective-permute-start(bf16[192,768]{1,0:T(8,128)(2,1)} %collective-permute-done.refs_4_.refs_11_), channel_id=1, source_target_pairs={{0,4},{1,5},{2,6},{3,7},{4,0},{5,1},{6,2},{7,3},{8,12},{9,13},{10,... | collective-permute-start | bytes 884744 | tf_op jit(solution)/shard_map/ppermute | solution.py:43
  31.6 17.0 %collective-permute-start.3 = (bf16[192,768]{1,0:T(8,128)(2,1)}, bf16[192,768]{1,0:T(8,128)(2,1)S(1)}, u32[]{:S(2)}, u32[]{:S(2)}) collective-permute-start(bf16[192,768]{1,0:T(8,128)(2,1)} %collective-permute-done.refs_4_.refs_11_), channel_id=1, source_target_pairs={{0,8},{1,9},{2,10},{3,11},{4,12},{5,13},{6,14},{7,15},{8,0},{9,1},... | collective-permute-start | bytes 884744 | tf_op jit(solution)/shard_map/ppermute | solution.py:43
  52.0 19.5 %collective-permute-start.13 = (bf16[2,192,768]{2,1,0:T(8,128)(2,1)S(1)}, bf16[2,192,768]{2,1,0:T(8,128)(2,1)S(1)}, u32[]{:S(2)}, u32[]{:S(2)}) collective-permute-start(bf16[2,192,768]{2,1,0:T(8,128)(2,1)S(1)} %constant_dynamic-slice_fusion.5), channel_id=1, source_target_pairs={{0,2},{1,3},{2,0},{3,1},{4,6},{5,7},{6,4},{7,5},{8,10},{9,11},{10,... | collective-permute-start | bytes 1769480 | tf_op jit(solution)/shard_map/ppermute | solution.py:43
  52.4 19.2 %collective-permute-start.11 = (bf16[2,192,768]{2,1,0:T(8,128)(2,1)}, bf16[2,192,768]{2,1,0:T(8,128)(2,1)S(1)}, u32[]{:S(2)}, u32[]{:S(2)}) collective-permute-start(bf16[2,192,768]{2,1,0:T(8,128)(2,1)} %collective-permute-done.5.refs_2_), channel_id=1, source_target_pairs={{0,4},{1,5},{2,6},{3,7},{4,0},{5,1},{6,2},{7,3},{8,12},{9,13},{10,... | collective-permute-start | bytes 1769480 | tf_op jit(solution)/shard_map/ppermute | solution.py:43
  54.2 17.4 %collective-permute-start.12 = (bf16[2,192,768]{2,1,0:T(8,128)(2,1)}, bf16[2,192,768]{2,1,0:T(8,128)(2,1)S(1)}, u32[]{:S(2)}, u32[]{:S(2)}) collective-permute-start(bf16[2,192,768]{2,1,0:T(8,128)(2,1)} %collective-permute-done.5.refs_2_), channel_id=1, source_target_pairs={{0,8},{1,9},{2,10},{3,11},{4,12},{5,13},{6,14},{7,15},{8,0},{9,1},... | collective-permute-start | bytes 1769480 | tf_op jit(solution)/shard_map/ppermute | solution.py:43
  72.7 53.3 %collective-permute-start.23 = (bf16[4,192,768]{2,1,0:T(8,128)(2,1)S(1)}, bf16[4,192,768]{2,1,0:T(8,128)(2,1)}, u32[]{:S(2)}, u32[]{:S(2)}) collective-permute-start(bf16[4,192,768]{2,1,0:T(8,128)(2,1)S(1)} %pad_maximum_fusion.5.refs_5_.refs_7_), channel_id=1, source_target_pairs={{0,1},{1,0},{2,3},{3,2},{4,5},{5,4},{6,7},{7,6},{8,9},{9,8},{10,11... | collective-permute-start | bytes 3538952 | tf_op jit(solution)/shard_map/ppermute | solution.py:43
  74.0 18.4 %collective-permute-start.18 = (bf16[192,768]{1,0:T(8,128)(2,1)S(1)}, bf16[192,768]{1,0:T(8,128)(2,1)S(1)}, u32[]{:S(2)}, u32[]{:S(2)}) collective-permute-start(bf16[192,768]{1,0:T(8,128)(2,1)S(1)} %get-tuple-element.572), channel_id=1, source_target_pairs={{0,2},{1,3},{2,0},{3,1},{4,6},{5,7},{6,4},{7,5},{8,10},{9,11},{10,... | collective-permute-start | bytes 884744 | tf_op jit(solution)/shard_map/ppermute | solution.py:43
  92.4 30.8 %collective-permute-start.19 = (bf16[408,768]{1,0:T(8,128)(2,1)}, bf16[408,768]{1,0:T(8,128)(2,1)S(1)}, u32[]{:S(2)}, u32[]{:S(2)}) collective-permute-start(bf16[408,768]{1,0:T(8,128)(2,1)} %get-tuple-element.322), channel_id=1, source_target_pairs={{0,16},{1,17},{2,18},{3,19},{4,20},{5,21},{6,22},{7,23},{8,24},{9,... | collective-permute-start | bytes 1880072 | tf_op jit(solution)/shard_map/ppermute | solution.py:43
  94.7 17.5 %collective-permute-start.22 = (bf16[192,768]{1,0:T(8,128)(2,1)S(1)}, bf16[192,768]{1,0:T(8,128)(2,1)S(1)}, u32[]{:S(2)}, u32[]{:S(2)}) collective-permute-start(bf16[192,768]{1,0:T(8,128)(2,1)S(1)} %get-tuple-element.571), channel_id=1, source_target_pairs={{0,2},{1,3},{2,0},{3,1},{4,6},{5,7},{6,4},{7,5},{8,10},{9,11},{10,... | collective-permute-start | bytes 884744 | tf_op jit(solution)/shard_map/ppermute | solution.py:43
  96.8 18.2 %collective-permute-start.21 = (bf16[192,768]{1,0:T(8,128)(2,1)S(1)}, bf16[192,768]{1,0:T(8,128)(2,1)S(1)}, u32[]{:S(2)}, u32[]{:S(2)}) collective-permute-start(bf16[192,768]{1,0:T(8,128)(2,1)S(1)} %collective-permute-done.18.refs_7_.refs_9_), channel_id=1, source_target_pairs={{0,8},{1,9},{2,10},{3,11},{4,12},{5,13},{6,14},{7,15},{8,0},{9,1},... | collective-permute-start | bytes 884744 | tf_op jit(solution)/shard_map/ppermute | solution.py:43
  124.0 30.0 %collective-permute-start.28 = (bf16[3,136,768]{2,1,0:T(8,128)(2,1)}, bf16[3,136,768]{2,1,0:T(8,128)(2,1)}, u32[]{:S(2)}, u32[]{:S(2)}) collective-permute-start(bf16[3,136,768]{2,1,0:T(8,128)(2,1)} %slice.314), channel_id=1, source_target_pairs={{0,16},{1,17},{2,18},{3,19},{4,20},{5,21},{6,22},{7,23},{8,24},{9,... | collective-permute-start | bytes 1880072 | tf_op jit(solution)/shard_map/ppermute | solution.py:43
  155.2 21.1 %collective-permute-start.29 = (bf16[1,136,768]{2,1,0:T(8,128)(2,1)S(1)}, bf16[1,136,768]{2,1,0:T(8,128)(2,1)S(1)}, u32[]{:S(2)}, u32[]{:S(2)}) collective-permute-start(bf16[1,136,768]{2,1,0:T(8,128)(2,1)S(1)} %get-tuple-element.579), channel_id=1, source_target_pairs={{0,16},{1,17},{2,18},{3,19},{4,20},{5,21},{6,22},{7,23},{8,24},{9,... | collective-permute-start | bytes 626696 | tf_op jit(solution)/shard_map/ppermute | solution.py:43
  156.6 20.3 %collective-permute-start.30 = (bf16[1,136,768]{2,1,0:T(8,128)(2,1)S(1)}, bf16[1,136,768]{2,1,0:T(8,128)(2,1)S(1)}, u32[]{:S(2)}, u32[]{:S(2)}) collective-permute-start(bf16[1,136,768]{2,1,0:T(8,128)(2,1)S(1)} %get-tuple-element.578), channel_id=1, source_target_pairs={{0,16},{1,17},{2,18},{3,19},{4,20},{5,21},{6,22},{7,23},{8,24},{9,... | collective-permute-start | bytes 626696 | tf_op jit(solution)/shard_map/ppermute | solution.py:43
  198.2 19.4 %collective-permute-start.33 = (bf16[1,2,2,2,64,768]{5,4,3,2,1,0:T(8,128)(2,1)}, bf16[1,2,2,2,64,768]{5,4,3,2,1,0:T(8,128)(2,1)S(1)}, u32[]{:S(2)}, u32[]{:S(2)}) collective-permute-start(bf16[1,2,2,2,64,768]{5,4,3,2,1,0:T(8,128)(2,1)} %get-tuple-element.361), channel_id=1, source_target_pairs={{0,2},{1,3},{2,0},{3,1},{4,6},{5,7},{6,4},{7,5},{8,10},{9,11},{10,... | collective-permute-start | bytes 2359304 | tf_op jit(solution)/shard_map/ppermute | solution.py:43
  199.5 19.1 %collective-permute-start.34 = (bf16[2,2,2,1,64,768]{5,4,3,2,1,0:T(8,128)(2,1)}, bf16[2,2,2,1,64,768]{5,4,3,2,1,0:T(8,128)(2,1)S(1)}, u32[]{:S(2)}, u32[]{:S(2)}) collective-permute-start(bf16[2,2,2,1,64,768]{5,4,3,2,1,0:T(8,128)(2,1)} %get-tuple-element.363), channel_id=1, source_target_pairs={{0,4},{1,5},{2,6},{3,7},{4,0},{5,1},{6,2},{7,3},{8,12},{9,13},{10,... | collective-permute-start | bytes 2359304 | tf_op jit(solution)/shard_map/ppermute | solution.py:43
  199.8 18.8 %collective-permute-start.35 = (bf16[2,2,1,2,64,768]{5,4,3,2,1,0:T(8,128)(2,1)}, bf16[2,2,1,2,64,768]{5,4,3,2,1,0:T(8,128)(2,1)S(1)}, u32[]{:S(2)}, u32[]{:S(2)}) collective-permute-start(bf16[2,2,1,2,64,768]{5,4,3,2,1,0:T(8,128)(2,1)} %get-tuple-element.365), channel_id=1, source_target_pairs={{0,8},{1,9},{2,10},{3,11},{4,12},{5,13},{6,14},{7,15},{8,0},{9,1},... | collective-permute-start | bytes 2359304 | tf_op jit(solution)/shard_map/ppermute | solution.py:43
  218.6 30.5 %collective-permute-start.36 = (bf16[408,768]{1,0:T(8,128)(2,1)}, bf16[408,768]{1,0:T(8,128)(2,1)S(1)}, u32[]{:S(2)}, u32[]{:S(2)}) collective-permute-start(bf16[408,768]{1,0:T(8,128)(2,1)} %get-tuple-element.371), channel_id=1, source_target_pairs={{0,16},{1,17},{2,18},{3,19},{4,20},{5,21},{6,22},{7,23},{8,24},{9,... | collective-permute-start | bytes 1880072 | tf_op jit(solution)/shard_map/ppermute | solution.py:43
  226.5 22.7 %collective-permute-start.38 = (bf16[2,2,1,1,64,768]{5,4,1,3,2,0:T(8,128)(2,1)}, bf16[2,2,1,1,64,768]{5,4,1,3,2,0:T(8,128)(2,1)S(1)}, u32[]{:S(2)}, u32[]{:S(2)}) collective-permute-start(bf16[2,2,1,1,64,768]{5,4,1,3,2,0:T(8,128)(2,1)} %bitcast.199), channel_id=1, source_target_pairs={{0,8},{1,9},{2,10},{3,11},{4,12},{5,13},{6,14},{7,15},{8,0},{9,1},... | collective-permute-start | bytes 1179656 | tf_op jit(solution)/shard_map/ppermute | solution.py:43
  228.2 20.9 %collective-permute-start.39 = (bf16[1,2,1,2,64,768]{5,4,3,2,1,0:T(8,128)(2,1)}, bf16[1,2,1,2,64,768]{5,4,3,2,1,0:T(8,128)(2,1)S(1)}, u32[]{:S(2)}, u32[]{:S(2)}) collective-permute-start(bf16[1,2,1,2,64,768]{5,4,3,2,1,0:T(8,128)(2,1)} %get-tuple-element.383), channel_id=1, source_target_pairs={{0,2},{1,3},{2,0},{3,1},{4,6},{5,7},{6,4},{7,5},{8,10},{9,11},{10,... | collective-permute-start | bytes 1179656 | tf_op jit(solution)/shard_map/ppermute | solution.py:43
  259.6 28.9 %collective-permute-start.45 = (bf16[2,1,2,1,96,768]{5,4,3,2,1,0:T(8,128)(2,1)S(1)}, bf16[2,1,2,1,96,768]{5,4,3,2,1,0:T(8,128)(2,1)S(1)}, u32[]{:S(2)}, u32[]{:S(2)}) collective-permute-start(bf16[2,1,2,1,96,768]{5,4,3,2,1,0:T(8,128)(2,1)S(1)} %get-tuple-element.569), channel_id=1, source_target_pairs={{0,4},{1,5},{2,6},{3,7},{4,0},{5,1},{6,2},{7,3},{8,12},{9,13},{10,... | collective-permute-start | bytes 1769480 | tf_op jit(solution)/shard_map/ppermute | solution.py:43
  260.1 28.5 %collective-permute-start.46 = (bf16[1,1,2,2,96,768]{5,4,3,2,1,0:T(8,128)(2,1)S(1)}, bf16[1,1,2,2,96,768]{5,4,3,2,1,0:T(8,128)(2,1)S(1)}, u32[]{:S(2)}, u32[]{:S(2)}) collective-permute-start(bf16[1,1,2,2,96,768]{5,4,3,2,1,0:T(8,128)(2,1)S(1)} %get-tuple-element.567), channel_id=1, source_target_pairs={{0,2},{1,3},{2,0},{3,1},{4,6},{5,7},{6,4},{7,5},{8,10},{9,11},{10,... | collective-permute-start | bytes 1769480 | tf_op jit(solution)/shard_map/ppermute | solution.py:43
  261.7 27.9 %collective-permute-start.44 = (bf16[2,192,768]{2,1,0:T(8,128)(2,1)S(1)}, bf16[2,192,768]{2,1,0:T(8,128)(2,1)S(1)}, u32[]{:S(2)}, u32[]{:S(2)}) collective-permute-start(bf16[2,192,768]{2,1,0:T(8,128)(2,1)S(1)} %pad_maximum_fusion.8), channel_id=1, source_target_pairs={{0,16},{1,17},{2,18},{3,19},{4,20},{5,21},{6,22},{7,23},{8,24},{9,... | collective-permute-start | bytes 1769480 | tf_op jit(solution)/shard_map/ppermute | solution.py:43
  289.6 16.2 %collective-permute-start.47 = (bf16[2,2,768,768]{3,2,1,0:T(8,128)(2,1)}, bf16[2,2,768,768]{3,2,1,0:T(8,128)(2,1)S(1)}, u32[]{:S(2)}, u32[]{:S(2)}) collective-permute-start(bf16[2,2,768,768]{3,2,1,0:T(8,128)(2,1)} %get-tuple-element.427), channel_id=1, source_target_pairs={{0,1},{1,0},{2,3},{3,2},{4,5},{5,4},{6,7},{7,6},{8,9},{9,8},{10,11... | collective-permute-start | bytes 14155784 | tf_op jit(solution)/shard_map/ppermute | solution.py:43
  312.3 33.6 %collective-permute-start.51 = (bf16[1,2,2,2,96,768]{5,4,1,3,2,0:T(8,128)(2,1)}, bf16[1,2,2,2,96,768]{5,4,1,3,2,0:T(8,128)(2,1)S(1)}, u32[]{:S(2)}, u32[]{:S(2)}) collective-permute-start(bf16[1,2,2,2,96,768]{5,4,1,3,2,0:T(8,128)(2,1)} %get-tuple-element.547), channel_id=1, source_target_pairs={{0,2},{1,3},{2,0},{3,1},{4,6},{5,7},{6,4},{7,5},{8,10},{9,11},{10,... | collective-permute-start | bytes 3538952 | tf_op jit(solution)/shard_map/ppermute | solution.py:43
  314.0 31.9 %collective-permute-start.52 = (bf16[2,2,2,1,96,768]{5,4,1,3,2,0:T(8,128)(2,1)}, bf16[2,2,2,1,96,768]{5,4,1,3,2,0:T(8,128)(2,1)S(1)}, u32[]{:S(2)}, u32[]{:S(2)}) collective-permute-start(bf16[2,2,2,1,96,768]{5,4,1,3,2,0:T(8,128)(2,1)} %get-tuple-element.545), channel_id=1, source_target_pairs={{0,4},{1,5},{2,6},{3,7},{4,0},{5,1},{6,2},{7,3},{8,12},{9,13},{10,... | collective-permute-start | bytes 3538952 | tf_op jit(solution)/shard_map/ppermute | solution.py:43
  315.7 30.2 %collective-permute-start.55 = (bf16[2,2,192,768]{3,2,1,0:T(8,128)(2,1)S(1)}, bf16[2,2,192,768]{3,2,1,0:T(8,128)(2,1)}, u32[]{:S(2)}, u32[]{:S(2)}) collective-permute-start(bf16[2,2,192,768]{3,2,1,0:T(8,128)(2,1)S(1)} %pad_maximum_fusion.6), channel_id=1, source_target_pairs={{0,8},{1,9},{2,10},{3,11},{4,12},{5,13},{6,14},{7,15},{8,0},{9,1},... | collective-permute-start | bytes 3538952 | tf_op jit(solution)/shard_map/ppermute | solution.py:43
  316.5 29.4 %collective-permute-start.53 = (bf16[1,1,1,1,96,768]{5,4,3,2,1,0:T(8,128)(2,1)S(1)}, bf16[1,1,1,1,96,768]{5,4,3,2,1,0:T(8,128)(2,1)S(1)}, u32[]{:S(2)}, u32[]{:S(2)}) collective-permute-start(bf16[1,1,1,1,96,768]{5,4,3,2,1,0:T(8,128)(2,1)S(1)} %get-tuple-element.616), channel_id=1, source_target_pairs={{0,8},{1,9},{2,10},{3,11},{4,12},{5,13},{6,14},{7,15},{8,0},{9,1},... | collective-permute-start | bytes 442376 | tf_op jit(solution)/shard_map/ppermute | solution.py:43
  317.9 28.1 %collective-permute-start.54 = (bf16[1,1,1,1,96,768]{5,4,3,2,1,0:T(8,128)(2,1)S(1)}, bf16[1,1,1,1,96,768]{5,4,3,2,1,0:T(8,128)(2,1)S(1)}, u32[]{:S(2)}, u32[]{:S(2)}) collective-permute-start(bf16[1,1,1,1,96,768]{5,4,3,2,1,0:T(8,128)(2,1)S(1)} %get-tuple-element.614), channel_id=1, source_target_pairs={{0,4},{1,5},{2,6},{3,7},{4,0},{5,1},{6,2},{7,3},{8,12},{9,13},{10,... | collective-permute-start | bytes 442376 | tf_op jit(solution)/shard_map/ppermute | solution.py:43
  346.7 16.0 %collective-permute-start.56 = (bf16[1,2,2,1,96,768]{5,4,1,3,2,0:T(8,128)(2,1)S(1)}, bf16[1,2,2,1,96,768]{5,4,1,3,2,0:T(8,128)(2,1)S(1)}, u32[]{:S(2)}, u32[]{:S(2)}) collective-permute-start(bf16[1,2,2,1,96,768]{5,4,1,3,2,0:T(8,128)(2,1)S(1)} %get-tuple-element.565), channel_id=1, source_target_pairs={{0,4},{1,5},{2,6},{3,7},{4,0},{5,1},{6,2},{7,3},{8,12},{9,13},{10,... | collective-permute-start | bytes 1769480 | tf_op jit(solution)/shard_map/ppermute | solution.py:43
  362.8 19.6 %collective-permute-start.64 = (bf16[1,96,768]{2,1,0:T(8,128)(2,1)S(1)}, bf16[1,96,768]{2,1,0:T(8,128)(2,1)S(1)}, u32[]{:S(2)}, u32[]{:S(2)}) collective-permute-start(bf16[1,96,768]{2,1,0:T(8,128)(2,1)S(1)} %get-tuple-element.613), channel_id=1, source_target_pairs={{0,4},{1,5},{2,6},{3,7},{4,0},{5,1},{6,2},{7,3},{8,12},{9,13},{10,... | collective-permute-start | bytes 442376 | tf_op jit(solution)/shard_map/ppermute | solution.py:43
  363.7 18.7 %collective-permute-start.65 = (bf16[1,96,768]{2,1,0:T(8,128)(2,1)S(1)}, bf16[1,96,768]{2,1,0:T(8,128)(2,1)S(1)}, u32[]{:S(2)}, u32[]{:S(2)}) collective-permute-start(bf16[1,96,768]{2,1,0:T(8,128)(2,1)S(1)} %get-tuple-element.612), channel_id=1, source_target_pairs={{0,8},{1,9},{2,10},{3,11},{4,12},{5,13},{6,14},{7,15},{8,0},{9,1},... | collective-permute-start | bytes 442376 | tf_op jit(solution)/shard_map/ppermute | solution.py:43
  366.1 16.2 %collective-permute-start.63 = (bf16[1,2,1,1,96,768]{5,4,1,3,2,0:T(8,128)(2,1)S(1)}, bf16[1,2,1,1,96,768]{5,4,1,3,2,0:T(8,128)(2,1)S(1)}, u32[]{:S(2)}, u32[]{:S(2)}) collective-permute-start(bf16[1,2,1,1,96,768]{5,4,1,3,2,0:T(8,128)(2,1)S(1)} %slice.418), channel_id=1, source_target_pairs={{0,8},{1,9},{2,10},{3,11},{4,12},{5,13},{6,14},{7,15},{8,0},{9,1},... | collective-permute-start | bytes 884744 | tf_op jit(solution)/shard_map/ppermute | solution.py:43
  368.5 22.1 %collective-permute-start.61 = (bf16[2,1,2,1,112,768]{5,4,3,2,1,0:T(8,128)(2,1)S(1)}, bf16[2,1,2,1,112,768]{5,4,3,2,1,0:T(8,128)(2,1)S(1)}, u32[]{:S(2)}, u32[]{:S(2)}) collective-permute-start(bf16[2,1,2,1,112,768]{5,4,3,2,1,0:T(8,128)(2,1)S(1)} %get-tuple-element.533), channel_id=1, source_target_pairs={{0,4},{1,5},{2,6},{3,7},{4,0},{5,1},{6,2},{7,3},{8,12},{9,13},{10,... | collective-permute-start | bytes 2064392 | tf_op jit(solution)/shard_map/ppermute | solution.py:43
  404.2 24.6 %collective-permute-start.72 = (bf16[2,192,768]{2,1,0:T(8,128)(2,1)S(1)}, bf16[2,192,768]{2,1,0:T(8,128)(2,1)S(1)}, u32[]{:S(2)}, u32[]{:S(2)}) collective-permute-start(bf16[2,192,768]{2,1,0:T(8,128)(2,1)S(1)} %pad_maximum_fusion.9.refs_0_), channel_id=1, source_target_pairs={{0,16},{1,17},{2,18},{3,19},{4,20},{5,21},{6,22},{7,23},{8,24},{9,... | collective-permute-start | bytes 1769480 | tf_op jit(solution)/shard_map/ppermute | solution.py:43
  416.1 17.7 %collective-permute-start.77 = (bf16[2,2,96,768]{3,2,1,0:T(8,128)(2,1)S(1)}, bf16[2,2,96,768]{3,2,1,0:T(8,128)(2,1)S(1)}, u32[]{:S(2)}, u32[]{:S(2)}) collective-permute-start(bf16[2,2,96,768]{3,2,1,0:T(8,128)(2,1)S(1)} %pad_maximum_fusion.11), channel_id=1, source_target_pairs={{0,4},{1,5},{2,6},{3,7},{4,0},{5,1},{6,2},{7,3},{8,12},{9,13},{10,... | collective-permute-start | bytes 1769480 | tf_op jit(solution)/shard_map/ppermute | solution.py:43
  416.9 28.5 %collective-permute-start.76 = (bf16[2,2,96,768]{3,2,1,0:T(8,128)(2,1)S(1)}, bf16[2,2,96,768]{3,2,1,0:T(8,128)(2,1)}, u32[]{:S(2)}, u32[]{:S(2)}) collective-permute-start(bf16[2,2,96,768]{3,2,1,0:T(8,128)(2,1)S(1)} %pad_maximum_fusion.10), channel_id=1, source_target_pairs={{0,8},{1,9},{2,10},{3,11},{4,12},{5,13},{6,14},{7,15},{8,0},{9,1},... | collective-permute-start | bytes 1769480 | tf_op jit(solution)/shard_map/ppermute | solution.py:43
  431.0 19.8 %collective-permute-start.74 = (bf16[2,96,768]{2,1,0:T(8,128)(2,1)S(1)}, bf16[2,96,768]{2,1,0:T(8,128)(2,1)S(1)}, u32[]{:S(2)}, u32[]{:S(2)}) collective-permute-start(bf16[2,96,768]{2,1,0:T(8,128)(2,1)S(1)} %get-tuple-element.589), channel_id=1, source_target_pairs={{0,4},{1,5},{2,6},{3,7},{4,0},{5,1},{6,2},{7,3},{8,12},{9,13},{10,... | collective-permute-start | bytes 884744 | tf_op jit(solution)/shard_map/ppermute | solution.py:43
  431.2 19.6 %collective-permute-start.75 = (bf16[2,96,768]{2,1,0:T(8,128)(2,1)S(1)}, bf16[2,96,768]{2,1,0:T(8,128)(2,1)S(1)}, u32[]{:S(2)}, u32[]{:S(2)}) collective-permute-start(bf16[2,96,768]{2,1,0:T(8,128)(2,1)S(1)} %get-tuple-element.588), channel_id=1, source_target_pairs={{0,8},{1,9},{2,10},{3,11},{4,12},{5,13},{6,14},{7,15},{8,0},{9,1},... | collective-permute-start | bytes 884744 | tf_op jit(solution)/shard_map/ppermute | solution.py:43
  431.2 19.6 %collective-permute-start.73 = (bf16[1,208,768]{2,1,0:T(8,128)(2,1)S(1)}, bf16[1,208,768]{2,1,0:T(8,128)(2,1)S(1)}, u32[]{:S(2)}, u32[]{:S(2)}) collective-permute-start(bf16[1,208,768]{2,1,0:T(8,128)(2,1)S(1)} %pad_maximum_fusion.16), channel_id=1, source_target_pairs={{0,16},{1,17},{2,18},{3,19},{4,20},{5,21},{6,22},{7,23},{8,24},{9,... | collective-permute-start | bytes 958472 | tf_op jit(solution)/shard_map/ppermute | solution.py:43
  453.7 21.0 %collective-permute-start.83 = (bf16[2,2,96,768]{3,2,1,0:T(8,128)(2,1)}, bf16[2,2,96,768]{3,2,1,0:T(8,128)(2,1)}, u32[]{:S(2)}, u32[]{:S(2)}) collective-permute-start(bf16[2,2,96,768]{3,2,1,0:T(8,128)(2,1)} %pad_maximum_fusion.15), channel_id=1, source_target_pairs={{0,4},{1,5},{2,6},{3,7},{4,0},{5,1},{6,2},{7,3},{8,12},{9,13},{10,... | collective-permute-start | bytes 1769480 | tf_op jit(solution)/shard_map/ppermute | solution.py:43
  455.6 19.9 %collective-permute-start.82 = (bf16[2,2,96,768]{3,2,1,0:T(8,128)(2,1)}, bf16[2,2,96,768]{3,2,1,0:T(8,128)(2,1)S(1)}, u32[]{:S(2)}, u32[]{:S(2)}) collective-permute-start(bf16[2,2,96,768]{3,2,1,0:T(8,128)(2,1)} %pad_maximum_fusion.14), channel_id=1, source_target_pairs={{0,8},{1,9},{2,10},{3,11},{4,12},{5,13},{6,14},{7,15},{8,0},{9,1},... | collective-permute-start | bytes 1769480 | tf_op jit(solution)/shard_map/ppermute | solution.py:43
  463.0 20.4 %collective-permute-start.84 = (bf16[2,1,96,768]{3,2,1,0:T(8,128)(2,1)S(1)}, bf16[2,1,96,768]{3,2,1,0:T(8,128)(2,1)S(1)}, u32[]{:S(2)}, u32[]{:S(2)}) collective-permute-start(bf16[2,1,96,768]{3,2,1,0:T(8,128)(2,1)S(1)} %pad_maximum_fusion.18), channel_id=1, source_target_pairs={{0,4},{1,5},{2,6},{3,7},{4,0},{5,1},{6,2},{7,3},{8,12},{9,13},{10,... | collective-permute-start | bytes 884744 | tf_op jit(solution)/shard_map/ppermute | solution.py:43
  464.2 19.3 %collective-permute-start.85 = (bf16[2,1,96,768]{3,2,1,0:T(8,128)(2,1)S(1)}, bf16[2,1,96,768]{3,2,1,0:T(8,128)(2,1)S(1)}, u32[]{:S(2)}, u32[]{:S(2)}) collective-permute-start(bf16[2,1,96,768]{3,2,1,0:T(8,128)(2,1)S(1)} %pad_maximum_fusion.19), channel_id=1, source_target_pairs={{0,8},{1,9},{2,10},{3,11},{4,12},{5,13},{6,14},{7,15},{8,0},{9,1},... | collective-permute-start | bytes 884744 | tf_op jit(solution)/shard_map/ppermute | solution.py:43
  464.3 23.4 %collective-permute-start.80 = (bf16[2,2,96,768]{3,2,1,0:T(8,128)(2,1)S(1)}, bf16[2,2,96,768]{3,2,1,0:T(8,128)(2,1)S(1)}, u32[]{:S(2)}, u32[]{:S(2)}) collective-permute-start(bf16[2,2,96,768]{3,2,1,0:T(8,128)(2,1)S(1)} %pad_maximum_fusion.12), channel_id=1, source_target_pairs={{0,4},{1,5},{2,6},{3,7},{4,0},{5,1},{6,2},{7,3},{8,12},{9,13},{10,... | collective-permute-start | bytes 1769480 | tf_op jit(solution)/shard_map/ppermute | solution.py:43
  (107 other events, 861.3 us)
Sparse Core Ops, SparseCore 0:
  52.0 80.4 all-gather.2
